TPU v7x, 32 devices: a whole 2x2x4 slice. The times are simulated.
32 devices in a mesh: seq: 8 (over z, x), fsdp: 4 (over y, core).
Axes of the slice: x: 2, y: 2, z: 4, core: 2. Of those that a mesh axis runs over, the one named last changes fastest.
Arguments:
- hidden: bfloat16 [4, 2048, 1536], P('fsdp', 'seq'), may hold values from -6 to 6
- lengths: int32 [4], P('fsdp'), may hold values from 512 to 2048, as said below
- norm_gain: bfloat16 [1536], P('fsdp'), may hold values from 0.5 to 1.5
- in_weight: bfloat16 [1536, 6448], P('fsdp'), may hold values from -0.15625 to 0.15625
- conv_weight: bfloat16 [4, 3328], P(None, 'fsdp'), may hold values from -3 to 3
- conv_bias: bfloat16 [3328], P('fsdp'), may hold values from -3 to 3
- dt_bias: bfloat16 [48], P('fsdp'), may hold values from -5 to -3
- a_log: bfloat16 [48], P('fsdp'), may hold values from -9 to 1
- skip_d: bfloat16 [48], P('fsdp'), may hold values from 0.5 to 1.5
- gate_gain: bfloat16 [3072], P('fsdp'), may hold values from 0.5 to 1.5
- out_weight: bfloat16 [3072, 1536], P('fsdp'), may hold values from -0.109375 to 0.109375
- out_grad: bfloat16 [4, 2048, 1536], P('fsdp', 'seq'), may hold values from -6 to 6
Outputs:
- output: bfloat16 [4, 2048, 1536], P('fsdp', 'seq')
- hidden_grad: bfloat16 [4, 2048, 1536], P('fsdp', 'seq')
- norm_gain_grad: float32 [1536], P('fsdp')
- in_weight_grad: float32 [1536, 6448], P('fsdp')
- conv_weight_grad: float32 [4, 3328], P(None, 'fsdp')
- conv_bias_grad: float32 [3328], P('fsdp')
- dt_bias_grad: float32 [48], P('fsdp')
- a_log_grad: float32 [48], P('fsdp')
- skip_d_grad: float32 [48], P('fsdp')
- gate_gain_grad: float32 [3072], P('fsdp')
- out_weight_grad: float32 [3072, 1536], P('fsdp')
Inputs may be any that keep to these rules, and one draw needn't show every extreme that they name: `lengths`: a slot's live tokens are its first ones; in every draw one slot is full and one holds 512 tokens.
All inputs are finite; a program needn't handle non-finite values.
Results may differ from a plain program's by a relative error of at most 0.0075.
The roundings to bfloat16 on the way count: a program that leaves them out, or rounds other values in their place, can miss the bound.
Values may be sent and summed in bfloat16 or wider, within the bound.
No kernel may reach another device: no remote copies, remote signals or barrier semaphores. Data moves between devices by JAX's collectives and lax.ppermute only.
A program may use at most 256 MiB of HBM per device.

v0:
```python
from functools import partial

import jax
import jax.numpy as jnp
from jax import lax
from jax.sharding import PartitionSpec as P

HEADS = 48
HEADDIM = 64
STATE = 128
CONV = 4
INNER = 3072
CHANNELS = 3328
PROJ = 6448


epsilon = 1e-05


def from_behind(block, axis, distance):
    devices = range(lax.axis_size(axis))
    route = [(i - distance, i) for i in devices if i - distance in devices]
    return lax.ppermute(block, axis, route)


def entering(x, axis, combine, identity, reverse):
    size, mine = (lax.axis_size(axis), lax.axis_index(axis))
    everything = jax.tree.map(lambda part: lax.all_gather(part, axis), x)
    start = jax.tree.map(
        lambda part, zero: jnp.broadcast_to(jnp.asarray(zero, part.dtype), part.shape), x, identity
    )

    def step(k, before):
        at = size - 1 - k if reverse else k
        reached = at > mine if reverse else at < mine
        new = combine(before, jax.tree.map(lambda part: part[at], everything))
        return jax.tree.map(lambda a, b: jnp.where(reached, a, b), new, before)

    return lax.fori_loop(0, size, step, start)


def rms_scale(values, gain):
    return values * lax.rsqrt(jnp.mean(values * values, axis=-1, keepdims=True) + epsilon) * gain


def conv_silu(window, conv_weight, conv_bias):
    count = window.shape[1] - CONV + 1
    summed = conv_bias
    for offset in range(CONV):
        summed = summed + conv_weight[offset] * window[:, offset : offset + count]
    return jax.nn.silu(summed)


def step_sizes(dt_raw, dt_bias, a_log):
    step_size = jax.nn.softplus(dt_raw + dt_bias)
    return (step_size, jnp.cumsum(step_size * -jnp.exp(a_log), axis=1))


def gated_norm(mixer, gate_part, gate_gain):
    return rms_scale(mixer * jax.nn.silu(gate_part), gate_gain)


def link_states(earlier, later):
    return (earlier[0] * later[0], later[0][:, :, None, None] * earlier[1] + later[1])


def decay_table(head_decay):
    length = head_decay.shape[1]
    later = lax.broadcasted_iota(jnp.int32, (length, length), 0)
    earlier = lax.broadcasted_iota(jnp.int32, (length, length), 1)
    causal = (later >= earlier)[None]
    exponent = head_decay[:, :, None] - head_decay[:, None, :]
    return jnp.where(causal, jnp.exp(jnp.where(causal, exponent, 0.0)), 0.0)


def state_slot(bundle):
    heads_x, proj_b, step_size, log_decay = bundle
    to_end = jnp.exp(log_decay[-1:] - log_decay)
    weighted = (heads_x.astype(jnp.float32) * (to_end * step_size)[:, :, None]).astype(jnp.bfloat16)
    return jnp.einsum("thp,tn->hpn", weighted, proj_b, preferred_element_type=jnp.float32)


def mix_slot(bundle, skip_gain):
    heads_x, proj_b, proj_c, step_size, log_decay, incoming = bundle
    scores = jnp.einsum("tn,sn->ts", proj_c, proj_b, preferred_element_type=jnp.float32)
    decays = decay_table(log_decay.T)
    mixing = (scores[None] * decays * step_size.T[:, None, :]).astype(jnp.bfloat16)
    intra = jnp.einsum("hts,shp->thp", mixing, heads_x, preferred_element_type=jnp.float32)
    reached = jnp.einsum(
        "tn,hpn->thp", proj_c, incoming.astype(jnp.bfloat16), preferred_element_type=jnp.float32
    )
    return (
        intra
        + jnp.exp(log_decay)[:, :, None] * reached
        + skip_gain[:, None] * heads_x.astype(jnp.float32)
    )


def slot_back(bundle, skip_gain):
    heads_x, proj_b, proj_c, step_size, log_decay, incoming, grad_y, grad_reach, chain_grad = bundle
    grad_yf = grad_y.astype(jnp.float32)
    x_float = heads_x.astype(jnp.float32)
    grad_skip = jnp.sum(grad_yf * x_float, axis=(0, 2))
    grad_x = skip_gain[:, None] * grad_yf
    incoming_b = incoming.astype(jnp.bfloat16)
    from_start = jnp.exp(log_decay)
    reached = jnp.einsum("tn,hpn->thp", proj_c, incoming_b, preferred_element_type=jnp.float32)
    grad_cum = from_start * jnp.sum(grad_yf * reached, axis=2)
    grad_c = jnp.einsum("thp,hpn->tn", grad_reach, incoming_b, preferred_element_type=jnp.float32)
    scores = jnp.einsum("tn,sn->ts", proj_c, proj_b, preferred_element_type=jnp.float32)
    decays = decay_table(log_decay.T)
    step_heads = step_size.T[:, None, :]
    mixing = (scores[None] * decays * step_heads).astype(jnp.bfloat16)
    grad_mix = jnp.einsum("thp,shp->hts", grad_y, heads_x, preferred_element_type=jnp.float32)
    grad_x = grad_x + jnp.einsum("hts,thp->shp", mixing, grad_y, preferred_element_type=jnp.float32)
    grad_scores = jnp.sum(grad_mix * decays * step_heads, axis=0).astype(jnp.bfloat16)
    grad_step = jnp.sum(grad_mix * scores[None] * decays, axis=1).T
    grad_exp = grad_mix * scores[None] * step_heads * decays
    grad_cum = grad_cum + (jnp.sum(grad_exp, axis=2) - jnp.sum(grad_exp, axis=1)).T
    grad_c = grad_c + jnp.einsum(
        "ts,sn->tn", grad_scores, proj_b, preferred_element_type=jnp.float32
    )
    grad_b = jnp.einsum("ts,tn->sn", grad_scores, proj_c, preferred_element_type=jnp.float32)
    to_end = jnp.exp(log_decay[-1:] - log_decay)
    factor = to_end * step_size
    weighted = (x_float * factor[:, :, None]).astype(jnp.bfloat16)
    grad_fresh = chain_grad.astype(jnp.bfloat16)
    grad_weighted = jnp.einsum(
        "hpn,tn->thp", grad_fresh, proj_b, preferred_element_type=jnp.float32
    )
    grad_b = grad_b + jnp.einsum(
        "thp,hpn->tn", weighted, grad_fresh, preferred_element_type=jnp.float32
    )
    grad_x = grad_x + grad_weighted * factor[:, :, None]
    grad_factor = jnp.sum(grad_weighted * x_float, axis=2)
    grad_step = grad_step + grad_factor * to_end
    grad_tail = grad_factor * step_size * to_end
    through = jnp.exp(log_decay[-1])
    grad_end = jnp.sum(grad_tail, axis=0) + through * jnp.sum(chain_grad * incoming, axis=(1, 2))
    last_row = lax.broadcasted_iota(jnp.int32, log_decay.shape, 0) == log_decay.shape[0] - 1
    grad_cum = grad_cum - grad_tail + jnp.where(last_row, grad_end[None, :], 0.0)
    return (grad_x, grad_b, grad_c, grad_step, grad_cum, grad_skip)


def local(
    hidden,
    lengths,
    norm_gain,
    in_weight,
    conv_weight,
    conv_bias,
    dt_bias,
    a_log,
    skip_d,
    gate_gain,
    out_weight,
    out_grad,
):
    slot_count, row_count, model_width = hidden.shape
    gathered = (
        lax.all_gather(norm_gain, "fsdp", axis=0, tiled=True),
        lax.all_gather(in_weight, "fsdp", axis=0, tiled=True),
        lax.all_gather(conv_weight, "fsdp", axis=1, tiled=True),
        lax.all_gather(conv_bias, "fsdp", axis=0, tiled=True),
        lax.all_gather(dt_bias, "fsdp", axis=0, tiled=True),
        lax.all_gather(a_log, "fsdp", axis=0, tiled=True),
        lax.all_gather(skip_d, "fsdp", axis=0, tiled=True),
        lax.all_gather(gate_gain, "fsdp", axis=0, tiled=True),
        lax.all_gather(out_weight, "fsdp", axis=0, tiled=True),
    )
    weight_in = gathered[1]
    weight_out = gathered[8]
    gain_norm = gathered[0].astype(jnp.float32)
    conv_taps = gathered[2].astype(jnp.float32)
    conv_shift = gathered[3].astype(jnp.float32)
    step_bias = gathered[4].astype(jnp.float32)
    rate_log = gathered[5].astype(jnp.float32)
    skip_gain = gathered[6].astype(jnp.float32)
    gain_gate = gathered[7].astype(jnp.float32)
    tokens = hidden.astype(jnp.float32)
    normed, pull_norm = jax.vjp(rms_scale, tokens, gain_norm)
    normed_flat = normed.astype(jnp.bfloat16).reshape(slot_count * row_count, model_width)
    projected = jnp.dot(normed_flat, weight_in, preferred_element_type=jnp.float32).astype(
        jnp.bfloat16
    )
    projected = projected.reshape(slot_count, row_count, PROJ)
    gate_part = projected[:, :, :INNER]
    conv_in = projected[:, :, INNER : INNER + CHANNELS]
    dt_raw = projected[:, :, INNER + CHANNELS :]
    edge_rows = from_behind(conv_in[:, row_count - CONV + 1 :], "seq", 1)
    window = jnp.concatenate([edge_rows, conv_in], axis=1).astype(jnp.float32)
    conv_out, pull_conv = jax.vjp(conv_silu, window, conv_taps, conv_shift)
    conv_low = conv_out.astype(jnp.bfloat16)
    heads_x = conv_low[:, :, :INNER].reshape(slot_count, row_count, HEADS, HEADDIM)
    proj_b = conv_low[:, :, INNER : INNER + STATE]
    proj_c = conv_low[:, :, INNER + STATE :]
    (step_size, log_decay), pull_steps = jax.vjp(
        step_sizes, dt_raw.astype(jnp.float32), step_bias, rate_log
    )
    fresh_state = lax.map(state_slot, (heads_x, proj_b, step_size, log_decay))
    through = jnp.exp(log_decay[:, -1, :])
    identity = (jnp.ones_like(through), jnp.zeros_like(fresh_state))
    incoming = entering((through, fresh_state), "seq", link_states, identity, False)[1]
    mixer = lax.map(
        partial(mix_slot, skip_gain=skip_gain),
        (heads_x, proj_b, proj_c, step_size, log_decay, incoming),
    )
    mixed, pull_gate = jax.vjp(
        gated_norm,
        mixer.reshape(slot_count, row_count, INNER),
        gate_part.astype(jnp.float32),
        gain_gate,
    )
    mixed_flat = mixed.astype(jnp.bfloat16).reshape(slot_count * row_count, INNER)
    summed_out = tokens + jnp.dot(
        mixed_flat, weight_out, preferred_element_type=jnp.float32
    ).reshape(slot_count, row_count, model_width)
    output = summed_out.astype(jnp.bfloat16)
    position = lax.axis_index("seq") * row_count + lax.broadcasted_iota(
        jnp.int32, (slot_count, row_count), 1
    )
    live_rows = position < lengths[:, None]
    grad_out = jnp.where(live_rows[:, :, None], out_grad, jnp.zeros_like(out_grad))
    weight_in_back, weight_out_back = (
        lax.all_gather(in_weight, "fsdp", axis=0, tiled=True),
        lax.all_gather(out_weight, "fsdp", axis=0, tiled=True),
    )
    grad_flat = grad_out.reshape(slot_count * row_count, model_width)
    grad_mixed = jnp.einsum(
        "td,id->ti", grad_flat, weight_out_back, preferred_element_type=jnp.float32
    )
    grad_mixer, grad_gate, grad_g_gate = pull_gate(grad_mixed.reshape(slot_count, row_count, INNER))
    grad_y = grad_mixer.astype(jnp.bfloat16).reshape(slot_count, row_count, HEADS, HEADDIM)
    grad_reach = (grad_y.astype(jnp.float32) * jnp.exp(log_decay)[:, :, :, None]).astype(
        jnp.bfloat16
    )
    direct = jnp.einsum("kthp,ktn->khpn", grad_reach, proj_c, preferred_element_type=jnp.float32)
    chain_grad = entering((through, direct), "seq", link_states, identity, True)[1]
    pieces = lax.map(
        partial(slot_back, skip_gain=skip_gain),
        (heads_x, proj_b, proj_c, step_size, log_decay, incoming, grad_y, grad_reach, chain_grad),
    )
    grad_x, grad_b, grad_c, grad_step, grad_cum, grad_skip_rows = pieces
    grad_skip = jnp.sum(grad_skip_rows, axis=0)
    grad_dt_raw, grad_step_bias, grad_rate = pull_steps((grad_step, grad_cum))
    grad_conv_out = jnp.concatenate(
        [grad_x.reshape(slot_count, row_count, INNER), grad_b, grad_c], axis=2
    )
    grad_window, grad_taps, grad_shift = pull_conv(grad_conv_out)
    back_edge = from_behind(grad_window[:, : CONV - 1], "seq", -1)
    grad_conv_in = grad_window[:, CONV - 1 :] + jnp.concatenate(
        [jnp.zeros((slot_count, row_count - CONV + 1, CHANNELS), jnp.float32), back_edge], axis=1
    )
    grad_proj = (
        jnp.concatenate([grad_gate, grad_conv_in, grad_dt_raw], axis=2)
        .astype(jnp.bfloat16)
        .reshape(slot_count * row_count, PROJ)
    )
    grad_normed = jnp.einsum(
        "tj,dj->td", grad_proj, weight_in_back, preferred_element_type=jnp.float32
    )
    grad_tokens, grad_g_norm = pull_norm(grad_normed.reshape(slot_count, row_count, model_width))
    hidden_grad = (grad_tokens + grad_out.astype(jnp.float32)).astype(jnp.bfloat16)
    grad_w_out = jnp.einsum("ti,td->id", mixed_flat, grad_flat, preferred_element_type=jnp.float32)
    grad_w_in = jnp.einsum("td,tj->dj", normed_flat, grad_proj, preferred_element_type=jnp.float32)
    shares = (
        lax.psum_scatter(grad_g_norm, "fsdp", scatter_dimension=0, tiled=True),
        lax.psum_scatter(grad_w_in, "fsdp", scatter_dimension=0, tiled=True),
        lax.psum_scatter(grad_taps, "fsdp", scatter_dimension=1, tiled=True),
        lax.psum_scatter(grad_shift, "fsdp", scatter_dimension=0, tiled=True),
        lax.psum_scatter(grad_step_bias, "fsdp", scatter_dimension=0, tiled=True),
        lax.psum_scatter(grad_rate, "fsdp", scatter_dimension=0, tiled=True),
        lax.psum_scatter(grad_skip, "fsdp", scatter_dimension=0, tiled=True),
        lax.psum_scatter(grad_g_gate, "fsdp", scatter_dimension=0, tiled=True),
        lax.psum_scatter(grad_w_out, "fsdp", scatter_dimension=0, tiled=True),
    )
    totals = lax.psum(
        (
            shares[0],
            shares[1],
            shares[2],
            shares[3],
            shares[4],
            shares[5],
            shares[6],
            shares[7],
            shares[8],
        ),
        "seq",
    )
    return (
        output,
        hidden_grad,
        totals[0],
        totals[1],
        totals[2],
        totals[3],
        totals[4],
        totals[5],
        totals[6],
        totals[7],
        totals[8],
    )


def solution(mesh):
    placed = (
        P("fsdp", "seq", None),
        P("fsdp"),
        P("fsdp"),
        P("fsdp", None),
        P(None, "fsdp"),
        P("fsdp"),
        P("fsdp"),
        P("fsdp"),
        P("fsdp"),
        P("fsdp"),
        P("fsdp", None),
        P("fsdp", "seq", None),
    )
    return jax.shard_map(
        local,
        mesh=mesh,
        in_specs=placed,
        out_specs=(
            P("fsdp", "seq", None),
            P("fsdp", "seq", None),
            P("fsdp"),
            P("fsdp", None),
            P(None, "fsdp"),
            P("fsdp"),
            P("fsdp"),
            P("fsdp"),
            P("fsdp"),
            P("fsdp"),
            P("fsdp", None),
        ),
        check_vma=False,
    )
```

profile of v0, /device:TPU:0, one launch (start us, length us, event | category | flops | bytes accessed | tf_op | source)
XLA Modules:
  0.0 1543.7 jit_solution(17806640601309463371)
XLA Ops:
  8.1 6.1 all-gather.3
  14.2 5.5 all-gather.2
  22.8 7.5 all-reduce.22
  32.0 105.5 %all-gather.10.cloned.1.call-done = bf16[1536,6448]{0,1:T(8,128)(2,1)} async-done(((bf16[384,6448]{0,1:T(8,128)(2,1)}), bf16[1536,6448]{0,1:T(8,128)(2,1)}) %all-gather.10.cloned.1.call-update) | async-done | bytes 19808272 | tf_op jit(solution)/shard_map/all_gather | solution.py:162
  137.4 9.9 fusion.2
  152.1 4.0 collective-permute-start
  165.5 3.4 multiply_convert_fusion.3
  171.6 2.6 copy.168
  174.2 3.1 fusion.70
  178.8 5.2 all-gather.4
  192.1 2.7 mul.602
  194.9 3.5 copy.174
  198.4 18.9 %all_gather.53 = f32[8,1,48]{2,1,0:T(1,128)} all-gather(f32[1,1,48]{2,1,0:T(1,128)} %get-tuple-element.519), channel_id=1, replica_groups=mesh['seq'=8,'fsdp'=4] {'seq'}, dimensions={0}, use_global_device_ids=true | all-gather | bytes 1728 | tf_op jit(solution)/shard_map/all_gather | solution.py:28
  217.3 2.7 slice.105
  219.9 2.6 copy.159
  224.3 128.2 %all-gather.14.cloned.1.call-done = f32[384,64,128]{2,1,0:T(8,128)} async-done(((f32[48,64,128]{2,1,0:T(8,128)}), f32[384,64,128]{2,1,0:T(8,128)}) %all-gather.14.cloned.1.call-update) | async-done | bytes 12582928 | tf_op jit(solution)/shard_map/all_gather | solution.py:28
  352.5 36.0 %while.20 = (s32[]{:T(128)}, f32[1,48,64,128]{3,2,1,0:T(8,128)}, s32[]{:T(128)}, f32[8,1,48]{2,1,0:T(1,128)}, f32[8,1,48,64,128]{4,3,2,1,0:T(8,128)}, /*index=5*/s32[]{:T(128)}, s32[]{:T(128)}) while((s32[]{:T(128)}, f32[1,48,64,128]{3,2,1,0:T(8,128)}, s32[]{:T(128)}, f32[8,1,48]{2,1,0:T(1,128)}, f32[8,1,48,64,128]{4,3,2,1,0:T(8,128)}, ...), condition=%wide.region_4.5_spmd.clone, body=%wide.region_3.4_spmd.clone.sunk | while | flops 1572868 | bytes 4719281 | solution.py:39
  353.7 2.8 fusion.122
  357.6 3.7 fusion.122
  362.4 4.0 fusion.122
  367.5 3.3 fusion.122
  372.0 3.3 fusion.122
  376.5 3.3 fusion.122
  380.9 3.3 fusion.122
  385.3 3.3 fusion.122
  390.8 5.7 fusion.11
  396.6 3.6 copy.170
  400.2 5.1 multiply_reduce_fusion.6
  406.4 10.1 all-gather.12.cloned.1.call-done
  416.6 8.5 fusion.24
  425.1 5.6 fusion.17
  433.4 2.6 copy.175
  436.0 3.2 fusion.72
  439.3 12.7 fusion.47
  452.8 2.6 copy.172
  455.4 10.8 fusion.3
  469.3 3.6 fusion.15
  476.0 2.6 convolution_bitcast_fusion.1
  480.2 135.6 %all-gather.16.cloned.1.call-done = f32[384,64,128]{2,1,0:T(8,128)} async-done(((f32[48,64,128]{2,1,0:T(8,128)}), f32[384,64,128]{2,1,0:T(8,128)}) %all-gather.16.cloned.1.call-update) | async-done | bytes 12582928 | tf_op jit(solution)/shard_map/all_gather | solution.py:28
  615.8 39.0 %while.21 = (s32[]{:T(128)}, f32[1,48,64,128]{3,2,1,0:T(8,128)}, s32[]{:T(128)}, f32[8,1,48]{2,1,0:T(1,128)}, f32[8,1,48,64,128]{4,3,2,1,0:T(8,128)}, /*index=5*/s32[]{:T(128)}, s32[]{:T(128)}, s32[]{:T(128)}, s32[]{:T(128)}) while((s32[]{:T(128)}, f32[1,48,64,128]{3,2,1,0:T(8,128)}, s32[]{:T(128)}, f32[8,1,48]{2,1,0:T(1,128)}, ...), condition=%wide.region_8.9_spmd.clone, body=%wide.region_7.8_spmd.clone.sunk | while | flops 1572872 | bytes 4719343 | solution.py:39
  616.9 2.8 fusion.123
  620.9 4.0 fusion.123
  626.1 4.2 fusion.123
  631.5 4.1 fusion.123
  636.7 4.1 fusion.123
  641.9 3.5 fusion.123
  646.5 3.3 fusion.123
  651.0 3.8 fusion.123
  654.7 4.9 fusion.12
  668.0 3.8 reduce-window.16
  674.6 7.7 fusion.14
  682.3 3.7 copy.181
  686.0 2.8 convolution_bitcast_fusion.2
  690.0 5.8 multiply_reduce_fusion.5
  701.6 2.4 fusion.101
  706.3 18.2 %fusion.38 = f32[1536,6448]{0,1:T(8,128)} fusion(bf16[256,48]{1,0:T(8,128)(2,1)} %bitcast.285, bf16[256,3328]{1,0:T(8,128)(2,1)} %fusion.29, bf16[256,3072]{1,0:T(8,128)(2,1)} %get-tuple-element.508, bf16[1,256,1536]{2,1,0:T(8,128)(2,1)} %param.16, f32[1536]{0:T(1024)S(1)} %reshape.473, f32[256]{0:T(256)S(1)} %fusion.90), kind=kOutput, calls=%fused_computation.91 | convolution fusion | flops 5082390528 | bytes 43711488 | tf_op jit(solution)/shard_map/td,tj->dj/dot_general | solution.py:265
  727.2 28.7 %reduce-scatter.8.cloned.1.call-done = f32[768,1536]{1,0:T(8,128)} async-done(((f32[3072,1536]{1,0:T(8,128)}), f32[768,1536]{1,0:T(8,128)}) %reduce-scatter.8.cloned.1.call-update) | async-done | bytes 4718608 | tf_op jit(solution)/shard_map/reduce_scatter | solution.py:275
  755.9 279.1 %reduce-scatter.6.cloned.1.call-done = f32[384,6448]{0,1:T(8,128)} async-done(((f32[1536,6448]{0,1:T(8,128)}), f32[384,6448]{0,1:T(8,128)}) %reduce-scatter.6.cloned.1.call-update) | async-done | bytes 9904144 | tf_op jit(solution)/shard_map/reduce_scatter | solution.py:268
  1038.3 7.5 fusion.26
  1045.9 10.0 fusion.31
  1055.9 12.3 all-reduce.21
  1071.4 39.6 %all-reduce.19 = (f32[384]{0:T(512)}, f32[4,832]{1,0:T(4,128)}, f32[832]{0:T(1024)}, f32[12]{0:T(128)}, f32[12]{0:T(128)}, /*index=5*/f32[12]{0:T(128)}, f32[768]{0:T(1024)}) all-reduce(f32[384]{0:T(512)S(1)} %dynamic-slice.6, f32[4,832]{1,0:T(4,128)S(1)} %copy.200, ...), channel_id=1, replica_groups=mesh['seq'=8,'fsdp'=4] {'seq'}, use_global_device_ids=true, to_apply=%region_22.23 | all-reduce | flops 5348 | bytes 42784 | tf_op jit(solution)/shard_map/psum | solution.py:277
  1111.0 414.7 %all-reduce.25.cloned.1.call-done = (f32[384,6448]{0,1:T(8,128)}, f32[768,1536]{1,0:T(8,128)}) async-done(((f32[384,6448]{0,1:T(8,128)}, f32[768,1536]{1,0:T(8,128)}), (f32[384,6448]{0,1:T(8,128)}, f32[768,1536]{1,0:T(8,128)})) %all-reduce.25.cloned.1.call-update) | async-done | bytes 14622736 | tf_op jit(solution)/shard_map/psum | solution.py:277
  1525.7 8.5 copy.220
  (279 shorter events, 93.0 us)
Async XLA Ops:
  7.2 12.7 copy-start.61
  7.2 7.0 copy-start.58
  7.2 14.6 copy-start.68
  7.2 14.8 copy-start.69
  7.2 15.1 copy-start.70
  7.2 15.3 copy-start.62
  7.3 24.4 %copy-start.11 = (bf16[1,256,1536]{2,1,0:T(8,128)(2,1)S(1)}, bf16[1,256,1536]{2,1,0:T(8,128)(2,1)}, u32[]{:S(2)}) copy-start(bf16[1,256,1536]{2,1,0:T(8,128)(2,1)} %param.16) | copy-start | bytes 2359300
  7.3 130.2 %all-gather.10.cloned.1.call-start = ((), (), s32[]{:S(2)}) async-start(), calls=%async_computation.3 | async-start | bytes 24760320 | tf_op jit(solution)/shard_map/all_gather | solution.py:162
  8.0 344.5 %all-gather.14.cloned.1.call-start = ((), (), s32[]{:S(2)}) async-start(), calls=%async_computation.7 | async-start | bytes 14155776 | tf_op jit(solution)/shard_map/all_gather | solution.py:28
  30.3 117.0 %copy-start.71 = (bf16[48]{0:T(256)(128)(2,1)}, bf16[48]{0:T(256)(128)(2,1)S(1)}, u32[]{:S(2)}) copy-start(bf16[48]{0:T(256)(128)(2,1)S(1)} %get-tuple-element.494) | copy-start | bytes 292
  30.9 126.4 %copy-start.49 = (f32[48]{0:T(128)}, f32[48]{0:T(128)S(1)}, u32[]{:S(2)}) copy-start(f32[48]{0:T(128)S(1)} %convert_element_type.154) | copy-start | bytes 580
  31.9 115.4 %copy-start.52 = (f32[256]{0:T(256)}, f32[256]{0:T(256)S(1)}, u32[]{:S(2)}) copy-start(f32[256]{0:T(256)S(1)} %fusion.34) | copy-start | bytes 3076
  31.9 115.4 %copy-start.64 = (f32[48]{0:T(128)}, f32[48]{0:T(128)S(1)}, u32[]{:S(2)}) copy-start(f32[48]{0:T(128)S(1)} %fusion.92) | copy-start | bytes 580
  147.3 12.2 copy-start.10
  152.1 11.5 collective-permute-start
  157.3 3.9 copy-start.56
  165.5 4.6 copy-start.9
  174.2 4.5 copy-start.63
  177.4 239.1 %all-gather.12.cloned.1.call-start = ((), (), s32[]{:S(2)}) async-start(), calls=%async_computation.4 | async-start | bytes 11796480 | tf_op jit(solution)/shard_map/all_gather | solution.py:169
  178.2 437.6 %all-gather.16.cloned.1.call-start = ((), (), s32[]{:S(2)}) async-start(), calls=%async_computation.8 | async-start | bytes 14155776 | tf_op jit(solution)/shard_map/all_gather | solution.py:28
  388.6 2.2 copy-start.45
  390.8 5.8 copy-start.8
  416.6 8.5 copy-start.55
  416.6 8.5 copy-start
  416.6 8.6 copy-start.3
  416.6 8.6 copy-start.4
  416.6 8.6 copy-start.47
  425.1 6.7 copy-start.7
  439.2 316.7 %reduce-scatter.8.cloned.1.call-start = ((), (), s32[]{:S(2)}) async-start(), calls=%async_computation.6 | async-start | bytes 23592960 | tf_op jit(solution)/shard_map/reduce_scatter | solution.py:275
  452.0 583.1 %reduce-scatter.6.cloned.1.call-start = ((), (), s32[]{:S(2)}) async-start(), calls=%async_computation.5 | async-start | bytes 49520640 | tf_op jit(solution)/shard_map/reduce_scatter | solution.py:268
  476.0 2.6 copy-start.23
  661.2 3.5 copy-start.18
  661.2 3.6 copy-start.21
  661.2 3.6 copy-start.24
  661.2 3.6 copy-start.25
  661.2 3.6 copy-start.26
  686.0 4.0 copy-start.6
  686.0 4.0 copy-start.22
  690.0 5.8 copy-start.31
  690.0 5.8 copy-start.33
  690.0 5.8 copy-start.35
  697.5 2.5 copy-start.59
  697.5 4.0 copy-start.50
  697.5 4.0 copy-start.57
  697.6 6.5 collective-permute-start.1
  724.6 345.6 %reduce-scatter.10.cloned.1.call-start = ((), (), s32[]{:S(2)}) async-start(), calls=%async_computation.9 | async-start | bytes 2129920
  727.1 798.6 %all-reduce.25.cloned.1.call-start = ((), (), s32[]{:S(2)}) async-start(), calls=%async_computation.10 | async-start | bytes 29245440 | tf_op jit(solution)/shard_map/psum | solution.py:277
  1035.0 2.9 copy-start.43
  1035.0 3.1 copy-start.1
  1035.0 3.1 copy-start.48
  1038.2 7.6 copy-start.67
  1038.2 7.6 copy-start.72
  1038.2 7.6 copy-start.12
  1038.2 7.6 copy-start.14
  1038.2 7.6 copy-start.15
  1038.3 7.6 copy-start.28
  1045.8 10.1 copy-start.36
  1045.8 10.1 copy-start.51
  1045.8 10.1 copy-start.65
  1045.8 22.9 %copy-start.53 = (f32[256]{0:T(256)S(1)}, f32[256]{0:T(256)}, u32[]{:S(2)}) copy-start(f32[256]{0:T(256)} %copy-done.52) | copy-start | bytes 3076
  1045.9 22.9 %copy-start.13 = (bf16[1,256,1536]{2,1,0:T(8,128)(2,1)S(1)}, bf16[1,256,1536]{2,1,0:T(8,128)(2,1)}, u32[]{:S(2)}) copy-start(bf16[1,256,1536]{2,1,0:T(8,128)(2,1)} %param.16) | copy-start | bytes 2359300
  1045.9 22.9 %copy-start.20 = (bf16[1,256,1536]{2,1,0:T(8,128)(2,1)S(1)}, bf16[1,256,1536]{2,1,0:T(8,128)(2,1)}, u32[]{:S(2)}) copy-start(bf16[1,256,1536]{2,1,0:T(8,128)(2,1)} %param.27) | copy-start | bytes 2359300
  1045.9 22.9 %copy-start.60 = (pred[256]{0:T(512)(128)(4,1)S(1)}, pred[256]{0:T(512)(128)(4,1)}, u32[]{:S(2)}) copy-start(pred[256]{0:T(512)(128)(4,1)} %add_compare_fusion) | copy-start | bytes 772
  1525.7 8.5 copy-start.19
  (20 other events, 28.9 us)
Sparse Core Ops, SparseCore 0:
  9.7 127.6 all-gather.9
  177.5 174.9 all-gather.13
  354.1 62.4 all-gather.11
  439.3 176.4 all-gather.15
  618.2 137.6 reduce-scatter.7
  758.6 276.4 reduce-scatter.5
  1038.2 29.6 reduce-scatter.9
  1072.8 452.9 all-reduce.24
where the time goes:
time: 1550 us; the launch traced here: 1540 us
  waiting for transfers between devices  1100 us (71%)
  matrix products  114 us (7%)
  other arithmetic  110 us (7%)
  blocking collectives  95.1 us (6%)
  local copies, waits for them, and re-layouts  94.1 us (6%)
  between operations  20.5 us (1%)
    psum x1, waiting for transfers between devices, local(): lax.psum((shares[0], shares[1], shares[2], shares[3], shares[4], shares[5...  415 us
    reduce_scatter x1, waiting for transfers between devices, local(): lax.psum_scatter(grad_w_in, 'fsdp', scatter_dimension=0, tiled=True)  279 us
    all_gather x2, waiting for transfers between devices, entering(): everything = jax.tree.map(lambda part: lax.all_gather(part, axis), x)  264 us
    all_gather x1, waiting for transfers between devices, local(): lax.all_gather(in_weight, 'fsdp', axis=0, tiled=True)  105 us
    select_n x16, other arithmetic, step(): return jax.tree.map(lambda a, b: jnp.where(reached, a, b), new, before)  56.7 us
    psum x1, blocking collectives, local(): lax.psum((shares[0], shares[1], shares[2], shares[3], shares[4], shares[5...  39.6 us
  transfers between devices with their start and end apart: 10, of which 7 were waited for; matrix products, arithmetic and copies ran while one was open for 17% of the time, Pallas kernels for 0%

commit v1 on v0

v1 whole, which is shorter than its diff:
```python
import jax
import jax.numpy as jnp
from jax import lax
from jax.sharding import PartitionSpec as P

HEADS = 48
HEADDIM = 64
STATE = 128
CONV = 4
INNER = 3072
CHANNELS = 3328
PROJ = 6448
PLANES = 2
CORES = 2

f32 = jnp.float32
bf16 = jnp.bfloat16
epsilon = 1e-05


class Ring:
    def __init__(self, seq, fsdp):
        self.seq, self.fsdp = seq, fsdp
        self.clock = None
        self.line, self.row = seq // PLANES, fsdp // CORES

    def send(self, block, move):
        route = []
        for s in range(self.seq):
            for f in range(self.fsdp):
                there = move(s // PLANES, s % PLANES, f // CORES, f % CORES)
                if there is None:
                    continue
                z, x, y, c = there
                route.append((s * self.fsdp + f, (z * PLANES + x) * self.fsdp + y * CORES + c))
        arrived = lax.ppermute(block, ("seq", "fsdp"), route)
        self.clock.pending.append(arrived)
        return arrived

    def core(self, block):
        return self.send(block, lambda z, x, y, c: (z, x, y, 1 - c))

    def plane(self, block):
        return self.send(block, lambda z, x, y, c: (z, 1 - x, y, c))

    def from_row(self, block, distance):
        return self.send(block, lambda z, x, y, c: (z, x, (y - distance) % self.row, c))

    def far(self, block, distance):
        return self.send(block, lambda z, x, y, c: (z ^ distance, x, y, c))

    def next_block(self, block, distance):
        def move(z, x, y, c):
            s = z * PLANES + x + distance
            return (s // PLANES, s % PLANES, y, c) if 0 <= s < self.seq else None

        return self.send(block, move)


def rows_of(block, index, count):
    return lax.dynamic_slice_in_dim(block, index * count, count, axis=0)


def swapped(ring, distance):
    seq_index = lax.axis_index("seq")
    if distance == 0:
        return seq_index % PLANES, ring.plane
    bit = (seq_index // PLANES // distance) % 2
    return bit, lambda block: ring.far(block, distance)


def cube(ring):
    distances, distance = [0], 1
    while distance < ring.line:
        distances.append(distance)
        distance *= 2
    return distances


def halve(ring, distance, block):
    bit, send = swapped(ring, distance)
    half = block.shape[0] // 2
    arrived = send(rows_of(block, 1 - bit, half).astype(bf16))
    return rows_of(block, bit, half) + arrived.astype(f32)


def double(ring, distance, block):
    bit, send = swapped(ring, distance)
    other = send(block)
    low = jnp.where(bit == 0, block, other)
    high = jnp.where(bit == 0, other, block)
    return jnp.concatenate([low, high], axis=0)


class Total:
    def __init__(self, ring, grad):
        self.ring, self.value = ring, grad
        self.steps = [(halve, d) for d in cube(ring)] + [(double, d) for d in reversed(cube(ring))]

    def step(self):
        if self.steps:
            kind, distance = self.steps.pop(0)
            if kind is double and self.value.dtype != bf16:
                self.value = self.value.astype(bf16)
            self.value = kind(self.ring, distance, self.ring.clock.now(self.value))

    def finish(self):
        while self.steps:
            self.step()
        return self.value.astype(f32)

    def halves(self):
        while len(self.steps) > 1:
            self.step()
        if self.steps:
            self.steps = []
            self.value = (self.value, self.ring.plane(self.ring.clock.now(self.value)))
        return self.value


class Clock:
    def __init__(self, value):
        self.token = value
        self.pending = []
        self.later = []

    def tick(self, *values):
        out = lax.optimization_barrier((self.token,) + values + tuple(self.pending))
        self.token = out[0]
        self.pending, self.later = self.later, []
        return out[1 : 1 + len(values)]

    def now(self, value):
        return lax.optimization_barrier((value, self.token))[0]


class Spread:
    def __init__(self, ring, block):
        self.ring, self.block = ring, block
        self.quarter = -(-block.shape[0] // 64) * 16
        self.cut = -(-self.quarter // 32) * 16
        seq_index = lax.axis_index("seq")
        self.place = seq_index % 2 + 2 * ((seq_index // PLANES) % 2)
        self.found = {(0, 0): block, (0, 1): ring.core(block)}
        for d in range(1, ring.row):
            for e in range(CORES):
                self.found[d, e] = jnp.zeros_like(block)

    def start(self, index):
        return jnp.minimum((self.place ^ index) * self.quarter, self.block.shape[0] - self.quarter)

    def put(self, pieces, index, offset=0):
        for d in range(1, self.ring.row):
            for e in range(CORES):
                piece = pieces[d - 1]
                self.found[d, e] = lax.dynamic_update_slice_in_dim(
                    self.found[d, e],
                    self.ring.core(piece) if e else piece,
                    self.start(index) + offset,
                    axis=0,
                )

    def first(self):
        ring = self.ring
        mine = lax.dynamic_slice_in_dim(self.block, self.start(0), self.quarter, axis=0)
        mine = ring.clock.now(mine)
        self.mine = [ring.from_row(mine, d) for d in range(1, ring.row)]

    def second(self):
        ring = self.ring
        mine = [ring.clock.now(part) for part in self.mine]
        self.beside = [ring.plane(part) for part in mine]
        self.behind = [ring.far(part, 1) for part in mine]
        self.put(mine, 0)

    def third(self):
        ring, cut = self.ring, self.cut
        beside = [ring.clock.now(part) for part in self.beside]
        behind = [ring.clock.now(part) for part in self.behind]
        self.corner = (
            [ring.plane(part[:cut]) for part in behind],
            [ring.far(part[cut:], 1) for part in beside],
        )
        self.put(beside, 1)
        self.put(behind, 2)

    def fourth(self):
        now = self.ring.clock.now
        self.put([now(part) for part in self.corner[0]], 3)
        self.put([now(part) for part in self.corner[1]], 3, self.cut)
        return self.found


class Pieces:
    def __init__(self, ring, block, count=1):
        self.ring, self.block = ring, block
        self.rows = block.shape[0] // count
        self.parts = []

    def near(self):
        self.beside = self.ring.core(self.ring.clock.now(self.block))

    def send(self, later=False):
        clock = self.ring.clock
        at = len(self.parts) * self.rows
        piece = clock.now(self.block[at : at + self.rows])
        self.parts.append([self.ring.from_row(piece, d) for d in range(1, self.ring.row)])
        if later:
            for _ in range(1, self.ring.row):
                clock.later.append(clock.pending.pop())

    def whole(self):
        found = {(0, 0): self.block, (0, 1): self.beside}
        for d in range(1, self.ring.row):
            parts = [self.ring.clock.now(part[d - 1]) for part in self.parts]
            found[d, 0] = jnp.concatenate(parts, axis=0) if len(parts) > 1 else parts[0]
            found[d, 1] = self.ring.core(found[d, 0])
        return found


def gather_rows(ring, block):
    found = {}
    for d in range(ring.row):
        found[d, 0] = block if d == 0 else ring.from_row(block, d)
        found[d, 1] = ring.core(found[d, 0])
    return found


def places(ring):
    index = lax.axis_index("fsdp")
    y, c = index // CORES, index % CORES
    return {
        (d, e): ((y + d) % ring.row) * CORES + (c + e) % CORES
        for d in range(ring.row)
        for e in range(CORES)
    }


def trade_columns(ring, block):
    index = lax.axis_index("fsdp")
    y, c = index // CORES, index % CORES
    width = block.shape[1] // ring.fsdp
    found = {}
    for d in range(ring.row):
        for e in range(CORES):
            target = ((y - d) % ring.row) * CORES + (c + e) % CORES
            piece = lax.dynamic_slice_in_dim(block, target * width, width, axis=1)
            if d or e:
                piece = ring.send(
                    piece,
                    lambda z, x, y, c, d=d, e=e: (z, x, (y - d) % ring.row, (c + e) % CORES),
                )
            found[d, e] = piece
    return found


class SmallSum:
    def __init__(self, ring, vector):
        self.ring, self.value = ring, vector
        self.steps = ["core", "row"] + cube(ring)

    def step(self):
        if not self.steps:
            return
        kind = self.steps.pop(0)
        vector = self.ring.clock.now(self.value)
        if kind == "core":
            self.value = vector + self.ring.core(vector)
        elif kind == "row":
            self.value = sum([self.ring.from_row(vector, d) for d in range(1, self.ring.row)], vector)
        else:
            self.value = vector + swapped(self.ring, kind)[1](vector)

    def finish(self):
        while self.steps:
            self.step()
        return self.value


def spread_factors(ring, through):
    factor = jnp.repeat(through, HEADDIM).reshape(ring.seq, -1)
    size = 8 * STATE
    return jnp.pad(factor, ((0, 0), (0, size - factor.shape[1]))).reshape(ring.seq, 8, STATE)


def traded(ring, added, through=None):
    part = added.shape[0] // ring.seq
    added = added.reshape(ring.seq, part, STATE)
    if through is None:
        return lax.all_to_all(added, "seq", 0, 0, tiled=True)
    added = jnp.concatenate([added, spread_factors(ring, through)], axis=1)
    blocks = lax.all_to_all(added, "seq", 0, 0, tiled=True)
    factor = blocks[:, part:].reshape(ring.seq, 8 * STATE)[:, :part, None]
    return blocks[:, :part], factor


def carried(ring, blocks, factor, reverse):
    part = blocks.shape[1]
    state = jnp.zeros((part, STATE), f32)
    states = [None] * ring.seq
    order = range(ring.seq - 1, -1, -1) if reverse else range(ring.seq)
    for k in order:
        states[k] = state.astype(bf16)
        state = factor[k] * state + blocks[k]
    return jnp.stack(states)


def returned(ring, states):
    states = lax.all_to_all(states, "seq", 0, 0, tiled=True)
    return states.reshape(HEADS, HEADDIM, STATE)


def place_rows(whole, sides, start, rows):
    mine, other = sides
    first = (lax.axis_index("seq") % PLANES) == 0
    half = mine.shape[0]
    low = jnp.where(first, mine, other).astype(f32)
    high = jnp.where(first, other, mine)[: rows - half].astype(f32)
    whole = lax.dynamic_update_slice_in_dim(whole, low, start, axis=0)
    return lax.dynamic_update_slice_in_dim(whole, high, start + half, axis=0)


def rms_scale(values, gain):
    return values * lax.rsqrt(jnp.mean(values * values, axis=-1, keepdims=True) + epsilon) * gain


def conv_silu(window, conv_weight, conv_bias):
    count = window.shape[0] - CONV + 1
    summed = conv_bias
    for offset in range(CONV):
        summed = summed + conv_weight[offset] * window[offset : offset + count]
    return jax.nn.silu(summed)


def step_sizes(dt_raw, dt_bias, a_log):
    step_size = jax.nn.softplus(dt_raw + dt_bias)
    return (step_size, jnp.cumsum(step_size * -jnp.exp(a_log), axis=0))


def gated_norm(mixer, gate_part, gate_gain):
    return rms_scale(mixer * jax.nn.silu(gate_part), gate_gain)


def decay_table(head_decay):
    length = head_decay.shape[1]
    later = lax.broadcasted_iota(jnp.int32, (length, length), 0)
    earlier = lax.broadcasted_iota(jnp.int32, (length, length), 1)
    causal = (later >= earlier)[None]
    exponent = head_decay[:, :, None] - head_decay[:, None, :]
    return jnp.where(causal, jnp.exp(jnp.where(causal, exponent, 0.0)), 0.0)


def state_slot(heads_x, proj_b, step_size, log_decay):
    to_end = jnp.exp(log_decay[-1:] - log_decay)
    weighted = (heads_x.astype(f32) * (to_end * step_size)[:, :, None]).astype(bf16)
    return jnp.einsum("thp,tn->hpn", weighted, proj_b, preferred_element_type=f32)


def mix_slot(heads_x, proj_b, proj_c, step_size, log_decay, incoming, skip_gain):
    scores = jnp.einsum("tn,sn->ts", proj_c, proj_b, preferred_element_type=f32)
    decays = decay_table(log_decay.T)
    mixing = (scores[None] * decays * step_size.T[:, None, :]).astype(bf16)
    intra = jnp.einsum("hts,shp->thp", mixing, heads_x, preferred_element_type=f32)
    reached = jnp.einsum("tn,hpn->thp", proj_c, incoming, preferred_element_type=f32)
    return (
        intra
        + jnp.exp(log_decay)[:, :, None] * reached
        + skip_gain[:, None] * heads_x.astype(f32)
    )


def slot_back(
    heads_x, proj_b, proj_c, step_size, log_decay, incoming_b, grad_y, grad_reach, grad_fresh, skip_gain
):
    grad_yf = grad_y.astype(f32)
    x_float = heads_x.astype(f32)
    grad_skip = jnp.sum(grad_yf * x_float, axis=(0, 2))
    grad_x = skip_gain[:, None] * grad_yf
    from_start = jnp.exp(log_decay)
    reached = jnp.einsum("tn,hpn->thp", proj_c, incoming_b, preferred_element_type=f32)
    grad_cum = from_start * jnp.sum(grad_yf * reached, axis=2)
    grad_c = jnp.einsum("thp,hpn->tn", grad_reach, incoming_b, preferred_element_type=f32)
    scores = jnp.einsum("tn,sn->ts", proj_c, proj_b, preferred_element_type=f32)
    decays = decay_table(log_decay.T)
    step_heads = step_size.T[:, None, :]
    mixing = (scores[None] * decays * step_heads).astype(bf16)
    grad_mix = jnp.einsum("thp,shp->hts", grad_y, heads_x, preferred_element_type=f32)
    grad_x = grad_x + jnp.einsum("hts,thp->shp", mixing, grad_y, preferred_element_type=f32)
    grad_scores = jnp.sum(grad_mix * decays * step_heads, axis=0).astype(bf16)
    grad_step = jnp.sum(grad_mix * scores[None] * decays, axis=1).T
    grad_exp = grad_mix * scores[None] * step_heads * decays
    grad_cum = grad_cum + (jnp.sum(grad_exp, axis=2) - jnp.sum(grad_exp, axis=1)).T
    grad_c = grad_c + jnp.einsum("ts,sn->tn", grad_scores, proj_b, preferred_element_type=f32)
    grad_b = jnp.einsum("ts,tn->sn", grad_scores, proj_c, preferred_element_type=f32)
    to_end = jnp.exp(log_decay[-1:] - log_decay)
    factor = to_end * step_size
    weighted = (x_float * factor[:, :, None]).astype(bf16)
    grad_weighted = jnp.einsum("hpn,tn->thp", grad_fresh, proj_b, preferred_element_type=f32)
    grad_b = grad_b + jnp.einsum("thp,hpn->tn", weighted, grad_fresh, preferred_element_type=f32)
    grad_x = grad_x + grad_weighted * factor[:, :, None]
    grad_factor = jnp.sum(grad_weighted * x_float, axis=2)
    grad_step = grad_step + grad_factor * to_end
    grad_tail = grad_factor * step_size * to_end
    through = jnp.exp(log_decay[-1])
    crossed = jnp.sum(grad_fresh.astype(f32) * incoming_b.astype(f32), axis=(1, 2))
    grad_end = jnp.sum(grad_tail, axis=0) + through * crossed
    last_row = lax.broadcasted_iota(jnp.int32, log_decay.shape, 0) == log_decay.shape[0] - 1
    grad_cum = grad_cum - grad_tail + jnp.where(last_row, grad_end[None, :], 0.0)
    return (grad_x, grad_b, grad_c, grad_step, grad_cum, grad_skip)


def pack(arrays):
    flat = jnp.concatenate([a.reshape(-1) for a in arrays])
    pad = -flat.shape[0] % 1024
    return jnp.pad(flat, (0, pad)).reshape(-1, 128)


def local(
    hidden,
    lengths,
    norm_gain,
    in_weight,
    conv_weight,
    conv_bias,
    dt_bias,
    a_log,
    skip_d,
    gate_gain,
    out_weight,
    out_grad,
):
    ring = Ring(lax.axis_size("seq"), lax.axis_size("fsdp"))
    ring.clock = clock = Clock(hidden[0, :8, :128])
    _, row_count, model_width = hidden.shape
    fsdp_index = lax.axis_index("fsdp")
    where = places(ring)
    tokens = hidden[0].astype(f32)

    small = [norm_gain, conv_weight, conv_bias, dt_bias, a_log, skip_d, gate_gain]
    packed = pack(small)
    gathered = gather_rows(ring, packed)
    spread = jnp.zeros((ring.fsdp,) + packed.shape, bf16)
    for key, block in gathered.items():
        spread = lax.dynamic_update_slice_in_dim(spread, block[None], where[key], axis=0)
    spread = spread.reshape(ring.fsdp, -1)
    whole_small, at = [], 0
    for part in small:
        piece = spread[:, at : at + part.size]
        at += part.size
        if part.ndim == 2:
            piece = piece.reshape((ring.fsdp,) + part.shape).transpose(1, 0, 2)
            whole_small.append(piece.reshape(part.shape[0], -1).astype(f32))
        else:
            whole_small.append(piece.reshape(-1).astype(f32))
    gain_norm, conv_taps, conv_shift, step_bias, rate_log, skip_gain, gain_gate = whole_small

    in_rows = in_weight.T
    shared = Spread(ring, in_rows[INNER:])
    (spread,) = clock.tick(spread)
    gate_pieces = Pieces(ring, in_rows[:INNER], 3)
    out_pieces = Pieces(ring, out_weight, 2)
    shared.first()
    gate_pieces.near()
    out_pieces.near()
    clock.tick()
    shared.second()
    gate_pieces.send()
    clock.tick()
    shared.third()
    gate_pieces.send(later=True)
    clock.tick()
    gate_pieces.send(later=True)
    weight_conv = shared.fourth()

    position = lax.axis_index("seq") * row_count + lax.broadcasted_iota(
        jnp.int32, (row_count, 1), 0
    )
    grad_out = jnp.where(position < lengths[0], out_grad[0], jnp.zeros_like(out_grad[0]))

    normed, pull_norm = jax.vjp(rms_scale, tokens, gain_norm)
    normed = normed.astype(bf16)
    depth = in_weight.shape[0]

    def project(weights):
        total = None
        for key, weight in weights.items():
            columns = lax.dynamic_slice_in_dim(normed, where[key] * depth, depth, axis=1)
            term = jnp.einsum("td,jd->tj", columns, weight, preferred_element_type=f32)
            total = term if total is None else total + term
        return total.astype(bf16)

    projected = project(weight_conv)
    (projected,) = clock.tick(projected)
    out_pieces.send(later=True)
    conv_in = projected[:, :CHANNELS]
    dt_raw = projected[:, CHANNELS:]
    edge_rows = ring.next_block(conv_in[row_count - CONV + 1 :], 1)
    window = jnp.concatenate([edge_rows, conv_in], axis=0).astype(f32)
    conv_out, pull_conv = jax.vjp(conv_silu, window, conv_taps, conv_shift)
    conv_low = conv_out.astype(bf16)
    heads_x = conv_low[:, :INNER].reshape(row_count, HEADS, HEADDIM)
    proj_b = conv_low[:, INNER : INNER + STATE]
    proj_c = conv_low[:, INNER + STATE :]
    (step_size, log_decay), pull_steps = jax.vjp(
        step_sizes, dt_raw.astype(f32), step_bias, rate_log
    )
    through = jnp.exp(log_decay[-1])
    fresh_state = state_slot(heads_x, proj_b, step_size, log_decay)
    (fresh_state,) = clock.tick(fresh_state)
    blocks, factor = traded(ring, fresh_state.reshape(INNER, STATE), through)
    out_pieces.send()
    weight_gate = gate_pieces.whole()
    gate_part = project(weight_gate)
    blocks, factor, gate_part = clock.tick(blocks, factor, gate_part)
    incoming = returned(ring, carried(ring, blocks, factor, False))
    weight_out = out_pieces.whole()
    grad_pieces = Pieces(ring, grad_out)
    grad_pieces.send()
    grad_pieces.near()
    (incoming,) = clock.tick(incoming)
    mixer = mix_slot(heads_x, proj_b, proj_c, step_size, log_decay, incoming, skip_gain)
    mixed, pull_gate = jax.vjp(
        gated_norm, mixer.reshape(row_count, INNER), gate_part.astype(f32), gain_gate
    )
    mixed = mixed.astype(bf16)
    normed_all = trade_columns(ring, clock.now(normed))
    (mixed,) = clock.tick(mixed)
    mixed_all = trade_columns(ring, mixed)
    grad_out_all = grad_pieces.whole()
    wide = out_weight.shape[0]

    grad_mixed = jnp.zeros((row_count, INNER), f32)
    for key, weight in weight_out.items():
        term = jnp.einsum("td,id->ti", grad_out, weight, preferred_element_type=f32)
        grad_mixed = lax.dynamic_update_slice_in_dim(grad_mixed, term, where[key] * wide, axis=1)
    grad_mixer, grad_gate, grad_g_gate = pull_gate(grad_mixed)
    grad_y = grad_mixer.astype(bf16).reshape(row_count, HEADS, HEADDIM)
    grad_reach = (grad_y.astype(f32) * jnp.exp(log_decay)[:, :, None]).astype(bf16)
    direct = jnp.einsum("thp,tn->hpn", grad_reach, proj_c, preferred_element_type=f32)
    direct, grad_y, grad_reach, grad_gate = clock.tick(
        direct, grad_y, grad_reach, grad_gate.astype(bf16)
    )
    blocks = traded(ring, direct.reshape(INNER, STATE))
    gate_grads = Pieces(ring, grad_gate)
    gate_grads.send()
    gate_grads.near()

    def weight_grad(rows_all, columns_all):
        return sum(
            jnp.einsum(
                "ti,tj->ij", rows_all[key], columns_all[key], preferred_element_type=f32
            )
            for key in where
        )

    mixed_all = {key: clock.now(block) for key, block in mixed_all.items()}
    total_w_out = Total(ring, weight_grad(mixed_all, grad_out_all))
    total_w_out.step()
    (blocks,) = clock.tick(blocks)
    chain_grad = returned(ring, carried(ring, blocks, factor, True))
    total_w_out.step()
    total_w_gate = Total(ring, weight_grad(gate_grads.whole(), normed_all))
    chain_grad, total_w_gate.value = clock.tick(chain_grad, total_w_gate.value)
    total_w_out.step()
    total_w_gate.step()

    grad_x, grad_b, grad_c, grad_step, grad_cum, grad_skip = slot_back(
        heads_x,
        proj_b,
        proj_c,
        step_size,
        log_decay,
        incoming,
        grad_y,
        grad_reach,
        chain_grad,
        skip_gain,
    )
    (grad_x,) = clock.tick(grad_x)
    total_w_out.step()
    total_w_gate.step()
    grad_dt_raw, grad_step_bias, grad_rate = pull_steps((grad_step, grad_cum))
    grad_conv_out = jnp.concatenate([grad_x.reshape(row_count, INNER), grad_b, grad_c], axis=1)
    grad_window, grad_taps, grad_shift = pull_conv(grad_conv_out)
    back_edge = ring.next_block(grad_window[: CONV - 1], -1)
    grad_conv_in = grad_window[CONV - 1 :] + jnp.concatenate(
        [jnp.zeros((row_count - CONV + 1, CHANNELS), f32), back_edge], axis=0
    )
    grad_tail = jnp.concatenate([grad_conv_in, grad_dt_raw], axis=1).astype(bf16)
    (grad_tail,) = clock.tick(grad_tail)

    cut = 1792
    first = Pieces(ring, grad_tail[:, :cut])
    last = Pieces(ring, jnp.pad(grad_tail[:, cut:], ((0, 0), (0, 80))))
    first.send()
    first.near()
    last.near()
    total_w_out.step()
    total_w_gate.step()
    clock.tick()
    last.send()
    total_first = Total(ring, weight_grad(first.whole(), normed_all))
    total_first.step()
    total_w_gate.step()
    clock.tick()
    total_last = Total(ring, weight_grad(last.whole(), normed_all))
    total_last.step()
    total_first.step()
    (grad_gate, grad_tail, mixed) = clock.tick(grad_gate, grad_tail, mixed)
    total_first.step()
    total_w_out.step()
    total_w_gate.step()
    summed_out = tokens
    for key, weight in weight_out.items():
        columns = lax.dynamic_slice_in_dim(mixed, where[key] * wide, wide, axis=1)
        summed_out = summed_out + jnp.dot(columns, weight, preferred_element_type=f32)
    output = summed_out.astype(bf16)

    grad_normed = jnp.zeros((row_count, model_width), f32)
    for key in where:
        term = jnp.einsum(
            "tj,jd->td", grad_gate, weight_gate[key], preferred_element_type=f32
        ) + jnp.einsum("tj,jd->td", grad_tail, weight_conv[key], preferred_element_type=f32)
        grad_normed = lax.dynamic_update_slice_in_dim(grad_normed, term, where[key] * depth, axis=1)
    grad_tokens, grad_g_norm = pull_norm(grad_normed)
    hidden_grad = (grad_tokens + grad_out.astype(f32)).astype(bf16)

    parts = [grad_g_norm, grad_taps, grad_shift, grad_step_bias, grad_rate, grad_skip, grad_g_gate]
    small_total = SmallSum(ring, pack(parts))
    clock.tick()
    total_last.step()
    total_first.step()
    total_w_gate.halves()
    small_total.step()
    clock.tick()
    total_last.step()
    total_first.step()
    small_total.step()
    clock.tick()
    total_last.step()
    total_first.halves()
    small_total.step()
    clock.tick()
    total_last.step()
    small_total.step()
    clock.tick()
    total_last.halves()
    small_total.step()
    summed = small_total.finish().reshape(-1)
    shares, at = [], 0
    for part in parts:
        piece = summed[at : at + part.size].reshape(part.shape)
        at += part.size
        width = part.shape[-1] // ring.fsdp
        shares.append(
            lax.dynamic_slice_in_dim(piece, fsdp_index * width, width, axis=part.ndim - 1)
        )
    total_w_in = jnp.zeros((PROJ, depth), f32)
    total_w_in = place_rows(total_w_in, total_w_gate.halves(), 0, INNER)
    total_w_in = place_rows(total_w_in, total_first.halves(), INNER, cut)
    total_w_in = place_rows(total_w_in, total_last.halves(), INNER + cut, PROJ - INNER - cut)
    total_w_in = total_w_in.T
    total_w_out = total_w_out.finish()
    return (
        output[None],
        hidden_grad[None],
        shares[0],
        total_w_in,
        shares[1],
        shares[2],
        shares[3],
        shares[4],
        shares[5],
        shares[6],
        total_w_out,
    )


def solution(mesh):
    placed = (
        P("fsdp", "seq", None),
        P("fsdp"),
        P("fsdp"),
        P("fsdp", None),
        P(None, "fsdp"),
        P("fsdp"),
        P("fsdp"),
        P("fsdp"),
        P("fsdp"),
        P("fsdp"),
        P("fsdp", None),
        P("fsdp", "seq", None),
    )
    return jax.shard_map(
        local,
        mesh=mesh,
        in_specs=placed,
        out_specs=(
            P("fsdp", "seq", None),
            P("fsdp", "seq", None),
            P("fsdp"),
            P("fsdp", None),
            P(None, "fsdp"),
            P("fsdp"),
            P("fsdp"),
            P("fsdp"),
            P("fsdp"),
            P("fsdp"),
            P("fsdp", None),
        ),
        check_vma=False,
    )
```

time: 1550 us -> 710 us (0.46)
  waiting for transfers between devices: 1100 us -> 230 us
  blocking collectives: 95.1 us -> 0 us
  starting transfers between devices: 5.92 us -> 86.7 us
  matrix products: 114 us -> 142 us
  local copies, waits for them, and re-layouts: 94.1 us -> 121 us
  between operations: 20.5 us -> 3.8 us
    psum x1 -> x0, waiting for transfers between devices: 415 us -> none  [local(): lax.psum((shares[0], shares[1], shares[2], shares[3], shares[4], shares[5...]
    all_gather x4 -> x0, waiting for transfers between devices: 379 us -> none  [the longest x2 264 us: entering(): everything = jax.tree.map(lambda part: lax.all_gather(part, axis), x)]
    reduce_scatter x2 -> x0, waiting for transfers between devices: 308 us -> none  [the longest x1 279 us: local(): lax.psum_scatter(grad_w_in, 'fsdp', scatter_dimension=0, tiled=True)]
    ppermute x2 -> x72, waiting for transfers between devices: 0.01 us -> 202 us  [send(): arrived = lax.ppermute(block, ('seq', 'fsdp'), route)]
    ppermute x2 -> x72, starting transfers between devices: 5.38 us -> 64.7 us  [send(): arrived = lax.ppermute(block, ('seq', 'fsdp'), route)]
    select_n x16 -> x11, other arithmetic: 56.7 us -> 6.77 us  [the longest x9 5.44 us: double(): low = jnp.where(bit == 0, block, other)]
    psum x1 -> x0, blocking collectives: 39.6 us -> none  [local(): lax.psum((shares[0], shares[1], shares[2], shares[3], shares[4], shares[5...]
    dynamic_update_slice x0 -> x14, local copies, waits for them, and re-layouts: none -> 35.6 us  [the longest x10 35.6 us: put(): lax.dynamic_update_slice_in_dim(self.found[d, e], self.ring.core(piece) i...]
  transfers between devices with their start and end apart: 10 -> 76, of which waited for: 7 -> 30; matrix products, arithmetic and copies ran while one was open for 17% -> 44% of each run, Pallas kernels for 0% -> 0%
where the time goes in v1:
time: 710 us; the launch traced here: 698 us
  waiting for transfers between devices  230 us (32%)
  matrix products  142 us (20%)
  local copies, waits for them, and re-layouts  121 us (17%)
  other arithmetic  115 us (16%)
  starting transfers between devices  86.7 us (12%)
    ppermute x72, waiting for transfers between devices, send(): arrived = lax.ppermute(block, ('seq', 'fsdp'), route)  202 us
    ppermute x72, starting transfers between devices, send(): arrived = lax.ppermute(block, ('seq', 'fsdp'), route)  64.7 us
    dot_general x16, matrix products, weight_grad(): jnp.einsum('ti,tj->ij', rows_all[key], columns_all[key], preferred_elemen...  35.9 us
    dynamic_update_slice x10, local copies, waits for them, and re-layouts, put(): lax.dynamic_update_slice_in_dim(self.found[d, e], self.ring.core(piece) i...  35.6 us
    dot_general x8, matrix products, project(): term = jnp.einsum('td,jd->tj', columns, weight, preferred_element_type=f32)  32 us
    all_to_all x1, waiting for transfers between devices, traded(): blocks = lax.all_to_all(added, 'seq', 0, 0, tiled=True)  19.9 us
    unnamed x224, local copies, waits for them, and re-layouts  17.3 us
  transfers between devices with their start and end apart: 76, of which 30 were waited for; matrix products, arithmetic and copies ran while one was open for 44% of the time, Pallas kernels for 0%

profile of v1, /device:TPU:0, one launch (start us, length us, event | category | flops | bytes accessed | tf_op | source)
XLA Modules:
  0.0 698.1 jit_solution(3696069821673183459)
XLA Ops:
  0.7 3.6 slice.318
  5.1 3.0 collective-permute-start.1
  9.0 3.5 slice.319
  17.7 3.1 fusion.144
  24.7 14.2 %collective-permute-done.4 = bf16[848,384]{1,0:T(8,128)(2,1)} collective-permute-done((bf16[848,384]{1,0:T(8,128)(2,1)}, bf16[848,384]{1,0:T(8,128)(2,1)}, u32[]{:S(2)}, u32[]{:S(2)}) %collective-permute-start.4) | collective-permute-done | bytes 651296 | tf_op jit(solution)/shard_map/ppermute | solution.py:36
  42.8 4.9 fusion.69
  47.7 8.5 %collective-permute-done.7 = bf16[848,384]{1,0:T(8,128)(2,1)S(1)} collective-permute-done((bf16[848,384]{1,0:T(8,128)(2,1)}, bf16[848,384]{1,0:T(8,128)(2,1)S(1)}, u32[]{:S(2)}, u32[]{:S(2)}) %collective-permute-start.7) | collective-permute-done | bytes 651296 | tf_op jit(solution)/shard_map/ppermute | solution.py:36
  57.3 4.2 collective-permute-done.10
  66.8 5.6 convolution_add_fusion.2
  74.1 4.2 dynamic_update_slice.90
  80.0 4.2 dynamic_update_slice.95
  84.5 4.0 dynamic_update_slice.91
  88.5 3.9 dynamic_update_slice.92
  94.7 2.9 dynamic_update_slice.93
  100.4 4.0 dynamic_update_slice.96
  104.4 4.2 dynamic_update_slice.97
  108.5 5.6 convolution_add_fusion.1
  119.6 3.9 fusion.4
  130.3 4.4 collective-permute-start.18
  140.1 7.1 %multiply_convert_fusion.3 = (bf16[256,3328]{0,1:T(8,128)(2,1)S(1)}, f32[256,3328]{0,1:T(8,128)}) fusion(f32[259,3328]{0,1:T(8,128)S(1)} %maximum_convert_fusion, f32[3328]{0:T(1024)S(1)} %copy-done.62, f32[3328]{0:T(1024)S(1)} %copy-done.60, f32[3328]{0:T(1024)S(1)} %copy-done.58, f32[3328]{0:T(1024)S(1)} %mul.748, f32[3328]{0:T(1024)S(1)} %copy-done.70), kind=kLoop, calls=%fused_computation.42 | loop fusion | flops 11075584 | bytes 18809856 | tf_op jit(solution)/shard_map/convert_element_type | solution.py:500
  155.5 6.2 all-to-all-start
  162.9 3.2 fusion.145
  176.3 3.9 fusion.5
  180.2 19.9 %all-to-all-done = f32[8,392,128]{2,1,0:T(8,128)S(1)} async-done(((f32[8,392,128]{2,1,0:T(8,128)}), f32[8,392,128]{2,1,0:T(8,128)S(1)}, u32[]{:S(2)}, u32[]{:S(2)}) %all-to-all-start) | async-done | bytes 1605664 | tf_op jit(solution)/shard_map/all_to_all | solution.py:292
  200.6 24.6 %collective-permute-done.22 = bf16[384,1536]{1,0:T(8,128)(2,1)} collective-permute-done((bf16[384,1536]{1,0:T(8,128)(2,1)}, bf16[384,1536]{1,0:T(8,128)(2,1)}, u32[]{:S(2)}, u32[]{:S(2)}) %collective-permute-start.22) | collective-permute-done | bytes 1179680 | tf_op jit(solution)/shard_map/ppermute | solution.py:36
  235.5 6.2 all-to-all-start.1
  252.8 12.5 %collective-permute-done.24 = bf16[256,1536]{1,0:T(8,128)(2,1)} collective-permute-done((bf16[256,1536]{1,0:T(8,128)(2,1)}, bf16[256,1536]{1,0:T(8,128)(2,1)}, u32[]{:S(2)}, u32[]{:S(2)}) %collective-permute-start.24) | collective-permute-done | bytes 786464 | tf_op jit(solution)/shard_map/ppermute | solution.py:36
  271.1 5.7 fusion.19
  287.2 3.9 fusion.14
  296.5 2.8 fusion.80
  299.4 6.9 collective-permute-done.30
  306.3 7.3 %collective-permute-done.31 = bf16[256,768]{1,0:T(8,128)(2,1)S(1)} collective-permute-done((bf16[256,768]{1,0:T(8,128)(2,1)S(1)}, bf16[256,768]{1,0:T(8,128)(2,1)S(1)}, u32[]{:S(2)}, u32[]{:S(2)}) %collective-permute-start.31) | collective-permute-done | bytes 393248 | tf_op jit(solution)/shard_map/ppermute | solution.py:36
  326.0 4.6 all-to-all-start.2
  330.6 10.6 %fusion = (f32[48,256]{1,0:T(8,128)}, f32[48,256]{1,0:T(8,128)}, f32[48,256]{1,0:T(8,128)}, bf16[256,256]{1,0:T(8,128)(2,1)S(1)}) fusion(f32[48,256]{1,0:T(8,128)} %get-tuple-element.275, f32[48,256]{1,0:T(8,128)} %get-tuple-element.306, f32[256,256]{1,0:T(8,128)} %fusion.104, pred[256,256]{1,0:T(8,128)(4,1)} %iota_compare_fusion, ...), kind=kOutput, calls=%fused_computation.5 | convolution fusion | flops 443445248 | bytes 3850240 | tf_op jit(solution)/shard_map/thp,shp->hts/dot_general | solution.py:387
  346.3 3.2 fusion.74
  349.5 16.5 %collective-permute-done.35 = bf16[384,1536]{1,0:T(8,128)(2,1)} collective-permute-done((bf16[384,1536]{1,0:T(8,128)(2,1)}, bf16[384,1536]{1,0:T(8,128)(2,1)}, u32[]{:S(2)}, u32[]{:S(2)}) %collective-permute-start.35) | collective-permute-done | bytes 1179680 | tf_op jit(solution)/shard_map/ppermute | solution.py:36
  366.0 3.0 convert_add_fusion.2
  369.0 4.6 fusion.151
  387.6 5.0 all-to-all-start.3
  397.4 7.7 %add_add_fusion.1 = f32[3072,384]{1,0:T(8,128)} fusion(f32[3072,384]{1,0:T(8,128)S(1)} %fusion.152, f32[3072,384]{1,0:T(8,128)} %fusion.74, f32[3072,384]{1,0:T(8,128)} %fusion.151, bf16[256,3072]{1,0:T(8,128)(2,1)} %collective-permute-done.36, bf16[256,384]{1,0:T(8,128)(2,1)S(1)} %collective-permute-done.28), kind=kOutput, calls=%fused_computation.27 | convolution fusion | flops 607518720 | bytes 20643840 | tf_op jit(solution)/shard_map/ti,tj->ij/dot_general | solution.py:550
  405.1 8.2 %all-to-all-done.3 = bf16[8,384,128]{2,1,0:T(8,128)(2,1)S(1)} async-done(((bf16[8,384,128]{2,1,0:T(8,128)(2,1)}), bf16[8,384,128]{2,1,0:T(8,128)(2,1)S(1)}, u32[]{:S(2)}, u32[]{:S(2)}) %all-to-all-start.3) | async-done | bytes 786464 | tf_op jit(solution)/shard_map/all_to_all | solution.py:309
  413.4 4.7 fusion.21
  425.9 5.6 fusion.16
  443.2 8.8 %collective-permute-done.39 = bf16[1536,384]{1,0:T(8,128)(2,1)} collective-permute-done((bf16[1536,384]{1,0:T(8,128)(2,1)}, bf16[1536,384]{1,0:T(8,128)(2,1)}, u32[]{:S(2)}, u32[]{:S(2)}) %collective-permute-start.39) | collective-permute-done | bytes 1179680 | tf_op jit(solution)/shard_map/ppermute | solution.py:36
  452.0 13.8 %multiply_reduce_fusion.5 = (f32[3328]{0:T(1024)}, f32[3328]{0:T(1024)S(1)}, f32[3328]{0:T(1024)S(1)}, f32[3328]{0:T(1024)S(1)}, f32[3328]{0:T(1024)}, /*index=5*/f32[256,3328]{0,1:T(8,128)S(1)}) fusion(f32[259,3328]{0,1:T(8,128)} %copy-done, f32[256,3328]{0,1:T(8,128)S(1)} %copy-done.19, f32[256,128]{0,1:T(8,128)S(1)} %copy-done.46, ...), kind=kLoop, calls=%fused_computation.41 | loop fusion | flops 17022720 | bytes 23921664 | tf_op jit(solution)/shard_map/transpose(jvp())/reduce_sum | solution.py:331
  470.4 5.7 pad_add_fusion
  478.7 2.9 convert_add_fusion.1
  487.0 3.6 collective-permute-start.42
  493.1 4.1 fusion.8
  498.6 5.9 collective-permute-done.42
  514.5 14.8 %collective-permute-done.47 = bf16[384,384]{1,0:T(8,128)(2,1)} collective-permute-done((bf16[384,384]{1,0:T(8,128)(2,1)}, bf16[384,384]{1,0:T(8,128)(2,1)}, u32[]{:S(2)}, u32[]{:S(2)}) %collective-permute-start.47) | collective-permute-done | bytes 294944 | tf_op jit(solution)/shard_map/ppermute | solution.py:36
  543.9 13.7 %collective-permute-done.51 = bf16[384,384]{1,0:T(8,128)(2,1)S(1)} collective-permute-done((bf16[384,384]{1,0:T(8,128)(2,1)S(1)}, bf16[384,384]{1,0:T(8,128)(2,1)S(1)}, u32[]{:S(2)}, u32[]{:S(2)}) %collective-permute-start.51) | collective-permute-done | bytes 294944 | tf_op jit(solution)/shard_map/ppermute | solution.py:36
  564.9 9.3 %collective-permute-done.54 = bf16[448,384]{1,0:T(8,128)(2,1)S(1)} collective-permute-done((bf16[448,384]{1,0:T(8,128)(2,1)S(1)}, bf16[448,384]{1,0:T(8,128)(2,1)S(1)}, u32[]{:S(2)}, u32[]{:S(2)}) %collective-permute-start.54) | collective-permute-done | bytes 344096 | tf_op jit(solution)/shard_map/ppermute | solution.py:36
  574.2 4.9 collective-permute-done.53
  593.2 2.9 fusion.156
  609.2 3.3 fusion.26
  620.5 2.8 maximum_convert_fusion.1
  627.6 14.8 %collective-permute-done.61 = bf16[1536,384]{1,0:T(8,128)(2,1)S(1)} collective-permute-done((bf16[1536,384]{1,0:T(8,128)(2,1)S(1)}, bf16[1536,384]{1,0:T(8,128)(2,1)S(1)}, u32[]{:S(2)}, u32[]{:S(2)}) %collective-permute-start.61) | collective-permute-done | bytes 1179680 | tf_op jit(solution)/shard_map/ppermute | solution.py:36
  646.9 4.5 pad_convert_fusion
  651.5 2.8 collective-permute-done.64
  659.7 12.2 %collective-permute-done.65 = f32[168,128]{1,0:T(8,128)S(1)} collective-permute-done((f32[168,128]{1,0:T(8,128)S(1)}, f32[168,128]{1,0:T(8,128)S(1)}, u32[]{:S(2)}, u32[]{:S(2)}) %collective-permute-start.65) | collective-permute-done | bytes 86048 | tf_op jit(solution)/shard_map/ppermute | solution.py:36
  676.7 4.7 collective-permute-done.68
  684.7 3.1 collective-permute-done.70
  692.4 3.0 collective-permute-done.71
  (573 shorter events, 277.2 us)
Async XLA Ops:
  4.3 9.4 %collective-permute-start.3 = (bf16[3376,384]{1,0:T(8,128)(2,1)}, bf16[3376,384]{1,0:T(8,128)(2,1)}, u32[]{:S(2)}, u32[]{:S(2)}) collective-permute-start(bf16[3376,384]{1,0:T(8,128)(2,1)} %slice.318), channel_id=1, source_target_pairs={{0,1},{1,0},{2,3},{3,2},{4,5},{5,4},{6,7},{7,6},{8,9},{9,8},{10,11... | collective-permute-start | bytes 7778312 | tf_op jit(solution)/shard_map/ppermute | solution.py:36
  13.7 25.1 %collective-permute-start.5 = (bf16[3072,384]{1,0:T(8,128)(2,1)}, bf16[3072,384]{1,0:T(8,128)(2,1)}, u32[]{:S(2)}, u32[]{:S(2)}) collective-permute-start(bf16[3072,384]{1,0:T(8,128)(2,1)} %slice.319), channel_id=1, source_target_pairs={{0,1},{1,0},{2,3},{3,2},{4,5},{5,4},{6,7},{7,6},{8,9},{9,8},{10,11... | collective-permute-start | bytes 7077896 | tf_op jit(solution)/shard_map/ppermute | solution.py:36
  14.0 24.9 %collective-permute-start.6 = (bf16[768,1536]{1,0:T(8,128)(2,1)S(1)}, bf16[768,1536]{1,0:T(8,128)(2,1)}, u32[]{:S(2)}, u32[]{:S(2)}) collective-permute-start(bf16[768,1536]{1,0:T(8,128)(2,1)S(1)} %copy-done.26), channel_id=1, source_target_pairs={{0,1},{1,0},{2,3},{3,2},{4,5},{5,4},{6,7},{7,6},{8,9},{9,8},{10,11... | collective-permute-start | bytes 7077896 | tf_op jit(solution)/shard_map/ppermute | solution.py:36
  21.7 17.1 %collective-permute-start.4 = (bf16[848,384]{1,0:T(8,128)(2,1)}, bf16[848,384]{1,0:T(8,128)(2,1)}, u32[]{:S(2)}, u32[]{:S(2)}) collective-permute-start(bf16[848,384]{1,0:T(8,128)(2,1)} %constant_dynamic-slice_fusion.8), channel_id=1, source_target_pairs={{0,2},{1,3},{2,0},{3,1},{4,6},{5,7},{6,4},{7,5},{8,10},{9,11},{10,... | collective-permute-start | bytes 1953800 | tf_op jit(solution)/shard_map/ppermute | solution.py:36
  38.8 8.8 %collective-permute-start.9 = (bf16[848,384]{1,0:T(8,128)(2,1)}, bf16[848,384]{1,0:T(8,128)(2,1)S(1)}, u32[]{:S(2)}, u32[]{:S(2)}) collective-permute-start(bf16[848,384]{1,0:T(8,128)(2,1)} %collective-permute-done.4), channel_id=1, source_target_pairs={{0,1},{1,0},{2,3},{3,2},{4,5},{5,4},{6,7},{7,6},{8,9},{9,8},{10,11... | collective-permute-start | bytes 1953800 | tf_op jit(solution)/shard_map/ppermute | solution.py:36
  38.9 17.3 %collective-permute-start.7 = (bf16[848,384]{1,0:T(8,128)(2,1)}, bf16[848,384]{1,0:T(8,128)(2,1)S(1)}, u32[]{:S(2)}, u32[]{:S(2)}) collective-permute-start(bf16[848,384]{1,0:T(8,128)(2,1)} %collective-permute-done.4), channel_id=1, source_target_pairs={{0,4},{1,5},{2,6},{3,7},{4,0},{5,1},{6,2},{7,3},{8,12},{9,13},{10,... | collective-permute-start | bytes 1953800 | tf_op jit(solution)/shard_map/ppermute | solution.py:36
  40.4 16.9 %collective-permute-start.8 = (bf16[848,384]{1,0:T(8,128)(2,1)}, bf16[848,384]{1,0:T(8,128)(2,1)S(1)}, u32[]{:S(2)}, u32[]{:S(2)}) collective-permute-start(bf16[848,384]{1,0:T(8,128)(2,1)} %collective-permute-done.4), channel_id=1, source_target_pairs={{0,8},{1,9},{2,10},{3,11},{4,12},{5,13},{6,14},{7,15},{8,0},{9,1},... | collective-permute-start | bytes 1953800 | tf_op jit(solution)/shard_map/ppermute | solution.py:36
  42.0 19.5 %collective-permute-start.10 = (bf16[1024,384]{1,0:T(8,128)(2,1)}, bf16[1024,384]{1,0:T(8,128)(2,1)S(1)}, u32[]{:S(2)}, u32[]{:S(2)}) collective-permute-start(bf16[1024,384]{1,0:T(8,128)(2,1)} %get-tuple-element.119), channel_id=1, source_target_pairs={{0,2},{1,3},{2,0},{3,1},{4,6},{5,7},{6,4},{7,5},{8,10},{9,11},{10,... | collective-permute-start | bytes 2359304 | tf_op jit(solution)/shard_map/ppermute | solution.py:36
  62.4 30.0 %collective-permute-start.13 = (bf16[848,384]{1,0:T(8,128)(2,1)S(1)}, bf16[848,384]{1,0:T(8,128)(2,1)S(1)}, u32[]{:S(2)}, u32[]{:S(2)}) collective-permute-start(bf16[848,384]{1,0:T(8,128)(2,1)S(1)} %collective-permute-done.7), channel_id=1, source_target_pairs={{0,1},{1,0},{2,3},{3,2},{4,5},{5,4},{6,7},{7,6},{8,9},{9,8},{10,11... | collective-permute-start | bytes 1953800 | tf_op jit(solution)/shard_map/ppermute | solution.py:36
  62.4 30.0 %collective-permute-start.14 = (bf16[848,384]{1,0:T(8,128)(2,1)S(1)}, bf16[848,384]{1,0:T(8,128)(2,1)}, u32[]{:S(2)}, u32[]{:S(2)}) collective-permute-start(bf16[848,384]{1,0:T(8,128)(2,1)S(1)} %collective-permute-done.8), channel_id=1, source_target_pairs={{0,1},{1,0},{2,3},{3,2},{4,5},{5,4},{6,7},{7,6},{8,9},{9,8},{10,11... | collective-permute-start | bytes 1953800 | tf_op jit(solution)/shard_map/ppermute | solution.py:36
  65.8 26.6 %collective-permute-start.12 = (bf16[416,384]{1,0:T(8,128)(2,1)}, bf16[416,384]{1,0:T(8,128)(2,1)}, u32[]{:S(2)}, u32[]{:S(2)}) collective-permute-start(bf16[416,384]{1,0:T(8,128)(2,1)} %slice.248), channel_id=1, source_target_pairs={{0,8},{1,9},{2,10},{3,11},{4,12},{5,13},{6,14},{7,15},{8,0},{9,1},... | collective-permute-start | bytes 958472 | tf_op jit(solution)/shard_map/ppermute | solution.py:36
  66.3 26.2 %collective-permute-start.11 = (bf16[432,384]{1,0:T(8,128)(2,1)}, bf16[432,384]{1,0:T(8,128)(2,1)}, u32[]{:S(2)}, u32[]{:S(2)}) collective-permute-start(bf16[432,384]{1,0:T(8,128)(2,1)} %slice.247), channel_id=1, source_target_pairs={{0,4},{1,5},{2,6},{3,7},{4,0},{5,1},{6,2},{7,3},{8,12},{9,13},{10,... | collective-permute-start | bytes 995336 | tf_op jit(solution)/shard_map/ppermute | solution.py:36
  84.2 39.3 %collective-permute-start.17 = (bf16[1024,384]{1,0:T(8,128)(2,1)}, bf16[1024,384]{1,0:T(8,128)(2,1)}, u32[]{:S(2)}, u32[]{:S(2)}) collective-permute-start(bf16[1024,384]{1,0:T(8,128)(2,1)} %get-tuple-element.126), channel_id=1, source_target_pairs={{0,2},{1,3},{2,0},{3,1},{4,6},{5,7},{6,4},{7,5},{8,10},{9,11},{10,... | collective-permute-start | bytes 2359304 | tf_op jit(solution)/shard_map/ppermute | solution.py:36
  92.5 21.7 %collective-permute-start.15 = (bf16[432,384]{1,0:T(8,128)(2,1)}, bf16[432,384]{1,0:T(8,128)(2,1)S(1)}, u32[]{:S(2)}, u32[]{:S(2)}) collective-permute-start(bf16[432,384]{1,0:T(8,128)(2,1)} %collective-permute-done.11), channel_id=1, source_target_pairs={{0,1},{1,0},{2,3},{3,2},{4,5},{5,4},{6,7},{7,6},{8,9},{9,8},{10,11... | collective-permute-start | bytes 995336 | tf_op jit(solution)/shard_map/ppermute | solution.py:36
  92.5 24.4 %collective-permute-start.16 = (bf16[416,384]{1,0:T(8,128)(2,1)}, bf16[416,384]{1,0:T(8,128)(2,1)S(1)}, u32[]{:S(2)}, u32[]{:S(2)}) collective-permute-start(bf16[416,384]{1,0:T(8,128)(2,1)} %collective-permute-done.12), channel_id=1, source_target_pairs={{0,1},{1,0},{2,3},{3,2},{4,5},{5,4},{6,7},{7,6},{8,9},{9,8},{10,11... | collective-permute-start | bytes 958472 | tf_op jit(solution)/shard_map/ppermute | solution.py:36
  93.0 55.4 %collective-permute-start.19 = (bf16[1024,384]{1,0:T(8,128)(2,1)S(1)}, bf16[1024,384]{1,0:T(8,128)(2,1)}, u32[]{:S(2)}, u32[]{:S(2)}) collective-permute-start(bf16[1024,384]{1,0:T(8,128)(2,1)S(1)} %copy-done.42), channel_id=1, source_target_pairs={{0,2},{1,3},{2,0},{3,1},{4,6},{5,7},{6,4},{7,5},{8,10},{9,11},{10,... | collective-permute-start | bytes 2359304 | tf_op jit(solution)/shard_map/ppermute | solution.py:36
  154.2 22.0 %collective-permute-start.20 = (bf16[3072,384]{1,0:T(8,128)(2,1)}, bf16[3072,384]{1,0:T(8,128)(2,1)}, u32[]{:S(2)}, u32[]{:S(2)}) collective-permute-start(bf16[3072,384]{1,0:T(8,128)(2,1)} %constant_dynamic-update-slice_fusion), channel_id=1, source_target_pairs={{0,1},{1,0},{2,3},{3,2},{4,5},{5,4},{6,7},{7,6},{8,9},{9,8},{10,11... | collective-permute-start | bytes 7077896 | tf_op jit(solution)/shard_map/ppermute | solution.py:36
  155.5 44.6 %all-to-all-start = ((f32[8,392,128]{2,1,0:T(8,128)}), f32[8,392,128]{2,1,0:T(8,128)S(1)}, u32[]{:S(2)}, u32[]{:S(2)}) async-start(f32[8,392,128]{2,1,0:T(8,128)} %pad_maximum_fusion.2), calls=%async_computation | async-start | bytes 3211264 | tf_op jit(solution)/shard_map/all_to_all | solution.py:292
  171.4 29.2 %collective-permute-start.21 = (bf16[384,1536]{1,0:T(8,128)(2,1)}, bf16[384,1536]{1,0:T(8,128)(2,1)}, u32[]{:S(2)}, u32[]{:S(2)}) collective-permute-start(bf16[384,1536]{1,0:T(8,128)(2,1)} %get-tuple-element.135), channel_id=1, source_target_pairs={{0,2},{1,3},{2,0},{3,1},{4,6},{5,7},{6,4},{7,5},{8,10},{9,11},{10,... | collective-permute-start | bytes 3538952 | tf_op jit(solution)/shard_map/ppermute | solution.py:36
  172.1 53.2 %collective-permute-start.22 = (bf16[384,1536]{1,0:T(8,128)(2,1)}, bf16[384,1536]{1,0:T(8,128)(2,1)}, u32[]{:S(2)}, u32[]{:S(2)}) collective-permute-start(bf16[384,1536]{1,0:T(8,128)(2,1)} %get-tuple-element.136), channel_id=1, source_target_pairs={{0,2},{1,3},{2,0},{3,1},{4,6},{5,7},{6,4},{7,5},{8,10},{9,11},{10,... | collective-permute-start | bytes 3538952 | tf_op jit(solution)/shard_map/ppermute | solution.py:36
  230.0 35.3 %collective-permute-start.23 = (bf16[768,1536]{1,0:T(8,128)(2,1)}, bf16[768,1536]{1,0:T(8,128)(2,1)}, u32[]{:S(2)}, u32[]{:S(2)}) collective-permute-start(bf16[768,1536]{1,0:T(8,128)(2,1)} %constant_dynamic-update-slice_fusion.3), channel_id=1, source_target_pairs={{0,1},{1,0},{2,3},{3,2},{4,5},{5,4},{6,7},{7,6},{8,9},{9,8},{10,11... | collective-permute-start | bytes 7077896 | tf_op jit(solution)/shard_map/ppermute | solution.py:36
  235.5 29.8 %all-to-all-start.1 = ((bf16[8,384,128]{2,1,0:T(8,128)(2,1)}), bf16[8,384,128]{2,1,0:T(8,128)(2,1)}, u32[]{:S(2)}, u32[]{:S(2)}) async-start(bf16[8,384,128]{2,1,0:T(8,128)(2,1)} %fusion.78), calls=%async_computation.1 | async-start | bytes 1572864 | tf_op jit(solution)/shard_map/all_to_all | solution.py:309
  245.3 20.1 %collective-permute-start.24 = (bf16[256,1536]{1,0:T(8,128)(2,1)}, bf16[256,1536]{1,0:T(8,128)(2,1)}, u32[]{:S(2)}, u32[]{:S(2)}) collective-permute-start(bf16[256,1536]{1,0:T(8,128)(2,1)} %bitcast_select_fusion), channel_id=1, source_target_pairs={{0,2},{1,3},{2,0},{3,1},{4,6},{5,7},{6,4},{7,5},{8,10},{9,11},{10,... | collective-permute-start | bytes 2359304 | tf_op jit(solution)/shard_map/ppermute | solution.py:36
  245.8 19.5 %collective-permute-start.25 = (bf16[256,1536]{1,0:T(8,128)(2,1)}, bf16[256,1536]{1,0:T(8,128)(2,1)}, u32[]{:S(2)}, u32[]{:S(2)}) collective-permute-start(bf16[256,1536]{1,0:T(8,128)(2,1)} %bitcast_select_fusion), channel_id=1, source_target_pairs={{0,1},{1,0},{2,3},{3,2},{4,5},{5,4},{6,7},{7,6},{8,9},{9,8},{10,11... | collective-permute-start | bytes 2359304 | tf_op jit(solution)/shard_map/ppermute | solution.py:36
  267.5 23.6 %collective-permute-start.26 = (bf16[256,384]{1,0:T(8,128)(2,1)}, bf16[256,384]{1,0:T(8,128)(2,1)}, u32[]{:S(2)}, u32[]{:S(2)}) collective-permute-start(bf16[256,384]{1,0:T(8,128)(2,1)} %get-tuple-element.287), channel_id=1, source_target_pairs={{0,1},{1,0},{2,3},{3,2},{4,5},{5,4},{6,7},{7,6},{8,9},{9,8},{10,11... | collective-permute-start | bytes 589832 | tf_op jit(solution)/shard_map/ppermute | solution.py:36
  267.5 23.6 %collective-permute-start.27 = (bf16[256,384]{1,0:T(8,128)(2,1)}, bf16[256,384]{1,0:T(8,128)(2,1)}, u32[]{:S(2)}, u32[]{:S(2)}) collective-permute-start(bf16[256,384]{1,0:T(8,128)(2,1)} %get-tuple-element.286), channel_id=1, source_target_pairs={{0,2},{1,3},{2,0},{3,1},{4,6},{5,7},{6,4},{7,5},{8,10},{9,11},{10,... | collective-permute-start | bytes 589832 | tf_op jit(solution)/shard_map/ppermute | solution.py:36
  268.0 23.1 %collective-permute-start.28 = (bf16[256,384]{1,0:T(8,128)(2,1)}, bf16[256,384]{1,0:T(8,128)(2,1)S(1)}, u32[]{:S(2)}, u32[]{:S(2)}) collective-permute-start(bf16[256,384]{1,0:T(8,128)(2,1)} %get-tuple-element.285), channel_id=1, source_target_pairs={{0,3},{1,2},{2,1},{3,0},{4,7},{5,6},{6,5},{7,4},{8,11},{9,10},{10,... | collective-permute-start | bytes 589832 | tf_op jit(solution)/shard_map/ppermute | solution.py:36
  291.1 22.4 %collective-permute-start.32 = (bf16[256,1536]{1,0:T(8,128)(2,1)}, bf16[256,1536]{1,0:T(8,128)(2,1)}, u32[]{:S(2)}, u32[]{:S(2)}) collective-permute-start(bf16[256,1536]{1,0:T(8,128)(2,1)} %collective-permute-done.24), channel_id=1, source_target_pairs={{0,1},{1,0},{2,3},{3,2},{4,5},{5,4},{6,7},{7,6},{8,9},{9,8},{10,11... | collective-permute-start | bytes 2359304 | tf_op jit(solution)/shard_map/ppermute | solution.py:36
  294.3 11.9 %collective-permute-start.30 = (bf16[256,768]{1,0:T(8,128)(2,1)S(1)}, bf16[256,768]{1,0:T(8,128)(2,1)S(1)}, u32[]{:S(2)}, u32[]{:S(2)}) collective-permute-start(bf16[256,768]{1,0:T(8,128)(2,1)S(1)} %get-tuple-element.279), channel_id=1, source_target_pairs={{0,2},{1,3},{2,0},{3,1},{4,6},{5,7},{6,4},{7,5},{8,10},{9,11},{10,... | collective-permute-start | bytes 1179656 | tf_op jit(solution)/shard_map/ppermute | solution.py:36
  294.8 18.7 %collective-permute-start.31 = (bf16[256,768]{1,0:T(8,128)(2,1)S(1)}, bf16[256,768]{1,0:T(8,128)(2,1)S(1)}, u32[]{:S(2)}, u32[]{:S(2)}) collective-permute-start(bf16[256,768]{1,0:T(8,128)(2,1)S(1)} %get-tuple-element.278), channel_id=1, source_target_pairs={{0,3},{1,2},{2,1},{3,0},{4,7},{5,6},{6,5},{7,4},{8,11},{9,10},{10,... | collective-permute-start | bytes 1179656 | tf_op jit(solution)/shard_map/ppermute | solution.py:36
  313.6 60.0 %collective-permute-start.33 = (bf16[256,3072]{1,0:T(8,128)(2,1)S(1)}, bf16[256,3072]{1,0:T(8,128)(2,1)}, u32[]{:S(2)}, u32[]{:S(2)}) collective-permute-start(bf16[256,3072]{1,0:T(8,128)(2,1)S(1)} %copy-done.1), channel_id=1, source_target_pairs={{0,2},{1,3},{2,0},{3,1},{4,6},{5,7},{6,4},{7,5},{8,10},{9,11},{10,... | collective-permute-start | bytes 4718600 | tf_op jit(solution)/shard_map/ppermute | solution.py:36
  314.1 54.9 %collective-permute-start.34 = (bf16[256,3072]{1,0:T(8,128)(2,1)S(1)}, bf16[256,3072]{1,0:T(8,128)(2,1)}, u32[]{:S(2)}, u32[]{:S(2)}) collective-permute-start(bf16[256,3072]{1,0:T(8,128)(2,1)S(1)} %copy-done.1), channel_id=1, source_target_pairs={{0,1},{1,0},{2,3},{3,2},{4,5},{5,4},{6,7},{7,6},{8,9},{9,8},{10,11... | collective-permute-start | bytes 4718600 | tf_op jit(solution)/shard_map/ppermute | solution.py:36
  324.3 41.7 %collective-permute-start.35 = (bf16[384,1536]{1,0:T(8,128)(2,1)}, bf16[384,1536]{1,0:T(8,128)(2,1)}, u32[]{:S(2)}, u32[]{:S(2)}) collective-permute-start(bf16[384,1536]{1,0:T(8,128)(2,1)} %dynamic-slice_convert_fusion.1), channel_id=1, source_target_pairs={{0,4},{1,5},{2,6},{3,7},{4,0},{5,1},{6,2},{7,3},{8,12},{9,13},{10,... | collective-permute-start | bytes 3538952 | tf_op jit(solution)/shard_map/ppermute | solution.py:36
  326.0 47.6 %all-to-all-start.2 = ((f32[8,384,128]{2,1,0:T(8,128)}), f32[8,384,128]{2,1,0:T(8,128)}, u32[]{:S(2)}, u32[]{:S(2)}) async-start(f32[8,384,128]{2,1,0:T(8,128)} %bitcast.281), calls=%async_computation.2 | async-start | bytes 3145728 | tf_op jit(solution)/shard_map/all_to_all | solution.py:290
  375.7 19.4 %collective-permute-start.37 = (bf16[192,1536]{1,0:T(8,128)(2,1)}, bf16[192,1536]{1,0:T(8,128)(2,1)}, u32[]{:S(2)}, u32[]{:S(2)}) collective-permute-start(bf16[192,1536]{1,0:T(8,128)(2,1)} %dynamic-slice_convert_fusion.5), channel_id=1, source_target_pairs={{0,8},{1,9},{2,10},{3,11},{4,12},{5,13},{6,14},{7,15},{8,0},{9,1},... | collective-permute-start | bytes 1769480 | tf_op jit(solution)/shard_map/ppermute | solution.py:36
  377.5 20.0 %collective-permute-start.36 = (bf16[256,3072]{1,0:T(8,128)(2,1)}, bf16[256,3072]{1,0:T(8,128)(2,1)}, u32[]{:S(2)}, u32[]{:S(2)}) collective-permute-start(bf16[256,3072]{1,0:T(8,128)(2,1)} %collective-permute-done.33), channel_id=1, source_target_pairs={{0,1},{1,0},{2,3},{3,2},{4,5},{5,4},{6,7},{7,6},{8,9},{9,8},{10,11... | collective-permute-start | bytes 4718600 | tf_op jit(solution)/shard_map/ppermute | solution.py:36
  387.6 25.8 %all-to-all-start.3 = ((bf16[8,384,128]{2,1,0:T(8,128)(2,1)}), bf16[8,384,128]{2,1,0:T(8,128)(2,1)S(1)}, u32[]{:S(2)}, u32[]{:S(2)}) async-start(bf16[8,384,128]{2,1,0:T(8,128)(2,1)} %broadcast_dynamic-update-slice_fusion), calls=%async_computation.3 | async-start | bytes 1572864 | tf_op jit(solution)/shard_map/all_to_all | solution.py:309
  421.6 20.6 %collective-permute-start.38 = (bf16[96,1536]{1,0:T(8,128)(2,1)}, bf16[96,1536]{1,0:T(8,128)(2,1)}, u32[]{:S(2)}, u32[]{:S(2)}) collective-permute-start(bf16[96,1536]{1,0:T(8,128)(2,1)} %dynamic-slice_convert_fusion.9), channel_id=1, source_target_pairs={{0,16},{1,17},{2,18},{3,19},{4,20},{5,21},{6,22},{7,23},{8,24},{9,... | collective-permute-start | bytes 884744 | tf_op jit(solution)/shard_map/ppermute | solution.py:36
  424.4 27.6 %collective-permute-start.39 = (bf16[1536,384]{1,0:T(8,128)(2,1)}, bf16[1536,384]{1,0:T(8,128)(2,1)}, u32[]{:S(2)}, u32[]{:S(2)}) collective-permute-start(bf16[1536,384]{1,0:T(8,128)(2,1)} %dynamic-slice_convert_fusion), channel_id=1, source_target_pairs={{0,4},{1,5},{2,6},{3,7},{4,0},{5,1},{6,2},{7,3},{8,12},{9,13},{10,... | collective-permute-start | bytes 3538952 | tf_op jit(solution)/shard_map/ppermute | solution.py:36
  476.1 21.3 %collective-permute-start.41 = (bf16[96,1536]{1,0:T(8,128)(2,1)S(1)}, bf16[96,1536]{1,0:T(8,128)(2,1)}, u32[]{:S(2)}, u32[]{:S(2)}) collective-permute-start(bf16[96,1536]{1,0:T(8,128)(2,1)S(1)} %add_convert_fusion.1), channel_id=1, source_target_pairs={{0,16},{1,17},{2,18},{3,19},{4,20},{5,21},{6,22},{7,23},{8,24},{9,... | collective-permute-start | bytes 884744 | tf_op jit(solution)/shard_map/ppermute | solution.py:36
  487.0 17.6 %collective-permute-start.42 = (bf16[768,384]{1,0:T(8,128)(2,1)S(1)}, bf16[768,384]{1,0:T(8,128)(2,1)}, u32[]{:S(2)}, u32[]{:S(2)}) collective-permute-start(bf16[768,384]{1,0:T(8,128)(2,1)S(1)} %dynamic-slice_convert_fusion.4), channel_id=1, source_target_pairs={{0,8},{1,9},{2,10},{3,11},{4,12},{5,13},{6,14},{7,15},{8,0},{9,1},... | collective-permute-start | bytes 1769480 | tf_op jit(solution)/shard_map/ppermute | solution.py:36
  505.6 25.9 %collective-permute-start.44 = (bf16[256,1792]{0,1:T(8,128)(2,1)}, bf16[256,1792]{0,1:T(8,128)(2,1)}, u32[]{:S(2)}, u32[]{:S(2)}) collective-permute-start(bf16[256,1792]{0,1:T(8,128)(2,1)} %slice.306), channel_id=1, source_target_pairs={{0,1},{1,0},{2,3},{3,2},{4,5},{5,4},{6,7},{7,6},{8,9},{9,8},{10,11... | collective-permute-start | bytes 2752520 | tf_op jit(solution)/shard_map/ppermute | solution.py:36
  505.7 25.8 %collective-permute-start.43 = (bf16[256,1792]{0,1:T(8,128)(2,1)}, bf16[256,1792]{0,1:T(8,128)(2,1)}, u32[]{:S(2)}, u32[]{:S(2)}) collective-permute-start(bf16[256,1792]{0,1:T(8,128)(2,1)} %slice.306), channel_id=1, source_target_pairs={{0,2},{1,3},{2,0},{3,1},{4,6},{5,7},{6,4},{7,5},{8,10},{9,11},{10,... | collective-permute-start | bytes 2752520 | tf_op jit(solution)/shard_map/ppermute | solution.py:36
  508.3 23.2 %collective-permute-start.45 = (bf16[256,1664]{0,1:T(8,128)(2,1)}, bf16[256,1664]{0,1:T(8,128)(2,1)}, u32[]{:S(2)}, u32[]{:S(2)}) collective-permute-start(bf16[256,1664]{0,1:T(8,128)(2,1)} %pad.49), channel_id=1, source_target_pairs={{0,1},{1,0},{2,3},{3,2},{4,5},{5,4},{6,7},{7,6},{8,9},{9,8},{10,11... | collective-permute-start | bytes 2555912 | tf_op jit(solution)/shard_map/ppermute | solution.py:36
  509.3 22.2 %collective-permute-start.46 = (bf16[192,1536]{1,0:T(8,128)(2,1)}, bf16[192,1536]{1,0:T(8,128)(2,1)}, u32[]{:S(2)}, u32[]{:S(2)}) collective-permute-start(bf16[192,1536]{1,0:T(8,128)(2,1)} %pad_maximum_fusion.7), channel_id=1, source_target_pairs={{0,8},{1,9},{2,10},{3,11},{4,12},{5,13},{6,14},{7,15},{8,0},{9,1},... | collective-permute-start | bytes 1769480 | tf_op jit(solution)/shard_map/ppermute | solution.py:36
  512.2 17.1 %collective-permute-start.47 = (bf16[384,384]{1,0:T(8,128)(2,1)}, bf16[384,384]{1,0:T(8,128)(2,1)}, u32[]{:S(2)}, u32[]{:S(2)}) collective-permute-start(bf16[384,384]{1,0:T(8,128)(2,1)} %dynamic-slice_convert_fusion.8), channel_id=1, source_target_pairs={{0,16},{1,17},{2,18},{3,19},{4,20},{5,21},{6,22},{7,23},{8,24},{9,... | collective-permute-start | bytes 884744 | tf_op jit(solution)/shard_map/ppermute | solution.py:36
  532.9 24.7 %collective-permute-start.48 = (bf16[256,1664]{0,1:T(8,128)(2,1)}, bf16[256,1664]{0,1:T(8,128)(2,1)S(1)}, u32[]{:S(2)}, u32[]{:S(2)}) collective-permute-start(bf16[256,1664]{0,1:T(8,128)(2,1)} %pad.49), channel_id=1, source_target_pairs={{0,2},{1,3},{2,0},{3,1},{4,6},{5,7},{6,4},{7,5},{8,10},{9,11},{10,... | collective-permute-start | bytes 2555912 | tf_op jit(solution)/shard_map/ppermute | solution.py:36
  539.9 17.8 %collective-permute-start.50 = (bf16[896,384]{1,0:T(8,128)(2,1)S(1)}, bf16[896,384]{1,0:T(8,128)(2,1)S(1)}, u32[]{:S(2)}, u32[]{:S(2)}) collective-permute-start(bf16[896,384]{1,0:T(8,128)(2,1)S(1)} %dynamic-slice_convert_fusion.2), channel_id=1, source_target_pairs={{0,4},{1,5},{2,6},{3,7},{4,0},{5,1},{6,2},{7,3},{8,12},{9,13},{10,... | collective-permute-start | bytes 2064392 | tf_op jit(solution)/shard_map/ppermute | solution.py:36
  541.3 16.3 %collective-permute-start.51 = (bf16[384,384]{1,0:T(8,128)(2,1)S(1)}, bf16[384,384]{1,0:T(8,128)(2,1)S(1)}, u32[]{:S(2)}, u32[]{:S(2)}) collective-permute-start(bf16[384,384]{1,0:T(8,128)(2,1)S(1)} %add_convert_fusion), channel_id=1, source_target_pairs={{0,16},{1,17},{2,18},{3,19},{4,20},{5,21},{6,22},{7,23},{8,24},{9,... | collective-permute-start | bytes 884744 | tf_op jit(solution)/shard_map/ppermute | solution.py:36
  562.6 16.5 %collective-permute-start.53 = (bf16[832,384]{1,0:T(8,128)(2,1)S(1)}, bf16[832,384]{1,0:T(8,128)(2,1)S(1)}, u32[]{:S(2)}, u32[]{:S(2)}) collective-permute-start(bf16[832,384]{1,0:T(8,128)(2,1)S(1)} %dynamic-slice_convert_fusion.3), channel_id=1, source_target_pairs={{0,4},{1,5},{2,6},{3,7},{4,0},{5,1},{6,2},{7,3},{8,12},{9,13},{10,... | collective-permute-start | bytes 1916936 | tf_op jit(solution)/shard_map/ppermute | solution.py:36
  564.2 9.9 %collective-permute-start.54 = (bf16[448,384]{1,0:T(8,128)(2,1)S(1)}, bf16[448,384]{1,0:T(8,128)(2,1)S(1)}, u32[]{:S(2)}, u32[]{:S(2)}) collective-permute-start(bf16[448,384]{1,0:T(8,128)(2,1)S(1)} %dynamic-slice_convert_fusion.6), channel_id=1, source_target_pairs={{0,8},{1,9},{2,10},{3,11},{4,12},{5,13},{6,14},{7,15},{8,0},{9,1},... | collective-permute-start | bytes 1032200 | tf_op jit(solution)/shard_map/ppermute | solution.py:36
  587.4 28.4 %collective-permute-start.56 = (bf16[384,1536]{1,0:T(8,128)(2,1)S(1)}, bf16[384,1536]{1,0:T(8,128)(2,1)}, u32[]{:S(2)}, u32[]{:S(2)}) collective-permute-start(bf16[384,1536]{1,0:T(8,128)(2,1)S(1)} %pad_maximum_fusion.3), channel_id=1, source_target_pairs={{0,4},{1,5},{2,6},{3,7},{4,0},{5,1},{6,2},{7,3},{8,12},{9,13},{10,... | collective-permute-start | bytes 3538952 | tf_op jit(solution)/shard_map/ppermute | solution.py:36
  589.0 25.5 %collective-permute-start.57 = (bf16[768,384]{1,0:T(8,128)(2,1)S(1)}, bf16[768,384]{1,0:T(8,128)(2,1)}, u32[]{:S(2)}, u32[]{:S(2)}) collective-permute-start(bf16[768,384]{1,0:T(8,128)(2,1)S(1)} %pad_maximum_fusion.8), channel_id=1, source_target_pairs={{0,8},{1,9},{2,10},{3,11},{4,12},{5,13},{6,14},{7,15},{8,0},{9,1},... | collective-permute-start | bytes 1769480 | tf_op jit(solution)/shard_map/ppermute | solution.py:36
  590.1 23.3 %collective-permute-start.55 = (bf16[224,384]{1,0:T(8,128)(2,1)}, bf16[224,384]{1,0:T(8,128)(2,1)S(1)}, u32[]{:S(2)}, u32[]{:S(2)}) collective-permute-start(bf16[224,384]{1,0:T(8,128)(2,1)} %dynamic-slice_convert_fusion.10), channel_id=1, source_target_pairs={{0,16},{1,17},{2,18},{3,19},{4,20},{5,21},{6,22},{7,23},{8,24},{9,... | collective-permute-start | bytes 516104 | tf_op jit(solution)/shard_map/ppermute | solution.py:36
  615.9 11.7 %collective-permute-start.59 = (bf16[416,384]{1,0:T(8,128)(2,1)S(1)}, bf16[416,384]{1,0:T(8,128)(2,1)S(1)}, u32[]{:S(2)}, u32[]{:S(2)}) collective-permute-start(bf16[416,384]{1,0:T(8,128)(2,1)S(1)} %dynamic-slice_convert_fusion.7), channel_id=1, source_target_pairs={{0,8},{1,9},{2,10},{3,11},{4,12},{5,13},{6,14},{7,15},{8,0},{9,1},... | collective-permute-start | bytes 958472 | tf_op jit(solution)/shard_map/ppermute | solution.py:36
  615.9 26.4 %collective-permute-start.61 = (bf16[1536,384]{1,0:T(8,128)(2,1)S(1)}, bf16[1536,384]{1,0:T(8,128)(2,1)S(1)}, u32[]{:S(2)}, u32[]{:S(2)}) collective-permute-start(bf16[1536,384]{1,0:T(8,128)(2,1)S(1)} %pad_maximum_fusion.4), channel_id=1, source_target_pairs={{0,4},{1,5},{2,6},{3,7},{4,0},{5,1},{6,2},{7,3},{8,12},{9,13},{10,... | collective-permute-start | bytes 3538952 | tf_op jit(solution)/shard_map/ppermute | solution.py:36
  617.3 8.1 %collective-permute-start.60 = (bf16[224,384]{1,0:T(8,128)(2,1)S(1)}, bf16[224,384]{1,0:T(8,128)(2,1)S(1)}, u32[]{:S(2)}, u32[]{:S(2)}) collective-permute-start(bf16[224,384]{1,0:T(8,128)(2,1)S(1)} %add_convert_fusion.2), channel_id=1, source_target_pairs={{0,16},{1,17},{2,18},{3,19},{4,20},{5,21},{6,22},{7,23},{8,24},{9,... | collective-permute-start | bytes 516104 | tf_op jit(solution)/shard_map/ppermute | solution.py:36
  642.4 9.0 %collective-permute-start.63 = (bf16[208,384]{1,0:T(8,128)(2,1)S(1)}, bf16[208,384]{1,0:T(8,128)(2,1)S(1)}, u32[]{:S(2)}, u32[]{:S(2)}) collective-permute-start(bf16[208,384]{1,0:T(8,128)(2,1)S(1)} %dynamic-slice_convert_fusion.11), channel_id=1, source_target_pairs={{0,16},{1,17},{2,18},{3,19},{4,20},{5,21},{6,22},{7,23},{8,24},{9,... | collective-permute-start | bytes 479240 | tf_op jit(solution)/shard_map/ppermute | solution.py:36
  644.7 9.6 %collective-permute-start.64 = (bf16[448,384]{1,0:T(8,128)(2,1)S(1)}, bf16[448,384]{1,0:T(8,128)(2,1)S(1)}, u32[]{:S(2)}, u32[]{:S(2)}) collective-permute-start(bf16[448,384]{1,0:T(8,128)(2,1)S(1)} %pad_maximum_fusion.9), channel_id=1, source_target_pairs={{0,8},{1,9},{2,10},{3,11},{4,12},{5,13},{6,14},{7,15},{8,0},{9,1},... | collective-permute-start | bytes 1032200 | tf_op jit(solution)/shard_map/ppermute | solution.py:36
  654.3 17.6 %collective-permute-start.66 = (bf16[208,384]{1,0:T(8,128)(2,1)S(1)}, bf16[208,384]{1,0:T(8,128)(2,1)S(1)}, u32[]{:S(2)}, u32[]{:S(2)}) collective-permute-start(bf16[208,384]{1,0:T(8,128)(2,1)S(1)} %add_convert_fusion.3), channel_id=1, source_target_pairs={{0,16},{1,17},{2,18},{3,19},{4,20},{5,21},{6,22},{7,23},{8,24},{9,... | collective-permute-start | bytes 479240 | tf_op jit(solution)/shard_map/ppermute | solution.py:36
  655.9 16.1 %collective-permute-start.67 = (bf16[896,384]{1,0:T(8,128)(2,1)S(1)}, bf16[896,384]{1,0:T(8,128)(2,1)S(1)}, u32[]{:S(2)}, u32[]{:S(2)}) collective-permute-start(bf16[896,384]{1,0:T(8,128)(2,1)S(1)} %pad_maximum_fusion.6), channel_id=1, source_target_pairs={{0,4},{1,5},{2,6},{3,7},{4,0},{5,1},{6,2},{7,3},{8,12},{9,13},{10,... | collective-permute-start | bytes 2064392 | tf_op jit(solution)/shard_map/ppermute | solution.py:36
  657.0 15.0 %collective-permute-start.65 = (f32[168,128]{1,0:T(8,128)S(1)}, f32[168,128]{1,0:T(8,128)S(1)}, u32[]{:S(2)}, u32[]{:S(2)}) collective-permute-start(f32[168,128]{1,0:T(8,128)S(1)} %add.792), channel_id=1, source_target_pairs={{0,4},{1,5},{2,6},{3,7},{4,0},{5,1},{6,2},{7,3},{8,12},{9,13},{10,... | collective-permute-start | bytes 258056 | tf_op jit(solution)/shard_map/ppermute | solution.py:36
  672.0 9.4 %collective-permute-start.69 = (bf16[416,384]{1,0:T(8,128)(2,1)S(1)}, bf16[416,384]{1,0:T(8,128)(2,1)S(1)}, u32[]{:S(2)}, u32[]{:S(2)}) collective-permute-start(bf16[416,384]{1,0:T(8,128)(2,1)S(1)} %pad_maximum_fusion.10), channel_id=1, source_target_pairs={{0,8},{1,9},{2,10},{3,11},{4,12},{5,13},{6,14},{7,15},{8,0},{9,1},... | collective-permute-start | bytes 958472 | tf_op jit(solution)/shard_map/ppermute | solution.py:36
  684.2 11.2 %collective-permute-start.71 = (bf16[832,384]{1,0:T(8,128)(2,1)S(1)}, bf16[832,384]{1,0:T(8,128)(2,1)S(1)}, u32[]{:S(2)}, u32[]{:S(2)}) collective-permute-start(bf16[832,384]{1,0:T(8,128)(2,1)S(1)} %pad_maximum_fusion.5), channel_id=1, source_target_pairs={{0,4},{1,5},{2,6},{3,7},{4,0},{5,1},{6,2},{7,3},{8,12},{9,13},{10,... | collective-permute-start | bytes 1916936 | tf_op jit(solution)/shard_map/ppermute | solution.py:36
  (120 other events, 1175.4 us)

commit v2 on v1

v2 whole, which is shorter than its diff:
```python
import functools

import jax
import jax.numpy as jnp
from jax import lax
from jax.experimental import pallas as pl
from jax.experimental.pallas import tpu as pltpu
from jax.sharding import PartitionSpec as P

HEADS = 48
HEADDIM = 64
STATE = 128
CONV = 4
INNER = 3072
CHANNELS = 3328
PROJ = 6448
PLANES = 2
CORES = 2

f32 = jnp.float32
bf16 = jnp.bfloat16
epsilon = 1e-05
no_cost = pl.CostEstimate(flops=0, bytes_accessed=0, transcendentals=0)


class Ring:
    def __init__(self, seq, fsdp):
        self.seq, self.fsdp = seq, fsdp
        self.clock = None
        self.line, self.row = seq // PLANES, fsdp // CORES

    def send(self, block, move):
        route = []
        for s in range(self.seq):
            for f in range(self.fsdp):
                there = move(s // PLANES, s % PLANES, f // CORES, f % CORES)
                if there is None:
                    continue
                z, x, y, c = there
                route.append((s * self.fsdp + f, (z * PLANES + x) * self.fsdp + y * CORES + c))
        arrived = lax.ppermute(block, ("seq", "fsdp"), route)
        self.clock.sent(arrived)
        return arrived

    def core(self, block):
        return self.send(block, lambda z, x, y, c: (z, x, y, 1 - c))

    def plane(self, block):
        return self.send(block, lambda z, x, y, c: (z, 1 - x, y, c))

    def from_row(self, block, distance):
        return self.send(block, lambda z, x, y, c: (z, x, (y - distance) % self.row, c))

    def far(self, block, distance):
        return self.send(block, lambda z, x, y, c: (z ^ distance, x, y, c))

    def relative(self, block, d, e):
        if not d and not e:
            return block
        return self.send(
            block, lambda z, x, y, c: (z, x, (y - d) % self.row, (c + e) % CORES)
        )

    def relative_back(self, block, d, e):
        return self.relative(block, d, e)

    def next_block(self, block, distance):
        def move(z, x, y, c):
            s = z * PLANES + x + distance
            return (s // PLANES, s % PLANES, y, c) if 0 <= s < self.seq else None

        return self.send(block, move)


def rows_of(block, index, count):
    return lax.dynamic_slice_in_dim(block, index * count, count, axis=0)


def swapped(ring, distance):
    seq_index = lax.axis_index("seq")
    if distance == 0:
        return seq_index % PLANES, ring.plane
    bit = (seq_index // PLANES // distance) % 2
    return bit, lambda block: ring.far(block, distance)


def cube(ring):
    distances, distance = [0], 1
    while distance < ring.line:
        distances.append(distance)
        distance *= 2
    return distances


def halve(ring, distance, block):
    bit, send = swapped(ring, distance)
    half = block.shape[0] // 2
    arrived = send(rows_of(block, 1 - bit, half).astype(bf16))
    return rows_of(block, bit, half) + arrived.astype(f32)


def double(ring, distance, block):
    bit, send = swapped(ring, distance)
    other = send(block)
    low = jnp.where(bit == 0, block, other)
    high = jnp.where(bit == 0, other, block)
    return jnp.concatenate([low, high], axis=0)


class Total:
    def __init__(self, ring, grad):
        self.ring, self.value = ring, grad
        self.steps = [(halve, d) for d in cube(ring)] + [(double, d) for d in reversed(cube(ring))]

    def step(self):
        if self.steps:
            kind, distance = self.steps.pop(0)
            if kind is double and self.value.dtype != bf16:
                self.value = self.value.astype(bf16)
            self.value = kind(self.ring, distance, self.ring.clock.now(self.value))

    def finish(self):
        while self.steps:
            self.step()
        return self.value.astype(f32)

    def halves(self):
        while len(self.steps) > 1:
            self.step()
        if self.steps:
            self.steps = []
            self.value = (self.value, self.ring.plane(self.ring.clock.now(self.value)))
        return self.value


class Clock:
    def __init__(self, value):
        self.token = value
        self.pending = []

    def sent(self, value):
        self.pending.append([1, value])

    def tick(self, *values):
        due = [value for ticks, value in self.pending if ticks == 1]
        out = lax.optimization_barrier((self.token,) + values + tuple(due))
        self.token = out[0]
        self.pending = [[ticks - 1, value] for ticks, value in self.pending if ticks > 1]
        return out[1 : 1 + len(values)]

    def defer(self, count=1, ticks=1):
        for entry in self.pending[len(self.pending) - count :]:
            entry[0] += ticks

    def now(self, value):
        return lax.optimization_barrier((value, self.token))[0]


class Spread:
    def __init__(self, ring, source, origin=0, whole_only=False):
        self.ring, self.source, self.origin, self.whole_only = ring, source, origin, whole_only
        block = self.block = source[origin:]
        self.quarter = -(-block.shape[0] // 64) * 16
        self.cut = -(-self.quarter // 32) * 16
        seq_index = lax.axis_index("seq")
        self.place = seq_index % 2 + 2 * ((seq_index // PLANES) % 2)
        self.arrived = []

    def start(self, index):
        return jnp.minimum((self.place ^ index) * self.quarter, self.block.shape[0] - self.quarter)

    def put(self, pieces):
        sides = (pieces,)
        if not self.whole_only:
            sides += ([self.ring.core(piece) for piece in pieces],)
        self.arrived.append(sides)

    def near(self):
        self.beside_it = self.ring.core(self.ring.clock.now(self.block))

    def first(self, at_once=False):
        ring = self.ring
        mine = lax.dynamic_slice_in_dim(self.source, self.origin + self.start(0), self.quarter, axis=0)
        mine = mine if at_once else ring.clock.now(mine)
        self.mine = [ring.from_row(mine, d) for d in range(1, ring.row)]

    def second(self):
        ring = self.ring
        mine = [ring.clock.now(part) for part in self.mine]
        self.beside = [ring.plane(part) for part in mine]
        self.behind = [ring.far(part, 1) for part in mine]
        self.put(mine)

    def third(self):
        ring, cut = self.ring, self.cut
        beside = [ring.clock.now(part) for part in self.beside]
        behind = [ring.clock.now(part) for part in self.behind]
        self.corner = (
            [ring.plane(part[:cut]) for part in behind],
            [ring.far(part[cut:], 1) for part in beside],
        )
        self.put(beside)
        self.put(behind)

    def fourth(self):
        now = self.ring.clock.now
        self.put([now(part) for part in self.corner[0]])
        self.put([now(part) for part in self.corner[1]])

    def whole(self):
        found = {(0, 0): self.block, (0, 1): self.beside_it}
        index = jnp.stack([self.place ^ k for k in range(4)]).astype(jnp.int32)
        for d in range(1, self.ring.row):
            sides = [[side[d - 1] for side in pieces] for pieces in zip(*self.arrived)]
            shards = laid(self.block, self.quarter, self.cut, index, sides)
            found[d, 0] = shards[0]
            found[d, 1] = self.ring.core(shards[0]) if self.whole_only else shards[1]
        return found


def sum_body(count, *refs):
    out_ref = refs[-1]
    total = None
    for left, right in zip(refs[:count], refs[count:-1]):
        term = lax.dot_general(
            left[...], right[...], (((0,), (0,)), ((), ())), preferred_element_type=f32
        )
        total = term if total is None else total + term
    out_ref[...] = total


def weight_grad(rows_all, columns_all, tile):
    keys = list(rows_all)
    tokens, rows = rows_all[keys[0]].shape
    width = columns_all[keys[0]].shape[1]
    return pl.pallas_call(
        functools.partial(sum_body, len(keys)),
        grid=(rows // tile,),
        in_specs=[pl.BlockSpec((tokens, tile), lambda i: (0, i))] * len(keys)
        + [pl.BlockSpec((tokens, width), lambda i: (0, 0))] * len(keys),
        out_specs=pl.BlockSpec((tile, width), lambda i: (i, 0)),
        out_shape=jax.ShapeDtypeStruct((rows, width), f32),
        name="weight_grad",
        cost_estimate=no_cost,
        compiler_params=pltpu.CompilerParams(vmem_limit_bytes=40 * 2**20),
    )(*[rows_all[key] for key in keys], *[columns_all[key] for key in keys])


def to_inner_body(tiles, place_ref, grad_ref, *refs):
    out_ref = refs[-1]
    shard = pl.program_id(0) // tiles
    for k, weight in enumerate(refs[:-1]):

        @pl.when(shard == k)
        def _(weight=weight):
            out_ref[...] = dot_last(grad_ref[...], weight[...])


def to_inner(grad, weights, places):
    tokens, width = grad.shape
    rows = weights[0].shape[0]
    tile = 384
    tiles = rows // tile
    return pl.pallas_call(
        functools.partial(to_inner_body, tiles),
        grid_spec=pltpu.PrefetchScalarGridSpec(
            num_scalar_prefetch=1,
            grid=(len(weights) * tiles,),
            in_specs=[pl.BlockSpec((tokens, width), lambda i, place: (0, 0))]
            + [
                pl.BlockSpec(
                    (tile, width), lambda i, place, k=k: (jnp.clip(i - k * tiles, 0, tiles - 1), 0)
                )
                for k in range(len(weights))
            ],
            out_specs=pl.BlockSpec(
                (tokens, tile), lambda i, place: (0, place[i // tiles] * tiles + i % tiles)
            ),
        ),
        out_shape=jax.ShapeDtypeStruct((tokens, rows * len(weights)), f32),
        name="to_inner",
        cost_estimate=no_cost,
        compiler_params=pltpu.CompilerParams(vmem_limit_bytes=40 * 2**20),
    )(places, grad, *weights)


def to_model_body(layout, gate_ref, tail_ref, *refs):
    out_ref = refs[-1]
    at = 0
    for k, (blocks, rows) in enumerate(layout):
        total = jnp.dot(tail_ref[...], refs[at][...], preferred_element_type=f32)
        at += 1
        for piece, block in enumerate(blocks):
            columns = gate_ref[:, piece * rows : (piece + 1) * rows]
            weight = refs[at][block * rows : (block + 1) * rows]
            at += 1
            total = total + jnp.dot(columns, weight, preferred_element_type=f32)
        out_ref[k] = total


def to_model(grad_gate, grad_tail, gate_weights, tail_weights):
    rows = grad_gate.shape[1] // len(gate_weights[0])
    flat, layout = [], []
    for pieces, tail in zip(gate_weights, tail_weights):
        if all(array is pieces[0][0] for array, _ in pieces):
            layout.append(([0], grad_gate.shape[1]))
            flat += [tail, pieces[0][0]]
        else:
            layout.append(([block for _, block in pieces], rows))
            flat += [tail] + [array for array, _ in pieces]
    inside = pl.BlockSpec(memory_space=pltpu.VMEM)
    return pl.pallas_call(
        functools.partial(to_model_body, layout),
        in_specs=[inside] * (2 + len(flat)),
        out_specs=inside,
        out_shape=jax.ShapeDtypeStruct(
            (len(layout), grad_gate.shape[0], tail_weights[0].shape[1]), f32
        ),
        name="to_model",
        cost_estimate=no_cost,
        compiler_params=pltpu.CompilerParams(vmem_limit_bytes=48 * 2**20),
    )(grad_gate, grad_tail, *flat)


def output_body(count, token_ref, *refs):
    out_ref = refs[-1]
    total = token_ref[...].astype(f32)
    for columns, weight in zip(refs[:count], refs[count:-1]):
        total = total + jnp.dot(columns[...], weight[...], preferred_element_type=f32)
    out_ref[...] = total.astype(bf16)


def output_rows(tokens, columns, weights):
    inside = pl.BlockSpec(memory_space=pltpu.VMEM)
    return pl.pallas_call(
        functools.partial(output_body, len(columns)),
        in_specs=[inside] * (1 + 2 * len(columns)),
        out_specs=inside,
        out_shape=jax.ShapeDtypeStruct(tokens.shape, bf16),
        name="output_rows",
        cost_estimate=no_cost,
        compiler_params=pltpu.CompilerParams(vmem_limit_bytes=48 * 2**20),
    )(tokens, *columns, *weights)


def laid_body(quarter, cut, index_ref, *refs):
    count = len(refs) // 6
    pieces, shards = refs[:-count], refs[-count:]
    for e, shard in enumerate(shards):
        own = pieces[e * 5 : e * 5 + 5]
        for piece, quarter_of, offset in zip(own, (0, 1, 2, 3, 3), (0, 0, 0, 0, cut)):
            start = jnp.minimum(index_ref[quarter_of] * quarter, shard.shape[0] - quarter)
            start = pl.multiple_of(start + offset, 16)
            shard[pl.ds(start, piece.shape[0]), :] = piece[...]


def laid(block, quarter, cut, index, sides):
    flat = [piece for side in sides for piece in side]
    inside = pl.BlockSpec(memory_space=pltpu.VMEM)
    return pl.pallas_call(
        functools.partial(laid_body, quarter, cut),
        grid_spec=pltpu.PrefetchScalarGridSpec(
            num_scalar_prefetch=1,
            grid=(),
            in_specs=[inside] * len(flat),
            out_specs=[inside] * len(sides),
        ),
        out_shape=[jax.ShapeDtypeStruct(block.shape, block.dtype)] * len(sides),
        name="laid",
        cost_estimate=no_cost,
        compiler_params=pltpu.CompilerParams(vmem_limit_bytes=40 * 2**20),
    )(index, *flat)


def project_body(count, *refs):
    out_ref = refs[-1]
    total = None
    for columns, weight in zip(refs[:count], refs[count:-1]):
        term = lax.dot_general(
            columns[...], weight[...], (((1,), (1,)), ((), ())), preferred_element_type=f32
        )
        total = term if total is None else total + term
    out_ref[...] = total.astype(out_ref.dtype)


def project(columns, weights, tile, width=None):
    count = len(columns)
    tokens, depth = columns[0].shape
    at = [0] * count
    if width is not None:
        at = [block for _, block in weights]
        weights = [array for array, _ in weights]
    else:
        width = weights[0].shape[0]
    return pl.pallas_call(
        functools.partial(project_body, count),
        grid=(pl.cdiv(width, tile),),
        in_specs=[pl.BlockSpec((tokens, depth), lambda i: (0, 0))] * count
        + [pl.BlockSpec((tile, depth), lambda i, k=k: (i + k, 0)) for k in at],
        out_specs=pl.BlockSpec((tokens, tile), lambda i: (0, i)),
        out_shape=jax.ShapeDtypeStruct((tokens, width), bf16),
        name="project",
        cost_estimate=no_cost,
        compiler_params=pltpu.CompilerParams(vmem_limit_bytes=40 * 2**20),
    )(*columns, *weights)


class Pieces:
    def __init__(self, ring, block, count=1):
        self.ring, self.block = ring, block
        self.rows = block.shape[0] // count
        self.parts = []

    def near(self):
        self.beside = self.ring.core(self.ring.clock.now(self.block))

    def send(self, later=0):
        clock = self.ring.clock
        at = len(self.parts) * self.rows
        piece = clock.now(self.block[at : at + self.rows])
        self.parts.append([self.ring.from_row(piece, d) for d in range(1, self.ring.row)])
        clock.defer(self.ring.row - 1, later)

    def pass_on(self, at):
        far = [self.ring.clock.now(piece) for piece in self.parts[at]]
        self.parts[at] = [(piece, self.ring.core(piece)) for piece in far]

    def pieces(self):
        count = len(self.parts)
        found = {
            (0, 0): [(self.block, at) for at in range(count)],
            (0, 1): [(self.beside, at) for at in range(count)],
        }
        for d in range(1, self.ring.row):
            for e in range(CORES):
                found[d, e] = [(part[d - 1][e], 0) for part in self.parts]
        return found

    def whole(self):
        found = {(0, 0): self.block, (0, 1): self.beside}
        for d in range(1, self.ring.row):
            found[d, 0] = self.ring.clock.now(self.parts[0][d - 1])
            found[d, 1] = self.ring.core(found[d, 0])
        return found


def gather_rows(ring, block):
    found = {}
    for d in range(ring.row):
        found[d, 0] = block if d == 0 else ring.from_row(block, d)
        found[d, 1] = ring.core(found[d, 0])
    return found


def places(ring):
    index = lax.axis_index("fsdp")
    y, c = index // CORES, index % CORES
    return {
        (d, e): ((y + d) % ring.row) * CORES + (c + e) % CORES
        for d in range(ring.row)
        for e in range(CORES)
    }


def columns_for(ring, block):
    index = lax.axis_index("fsdp")
    y, c = index // CORES, index % CORES
    width = block.shape[1] // ring.fsdp
    return {
        (d, e): lax.dynamic_slice_in_dim(
            block, (((y - d) % ring.row) * CORES + (c + e) % CORES) * width, width, axis=1
        )
        for d in range(ring.row)
        for e in range(CORES)
    }


def trade_columns(ring, pieces):
    return {key: ring.relative_back(piece, *key) for key, piece in pieces.items()}


class SmallSum:
    def __init__(self, ring, vector):
        self.ring, self.value = ring, vector
        self.steps = ["core", "row"] + cube(ring)

    def step(self):
        if not self.steps:
            return
        kind = self.steps.pop(0)
        vector = self.ring.clock.now(self.value)
        if kind == "core":
            self.value = vector + self.ring.core(vector)
        elif kind == "row":
            self.value = sum([self.ring.from_row(vector, d) for d in range(1, self.ring.row)], vector)
        else:
            self.value = vector + swapped(self.ring, kind)[1](vector)

    def finish(self):
        while self.steps:
            self.step()
        return self.value


def head_rows(ring):
    part = INNER // ring.seq
    run = HEADDIM
    while part % run:
        run //= 2
    return part, run


def spread_factors(ring, through):
    part, run = head_rows(ring)
    factor = jnp.repeat(through, HEADDIM // run).reshape(ring.seq, part // run)
    factor = jnp.pad(factor, ((0, 0), (0, 8 - part // run)))
    return jnp.broadcast_to(factor[:, :, None], (ring.seq, 8, STATE))


def carried_body(reverse, run, blocks_ref, factor_ref, out_ref):
    count, part = out_ref.shape[0], out_ref.shape[1]
    state = jnp.zeros((part, STATE), f32)
    for k in reversed(range(count)) if reverse else range(count):
        out_ref[k] = state.astype(bf16)
        factor = factor_ref[k]
        spread = [jnp.broadcast_to(factor[j : j + 1], (run, STATE)) for j in range(part // run)]
        state = jnp.concatenate(spread, axis=0) * state + blocks_ref[k, :part]


def carried(ring, blocks, factor, reverse):
    part, run = head_rows(ring)
    return pl.pallas_call(
        functools.partial(carried_body, reverse, run),
        out_shape=jax.ShapeDtypeStruct((ring.seq, part, STATE), bf16),
        name="carried",
        cost_estimate=no_cost,
    )(blocks, factor)


def returned(ring, states):
    states = lax.all_to_all(states, "seq", 0, 0, tiled=True)
    return states.reshape(HEADS, HEADDIM, STATE)


def place_rows(whole, sides, start, rows):
    mine, other = sides
    first = (lax.axis_index("seq") % PLANES) == 0
    half = mine.shape[0]
    low = jnp.where(first, mine, other).astype(f32)
    high = jnp.where(first, other, mine)[: rows - half].astype(f32)
    whole = lax.dynamic_update_slice_in_dim(whole, low, start, axis=0)
    return lax.dynamic_update_slice_in_dim(whole, high, start + half, axis=0)


def steps_body(dt_ref, bias_ref, rate_ref, cum_ref, weigh_ref, decay_ref, cum_rows, step_rows, through_ref):
    raw = dt_ref[...].astype(f32) + bias_ref[...]
    step = jnp.maximum(raw, 0.0) + jnp.log1p(jnp.exp(-jnp.abs(raw)))
    tokens = step.shape[0]
    row = lax.broadcasted_iota(jnp.int32, step.shape, 0)
    cum = step * -jnp.exp(rate_ref[...])
    distance = 1
    while distance < tokens:
        cum = cum + jnp.where(row >= distance, pltpu.roll(cum, distance, 0), 0.0)
        distance *= 2
    end = cum[tokens - 1 :]
    cum_ref[...] = cum
    weigh_ref[...] = jnp.exp(end - cum) * step
    decay_ref[...] = jnp.exp(cum)
    cum_rows[...] = cum.T[:HEADS]
    step_rows[...] = step.T[:HEADS]
    through_ref[...] = jnp.exp(end)


def steps(projected, bias, rate):
    tokens = projected.shape[0]
    row = pl.BlockSpec((1, STATE), lambda i: (0, 0))
    by_token = pl.BlockSpec((tokens, STATE), lambda i: (0, 0))
    by_head = pl.BlockSpec((HEADS, tokens), lambda i: (0, 0))
    pad = lambda v: jnp.pad(v, (0, STATE - HEADS))[None]
    return pl.pallas_call(
        steps_body,
        grid=(1,),
        in_specs=[pl.BlockSpec((tokens, STATE), lambda i: (0, CHANNELS // STATE)), row, row],
        out_specs=[by_token] * 3 + [by_head] * 2 + [row],
        out_shape=[jax.ShapeDtypeStruct((tokens, STATE), f32)] * 3
        + [jax.ShapeDtypeStruct((HEADS, tokens), f32)] * 2
        + [jax.ShapeDtypeStruct((1, STATE), f32)],
        name="steps",
        cost_estimate=no_cost,
    )(projected, pad(bias), pad(rate))


def steps_back_body(
    dt_ref, bias_ref, rate_ref, step_ref, cum_ref, grad_step_ref, grad_cum_ref, factor_ref, crossed_ref,
    grad_ref, bias_grad_ref, rate_grad_ref,
):
    step, cum, factor = step_ref[...], cum_ref[...], factor_ref[...]
    tokens = step.shape[1]
    lane = lax.broadcasted_iota(jnp.int32, step.shape, 1)
    end = cum[:, tokens - 1 :]
    to_end = jnp.exp(end - cum)
    tail = factor * step * to_end
    grad_end = jnp.sum(tail, axis=1, keepdims=True) + jnp.exp(end) * jnp.sum(
        crossed_ref[...], axis=1, keepdims=True
    )
    total = grad_cum_ref[...] - tail + jnp.where(lane == tokens - 1, grad_end, 0.0)
    distance = 1
    while distance < tokens:
        moved = pltpu.roll(total, tokens - distance, 1)
        total = total + jnp.where(lane < tokens - distance, moved, 0.0)
        distance *= 2
    rate = -jnp.exp(rate_ref[...])
    rate_grad_ref[...] = rate * jnp.sum(total * step, axis=1, keepdims=True)
    raw = dt_ref[...].astype(f32).T[:HEADS] + bias_ref[...]
    grad = (grad_step_ref[...] + factor * to_end + total * rate) * jax.nn.sigmoid(raw)
    bias_grad_ref[...] = jnp.sum(grad, axis=1, keepdims=True)
    none = jnp.zeros((STATE - HEADS, tokens), f32)
    grad_ref[...] = jnp.concatenate([grad, none], axis=0).T.astype(bf16)


def steps_back(projected, bias, rate, step_rows, cum_rows, grad_step, grad_cum, factor, crossed):
    tokens = projected.shape[0]
    column = pl.BlockSpec((HEADS, 1), lambda i: (0, 0))
    by_head = pl.BlockSpec((HEADS, tokens), lambda i: (0, 0))
    return pl.pallas_call(
        steps_back_body,
        grid=(1,),
        in_specs=[pl.BlockSpec((tokens, STATE), lambda i: (0, CHANNELS // STATE)), column, column]
        + [by_head] * 5
        + [pl.BlockSpec((HEADS, STATE), lambda i: (0, 0))],
        out_specs=[pl.BlockSpec((tokens, STATE), lambda i: (0, 0)), column, column],
        out_shape=[
            jax.ShapeDtypeStruct((tokens, STATE), bf16),
            jax.ShapeDtypeStruct((HEADS, 1), f32),
            jax.ShapeDtypeStruct((HEADS, 1), f32),
        ],
        name="steps_back",
        cost_estimate=no_cost,
    )(
        projected, bias[:, None], rate[:, None], step_rows, cum_rows, grad_step, grad_cum, factor,
        crossed,
    )


def group_columns(wide_ref, group, heads):
    shift = lax.rem(STATE - heads * group, STATE)
    return pltpu.roll(wide_ref[...], shift, 1)[:, :heads]


def keep_columns(wide_ref, at, columns):
    wide = wide_ref[...]
    lane = lax.broadcasted_iota(jnp.int32, wide.shape, 1)
    for k, column in enumerate(columns):
        wide = jnp.where(lane == at + k, column, wide)
    wide_ref[...] = wide


def along(column_pair):
    lane = lax.broadcasted_iota(jnp.int32, (column_pair.shape[0], 2 * HEADDIM), 1)
    return jnp.where(lane < HEADDIM, column_pair[:, :1], column_pair[:, 1:2])


def conv_sum(edge, rows, taps, shift):
    window = jnp.concatenate([edge, rows], axis=0)
    total = shift
    for k in range(CONV):
        moved = window if k == CONV - 1 else pltpu.roll(window, CONV - 1 - k, 0)
        total = total + taps[k : k + 1] * moved[8:]
    return total


def enter_body(part, proj_ref, edge_ref, taps_ref, shift_ref, weigh_ref, factor_ref, low_ref, fresh_ref):
    def conv(at, width):
        columns = slice(at, at + width)
        total = conv_sum(
            edge_ref[:, columns].astype(f32),
            proj_ref[:, columns].astype(f32),
            taps_ref[:, columns],
            shift_ref[:, columns],
        )
        low = (total * jax.nn.sigmoid(total)).astype(bf16)
        low_ref[:, columns] = low
        return low

    proj_b = conv(INNER, 2 * STATE)[:, :STATE]
    fresh_ref[:, part:] = factor_ref[...]
    for at in range(0, INNER, 2 * HEADDIM):
        low = conv(at, 2 * HEADDIM)
        head = at // HEADDIM
        weighted = (low.astype(f32) * along(weigh_ref[:, head : head + 2])).astype(bf16)
        fresh = lax.dot_general(
            weighted, proj_b, (((0,), (0,)), ((), ())), preferred_element_type=f32
        )
        row = at
        while row < at + 2 * HEADDIM:
            device, offset = row // part, row % part
            count = min(part - offset, at + 2 * HEADDIM - row)
            fresh_ref[device, offset : offset + count] = fresh[row - at : row - at + count]
            row += count


def enter(ring, projected, edge, taps, shift, weigh, factor):
    part, _ = head_rows(ring)
    return pl.pallas_call(
        functools.partial(enter_body, part),
        out_shape=[
            jax.ShapeDtypeStruct((projected.shape[0], CHANNELS), bf16),
            jax.ShapeDtypeStruct((ring.seq, part + 8, STATE), f32),
        ],
        name="enter",
        cost_estimate=no_cost,
        compiler_params=pltpu.CompilerParams(vmem_limit_bytes=40 * 2**20),
    )(projected, edge, taps, shift[None], weigh, factor)


def pairs_along(columns):
    return jnp.concatenate(
        [along(columns[:, i : i + 2]) for i in range(0, columns.shape[1], 2)], axis=1
    )


def turn_body(
    base_ref, incoming_ref, c_ref, decay_ref, grad_ref, gain_ref, *refs,
):
    count = len(refs) - 10
    gate_refs = refs[:count]
    (
    mixed_ref, grad_y_ref, grad_gate_ref, grad_reach_ref, direct_ref, gain_grad_ref,
    mixer, grads, squares, products,
    ) = refs[count:]
    later, j = pl.program_id(0), pl.program_id(1)
    gate = gate_refs[0][...]
    for k in range(1, count):
        gate = jnp.where(j * count >= k * pl.num_programs(1), gate_refs[k][...], gate)
    gate = gate.astype(f32)
    sig = jax.nn.sigmoid(gate)
    silu = gate * sig
    gain = gain_ref[...]

    @pl.when((later == 0) & (j == 0))
    def _():
        squares[...] = jnp.zeros_like(squares)
        products[...] = jnp.zeros_like(products)

    @pl.when(later == 0)
    def _():
        reached = lax.dot_general(
            c_ref[...], incoming_ref[...], (((1,), (1,)), ((), ())), preferred_element_type=f32
        )
        ssd = base_ref[...] + pairs_along(group_columns(decay_ref, j, gain.shape[1] // HEADDIM)) * reached
        gated = ssd * silu
        mixer[j] = ssd
        grads[j] = grad_ref[...]
        squares[...] += jnp.sum(gated * gated, axis=1, keepdims=True)
        products[...] += jnp.sum(gated * grad_ref[...] * gain, axis=1, keepdims=True)

    @pl.when(later == 1)
    def _():
        scale = lax.rsqrt(squares[...] / INNER + epsilon)
        ssd = mixer[j]
        grad = grads[j]
        normal = ssd * silu * scale
        mixed_ref[...] = (normal * gain).astype(bf16)
        gain_grad_ref[...] = jnp.sum(grad * normal, axis=0, keepdims=True)
        grad_gated = scale * (grad * gain - normal * (scale * products[...] / INNER))
        grad_y = (grad_gated * silu).astype(bf16)
        grad_y_ref[...] = grad_y
        grad_gate_ref[...] = (grad_gated * ssd * (sig + silu * (1.0 - sig))).astype(bf16)
        grad_reach = (grad_y.astype(f32) * pairs_along(group_columns(decay_ref, j, gain.shape[1] // HEADDIM))).astype(bf16)
        grad_reach_ref[...] = grad_reach
        direct_ref[...] = lax.dot_general(
            grad_reach, c_ref[...], (((0,), (0,)), ((), ())), preferred_element_type=f32
        )


def later_or_same(tokens):
    t = lax.broadcasted_iota(jnp.int32, (tokens, tokens), 0)
    return t >= lax.broadcasted_iota(jnp.int32, (tokens, tokens), 1)


def dot_last(a, b):
    return lax.dot_general(a, b, (((1,), (1,)), ((), ())), preferred_element_type=f32)


def dot_first(a, b):
    return lax.dot_general(a, b, (((0,), (0,)), ((), ())), preferred_element_type=f32)


def inside_body(x_ref, b_ref, c_ref, cum_ref, cum_rows_ref, step_rows_ref, skip_ref, out_ref, scores):
    tokens = x_ref.shape[0]

    @pl.when(pl.program_id(0) == 0)
    def _():
        table = dot_last(c_ref[...], b_ref[...])
        scores[...] = jnp.where(later_or_same(tokens), table, 0.0)

    x = x_ref[...]
    j = pl.program_id(0)
    same = later_or_same(tokens)
    cum = group_columns(cum_ref, j, 2)
    parts = []
    for head in range(2):
        row = pl.ds(2 * j + head, 1)
        exponent = cum[:, head : head + 1] - cum_rows_ref[row, :]
        decay = jnp.exp(jnp.where(same, exponent, 0.0))
        mixing = (scores[...] * decay * step_rows_ref[row, :]).astype(bf16)
        parts.append(jnp.dot(mixing, x, preferred_element_type=f32))
    first = lax.broadcasted_iota(jnp.int32, x.shape, 1) < HEADDIM
    out_ref[...] = jnp.where(first, parts[0], parts[1]) + skip_ref[...] * x.astype(f32)


def pair_specs(tokens):
    columns = pl.BlockSpec((tokens, 2 * HEADDIM), lambda j: (0, j))
    by_token = pl.BlockSpec((tokens, STATE), lambda j: (0, 0))
    by_head = pl.BlockSpec((HEADS, tokens), lambda j: (0, 0))
    row = pl.BlockSpec((1, 2 * HEADDIM), lambda j: (0, j))
    proj_b = pl.BlockSpec((tokens, STATE), lambda j: (0, INNER // STATE))
    proj_c = pl.BlockSpec((tokens, STATE), lambda j: (0, INNER // STATE + 1))
    return columns, by_token, by_head, row, proj_b, proj_c


def inside(conv_low, cum_pairs, cum_rows, step_rows, skip_row):
    tokens = conv_low.shape[0]
    columns, by_token, by_head, row, proj_b, proj_c = pair_specs(tokens)
    return pl.pallas_call(
        inside_body,
        grid=(HEADS // 2,),
        in_specs=[columns, proj_b, proj_c, by_token, by_head, by_head, row],
        out_specs=columns,
        out_shape=jax.ShapeDtypeStruct((tokens, INNER), f32),
        scratch_shapes=[pltpu.VMEM((tokens, tokens), f32)],
        name="inside",
        cost_estimate=no_cost,
        compiler_params=pltpu.CompilerParams(vmem_limit_bytes=40 * 2**20),
    )(conv_low, conv_low, conv_low, cum_pairs, cum_rows, step_rows, skip_row)


def inside_back_body(
    y_ref, reach_ref, x_ref, b_ref, c_ref, incoming_ref, cum_ref, cum_rows_ref, step_rows_ref, skip_ref,
    x_out, b_out, c_out, step_out, cum_out, skip_out,
    scores, grad_scores, wide_sums,
):
    tokens = x_ref.shape[0]
    j = pl.program_id(0)

    @pl.when(j == 0)
    def _():
        table = dot_last(c_ref[...], b_ref[...])
        scores[...] = jnp.where(later_or_same(tokens), table, 0.0)
        grad_scores[...] = jnp.zeros_like(grad_scores)
        c_out[...] = jnp.zeros_like(c_out)

    x, y = x_ref[...], y_ref[...]
    wide = y.astype(f32)
    incoming = incoming_ref[...]
    reached = wide * dot_last(c_ref[...], incoming)
    c_out[...] += jnp.dot(reach_ref[...], incoming, preferred_element_type=f32)
    skip_out[...] = jnp.sum(wide * x.astype(f32), axis=0, keepdims=True)
    same = later_or_same(tokens)
    first = lax.broadcasted_iota(jnp.int32, x.shape, 1) < HEADDIM
    parts, total, sums = [], 0.0, []
    wide_cum = group_columns(cum_ref, j, 2)
    for head in range(2):
        cum = wide_cum[:, head : head + 1]
        row = pl.ds(2 * j + head, 1)
        step = step_rows_ref[row, :]
        decay = jnp.exp(jnp.where(same, cum - cum_rows_ref[row, :], 0.0))
        both = scores[...] * decay
        own = jnp.where(first == (head == 0), y, jnp.zeros_like(y))
        grad_mix = dot_last(own, x)
        total = total + grad_mix * decay * step
        by_source = grad_mix * both
        step_out[row, :] = jnp.sum(by_source, axis=0, keepdims=True)
        mine = reached[:, head * HEADDIM : (head + 1) * HEADDIM]
        sums.append(
            jnp.sum(by_source * step, axis=1, keepdims=True)
            + jnp.exp(cum) * jnp.sum(mine, axis=1, keepdims=True)
        )
        parts.append(dot_first((both * step).astype(bf16), y))
    keep_columns(wide_sums, 2 * j, sums)
    grad_scores[...] += total
    x_out[...] = jnp.where(first, parts[0], parts[1]) + skip_ref[...] * wide

    @pl.when(j == pl.num_programs(0) - 1)
    def _():
        grad = jnp.where(same, grad_scores[...], 0.0).astype(bf16)
        c_out[...] += jnp.dot(grad, b_ref[...], preferred_element_type=f32)
        b_out[...] = dot_first(grad, c_ref[...])
        cum_out[...] = wide_sums[...].T[:HEADS] - step_out[...] * step_rows_ref[...]


def inside_back(grad_y, grad_reach, conv_low, incoming, cum_pairs, cum_rows, step_rows, skip_row):
    tokens = conv_low.shape[0]
    columns, by_token, by_head, row, proj_b, proj_c = pair_specs(tokens)
    whole = pl.BlockSpec((tokens, STATE), lambda j: (0, 0))
    pairs = HEADS // 2
    return pl.pallas_call(
        inside_back_body,
        grid=(pairs,),
        in_specs=[columns, columns, columns, proj_b, proj_c]
        + [pl.BlockSpec((2 * HEADDIM, STATE), lambda j: (j, 0)), by_token, by_head, by_head, row],
        out_specs=[columns, whole, whole, by_head, by_head, row],
        out_shape=[
            jax.ShapeDtypeStruct((tokens, INNER), f32),
            jax.ShapeDtypeStruct((tokens, STATE), f32),
            jax.ShapeDtypeStruct((tokens, STATE), f32),
            jax.ShapeDtypeStruct((HEADS, tokens), f32),
            jax.ShapeDtypeStruct((HEADS, tokens), f32),
            jax.ShapeDtypeStruct((1, INNER), f32),
        ],
        scratch_shapes=[
            pltpu.VMEM((tokens, tokens), f32),
            pltpu.VMEM((tokens, tokens), f32),
            pltpu.VMEM((tokens, STATE), f32),
        ],
        name="inside_back",
        cost_estimate=no_cost,
        compiler_params=pltpu.CompilerParams(vmem_limit_bytes=40 * 2**20),
    )(
        grad_y, grad_reach, conv_low, conv_low, conv_low, incoming, cum_pairs, cum_rows, step_rows,
        skip_row,
    )


def turn(base, incoming, proj_c, decay, gate_parts, grad_mixed, gain):
    tokens, heads = base.shape[0], 8
    width = heads * HEADDIM
    groups = INNER // width
    share = groups // len(gate_parts)
    once = lambda p, j: (0, jnp.where(p == 0, j, groups - 1))
    last = lambda p, j: (0, jnp.where(p == 0, 0, j))
    wide = jax.ShapeDtypeStruct((tokens, INNER), bf16)
    return pl.pallas_call(
        turn_body,
        grid=(2, groups),
        in_specs=[
            pl.BlockSpec((tokens, width), once),
            pl.BlockSpec((width, STATE), lambda p, j: (jnp.where(p == 0, j, groups - 1), 0)),
            pl.BlockSpec((tokens, STATE), lambda p, j: (0, 0)),
            pl.BlockSpec((tokens, STATE), lambda p, j: (0, 0)),
            pl.BlockSpec((tokens, width), once),
            pl.BlockSpec((1, width), lambda p, j: (0, j)),
        ]
        + [
            pl.BlockSpec(
                (tokens, width), lambda p, j, k=k: (0, jnp.clip(j - k * share, 0, share - 1))
            )
            for k in range(len(gate_parts))
        ],
        out_specs=[pl.BlockSpec((tokens, width), last)] * 4
        + [
            pl.BlockSpec((width, STATE), lambda p, j: (jnp.where(p == 0, 0, j), 0)),
            pl.BlockSpec((1, width), last),
        ],
        out_shape=[wide] * 4
        + [jax.ShapeDtypeStruct((INNER, STATE), f32), jax.ShapeDtypeStruct((1, INNER), f32)],
        scratch_shapes=[
            pltpu.VMEM((groups, tokens, width), f32),
            pltpu.VMEM((groups, tokens, width), f32),
            pltpu.VMEM((tokens, 1), f32),
            pltpu.VMEM((tokens, 1), f32),
        ],
        name="turn",
        cost_estimate=no_cost,
        compiler_params=pltpu.CompilerParams(vmem_limit_bytes=40 * 2**20),
    )(base, incoming, proj_c, decay, grad_mixed, gain[None], *gate_parts)


def ahead(rows, count, distance):
    return (pltpu.roll(rows, rows.shape[0] - distance, 0) if distance else rows)[:count]


def leave_body(
    steps, proj_ref, edge_ref, taps_ref, shift_ref, low_ref, part_ref, fresh_ref, incoming_ref, b_ref,
    weigh_ref, b_part_ref, c_part_ref,
    grad_ref, first_ref, last_ref, taps_grad_ref, shift_grad_ref, factor_ref, crossed_ref,
    b_total, wide_factor,
):
    j = pl.program_id(0)

    def conv_back(grad_out):
        rows = proj_ref[...].astype(f32)
        window = jnp.concatenate([edge_ref[...].astype(f32), rows], axis=0)
        taps = taps_ref[...]
        moved = [
            (pltpu.roll(window, CONV - 1 - k, 0) if k < CONV - 1 else window)[8:]
            for k in range(CONV)
        ]
        total = shift_ref[...]
        for k in range(CONV):
            total = total + taps[k : k + 1] * moved[k]
        sig = jax.nn.sigmoid(total)
        grad = grad_out * (sig * (1.0 + total * (1.0 - sig)))
        shift_grad_ref[...] = jnp.sum(grad, axis=0, keepdims=True)
        taps_grad_ref[...] = jnp.concatenate(
            [jnp.sum(grad * part, axis=0, keepdims=True) for part in moved], axis=0
        )
        none = jnp.zeros((8, grad.shape[1]), f32)
        after_it = jnp.concatenate([grad, none], axis=0)
        before_it = jnp.concatenate([none, grad[:8]], axis=0)
        inner, outer = 0.0, 0.0
        for k in range(CONV):
            tap = taps[k : k + 1]
            inner = inner + tap * ahead(after_it, grad.shape[0], CONV - 1 - k)
            outer = outer + tap * ahead(before_it, 8, CONV - 1 - k)
        grad_ref[...] = inner.astype(bf16)
        last_ref[...] = inner[grad.shape[0] - 8 :]
        first_ref[...] = outer

    @pl.when(j == 0)
    def _():
        b_total[...] = b_part_ref[...]

    @pl.when(j < steps)
    def _():
        fresh = fresh_ref[...]
        x = low_ref[...].astype(f32)
        heads = x.shape[1] // HEADDIM
        weigh = pairs_along(group_columns(weigh_ref, j, heads))
        grad_weighted = lax.dot_general(
            b_ref[...], fresh, (((1,), (1,)), ((), ())), preferred_element_type=f32
        )
        weighted = (x * weigh).astype(bf16)
        b_total[...] += jnp.dot(weighted, fresh, preferred_element_type=f32)
        product = grad_weighted * x
        keep_columns(
            wide_factor,
            heads * j,
            [
                jnp.sum(product[:, i * HEADDIM : (i + 1) * HEADDIM], axis=1, keepdims=True)
                for i in range(heads)
            ],
        )
        both = fresh.astype(f32) * incoming_ref[...].astype(f32)
        for i in range(heads):
            row = pl.ds(heads * j + i, 1)
            crossed_ref[row, :] = jnp.sum(
                both[i * HEADDIM : (i + 1) * HEADDIM], axis=0, keepdims=True
            )
        conv_back(part_ref[...] + grad_weighted * weigh)

    @pl.when(j == steps)
    def _():
        factor_ref[...] = wide_factor[...].T[:HEADS]
        conv_back(jnp.concatenate([b_total[...], c_part_ref[...]], axis=1))


def leave(projected, edge, taps, shift, conv_low, part, grad_fresh, incoming, weigh, b_part, c_part):
    tokens, heads = part.shape[0], 4
    width = heads * HEADDIM
    steps = INNER // width
    inside = lambda j: jnp.minimum(j, steps - 1)
    block = lambda rows: pl.BlockSpec((rows, width), lambda j: (0, j))
    whole = lambda rows: pl.BlockSpec((rows, STATE), lambda j: (0, 0))
    state = pl.BlockSpec((width, STATE), lambda j: (inside(j), 0))
    return pl.pallas_call(
        functools.partial(leave_body, steps),
        grid=(steps + 1,),
        in_specs=[
            block(tokens),
            block(8),
            block(CONV),
            block(1),
            block(tokens),
            pl.BlockSpec((tokens, width), lambda j: (0, inside(j))),
            state,
            state,
            pl.BlockSpec((tokens, STATE), lambda j: (0, INNER // STATE)),
            whole(tokens),
            whole(tokens),
            whole(tokens),
        ],
        out_specs=[
            block(tokens),
            block(8),
            block(8),
            block(CONV),
            block(1),
            pl.BlockSpec((HEADS, tokens), lambda j: (0, 0)),
            whole(HEADS),
        ],
        out_shape=[
            jax.ShapeDtypeStruct((tokens, CHANNELS), bf16),
            jax.ShapeDtypeStruct((8, CHANNELS), f32),
            jax.ShapeDtypeStruct((8, CHANNELS), f32),
            jax.ShapeDtypeStruct((CONV, CHANNELS), f32),
            jax.ShapeDtypeStruct((1, CHANNELS), f32),
            jax.ShapeDtypeStruct((HEADS, tokens), f32),
            jax.ShapeDtypeStruct((HEADS, STATE), f32),
        ],
        scratch_shapes=[pltpu.VMEM((tokens, STATE), f32), pltpu.VMEM((tokens, STATE), f32)],
        name="leave",
        cost_estimate=no_cost,
        compiler_params=pltpu.CompilerParams(vmem_limit_bytes=40 * 2**20),
    )(
        projected, edge, taps, shift[None], conv_low, part, grad_fresh, incoming, conv_low,
        weigh, b_part, c_part,
    )


def rms_scale(values, gain):
    return values * lax.rsqrt(jnp.mean(values * values, axis=-1, keepdims=True) + epsilon) * gain


def pack(arrays):
    flat = jnp.concatenate([a.reshape(-1) for a in arrays])
    pad = -flat.shape[0] % 1024
    return jnp.pad(flat, (0, pad)).reshape(-1, 128)


def local(
    hidden,
    lengths,
    norm_gain,
    in_weight,
    conv_weight,
    conv_bias,
    dt_bias,
    a_log,
    skip_d,
    gate_gain,
    out_weight,
    out_grad,
):
    ring = Ring(lax.axis_size("seq"), lax.axis_size("fsdp"))
    ring.clock = clock = Clock(hidden[0, :8, :128])
    _, row_count, model_width = hidden.shape
    fsdp_index = lax.axis_index("fsdp")
    where = places(ring)
    tokens = hidden[0].astype(f32)

    small = [norm_gain, conv_weight, conv_bias, dt_bias, a_log, skip_d, gate_gain]
    in_rows = in_weight.T
    shared = Spread(ring, in_rows, INNER)
    shared.first(at_once=True)
    shared.near()
    packed = pack(small)
    spread = jnp.zeros((ring.fsdp,) + packed.shape, bf16)
    for (d, e), place in where.items():
        block = ring.relative(packed, d, e)
        spread = lax.dynamic_update_slice_in_dim(spread, block[None], place, axis=0)
    spread = spread.reshape(ring.fsdp, -1)
    whole_small, at = [], 0
    for part in small:
        piece = spread[:, at : at + part.size]
        at += part.size
        if part.ndim == 2:
            piece = piece.reshape((ring.fsdp,) + part.shape).transpose(1, 0, 2)
            whole_small.append(piece.reshape(part.shape[0], -1).astype(f32))
        else:
            whole_small.append(piece.reshape(-1).astype(f32))
    gain_norm, conv_taps, conv_shift, step_bias, rate_log, skip_gain, gain_gate = whole_small

    gate_pieces = Pieces(ring, in_rows[:INNER], 3)
    out_spread = Spread(ring, out_weight, 0, whole_only=True)
    (spread,) = clock.tick(spread)
    shared.second()
    out_spread.first()
    clock.tick()
    shared.third()
    gate_pieces.send(later=1)
    clock.tick()
    shared.fourth()
    gate_pieces.send(later=1)
    out_spread.second()
    clock.tick()
    weight_conv = shared.whole()

    position = lax.axis_index("seq") * row_count + lax.broadcasted_iota(
        jnp.int32, (row_count, 1), 0
    )
    grad_out = jnp.where(position < lengths[0], out_grad[0], jnp.zeros_like(out_grad[0]))

    normed, pull_norm = jax.vjp(rms_scale, tokens, gain_norm)
    normed = normed.astype(bf16)
    depth = in_weight.shape[0]

    normed_columns = [
        lax.dynamic_slice_in_dim(normed, place * depth, depth, axis=1) for place in where.values()
    ]
    normed_for = columns_for(ring, normed)
    projected = project(normed_columns, list(weight_conv.values()), 896)
    (projected,) = clock.tick(projected)
    gate_pieces.send(later=1)
    out_spread.third()
    edge_rows = ring.next_block(projected[row_count - 8 :, :CHANNELS], 1)
    cum, weigh, decay, cum_rows, step_rows, through = steps(projected, step_bias, rate_log)
    conv_low, fresh_state = enter(
        ring,
        projected,
        edge_rows,
        conv_taps,
        conv_shift,
        weigh,
        spread_factors(ring, through[0, :HEADS]),
    )
    proj_b = conv_low[:, INNER : INNER + STATE]
    proj_c = conv_low[:, INNER + STATE :]
    (fresh_state,) = clock.tick(fresh_state)
    blocks = lax.all_to_all(fresh_state, "seq", 0, 0, tiled=True)
    gate_pieces.pass_on(0)
    gate_pieces.pass_on(1)
    out_spread.fourth()
    gate_pieces.near()
    out_spread.near()
    skip_row = jnp.repeat(skip_gain, HEADDIM)[None]
    base = inside(conv_low, cum, cum_rows, step_rows, skip_row)
    blocks, base = clock.tick(blocks, base)
    factor = blocks[:, INNER // ring.seq :]
    (states,) = clock.tick(carried(ring, blocks, factor, False))
    incoming = returned(ring, states).reshape(INNER, STATE)
    gate_pieces.pass_on(2)
    weight_gate = gate_pieces.pieces()
    weight_out = out_spread.whole()
    grad_pieces = Pieces(ring, grad_out)
    grad_pieces.send()
    gate_rows = gate_pieces.rows
    gate_parts = [
        project(normed_columns, [weight_gate[key][at] for key in where], gate_rows, gate_rows)
        for at in range(3)
    ]
    wide = out_weight.shape[0]
    place_row = jnp.stack(list(where.values())).astype(jnp.int32)
    grad_mixed = to_inner(grad_out, list(weight_out.values()), place_row)
    incoming, grad_mixed, *gate_parts = clock.tick(incoming, grad_mixed, *gate_parts)
    normed_all = trade_columns(ring, {key: clock.now(part) for key, part in normed_for.items()})
    grad_pieces.near()
    mixed, grad_y, grad_gate, grad_reach, direct, grad_g_gate = turn(
        base, incoming, proj_c, decay, gate_parts, grad_mixed, gain_gate
    )
    direct, mixed, grad_y, grad_reach, grad_gate = clock.tick(
        direct, mixed, grad_y, grad_reach, grad_gate
    )
    blocks = lax.all_to_all(direct.reshape(ring.seq, -1, STATE), "seq", 0, 0, tiled=True)
    mixed_all = trade_columns(ring, columns_for(ring, mixed))
    grad_out_all = grad_pieces.whole()
    x_part, b_part, c_part, grad_step, grad_cum, grad_skip = inside_back(
        grad_y, grad_reach, conv_low, incoming, cum, cum_rows, step_rows, skip_row
    )
    gate_grads = Pieces(ring, grad_gate)
    gate_grads.send()
    gate_grads.near()
    total_w_out = Total(ring, weight_grad(mixed_all, grad_out_all, 384))
    blocks, x_part, total_w_out.value = clock.tick(blocks, x_part, total_w_out.value)
    (states,) = clock.tick(carried(ring, blocks, factor, True))
    chain_grad = returned(ring, states)
    total_w_out.step()
    clock.defer()
    total_w_gate = Total(ring, weight_grad(gate_grads.whole(), normed_all, 768))
    (total_w_gate.value,) = clock.tick(total_w_gate.value)
    total_w_gate.step()
    clock.defer(1, 2)
    chain_grad, b_part, c_part = clock.tick(chain_grad, b_part, c_part)
    total_w_out.step()
    grad_conv, first_rows, last_rows, grad_taps, grad_shift, grad_factor, crossed = leave(
        projected,
        edge_rows,
        conv_taps,
        conv_shift,
        conv_low,
        x_part,
        chain_grad.reshape(INNER, STATE),
        incoming,
        weigh,
        b_part,
        c_part,
    )
    grad_conv, last_rows, first_rows = clock.tick(grad_conv, last_rows, first_rows)
    back_rows = ring.next_block(first_rows, -1)
    grad_conv = lax.dynamic_update_slice_in_dim(
        grad_conv, (last_rows + back_rows).astype(bf16), row_count - 8, axis=0
    )
    (grad_conv,) = clock.tick(grad_conv)
    grad_dt_raw, grad_step_bias, grad_rate = steps_back(
        projected,
        step_bias,
        rate_log,
        step_rows,
        cum_rows,
        grad_step,
        grad_cum,
        clock.now(grad_factor),
        crossed,
    )
    grad_tail = jnp.concatenate([grad_conv, grad_dt_raw[:, :HEADS]], axis=1)

    cut = 1792
    first = Pieces(ring, grad_conv[:, :cut])
    last = Pieces(ring, jnp.concatenate([grad_conv[:, cut:], grad_dt_raw], axis=1))
    first.send()
    first.near()
    total_w_out.step()
    total_w_gate.step()
    clock.tick()
    last.send(later=1)
    last.near()
    total_w_out.step()
    clock.defer()
    total_first = Total(ring, weight_grad(first.whole(), normed_all, 896))
    (total_first.value,) = clock.tick(total_first.value)
    total_first.step()
    total_w_gate.step()
    clock.tick()
    total_first.step()
    total_w_out.step()
    total_w_gate.step()
    clock.defer(3)
    total_last = Total(ring, weight_grad(last.whole(), normed_all, 1664))
    (total_last.value,) = clock.tick(total_last.value)
    total_last.step()
    (grad_gate, grad_tail, mixed) = clock.tick(grad_gate, grad_tail, mixed)
    total_w_out.step()
    clock.defer()
    total_first.step()
    total_last.step()
    total_w_gate.step()
    grad_shards = to_model(
        grad_gate, grad_tail, list(weight_gate.values()), list(weight_conv.values())
    )
    mixed_columns = [
        lax.dynamic_slice_in_dim(mixed, place * wide, wide, axis=1) for place in where.values()
    ]
    (grad_shards,) = clock.tick(grad_shards)
    grad_normed = jnp.zeros((row_count, model_width), f32)
    for k, place in enumerate(where.values()):
        grad_normed = lax.dynamic_update_slice_in_dim(
            grad_normed, grad_shards[k], place * depth, axis=1
        )
    grad_skip = jnp.sum(clock.now(grad_skip).reshape(HEADS, HEADDIM), axis=1)
    grad_tokens, grad_g_norm = pull_norm(grad_normed)
    hidden_grad = (grad_tokens + grad_out.astype(f32)).astype(bf16)

    parts = [grad_g_norm, grad_taps, grad_shift[0], grad_step_bias[:, 0], grad_rate[:, 0]]
    parts += [grad_skip, grad_g_gate[0]]
    output = output_rows(
        clock.now(hidden[0]), mixed_columns, list(weight_out.values())
    )
    total_first.step()
    total_last.step()
    total_w_gate.halves()
    clock.defer()
    (output,) = clock.tick(output)
    small_total = SmallSum(ring, pack(parts))
    small_total.step()
    small_total.step()
    total_first.step()
    total_last.step()
    clock.tick()
    small_total.step()
    small_total.step()
    total_first.halves()
    clock.defer()
    total_last.step()
    clock.tick()
    small_total.step()
    total_last.halves()
    summed = small_total.finish().reshape(-1)
    shares, at = [], 0
    for part in parts:
        piece = summed[at : at + part.size].reshape(part.shape)
        at += part.size
        width = part.shape[-1] // ring.fsdp
        shares.append(
            lax.dynamic_slice_in_dim(piece, fsdp_index * width, width, axis=part.ndim - 1)
        )
    total_w_in = jnp.zeros((PROJ, depth), f32)
    total_w_in = place_rows(total_w_in, total_w_gate.halves(), 0, INNER)
    total_w_in = place_rows(total_w_in, total_first.halves(), INNER, cut)
    total_w_in = place_rows(total_w_in, total_last.halves(), INNER + cut, PROJ - INNER - cut)
    total_w_in = total_w_in.T
    total_w_out = total_w_out.finish()
    return (
        output[None],
        hidden_grad[None],
        shares[0],
        total_w_in,
        shares[1],
        shares[2],
        shares[3],
        shares[4],
        shares[5],
        shares[6],
        total_w_out,
    )


def solution(mesh):
    placed = (
        P("fsdp", "seq", None),
        P("fsdp"),
        P("fsdp"),
        P("fsdp", None),
        P(None, "fsdp"),
        P("fsdp"),
        P("fsdp"),
        P("fsdp"),
        P("fsdp"),
        P("fsdp"),
        P("fsdp", None),
        P("fsdp", "seq", None),
    )
    return jax.shard_map(
        local,
        mesh=mesh,
        in_specs=placed,
        out_specs=(
            P("fsdp", "seq", None),
            P("fsdp", "seq", None),
            P("fsdp"),
            P("fsdp", None),
            P(None, "fsdp"),
            P("fsdp"),
            P("fsdp"),
            P("fsdp"),
            P("fsdp"),
            P("fsdp"),
            P("fsdp", None),
        ),
        check_vma=False,
    )
```

time: 710 us -> 594 us (0.84)
  Pallas kernels: 0 us -> 160 us
  matrix products: 142 us -> 0 us
  other arithmetic: 115 us -> 46.5 us
  waiting for transfers between devices: 230 us -> 178 us
  local copies, waits for them, and re-layouts: 121 us -> 99.1 us
  starting transfers between devices: 86.7 us -> 96 us
    pallas_call x0 -> x22, Pallas kernels: none -> 160 us  [the longest x1 29.4 us: inside_back(): pl.pallas_call(inside_back_body, grid=(pairs,), in_specs=[columns, column...]
    dot_general x52 -> x0, matrix products: 142 us -> none  [the longest x16 35.9 us: weight_grad(): jnp.einsum('ti,tj->ij', rows_all[key], columns_all[key], preferred_elemen...]
    unnamed x224 -> x276, local copies, waits for them, and re-layouts: 17.3 us -> 53.5 us
    dynamic_update_slice x14 -> x8, local copies, waits for them, and re-layouts: 35.6 us -> 0.23 us  [the longest x4 0.17 us: local(): lax.dynamic_update_slice_in_dim(grad_normed, grad_shards[k], place * dept...]
    ppermute x72 -> x77, waiting for transfers between devices: 202 us -> 178 us  [send(): arrived = lax.ppermute(block, ('seq', 'fsdp'), route)]
    all_to_all x2, waiting for transfers between devices: 19.9 us -> 0.01 us  [the longest x1 0.01 us: local(): blocks = lax.all_to_all(fresh_state, 'seq', 0, 0, tiled=True)]
    reduce_sum x4 -> x1, other arithmetic: 18.2 us -> 0.11 us  [local(): grad_skip = jnp.sum(clock.now(grad_skip).reshape(HEADS, HEADDIM), axis=1)]
    convert_element_type x4 -> x0, other arithmetic: 14 us -> none  [the longest x1 7.08 us: local(): conv_low = conv_out.astype(bf16)]
  transfers between devices with their start and end apart: 76 -> 81, of which waited for: 30 -> 22; matrix products, arithmetic and copies ran while one was open for 44% -> 14% of each run, Pallas kernels for 0% -> 27%
where the time goes in v2:
time: 594 us; the launch traced here: 584 us
  waiting for transfers between devices  178 us (30%)
  Pallas kernels  160 us (27%)
  local copies, waits for them, and re-layouts  99.1 us (17%)
  starting transfers between devices  96 us (16%)
  other arithmetic  46.5 us (8%)
    ppermute x77, waiting for transfers between devices, send(): arrived = lax.ppermute(block, ('seq', 'fsdp'), route)  178 us
    ppermute x77, starting transfers between devices, send(): arrived = lax.ppermute(block, ('seq', 'fsdp'), route)  73.9 us
    unnamed x276, local copies, waits for them, and re-layouts  53.5 us
    pallas_call x1, Pallas kernels, inside_back(): pl.pallas_call(inside_back_body, grid=(pairs,), in_specs=[columns, column...  29.4 us
    pallas_call x4, Pallas kernels, weight_grad(): pl.pallas_call(functools.partial(sum_body, len(keys)), grid=(rows // tile...  25.7 us
    pallas_call x4, Pallas kernels, project(): pl.pallas_call(functools.partial(project_body, count), grid=(pl.cdiv(widt...  16.1 us
    pallas_call x1, Pallas kernels, to_model(): pl.pallas_call(functools.partial(to_model_body, layout), in_specs=[inside...  15.3 us
    pallas_call x1, Pallas kernels, turn(): pl.pallas_call(turn_body, grid=(2, groups), in_specs=[pl.BlockSpec((token...  13.4 us
  transfers between devices with their start and end apart: 81, of which 22 were waited for; matrix products, arithmetic and copies ran while one was open for 14% of the time, Pallas kernels for 27%

profile of v2, /device:TPU:0, one launch (start us, length us, event | category | flops | bytes accessed | tf_op | source)
XLA Modules:
  0.0 584.1 jit_solution(3556275107718991841)
XLA Ops:
  0.7 2.0 slice.156.refs_4_.refs_0_
  3.6 3.0 collective-permute-start.1
  6.6 2.1 dynamic-slice_bitcast_fusion
  12.4 13.6 %collective-permute-done.3.refs_0_ = bf16[848,384]{1,0:T(8,128)(2,1)} collective-permute-done((bf16[848,384]{1,0:T(8,128)(2,1)}, bf16[848,384]{1,0:T(8,128)(2,1)}, u32[]{:S(2)}, u32[]{:S(2)}) %collective-permute-start.3) | collective-permute-done | bytes 651296 | tf_op jit(solution)/shard_map/ppermute | solution.py:41
  31.3 3.1 fusion.13
  34.3 11.4 %collective-permute-done.8.refs_0_ = bf16[192,1536]{1,0:T(8,128)(2,1)} collective-permute-done((bf16[192,1536]{1,0:T(8,128)(2,1)}, bf16[192,1536]{1,0:T(8,128)(2,1)}, u32[]{:S(2)}, u32[]{:S(2)}) %collective-permute-start.8) | collective-permute-done | bytes 589856 | tf_op jit(solution)/shard_map/ppermute | solution.py:41
  52.4 7.0 %collective-permute-done.10.refs_4_ = bf16[416,384]{1,0:T(8,128)(2,1)S(1)} collective-permute-done((bf16[416,384]{1,0:T(8,128)(2,1)}, bf16[416,384]{1,0:T(8,128)(2,1)S(1)}, u32[]{:S(2)}, u32[]{:S(2)}) %collective-permute-start.10) | collective-permute-done | bytes 319520 | tf_op jit(solution)/shard_map/ppermute | solution.py:41
  65.9 2.8 laid.2
  68.7 7.1 %project.4.dt_ref.proj_ref = bf16[256,3376]{1,0:T(8,128)(2,1)S(1)} custom-call(bf16[256,384]{1,0:T(8,128)(2,1)S(1)} %get-tuple-element.239.refs_0_.refs_4_, bf16[256,384]{1,0:T(8,128)(2,1)S(1)} %get-tuple-element.222.refs_1_, bf16[256,384]{1,0:T(8,128)(2,1)S(1)} %get-tuple-element.345.refs_2_, bf16[256,384]{1,0:T(8,128)(2,1)S(1)} %get-tuple-element.344.refs_3_, ...), custom_call_target="tpu_custom_call" | custom-call | tf_op jit(solution)/shard_map/project/pallas_call | solution.py:395
  75.9 10.8 %collective-permute-done.18.refs_6_ = bf16[1024,384]{1,0:T(8,128)(2,1)} collective-permute-done((bf16[1024,384]{1,0:T(8,128)(2,1)}, bf16[1024,384]{1,0:T(8,128)(2,1)}, u32[]{:S(2)}, u32[]{:S(2)}) %collective-permute-start.18) | collective-permute-done | bytes 786464 | tf_op jit(solution)/shard_map/ppermute | solution.py:41
  94.8 2.4 collective-permute-start.19
  102.3 3.8 enter.1
  108.1 5.8 all-to-all-start
  113.9 3.5 slice.166.refs_4_.refs_1_
  119.4 3.2 laid.3.refs_2_.refs_6_
  123.1 14.2 %collective-permute-done.22.refs_6_.refs_7_ = bf16[1024,384]{1,0:T(8,128)(2,1)S(1)} collective-permute-done((bf16[1024,384]{1,0:T(8,128)(2,1)S(1)}, bf16[1024,384]{1,0:T(8,128)(2,1)S(1)}, u32[]{:S(2)}, u32[]{:S(2)}) %collective-permute-start.22) | collective-permute-done | bytes 786464 | tf_op jit(solution)/shard_map/ppermute | solution.py:41
  142.1 10.7 %inside.1.base_ref = f32[256,3072]{1,0:T(8,128)S(1)} custom-call(bf16[256,3328]{1,0:T(8,128)(2,1)S(1)} %get-tuple-element.192.x_ref.b_ref.c_ref.low_ref, bf16[256,3328]{1,0:T(8,128)(2,1)S(1)} %get-tuple-element.192.x_ref.b_ref.c_ref.low_ref, bf16[256,3328]{1,0:T(8,128)(2,1)S(1)} %get-tuple-element.192.x_ref.b_ref.c_ref.low_ref, f32[256,128]{1,0:T(8,128)S(1)} %copy-done.72, ...), custom_call_target="tpu_custom_call" | custom-call | tf_op jit(solution)/shard_map/inside/pallas_call | solution.py:825
  155.9 2.4 carried.2
  158.3 6.0 %all-to-all-start.1 = ((bf16[8,384,128]{2,1,0:T(8,128)(2,1)}), bf16[8,384,128]{2,1,0:T(8,128)(2,1)S(1)}, u32[]{:S(2)}, u32[]{:S(2)}) async-start(bf16[8,384,128]{2,1,0:T(8,128)(2,1)} %carried.2), calls=%async_computation.1 | async-start | bytes 1572864 | tf_op jit(solution)/shard_map/all_to_all | solution.py:541
  167.7 3.2 project.6.refs_1_
  171.6 2.9 project.5.refs_0_
  175.4 10.1 %to_inner.1.grad_ref = f32[256,3072]{1,0:T(8,128)S(1)} custom-call(s32[4]{0:T(128)S(1)} %pad_add_fusion.1.place_ref, bf16[256,1536]{1,0:T(8,128)(2,1)S(1)} %bitcast_select_fusion.grad_ref.refs_4_, bf16[768,1536]{1,0:T(8,128)(2,1)} %refs_4_.1, bf16[768,1536]{1,0:T(8,128)(2,1)} %collective-permute-done.26.refs_1_.refs_5_, ...), custom_call_target="tpu_custom_call" | custom-call | tf_op jit(solution)/shard_map/to_inner/pallas_call | solution.py:264
  187.2 2.9 project.7.refs_2_
  199.9 13.4 %turn.1 = (bf16[256,3072]{1,0:T(8,128)(2,1)S(1)}, bf16[256,3072]{1,0:T(8,128)(2,1)S(1)}, bf16[256,3072]{1,0:T(8,128)(2,1)S(1)}, bf16[256,3072]{1,0:T(8,128)(2,1)...) custom-call(f32[256,3072]{1,0:T(8,128)S(1)} %copy-done.12, bf16[3072,128]{1,0:T(8,128)(2,1)S(1)} %bitcast.78, ...), custom_call_target="tpu_custom_call" | custom-call | tf_op jit(solution)/shard_map/turn/pallas_call | solution.py:933
  221.3 5.8 all-to-all-start.2
  227.6 2.4 constant_dynamic-slice_fusion.5
  240.0 29.4 %inside_back.1 = (f32[256,3072]{1,0:T(8,128)S(1)}, f32[256,128]{1,0:T(8,128)S(1)}, f32[256,128]{1,0:T(8,128)S(1)}, f32[48,256]{1,0:T(8,128)S(1)}, f32[48,256]{1,0:T(8,128)S(1)}, /*index=5*/f32[1,3072]{1,0:T(1,128)S(1)}) custom-call(bf16[256,3072]{1,0:T(8,128)(2,1)S(1)} %copy-done.60, bf16[256,3072]{1,0:T(8,128)(2,1)S(1)} %copy-done.62, ...), custom_call_target="tpu_custom_call" | custom-call | tf_op jit(solution)/shard_map/inside_back/pallas_call | solution.py:897
  274.2 5.9 %collective-permute-done.36.refs_3_ = bf16[256,768]{1,0:T(8,128)(2,1)} collective-permute-done((bf16[256,768]{1,0:T(8,128)(2,1)}, bf16[256,768]{1,0:T(8,128)(2,1)}, u32[]{:S(2)}, u32[]{:S(2)}) %collective-permute-start.36) | collective-permute-done | bytes 393248 | tf_op jit(solution)/shard_map/ppermute | solution.py:41
  280.1 4.5 weight_grad.4
  284.6 2.2 copy-done.7
  286.8 2.4 carried.3
  289.2 2.8 dynamic-slice_convert_fusion.1
  294.0 4.5 all-to-all-start.3
  298.6 28.8 %collective-permute-done.41 = bf16[384,1536]{1,0:T(8,128)(2,1)} collective-permute-done((bf16[384,1536]{1,0:T(8,128)(2,1)}, bf16[384,1536]{1,0:T(8,128)(2,1)}, u32[]{:S(2)}, u32[]{:S(2)}) %collective-permute-start.41) | collective-permute-done | bytes 1179680 | tf_op jit(solution)/shard_map/ppermute | solution.py:41
  327.5 3.8 convert_add_fusion.1
  331.3 5.7 weight_grad.5
  337.0 2.2 copy-done.8
  340.0 2.3 dynamic-slice_convert_fusion.5
  343.8 2.9 dynamic-slice_convert_fusion
  352.0 13.4 %leave.1 = (bf16[256,3328]{1,0:T(8,128)(2,1)S(1)}, f32[8,3328]{1,0:T(8,128)}, f32[8,3328]{1,0:T(8,128)S(1)}, f32[4,3328]{1,0:T(4,128)S(1)}, f32[1,3328]{1,0:T(1,...) custom-call(bf16[256,3376]{1,0:T(8,128)(2,1)S(1)} %copy-done.2, bf16[8,3328]{1,0:T(8,128)(2,1)S(1)} %copy-done.89, ...), custom_call_target="tpu_custom_call" | custom-call | tf_op jit(solution)/shard_map/leave/pallas_call | solution.py:1056
  371.0 5.8 collective-permute-done.43
  380.0 2.4 convert_add_fusion
  386.3 2.4 collective-permute-start.47
  391.1 2.5 steps_back.1
  394.9 8.8 %collective-permute-done.47 = bf16[96,1536]{1,0:T(8,128)(2,1)} collective-permute-done((bf16[96,1536]{1,0:T(8,128)(2,1)}, bf16[96,1536]{1,0:T(8,128)(2,1)}, u32[]{:S(2)}, u32[]{:S(2)}) %collective-permute-start.47) | collective-permute-done | bytes 294944 | tf_op jit(solution)/shard_map/ppermute | solution.py:41
  403.7 2.1 collective-permute-done.48
  415.2 12.4 %weight_grad.6 = f32[1792,384]{1,0:T(8,128)S(1)} custom-call(bf16[256,1792]{1,0:T(8,128)(2,1)S(1)} %slice.139.refs_0_, bf16[256,1792]{1,0:T(8,128)(2,1)} %collective-permute-done.46.refs_1_, bf16[256,1792]{1,0:T(8,128)(2,1)} %collective-permute-done.45.refs_2_, bf16[256,1792]{1,0:T(8,128)(2,1)} %collective-permute-done.49.refs_3_, ...), custom_call_target="tpu_custom_call" | custom-call | tf_op jit(solution)/shard_map/weight_grad/pallas_call | solution.py:236
  430.9 12.6 %collective-permute-done.54 = bf16[384,384]{1,0:T(8,128)(2,1)S(1)} collective-permute-done((bf16[384,384]{1,0:T(8,128)(2,1)S(1)}, bf16[384,384]{1,0:T(8,128)(2,1)S(1)}, u32[]{:S(2)}, u32[]{:S(2)}) %collective-permute-start.54) | collective-permute-done | bytes 294944 | tf_op jit(solution)/shard_map/ppermute | solution.py:41
  443.5 2.6 collective-permute-done.53
  446.2 2.4 collective-permute-start.57
  449.7 19.0 %collective-permute-done.58 = bf16[384,384]{1,0:T(8,128)(2,1)S(1)} collective-permute-done((bf16[384,384]{1,0:T(8,128)(2,1)S(1)}, bf16[384,384]{1,0:T(8,128)(2,1)S(1)}, u32[]{:S(2)}, u32[]{:S(2)}) %collective-permute-start.58) | collective-permute-done | bytes 294944 | tf_op jit(solution)/shard_map/ppermute | solution.py:41
  468.9 5.3 collective-permute-done.56
  474.2 3.1 weight_grad.7
  479.9 11.9 %collective-permute-done.59 = bf16[832,384]{1,0:T(8,128)(2,1)S(1)} collective-permute-done((bf16[832,384]{1,0:T(8,128)(2,1)S(1)}, bf16[832,384]{1,0:T(8,128)(2,1)S(1)}, u32[]{:S(2)}, u32[]{:S(2)}) %collective-permute-start.59) | collective-permute-done | bytes 639008 | tf_op jit(solution)/shard_map/ppermute | solution.py:41
  496.5 15.3 %to_model.1 = f32[4,256,384]{2,1,0:T(8,128)} custom-call(bf16[256,3072]{1,0:T(8,128)(2,1)} %copy-done.22, bf16[256,3376]{1,0:T(8,128)(2,1)} %pad_maximum_fusion.tail_ref, bf16[3376,384]{1,0:T(8,128)(2,1)} %copy-done.3, bf16[3072,384]{1,0:T(8,128)(2,1)} %slice.166.refs_4_.refs_1_, bf16[3376,384]{1,0:T(8,128)(2,1)} %collective-permute-done.4.refs_5_.refs_2_, ...), custom_call_target="tpu_custom_call" | custom-call | tf_op jit(solution)/shard_map/to_model/pallas_call | solution.py:312
  512.2 3.3 collective-permute-done.62
  526.0 7.3 %output_rows.1 = bf16[256,1536]{1,0:T(8,128)(2,1)} custom-call(bf16[256,1536]{1,0:T(8,128)(2,1)S(1)} %bitcast.77, bf16[256,768]{1,0:T(8,128)(2,1)S(1)} %get-tuple-element.333.refs_0_, bf16[256,768]{1,0:T(8,128)(2,1)S(1)} %get-tuple-element.332.refs_1_, bf16[256,768]{1,0:T(8,128)(2,1)S(1)} %get-tuple-element.331.refs_2_, ...), custom_call_target="tpu_custom_call" | custom-call | tf_op jit(solution)/shard_map/output_rows/pallas_call | solution.py:335
  539.8 2.8 maximum_convert_fusion
  543.4 4.3 collective-permute-done.67
  551.4 4.5 pad_convert_fusion
  557.7 2.9 convert_dynamic-update-slice_fusion
  561.8 2.7 collective-permute-start.76
  572.0 2.3 convert_dynamic-update-slice_fusion.1
  574.3 7.2 %collective-permute-done.76 = bf16[832,384]{1,0:T(8,128)(2,1)S(1)} collective-permute-done((bf16[832,384]{1,0:T(8,128)(2,1)S(1)}, bf16[832,384]{1,0:T(8,128)(2,1)S(1)}, u32[]{:S(2)}, u32[]{:S(2)}) %collective-permute-start.76) | collective-permute-done | bytes 639008 | tf_op jit(solution)/shard_map/ppermute | solution.py:41
  (538 shorter events, 167.7 us)
Async XLA Ops:
  2.8 23.2 %collective-permute-start.4 = (bf16[3376,384]{1,0:T(8,128)(2,1)S(1)}, bf16[3376,384]{1,0:T(8,128)(2,1)}, u32[]{:S(2)}, u32[]{:S(2)}) collective-permute-start(bf16[3376,384]{1,0:T(8,128)(2,1)S(1)} %slice.156.refs_4_.refs_0_), channel_id=1, source_target_pairs={{0,1},{1,0},{2,3},{3,2},{4,5},{5,4},{6,7},{7,6},{8,9},{9,8},{10,11... | collective-permute-start | bytes 7778312 | tf_op jit(solution)/shard_map/ppermute | solution.py:41
  8.7 17.3 %collective-permute-start.3 = (bf16[848,384]{1,0:T(8,128)(2,1)}, bf16[848,384]{1,0:T(8,128)(2,1)}, u32[]{:S(2)}, u32[]{:S(2)}) collective-permute-start(bf16[848,384]{1,0:T(8,128)(2,1)} %dynamic-slice_bitcast_fusion), channel_id=1, source_target_pairs={{0,2},{1,3},{2,0},{3,1},{4,6},{5,7},{6,4},{7,5},{8,10},{9,11},{10,... | collective-permute-start | bytes 1953800 | tf_op jit(solution)/shard_map/ppermute | solution.py:41
  26.0 19.8 %collective-permute-start.5 = (bf16[848,384]{1,0:T(8,128)(2,1)}, bf16[848,384]{1,0:T(8,128)(2,1)}, u32[]{:S(2)}, u32[]{:S(2)}) collective-permute-start(bf16[848,384]{1,0:T(8,128)(2,1)} %collective-permute-done.3.refs_0_), channel_id=1, source_target_pairs={{0,4},{1,5},{2,6},{3,7},{4,0},{5,1},{6,2},{7,3},{8,12},{9,13},{10,... | collective-permute-start | bytes 1953800 | tf_op jit(solution)/shard_map/ppermute | solution.py:41
  27.7 18.0 %collective-permute-start.6 = (bf16[848,384]{1,0:T(8,128)(2,1)}, bf16[848,384]{1,0:T(8,128)(2,1)}, u32[]{:S(2)}, u32[]{:S(2)}) collective-permute-start(bf16[848,384]{1,0:T(8,128)(2,1)} %collective-permute-done.3.refs_0_), channel_id=1, source_target_pairs={{0,8},{1,9},{2,10},{3,11},{4,12},{5,13},{6,14},{7,15},{8,0},{9,1},... | collective-permute-start | bytes 1953800 | tf_op jit(solution)/shard_map/ppermute | solution.py:41
  29.2 16.5 %collective-permute-start.7 = (bf16[848,384]{1,0:T(8,128)(2,1)}, bf16[848,384]{1,0:T(8,128)(2,1)}, u32[]{:S(2)}, u32[]{:S(2)}) collective-permute-start(bf16[848,384]{1,0:T(8,128)(2,1)} %collective-permute-done.3.refs_0_), channel_id=1, source_target_pairs={{0,1},{1,0},{2,3},{3,2},{4,5},{5,4},{6,7},{7,6},{8,9},{9,8},{10,11... | collective-permute-start | bytes 1953800 | tf_op jit(solution)/shard_map/ppermute | solution.py:41
  29.6 16.1 %collective-permute-start.8 = (bf16[192,1536]{1,0:T(8,128)(2,1)}, bf16[192,1536]{1,0:T(8,128)(2,1)}, u32[]{:S(2)}, u32[]{:S(2)}) collective-permute-start(bf16[192,1536]{1,0:T(8,128)(2,1)} %constant_dynamic-slice_fusion.15), channel_id=1, source_target_pairs={{0,2},{1,3},{2,0},{3,1},{4,6},{5,7},{6,4},{7,5},{8,10},{9,11},{10,... | collective-permute-start | bytes 1769480 | tf_op jit(solution)/shard_map/ppermute | solution.py:41
  45.7 14.2 %collective-permute-start.11 = (bf16[848,384]{1,0:T(8,128)(2,1)}, bf16[848,384]{1,0:T(8,128)(2,1)S(1)}, u32[]{:S(2)}, u32[]{:S(2)}) collective-permute-start(bf16[848,384]{1,0:T(8,128)(2,1)} %collective-permute-done.5.refs_1_), channel_id=1, source_target_pairs={{0,1},{1,0},{2,3},{3,2},{4,5},{5,4},{6,7},{7,6},{8,9},{9,8},{10,11... | collective-permute-start | bytes 1953800 | tf_op jit(solution)/shard_map/ppermute | solution.py:41
  49.2 10.7 %collective-permute-start.12 = (bf16[848,384]{1,0:T(8,128)(2,1)}, bf16[848,384]{1,0:T(8,128)(2,1)S(1)}, u32[]{:S(2)}, u32[]{:S(2)}) collective-permute-start(bf16[848,384]{1,0:T(8,128)(2,1)} %collective-permute-done.6.refs_2_), channel_id=1, source_target_pairs={{0,1},{1,0},{2,3},{3,2},{4,5},{5,4},{6,7},{7,6},{8,9},{9,8},{10,11... | collective-permute-start | bytes 1953800 | tf_op jit(solution)/shard_map/ppermute | solution.py:41
  50.6 25.3 %collective-permute-start.13 = (bf16[1024,384]{1,0:T(8,128)(2,1)}, bf16[1024,384]{1,0:T(8,128)(2,1)S(1)}, u32[]{:S(2)}, u32[]{:S(2)}) collective-permute-start(bf16[1024,384]{1,0:T(8,128)(2,1)} %get-tuple-element.175), channel_id=1, source_target_pairs={{0,2},{1,3},{2,0},{3,1},{4,6},{5,7},{6,4},{7,5},{8,10},{9,11},{10,... | collective-permute-start | bytes 2359304 | tf_op jit(solution)/shard_map/ppermute | solution.py:41
  60.0 15.9 %collective-permute-start.16 = (bf16[192,1536]{1,0:T(8,128)(2,1)}, bf16[192,1536]{1,0:T(8,128)(2,1)S(1)}, u32[]{:S(2)}, u32[]{:S(2)}) collective-permute-start(bf16[192,1536]{1,0:T(8,128)(2,1)} %collective-permute-done.8.refs_0_), channel_id=1, source_target_pairs={{0,4},{1,5},{2,6},{3,7},{4,0},{5,1},{6,2},{7,3},{8,12},{9,13},{10,... | collective-permute-start | bytes 1769480 | tf_op jit(solution)/shard_map/ppermute | solution.py:41
  60.4 15.5 %collective-permute-start.17 = (bf16[192,1536]{1,0:T(8,128)(2,1)}, bf16[192,1536]{1,0:T(8,128)(2,1)S(1)}, u32[]{:S(2)}, u32[]{:S(2)}) collective-permute-start(bf16[192,1536]{1,0:T(8,128)(2,1)} %collective-permute-done.8.refs_0_), channel_id=1, source_target_pairs={{0,8},{1,9},{2,10},{3,11},{4,12},{5,13},{6,14},{7,15},{8,0},{9,1},... | collective-permute-start | bytes 1769480 | tf_op jit(solution)/shard_map/ppermute | solution.py:41
  62.1 24.6 %collective-permute-start.18 = (bf16[1024,384]{1,0:T(8,128)(2,1)}, bf16[1024,384]{1,0:T(8,128)(2,1)}, u32[]{:S(2)}, u32[]{:S(2)}) collective-permute-start(bf16[1024,384]{1,0:T(8,128)(2,1)} %get-tuple-element.182), channel_id=1, source_target_pairs={{0,2},{1,3},{2,0},{3,1},{4,6},{5,7},{6,4},{7,5},{8,10},{9,11},{10,... | collective-permute-start | bytes 2359304 | tf_op jit(solution)/shard_map/ppermute | solution.py:41
  88.3 18.9 %collective-permute-start.21 = (bf16[96,1536]{1,0:T(8,128)(2,1)}, bf16[96,1536]{1,0:T(8,128)(2,1)S(1)}, u32[]{:S(2)}, u32[]{:S(2)}) collective-permute-start(bf16[96,1536]{1,0:T(8,128)(2,1)} %slice.132), channel_id=1, source_target_pairs={{0,8},{1,9},{2,10},{3,11},{4,12},{5,13},{6,14},{7,15},{8,0},{9,1},... | collective-permute-start | bytes 884744 | tf_op jit(solution)/shard_map/ppermute | solution.py:41
  91.6 15.6 %collective-permute-start.20 = (bf16[96,1536]{1,0:T(8,128)(2,1)}, bf16[96,1536]{1,0:T(8,128)(2,1)S(1)}, u32[]{:S(2)}, u32[]{:S(2)}) collective-permute-start(bf16[96,1536]{1,0:T(8,128)(2,1)} %slice.131), channel_id=1, source_target_pairs={{0,4},{1,5},{2,6},{3,7},{4,0},{5,1},{6,2},{7,3},{8,12},{9,13},{10,... | collective-permute-start | bytes 884744 | tf_op jit(solution)/shard_map/ppermute | solution.py:41
  108.1 46.5 %all-to-all-start = ((f32[8,392,128]{2,1,0:T(8,128)}), f32[8,392,128]{2,1,0:T(8,128)}, u32[]{:S(2)}, u32[]{:S(2)}) async-start(f32[8,392,128]{2,1,0:T(8,128)} %copy-done.57), calls=%async_computation | async-start | bytes 3211264 | tf_op jit(solution)/shard_map/all_to_all | solution.py:1200
  117.4 37.2 %collective-permute-start.25 = (bf16[3072,384]{1,0:T(8,128)(2,1)}, bf16[3072,384]{1,0:T(8,128)(2,1)}, u32[]{:S(2)}, u32[]{:S(2)}) collective-permute-start(bf16[3072,384]{1,0:T(8,128)(2,1)} %slice.166.refs_4_.refs_1_), channel_id=1, source_target_pairs={{0,1},{1,0},{2,3},{3,2},{4,5},{5,4},{6,7},{7,6},{8,9},{9,8},{10,11... | collective-permute-start | bytes 7077896 | tf_op jit(solution)/shard_map/ppermute | solution.py:41
  117.4 37.2 %collective-permute-start.26 = (bf16[768,1536]{1,0:T(8,128)(2,1)}, bf16[768,1536]{1,0:T(8,128)(2,1)}, u32[]{:S(2)}, u32[]{:S(2)}) collective-permute-start(bf16[768,1536]{1,0:T(8,128)(2,1)} %refs_4_.1), channel_id=1, source_target_pairs={{0,1},{1,0},{2,3},{3,2},{4,5},{5,4},{6,7},{7,6},{8,9},{9,8},{10,11... | collective-permute-start | bytes 7077896 | tf_op jit(solution)/shard_map/ppermute | solution.py:41
  117.9 19.4 %collective-permute-start.22 = (bf16[1024,384]{1,0:T(8,128)(2,1)S(1)}, bf16[1024,384]{1,0:T(8,128)(2,1)S(1)}, u32[]{:S(2)}, u32[]{:S(2)}) collective-permute-start(bf16[1024,384]{1,0:T(8,128)(2,1)S(1)} %copy-done.117), channel_id=1, source_target_pairs={{0,2},{1,3},{2,0},{3,1},{4,6},{5,7},{6,4},{7,5},{8,10},{9,11},{10,... | collective-permute-start | bytes 2359304 | tf_op jit(solution)/shard_map/ppermute | solution.py:41
  122.6 52.8 %collective-permute-start.27 = (bf16[768,1536]{1,0:T(8,128)(2,1)}, bf16[768,1536]{1,0:T(8,128)(2,1)}, u32[]{:S(2)}, u32[]{:S(2)}) collective-permute-start(bf16[768,1536]{1,0:T(8,128)(2,1)} %laid.3.refs_2_.refs_6_), channel_id=1, source_target_pairs={{0,1},{1,0},{2,3},{3,2},{4,5},{5,4},{6,7},{7,6},{8,9},{9,8},{10,11... | collective-permute-start | bytes 7077896 | tf_op jit(solution)/shard_map/ppermute | solution.py:41
  122.6 31.9 %collective-permute-start.24 = (bf16[1024,384]{1,0:T(8,128)(2,1)}, bf16[1024,384]{1,0:T(8,128)(2,1)}, u32[]{:S(2)}, u32[]{:S(2)}) collective-permute-start(bf16[1024,384]{1,0:T(8,128)(2,1)} %collective-permute-done.18.refs_6_), channel_id=1, source_target_pairs={{0,1},{1,0},{2,3},{3,2},{4,5},{5,4},{6,7},{7,6},{8,9},{9,8},{10,11... | collective-permute-start | bytes 2359304 | tf_op jit(solution)/shard_map/ppermute | solution.py:41
  137.3 17.2 %collective-permute-start.23 = (bf16[1024,384]{1,0:T(8,128)(2,1)S(1)}, bf16[1024,384]{1,0:T(8,128)(2,1)}, u32[]{:S(2)}, u32[]{:S(2)}) collective-permute-start(bf16[1024,384]{1,0:T(8,128)(2,1)S(1)} %collective-permute-done.13.refs_6_.refs_5_), channel_id=1, source_target_pairs={{0,1},{1,0},{2,3},{3,2},{4,5},{5,4},{6,7},{7,6},{8,9},{9,8},{10,11... | collective-permute-start | bytes 2359304 | tf_op jit(solution)/shard_map/ppermute | solution.py:41
  158.3 32.6 %all-to-all-start.1 = ((bf16[8,384,128]{2,1,0:T(8,128)(2,1)}), bf16[8,384,128]{2,1,0:T(8,128)(2,1)S(1)}, u32[]{:S(2)}, u32[]{:S(2)}) async-start(bf16[8,384,128]{2,1,0:T(8,128)(2,1)} %carried.2), calls=%async_computation.1 | async-start | bytes 1572864 | tf_op jit(solution)/shard_map/all_to_all | solution.py:541
  165.7 21.4 %collective-permute-start.28 = (bf16[1024,384]{1,0:T(8,128)(2,1)S(1)}, bf16[1024,384]{1,0:T(8,128)(2,1)S(1)}, u32[]{:S(2)}, u32[]{:S(2)}) collective-permute-start(bf16[1024,384]{1,0:T(8,128)(2,1)S(1)} %copy-done.38), channel_id=1, source_target_pairs={{0,1},{1,0},{2,3},{3,2},{4,5},{5,4},{6,7},{7,6},{8,9},{9,8},{10,11... | collective-permute-start | bytes 2359304 | tf_op jit(solution)/shard_map/ppermute | solution.py:41
  166.0 24.9 %collective-permute-start.29 = (bf16[256,1536]{1,0:T(8,128)(2,1)S(1)}, bf16[256,1536]{1,0:T(8,128)(2,1)}, u32[]{:S(2)}, u32[]{:S(2)}) collective-permute-start(bf16[256,1536]{1,0:T(8,128)(2,1)S(1)} %bitcast_select_fusion.grad_ref.refs_4_), channel_id=1, source_target_pairs={{0,2},{1,3},{2,0},{3,1},{4,6},{5,7},{6,4},{7,5},{8,10},{9,11},{10,... | collective-permute-start | bytes 2359304 | tf_op jit(solution)/shard_map/ppermute | solution.py:41
  190.9 29.5 %collective-permute-start.33 = (bf16[256,1536]{1,0:T(8,128)(2,1)S(1)}, bf16[256,1536]{1,0:T(8,128)(2,1)S(1)}, u32[]{:S(2)}, u32[]{:S(2)}) collective-permute-start(bf16[256,1536]{1,0:T(8,128)(2,1)S(1)} %bitcast_select_fusion.grad_ref.refs_4_), channel_id=1, source_target_pairs={{0,1},{1,0},{2,3},{3,2},{4,5},{5,4},{6,7},{7,6},{8,9},{9,8},{10,11... | collective-permute-start | bytes 2359304 | tf_op jit(solution)/shard_map/ppermute | solution.py:41
  191.0 26.4 %collective-permute-start.32 = (bf16[256,384]{1,0:T(8,128)(2,1)}, bf16[256,384]{1,0:T(8,128)(2,1)S(1)}, u32[]{:S(2)}, u32[]{:S(2)}) collective-permute-start(bf16[256,384]{1,0:T(8,128)(2,1)} %get-tuple-element.224), channel_id=1, source_target_pairs={{0,3},{1,2},{2,1},{3,0},{4,7},{5,6},{6,5},{7,4},{8,11},{9,10},{10,... | collective-permute-start | bytes 589832 | tf_op jit(solution)/shard_map/ppermute | solution.py:41
  191.6 27.4 %collective-permute-start.31 = (bf16[256,384]{1,0:T(8,128)(2,1)}, bf16[256,384]{1,0:T(8,128)(2,1)S(1)}, u32[]{:S(2)}, u32[]{:S(2)}) collective-permute-start(bf16[256,384]{1,0:T(8,128)(2,1)} %get-tuple-element.223), channel_id=1, source_target_pairs={{0,2},{1,3},{2,0},{3,1},{4,6},{5,7},{6,4},{7,5},{8,10},{9,11},{10,... | collective-permute-start | bytes 589832 | tf_op jit(solution)/shard_map/ppermute | solution.py:41
  193.1 26.6 %collective-permute-start.30 = (bf16[256,384]{1,0:T(8,128)(2,1)}, bf16[256,384]{1,0:T(8,128)(2,1)S(1)}, u32[]{:S(2)}, u32[]{:S(2)}) collective-permute-start(bf16[256,384]{1,0:T(8,128)(2,1)} %copy-done.24), channel_id=1, source_target_pairs={{0,1},{1,0},{2,3},{3,2},{4,5},{5,4},{6,7},{7,6},{8,9},{9,8},{10,11... | collective-permute-start | bytes 589832 | tf_op jit(solution)/shard_map/ppermute | solution.py:41
  221.3 65.5 %all-to-all-start.2 = ((f32[8,384,128]{2,1,0:T(8,128)}), f32[8,384,128]{2,1,0:T(8,128)}, u32[]{:S(2)}, u32[]{:S(2)}) async-start(f32[8,384,128]{2,1,0:T(8,128)} %bitcast.82), calls=%async_computation.2 | async-start | bytes 3145728 | tf_op jit(solution)/shard_map/all_to_all | solution.py:1234
  227.1 59.7 %collective-permute-start.38 = (bf16[256,3072]{1,0:T(8,128)(2,1)}, bf16[256,3072]{1,0:T(8,128)(2,1)}, u32[]{:S(2)}, u32[]{:S(2)}) collective-permute-start(bf16[256,3072]{1,0:T(8,128)(2,1)} %copy-done.22), channel_id=1, source_target_pairs={{0,2},{1,3},{2,0},{3,1},{4,6},{5,7},{6,4},{7,5},{8,10},{9,11},{10,... | collective-permute-start | bytes 4718600 | tf_op jit(solution)/shard_map/ppermute | solution.py:41
  227.6 59.2 %collective-permute-start.39 = (bf16[256,3072]{1,0:T(8,128)(2,1)}, bf16[256,3072]{1,0:T(8,128)(2,1)}, u32[]{:S(2)}, u32[]{:S(2)}) collective-permute-start(bf16[256,3072]{1,0:T(8,128)(2,1)} %copy-done.22), channel_id=1, source_target_pairs={{0,1},{1,0},{2,3},{3,2},{4,5},{5,4},{6,7},{7,6},{8,9},{9,8},{10,11... | collective-permute-start | bytes 4718600 | tf_op jit(solution)/shard_map/ppermute | solution.py:41
  230.5 49.6 %collective-permute-start.37 = (bf16[256,1536]{1,0:T(8,128)(2,1)}, bf16[256,1536]{1,0:T(8,128)(2,1)}, u32[]{:S(2)}, u32[]{:S(2)}) collective-permute-start(bf16[256,1536]{1,0:T(8,128)(2,1)} %collective-permute-done.29.refs_6_), channel_id=1, source_target_pairs={{0,1},{1,0},{2,3},{3,2},{4,5},{5,4},{6,7},{7,6},{8,9},{9,8},{10,11... | collective-permute-start | bytes 2359304 | tf_op jit(solution)/shard_map/ppermute | solution.py:41
  230.5 43.7 %collective-permute-start.35 = (bf16[256,768]{1,0:T(8,128)(2,1)}, bf16[256,768]{1,0:T(8,128)(2,1)}, u32[]{:S(2)}, u32[]{:S(2)}) collective-permute-start(bf16[256,768]{1,0:T(8,128)(2,1)} %get-tuple-element.335), channel_id=1, source_target_pairs={{0,2},{1,3},{2,0},{3,1},{4,6},{5,7},{6,4},{7,5},{8,10},{9,11},{10,... | collective-permute-start | bytes 1179656 | tf_op jit(solution)/shard_map/ppermute | solution.py:41
  233.1 47.0 %collective-permute-start.36 = (bf16[256,768]{1,0:T(8,128)(2,1)}, bf16[256,768]{1,0:T(8,128)(2,1)}, u32[]{:S(2)}, u32[]{:S(2)}) collective-permute-start(bf16[256,768]{1,0:T(8,128)(2,1)} %get-tuple-element.334), channel_id=1, source_target_pairs={{0,3},{1,2},{2,1},{3,0},{4,7},{5,6},{6,5},{7,4},{8,11},{9,10},{10,... | collective-permute-start | bytes 1179656 | tf_op jit(solution)/shard_map/ppermute | solution.py:41
  292.1 35.4 %collective-permute-start.41 = (bf16[384,1536]{1,0:T(8,128)(2,1)}, bf16[384,1536]{1,0:T(8,128)(2,1)}, u32[]{:S(2)}, u32[]{:S(2)}) collective-permute-start(bf16[384,1536]{1,0:T(8,128)(2,1)} %dynamic-slice_convert_fusion.1), channel_id=1, source_target_pairs={{0,4},{1,5},{2,6},{3,7},{4,0},{5,1},{6,2},{7,3},{8,12},{9,13},{10,... | collective-permute-start | bytes 3538952 | tf_op jit(solution)/shard_map/ppermute | solution.py:41
  293.5 37.8 %collective-permute-start.40 = (bf16[256,3072]{1,0:T(8,128)(2,1)}, bf16[256,3072]{1,0:T(8,128)(2,1)}, u32[]{:S(2)}, u32[]{:S(2)}) collective-permute-start(bf16[256,3072]{1,0:T(8,128)(2,1)} %collective-permute-done.38.refs_2_), channel_id=1, source_target_pairs={{0,1},{1,0},{2,3},{3,2},{4,5},{5,4},{6,7},{7,6},{8,9},{9,8},{10,11... | collective-permute-start | bytes 4718600 | tf_op jit(solution)/shard_map/ppermute | solution.py:41
  294.0 45.1 %all-to-all-start.3 = ((bf16[8,384,128]{2,1,0:T(8,128)(2,1)}), bf16[8,384,128]{2,1,0:T(8,128)(2,1)S(1)}, u32[]{:S(2)}, u32[]{:S(2)}) async-start(bf16[8,384,128]{2,1,0:T(8,128)(2,1)} %carried.3), calls=%async_computation.3 | async-start | bytes 1572864 | tf_op jit(solution)/shard_map/all_to_all | solution.py:541
  342.3 27.3 %collective-permute-start.42 = (bf16[192,1536]{1,0:T(8,128)(2,1)}, bf16[192,1536]{1,0:T(8,128)(2,1)}, u32[]{:S(2)}, u32[]{:S(2)}) collective-permute-start(bf16[192,1536]{1,0:T(8,128)(2,1)} %dynamic-slice_convert_fusion.5), channel_id=1, source_target_pairs={{0,8},{1,9},{2,10},{3,11},{4,12},{5,13},{6,14},{7,15},{8,0},{9,1},... | collective-permute-start | bytes 1769480 | tf_op jit(solution)/shard_map/ppermute | solution.py:41
  346.8 31.5 %collective-permute-start.44 = (bf16[1536,384]{1,0:T(8,128)(2,1)}, bf16[1536,384]{1,0:T(8,128)(2,1)}, u32[]{:S(2)}, u32[]{:S(2)}) collective-permute-start(bf16[1536,384]{1,0:T(8,128)(2,1)} %dynamic-slice_convert_fusion), channel_id=1, source_target_pairs={{0,4},{1,5},{2,6},{3,7},{4,0},{5,1},{6,2},{7,3},{8,12},{9,13},{10,... | collective-permute-start | bytes 3538952 | tf_op jit(solution)/shard_map/ppermute | solution.py:41
  379.5 26.4 %collective-permute-start.45 = (bf16[256,1792]{1,0:T(8,128)(2,1)S(1)}, bf16[256,1792]{1,0:T(8,128)(2,1)}, u32[]{:S(2)}, u32[]{:S(2)}) collective-permute-start(bf16[256,1792]{1,0:T(8,128)(2,1)S(1)} %slice.139.refs_0_), channel_id=1, source_target_pairs={{0,2},{1,3},{2,0},{3,1},{4,6},{5,7},{6,4},{7,5},{8,10},{9,11},{10,... | collective-permute-start | bytes 2752520 | tf_op jit(solution)/shard_map/ppermute | solution.py:41
  380.0 25.9 %collective-permute-start.46 = (bf16[256,1792]{1,0:T(8,128)(2,1)S(1)}, bf16[256,1792]{1,0:T(8,128)(2,1)}, u32[]{:S(2)}, u32[]{:S(2)}) collective-permute-start(bf16[256,1792]{1,0:T(8,128)(2,1)S(1)} %slice.139.refs_0_), channel_id=1, source_target_pairs={{0,1},{1,0},{2,3},{3,2},{4,5},{5,4},{6,7},{7,6},{8,9},{9,8},{10,11... | collective-permute-start | bytes 2752520 | tf_op jit(solution)/shard_map/ppermute | solution.py:41
  383.4 22.4 %collective-permute-start.48 = (bf16[768,384]{1,0:T(8,128)(2,1)}, bf16[768,384]{1,0:T(8,128)(2,1)}, u32[]{:S(2)}, u32[]{:S(2)}) collective-permute-start(bf16[768,384]{1,0:T(8,128)(2,1)} %dynamic-slice_convert_fusion.4), channel_id=1, source_target_pairs={{0,8},{1,9},{2,10},{3,11},{4,12},{5,13},{6,14},{7,15},{8,0},{9,1},... | collective-permute-start | bytes 1769480 | tf_op jit(solution)/shard_map/ppermute | solution.py:41
  386.3 17.4 %collective-permute-start.47 = (bf16[96,1536]{1,0:T(8,128)(2,1)}, bf16[96,1536]{1,0:T(8,128)(2,1)}, u32[]{:S(2)}, u32[]{:S(2)}) collective-permute-start(bf16[96,1536]{1,0:T(8,128)(2,1)} %dynamic-slice_convert_fusion.9), channel_id=1, source_target_pairs={{0,16},{1,17},{2,18},{3,19},{4,20},{5,21},{6,22},{7,23},{8,24},{9,... | collective-permute-start | bytes 884744 | tf_op jit(solution)/shard_map/ppermute | solution.py:41
  405.9 21.8 %collective-permute-start.50 = (bf16[256,1664]{1,0:T(8,128)(2,1)S(1)}, bf16[256,1664]{1,0:T(8,128)(2,1)}, u32[]{:S(2)}, u32[]{:S(2)}) collective-permute-start(bf16[256,1664]{1,0:T(8,128)(2,1)S(1)} %pad_maximum_fusion.3.refs_0_), channel_id=1, source_target_pairs={{0,1},{1,0},{2,3},{3,2},{4,5},{5,4},{6,7},{7,6},{8,9},{9,8},{10,11... | collective-permute-start | bytes 2555912 | tf_op jit(solution)/shard_map/ppermute | solution.py:41
  410.7 20.1 %collective-permute-start.52 = (bf16[96,1536]{1,0:T(8,128)(2,1)S(1)}, bf16[96,1536]{1,0:T(8,128)(2,1)S(1)}, u32[]{:S(2)}, u32[]{:S(2)}) collective-permute-start(bf16[96,1536]{1,0:T(8,128)(2,1)S(1)} %add_convert_fusion.1), channel_id=1, source_target_pairs={{0,16},{1,17},{2,18},{3,19},{4,20},{5,21},{6,22},{7,23},{8,24},{9,... | collective-permute-start | bytes 884744 | tf_op jit(solution)/shard_map/ppermute | solution.py:41
  413.6 29.9 %collective-permute-start.51 = (bf16[256,1664]{1,0:T(8,128)(2,1)S(1)}, bf16[256,1664]{1,0:T(8,128)(2,1)S(1)}, u32[]{:S(2)}, u32[]{:S(2)}) collective-permute-start(bf16[256,1664]{1,0:T(8,128)(2,1)S(1)} %pad_maximum_fusion.3.refs_0_), channel_id=1, source_target_pairs={{0,2},{1,3},{2,0},{3,1},{4,6},{5,7},{6,4},{7,5},{8,10},{9,11},{10,... | collective-permute-start | bytes 2555912 | tf_op jit(solution)/shard_map/ppermute | solution.py:41
  427.7 15.7 %collective-permute-start.54 = (bf16[384,384]{1,0:T(8,128)(2,1)S(1)}, bf16[384,384]{1,0:T(8,128)(2,1)S(1)}, u32[]{:S(2)}, u32[]{:S(2)}) collective-permute-start(bf16[384,384]{1,0:T(8,128)(2,1)S(1)} %dynamic-slice_convert_fusion.8), channel_id=1, source_target_pairs={{0,16},{1,17},{2,18},{3,19},{4,20},{5,21},{6,22},{7,23},{8,24},{9,... | collective-permute-start | bytes 884744 | tf_op jit(solution)/shard_map/ppermute | solution.py:41
  429.5 16.6 %collective-permute-start.53 = (bf16[896,384]{1,0:T(8,128)(2,1)S(1)}, bf16[896,384]{1,0:T(8,128)(2,1)S(1)}, u32[]{:S(2)}, u32[]{:S(2)}) collective-permute-start(bf16[896,384]{1,0:T(8,128)(2,1)S(1)} %dynamic-slice_convert_fusion.2), channel_id=1, source_target_pairs={{0,4},{1,5},{2,6},{3,7},{4,0},{5,1},{6,2},{7,3},{8,12},{9,13},{10,... | collective-permute-start | bytes 2064392 | tf_op jit(solution)/shard_map/ppermute | solution.py:41
  446.2 32.5 %collective-permute-start.57 = (bf16[192,1536]{1,0:T(8,128)(2,1)S(1)}, bf16[192,1536]{1,0:T(8,128)(2,1)S(1)}, u32[]{:S(2)}, u32[]{:S(2)}) collective-permute-start(bf16[192,1536]{1,0:T(8,128)(2,1)S(1)} %pad_maximum_fusion.6), channel_id=1, source_target_pairs={{0,8},{1,9},{2,10},{3,11},{4,12},{5,13},{6,14},{7,15},{8,0},{9,1},... | collective-permute-start | bytes 1769480 | tf_op jit(solution)/shard_map/ppermute | solution.py:41
  448.6 25.6 %collective-permute-start.55 = (bf16[256,1664]{1,0:T(8,128)(2,1)S(1)}, bf16[256,1664]{1,0:T(8,128)(2,1)S(1)}, u32[]{:S(2)}, u32[]{:S(2)}) collective-permute-start(bf16[256,1664]{1,0:T(8,128)(2,1)S(1)} %collective-permute-done.51.refs_2_), channel_id=1, source_target_pairs={{0,1},{1,0},{2,3},{3,2},{4,5},{5,4},{6,7},{7,6},{8,9},{9,8},{10,11... | collective-permute-start | bytes 2555912 | tf_op jit(solution)/shard_map/ppermute | solution.py:41
  448.6 20.1 %collective-permute-start.58 = (bf16[384,384]{1,0:T(8,128)(2,1)S(1)}, bf16[384,384]{1,0:T(8,128)(2,1)S(1)}, u32[]{:S(2)}, u32[]{:S(2)}) collective-permute-start(bf16[384,384]{1,0:T(8,128)(2,1)S(1)} %add_convert_fusion), channel_id=1, source_target_pairs={{0,16},{1,17},{2,18},{3,19},{4,20},{5,21},{6,22},{7,23},{8,24},{9,... | collective-permute-start | bytes 884744 | tf_op jit(solution)/shard_map/ppermute | solution.py:41
  449.3 24.8 %collective-permute-start.56 = (bf16[448,384]{1,0:T(8,128)(2,1)S(1)}, bf16[448,384]{1,0:T(8,128)(2,1)S(1)}, u32[]{:S(2)}, u32[]{:S(2)}) collective-permute-start(bf16[448,384]{1,0:T(8,128)(2,1)S(1)} %dynamic-slice_convert_fusion.6), channel_id=1, source_target_pairs={{0,8},{1,9},{2,10},{3,11},{4,12},{5,13},{6,14},{7,15},{8,0},{9,1},... | collective-permute-start | bytes 1032200 | tf_op jit(solution)/shard_map/ppermute | solution.py:41
  477.4 14.4 %collective-permute-start.59 = (bf16[832,384]{1,0:T(8,128)(2,1)S(1)}, bf16[832,384]{1,0:T(8,128)(2,1)S(1)}, u32[]{:S(2)}, u32[]{:S(2)}) collective-permute-start(bf16[832,384]{1,0:T(8,128)(2,1)S(1)} %dynamic-slice_convert_fusion.3), channel_id=1, source_target_pairs={{0,4},{1,5},{2,6},{3,7},{4,0},{5,1},{6,2},{7,3},{8,12},{9,13},{10,... | collective-permute-start | bytes 1916936 | tf_op jit(solution)/shard_map/ppermute | solution.py:41
  491.8 42.6 %collective-permute-start.63 = (bf16[384,1536]{1,0:T(8,128)(2,1)}, bf16[384,1536]{1,0:T(8,128)(2,1)}, u32[]{:S(2)}, u32[]{:S(2)}) collective-permute-start(bf16[384,1536]{1,0:T(8,128)(2,1)} %pad_maximum_fusion.1), channel_id=1, source_target_pairs={{0,4},{1,5},{2,6},{3,7},{4,0},{5,1},{6,2},{7,3},{8,12},{9,13},{10,... | collective-permute-start | bytes 3538952 | tf_op jit(solution)/shard_map/ppermute | solution.py:41
  493.2 18.9 %collective-permute-start.60 = (bf16[224,384]{1,0:T(8,128)(2,1)S(1)}, bf16[224,384]{1,0:T(8,128)(2,1)S(1)}, u32[]{:S(2)}, u32[]{:S(2)}) collective-permute-start(bf16[224,384]{1,0:T(8,128)(2,1)S(1)} %dynamic-slice_convert_fusion.10), channel_id=1, source_target_pairs={{0,16},{1,17},{2,18},{3,19},{4,20},{5,21},{6,22},{7,23},{8,24},{9,... | collective-permute-start | bytes 516104 | tf_op jit(solution)/shard_map/ppermute | solution.py:41
  494.4 17.7 %collective-permute-start.61 = (bf16[416,384]{1,0:T(8,128)(2,1)S(1)}, bf16[416,384]{1,0:T(8,128)(2,1)S(1)}, u32[]{:S(2)}, u32[]{:S(2)}) collective-permute-start(bf16[416,384]{1,0:T(8,128)(2,1)S(1)} %dynamic-slice_convert_fusion.7), channel_id=1, source_target_pairs={{0,8},{1,9},{2,10},{3,11},{4,12},{5,13},{6,14},{7,15},{8,0},{9,1},... | collective-permute-start | bytes 958472 | tf_op jit(solution)/shard_map/ppermute | solution.py:41
  495.7 19.7 %collective-permute-start.62 = (bf16[768,384]{1,0:T(8,128)(2,1)S(1)}, bf16[768,384]{1,0:T(8,128)(2,1)S(1)}, u32[]{:S(2)}, u32[]{:S(2)}) collective-permute-start(bf16[768,384]{1,0:T(8,128)(2,1)S(1)} %pad_maximum_fusion.7), channel_id=1, source_target_pairs={{0,8},{1,9},{2,10},{3,11},{4,12},{5,13},{6,14},{7,15},{8,0},{9,1},... | collective-permute-start | bytes 1769480 | tf_op jit(solution)/shard_map/ppermute | solution.py:41
  516.2 17.2 %collective-permute-start.65 = (bf16[208,384]{1,0:T(8,128)(2,1)}, bf16[208,384]{1,0:T(8,128)(2,1)}, u32[]{:S(2)}, u32[]{:S(2)}) collective-permute-start(bf16[208,384]{1,0:T(8,128)(2,1)} %dynamic-slice_convert_fusion.11), channel_id=1, source_target_pairs={{0,16},{1,17},{2,18},{3,19},{4,20},{5,21},{6,22},{7,23},{8,24},{9,... | collective-permute-start | bytes 479240 | tf_op jit(solution)/shard_map/ppermute | solution.py:41
  517.9 16.4 %collective-permute-start.64 = (bf16[224,384]{1,0:T(8,128)(2,1)S(1)}, bf16[224,384]{1,0:T(8,128)(2,1)S(1)}, u32[]{:S(2)}, u32[]{:S(2)}) collective-permute-start(bf16[224,384]{1,0:T(8,128)(2,1)S(1)} %add_convert_fusion.2), channel_id=1, source_target_pairs={{0,16},{1,17},{2,18},{3,19},{4,20},{5,21},{6,22},{7,23},{8,24},{9,... | collective-permute-start | bytes 516104 | tf_op jit(solution)/shard_map/ppermute | solution.py:41
  520.4 28.4 %collective-permute-start.68 = (bf16[1536,384]{1,0:T(8,128)(2,1)}, bf16[1536,384]{1,0:T(8,128)(2,1)}, u32[]{:S(2)}, u32[]{:S(2)}) collective-permute-start(bf16[1536,384]{1,0:T(8,128)(2,1)} %pad_maximum_fusion.2), channel_id=1, source_target_pairs={{0,4},{1,5},{2,6},{3,7},{4,0},{5,1},{6,2},{7,3},{8,12},{9,13},{10,... | collective-permute-start | bytes 3538952 | tf_op jit(solution)/shard_map/ppermute | solution.py:41
  536.3 11.4 %collective-permute-start.69 = (bf16[448,384]{1,0:T(8,128)(2,1)S(1)}, bf16[448,384]{1,0:T(8,128)(2,1)S(1)}, u32[]{:S(2)}, u32[]{:S(2)}) collective-permute-start(bf16[448,384]{1,0:T(8,128)(2,1)S(1)} %pad_maximum_fusion.8), channel_id=1, source_target_pairs={{0,8},{1,9},{2,10},{3,11},{4,12},{5,13},{6,14},{7,15},{8,0},{9,1},... | collective-permute-start | bytes 1032200 | tf_op jit(solution)/shard_map/ppermute | solution.py:41
  548.7 12.0 %collective-permute-start.73 = (bf16[416,384]{1,0:T(8,128)(2,1)S(1)}, bf16[416,384]{1,0:T(8,128)(2,1)S(1)}, u32[]{:S(2)}, u32[]{:S(2)}) collective-permute-start(bf16[416,384]{1,0:T(8,128)(2,1)S(1)} %pad_maximum_fusion.9), channel_id=1, source_target_pairs={{0,8},{1,9},{2,10},{3,11},{4,12},{5,13},{6,14},{7,15},{8,0},{9,1},... | collective-permute-start | bytes 958472 | tf_op jit(solution)/shard_map/ppermute | solution.py:41
  550.2 20.6 %collective-permute-start.75 = (bf16[896,384]{1,0:T(8,128)(2,1)}, bf16[896,384]{1,0:T(8,128)(2,1)}, u32[]{:S(2)}, u32[]{:S(2)}) collective-permute-start(bf16[896,384]{1,0:T(8,128)(2,1)} %pad_maximum_fusion.5), channel_id=1, source_target_pairs={{0,4},{1,5},{2,6},{3,7},{4,0},{5,1},{6,2},{7,3},{8,12},{9,13},{10,... | collective-permute-start | bytes 2064392 | tf_op jit(solution)/shard_map/ppermute | solution.py:41
  561.8 19.8 %collective-permute-start.76 = (bf16[832,384]{1,0:T(8,128)(2,1)S(1)}, bf16[832,384]{1,0:T(8,128)(2,1)S(1)}, u32[]{:S(2)}, u32[]{:S(2)}) collective-permute-start(bf16[832,384]{1,0:T(8,128)(2,1)S(1)} %pad_maximum_fusion.4), channel_id=1, source_target_pairs={{0,4},{1,5},{2,6},{3,7},{4,0},{5,1},{6,2},{7,3},{8,12},{9,13},{10,... | collective-permute-start | bytes 1916936 | tf_op jit(solution)/shard_map/ppermute | solution.py:41
  (154 other events, 1328.0 us)

commit v3 on v2

--- a/solution.py
+++ b/solution.py
@@ -16,10 +16,13 @@
 PROJ = 6448
 PLANES = 2
 CORES = 2
+FIRST = 1792
 
 f32 = jnp.float32
 bf16 = jnp.bfloat16
 epsilon = 1e-05
+scoped = 40 * 2**20
+whole_vmem = 60 * 2**20
 no_cost = pl.CostEstimate(flops=0, bytes_accessed=0, transcendentals=0)
 
 
@@ -92,45 +95,45 @@
     return distances
 
 
-def halve(ring, distance, block):
-    bit, send = swapped(ring, distance)
-    half = block.shape[0] // 2
-    arrived = send(rows_of(block, 1 - bit, half).astype(bf16))
-    return rows_of(block, bit, half) + arrived.astype(f32)
-
-
-def double(ring, distance, block):
-    bit, send = swapped(ring, distance)
-    other = send(block)
-    low = jnp.where(bit == 0, block, other)
-    high = jnp.where(bit == 0, other, block)
-    return jnp.concatenate([low, high], axis=0)
-
-
 class Total:
     def __init__(self, ring, grad):
-        self.ring, self.value = ring, grad
-        self.steps = [(halve, d) for d in cube(ring)] + [(double, d) for d in reversed(cube(ring))]
+        self.ring, self.value, self.other, self.merge = ring, grad, None, None
+        self.steps = [(True, d) for d in cube(ring)] + [(False, d) for d in reversed(cube(ring))]
+
+    def settle(self):
+        if self.merge is not None:
+            value, other = self.ring.clock.now((self.value, self.other))
+            self.value, self.merge = self.merge(value, other), None
+        else:
+            self.value = self.ring.clock.now(self.value)
 
     def step(self):
-        if self.steps:
-            kind, distance = self.steps.pop(0)
-            if kind is double and self.value.dtype != bf16:
-                self.value = self.value.astype(bf16)
-            self.value = kind(self.ring, distance, self.ring.clock.now(self.value))
+        if not self.steps:
+            return
+        self.settle()
+        halves, distance = self.steps.pop(0)
+        bit, send = swapped(self.ring, distance)
+        if halves:
+            half = self.value.shape[0] // 2
+            self.other = send(rows_of(self.value, 1 - bit, half).astype(bf16))
+            self.merge = lambda value, other: rows_of(value, bit, half) + other.astype(f32)
+        else:
+            self.value = self.value.astype(bf16)
+            self.other = send(self.value)
+            self.merge = lambda value, other: jnp.concatenate(
+                [jnp.where(bit == 0, value, other), jnp.where(bit == 0, other, value)], axis=0
+            )
 
     def finish(self):
         while self.steps:
             self.step()
+        self.settle()
         return self.value.astype(f32)
 
     def halves(self):
-        while len(self.steps) > 1:
+        while self.steps:
             self.step()
-        if self.steps:
-            self.steps = []
-            self.value = (self.value, self.ring.plane(self.ring.clock.now(self.value)))
-        return self.value
+        return self.value, self.other
 
 
 class Clock:
@@ -174,9 +177,6 @@
         if not self.whole_only:
             sides += ([self.ring.core(piece) for piece in pieces],)
         self.arrived.append(sides)
-
-    def near(self):
-        self.beside_it = self.ring.core(self.ring.clock.now(self.block))
 
     def first(self, at_once=False):
         ring = self.ring
@@ -207,8 +207,8 @@
         self.put([now(part) for part in self.corner[0]])
         self.put([now(part) for part in self.corner[1]])
 
-    def whole(self):
-        found = {(0, 0): self.block, (0, 1): self.beside_it}
+    def whole(self, near):
+        found = {(0, 0): self.block, (0, 1): near}
         index = jnp.stack([self.place ^ k for k in range(4)]).astype(jnp.int32)
         for d in range(1, self.ring.row):
             sides = [[side[d - 1] for side in pieces] for pieces in zip(*self.arrived)]
@@ -242,7 +242,7 @@
         out_shape=jax.ShapeDtypeStruct((rows, width), f32),
         name="weight_grad",
         cost_estimate=no_cost,
-        compiler_params=pltpu.CompilerParams(vmem_limit_bytes=40 * 2**20),
+        compiler_params=pltpu.CompilerParams(vmem_limit_bytes=scoped),
     )(*[rows_all[key] for key in keys], *[columns_all[key] for key in keys])
 
 
@@ -280,45 +280,52 @@
         out_shape=jax.ShapeDtypeStruct((tokens, rows * len(weights)), f32),
         name="to_inner",
         cost_estimate=no_cost,
-        compiler_params=pltpu.CompilerParams(vmem_limit_bytes=40 * 2**20),
+        compiler_params=pltpu.CompilerParams(vmem_limit_bytes=scoped),
     )(places, grad, *weights)
 
 
-def to_model_body(layout, gate_ref, tail_ref, *refs):
+def to_model_body(terms, gate_ref, tail_ref, *refs):
     out_ref = refs[-1]
-    at = 0
-    for k, (blocks, rows) in enumerate(layout):
-        total = jnp.dot(tail_ref[...], refs[at][...], preferred_element_type=f32)
-        at += 1
-        for piece, block in enumerate(blocks):
-            columns = gate_ref[:, piece * rows : (piece + 1) * rows]
-            weight = refs[at][block * rows : (block + 1) * rows]
-            at += 1
-            total = total + jnp.dot(columns, weight, preferred_element_type=f32)
+    for k, shard in enumerate(terms):
+        total = None
+        for tail, column, array, row, count in shard:
+            left = (tail_ref if tail else gate_ref)[:, column : column + count]
+            term = jnp.dot(left, refs[array][row : row + count], preferred_element_type=f32)
+            total = term if total is None else total + term
         out_ref[k] = total
 
 
 def to_model(grad_gate, grad_tail, gate_weights, tail_weights):
+    width = grad_tail.shape[1]
     rows = grad_gate.shape[1] // len(gate_weights[0])
-    flat, layout = [], []
-    for pieces, tail in zip(gate_weights, tail_weights):
-        if all(array is pieces[0][0] for array, _ in pieces):
-            layout.append(([0], grad_gate.shape[1]))
-            flat += [tail, pieces[0][0]]
+    flat, terms = [], []
+
+    def place(array):
+        for k, held in enumerate(flat):
+            if held is array:
+                return k
+        flat.append(array)
+        return len(flat) - 1
+
+    for pieces, (tail, start) in zip(gate_weights, tail_weights):
+        shard = [(True, 0, place(tail), start, width)]
+        if pieces[0][0] is tail:
+            shard.append((False, 0, place(tail), 0, grad_gate.shape[1]))
         else:
-            layout.append(([block for _, block in pieces], rows))
-            flat += [tail] + [array for array, _ in pieces]
+            shard += [
+                (False, at * rows, place(array), block * rows, rows)
+                for at, (array, block) in enumerate(pieces)
+            ]
+        terms.append(shard)
     inside = pl.BlockSpec(memory_space=pltpu.VMEM)
     return pl.pallas_call(
-        functools.partial(to_model_body, layout),
+        functools.partial(to_model_body, terms),
         in_specs=[inside] * (2 + len(flat)),
         out_specs=inside,
-        out_shape=jax.ShapeDtypeStruct(
-            (len(layout), grad_gate.shape[0], tail_weights[0].shape[1]), f32
-        ),
+        out_shape=jax.ShapeDtypeStruct((len(terms), grad_gate.shape[0], flat[0].shape[1]), f32),
         name="to_model",
         cost_estimate=no_cost,
-        compiler_params=pltpu.CompilerParams(vmem_limit_bytes=48 * 2**20),
+        compiler_params=pltpu.CompilerParams(vmem_limit_bytes=scoped),
     )(grad_gate, grad_tail, *flat)
 
 
@@ -339,7 +346,7 @@
         out_shape=jax.ShapeDtypeStruct(tokens.shape, bf16),
         name="output_rows",
         cost_estimate=no_cost,
-        compiler_params=pltpu.CompilerParams(vmem_limit_bytes=48 * 2**20),
+        compiler_params=pltpu.CompilerParams(vmem_limit_bytes=scoped),
     )(tokens, *columns, *weights)
 
 
@@ -368,7 +375,7 @@
         out_shape=[jax.ShapeDtypeStruct(block.shape, block.dtype)] * len(sides),
         name="laid",
         cost_estimate=no_cost,
-        compiler_params=pltpu.CompilerParams(vmem_limit_bytes=40 * 2**20),
+        compiler_params=pltpu.CompilerParams(vmem_limit_bytes=scoped),
     )(index, *flat)
 
 
@@ -383,26 +390,20 @@
     out_ref[...] = total.astype(out_ref.dtype)
 
 
-def project(columns, weights, tile, width=None):
+def project(columns, weights, tile, width):
     count = len(columns)
     tokens, depth = columns[0].shape
-    at = [0] * count
-    if width is not None:
-        at = [block for _, block in weights]
-        weights = [array for array, _ in weights]
-    else:
-        width = weights[0].shape[0]
     return pl.pallas_call(
         functools.partial(project_body, count),
         grid=(pl.cdiv(width, tile),),
         in_specs=[pl.BlockSpec((tokens, depth), lambda i: (0, 0))] * count
-        + [pl.BlockSpec((tile, depth), lambda i, k=k: (i + k, 0)) for k in at],
+        + [pl.BlockSpec((tile, depth), lambda i, k=k: (i + k, 0)) for _, k in weights],
         out_specs=pl.BlockSpec((tokens, tile), lambda i: (0, i)),
         out_shape=jax.ShapeDtypeStruct((tokens, width), bf16),
         name="project",
         cost_estimate=no_cost,
-        compiler_params=pltpu.CompilerParams(vmem_limit_bytes=40 * 2**20),
-    )(*columns, *weights)
+        compiler_params=pltpu.CompilerParams(vmem_limit_bytes=scoped),
+    )(*columns, *[array for array, _ in weights])
 
 
 class Pieces:
@@ -425,11 +426,11 @@
         far = [self.ring.clock.now(piece) for piece in self.parts[at]]
         self.parts[at] = [(piece, self.ring.core(piece)) for piece in far]
 
-    def pieces(self):
+    def pieces(self, own, near):
         count = len(self.parts)
         found = {
-            (0, 0): [(self.block, at) for at in range(count)],
-            (0, 1): [(self.beside, at) for at in range(count)],
+            (0, 0): [(own, at) for at in range(count)],
+            (0, 1): [(near, at) for at in range(count)],
         }
         for d in range(1, self.ring.row):
             for e in range(CORES):
@@ -534,6 +535,7 @@
         out_shape=jax.ShapeDtypeStruct((ring.seq, part, STATE), bf16),
         name="carried",
         cost_estimate=no_cost,
+        compiler_params=pltpu.CompilerParams(vmem_limit_bytes=scoped),
     )(blocks, factor)
 
 
@@ -587,6 +589,7 @@
         + [jax.ShapeDtypeStruct((1, STATE), f32)],
         name="steps",
         cost_estimate=no_cost,
+        compiler_params=pltpu.CompilerParams(vmem_limit_bytes=scoped),
     )(projected, pad(bias), pad(rate))
 
 
@@ -636,6 +639,7 @@
         ],
         name="steps_back",
         cost_estimate=no_cost,
+        compiler_params=pltpu.CompilerParams(vmem_limit_bytes=scoped),
     )(
         projected, bias[:, None], rate[:, None], step_rows, cum_rows, grad_step, grad_cum, factor,
         crossed,
@@ -709,7 +713,7 @@
         ],
         name="enter",
         cost_estimate=no_cost,
-        compiler_params=pltpu.CompilerParams(vmem_limit_bytes=40 * 2**20),
+        compiler_params=pltpu.CompilerParams(vmem_limit_bytes=scoped),
     )(projected, edge, taps, shift[None], weigh, factor)
 
 
@@ -831,7 +835,7 @@
         scratch_shapes=[pltpu.VMEM((tokens, tokens), f32)],
         name="inside",
         cost_estimate=no_cost,
-        compiler_params=pltpu.CompilerParams(vmem_limit_bytes=40 * 2**20),
+        compiler_params=pltpu.CompilerParams(vmem_limit_bytes=scoped),
     )(conv_low, conv_low, conv_low, cum_pairs, cum_rows, step_rows, skip_row)
 
 
@@ -856,34 +860,44 @@
     reached = wide * dot_last(c_ref[...], incoming)
     c_out[...] += jnp.dot(reach_ref[...], incoming, preferred_element_type=f32)
     skip_out[...] = jnp.sum(wide * x.astype(f32), axis=0, keepdims=True)
-    same = later_or_same(tokens)
     first = lax.broadcasted_iota(jnp.int32, x.shape, 1) < HEADDIM
-    parts, total, sums = [], 0.0, []
     wide_cum = group_columns(cum_ref, j, 2)
+    middle = tokens // 2
+    same = later_or_same(middle)
+    parts, sums = [], []
+    totals = [0.0, 0.0, 0.0]
     for head in range(2):
-        cum = wide_cum[:, head : head + 1]
         row = pl.ds(2 * j + head, 1)
-        step = step_rows_ref[row, :]
-        decay = jnp.exp(jnp.where(same, cum - cum_rows_ref[row, :], 0.0))
-        both = scores[...] * decay
+        steps_row, cum_row = step_rows_ref[row, :], cum_rows_ref[row, :]
         own = jnp.where(first == (head == 0), y, jnp.zeros_like(y))
-        grad_mix = dot_last(own, x)
-        total = total + grad_mix * decay * step
-        by_source = grad_mix * both
-        step_out[row, :] = jnp.sum(by_source, axis=0, keepdims=True)
-        mine = reached[:, head * HEADDIM : (head + 1) * HEADDIM]
-        sums.append(
-            jnp.sum(by_source * step, axis=1, keepdims=True)
-            + jnp.exp(cum) * jnp.sum(mine, axis=1, keepdims=True)
-        )
-        parts.append(dot_first((both * step).astype(bf16), y))
+        mine = jnp.sum(
+            reached[:, head * HEADDIM : (head + 1) * HEADDIM], axis=1, keepdims=True
+        ) * jnp.exp(wide_cum[:, head : head + 1])
+        by_row, by_column, given = [0.0, 0.0], [0.0, 0.0], [0.0, 0.0]
+        for k, (late, early) in enumerate(((0, 0), (1, 0), (1, 1))):
+            rows = slice(late * middle, (late + 1) * middle)
+            columns = slice(early * middle, (early + 1) * middle)
+            step = steps_row[:, columns]
+            exponent = wide_cum[rows, head : head + 1] - cum_row[:, columns]
+            decay = jnp.exp(jnp.where(same, exponent, 0.0) if late == early else exponent)
+            both = scores[rows, columns] * decay
+            grad_mix = dot_last(own[rows], x[columns])
+            totals[k] = totals[k] + grad_mix * (decay * step)
+            by_source = grad_mix * both
+            by_column[early] = by_column[early] + jnp.sum(by_source, axis=0, keepdims=True)
+            by_row[late] = by_row[late] + jnp.sum(by_source * step, axis=1, keepdims=True)
+            given[early] = given[early] + dot_first((both * step).astype(bf16), y[rows])
+        step_out[row, :] = jnp.concatenate(by_column, axis=1)
+        sums.append(jnp.concatenate(by_row, axis=0) + mine)
+        parts.append(jnp.concatenate(given, axis=0))
+    for total, (late, early) in zip(totals, ((0, 0), (1, 0), (1, 1))):
+        grad_scores[late * middle : (late + 1) * middle, early * middle : (early + 1) * middle] += total
     keep_columns(wide_sums, 2 * j, sums)
-    grad_scores[...] += total
     x_out[...] = jnp.where(first, parts[0], parts[1]) + skip_ref[...] * wide
 
     @pl.when(j == pl.num_programs(0) - 1)
     def _():
-        grad = jnp.where(same, grad_scores[...], 0.0).astype(bf16)
+        grad = jnp.where(later_or_same(tokens), grad_scores[...], 0.0).astype(bf16)
         c_out[...] += jnp.dot(grad, b_ref[...], preferred_element_type=f32)
         b_out[...] = dot_first(grad, c_ref[...])
         cum_out[...] = wide_sums[...].T[:HEADS] - step_out[...] * step_rows_ref[...]
@@ -915,7 +929,7 @@
         ],
         name="inside_back",
         cost_estimate=no_cost,
-        compiler_params=pltpu.CompilerParams(vmem_limit_bytes=40 * 2**20),
+        compiler_params=pltpu.CompilerParams(vmem_limit_bytes=scoped),
     )(
         grad_y, grad_reach, conv_low, conv_low, conv_low, incoming, cum_pairs, cum_rows, step_rows,
         skip_row,
@@ -962,7 +976,7 @@
         ],
         name="turn",
         cost_estimate=no_cost,
-        compiler_params=pltpu.CompilerParams(vmem_limit_bytes=40 * 2**20),
+        compiler_params=pltpu.CompilerParams(vmem_limit_bytes=whole_vmem),
     )(base, incoming, proj_c, decay, grad_mixed, gain[None], *gate_parts)
 
 
@@ -973,7 +987,7 @@
 def leave_body(
     steps, proj_ref, edge_ref, taps_ref, shift_ref, low_ref, part_ref, fresh_ref, incoming_ref, b_ref,
     weigh_ref, b_part_ref, c_part_ref,
-    grad_ref, first_ref, last_ref, taps_grad_ref, shift_grad_ref, factor_ref, crossed_ref,
+    grad_ref, grad_more_ref, first_ref, last_ref, taps_grad_ref, shift_grad_ref, factor_ref, crossed_ref,
     b_total, wide_factor,
 ):
     j = pl.program_id(0)
@@ -1003,7 +1017,16 @@
             tap = taps[k : k + 1]
             inner = inner + tap * ahead(after_it, grad.shape[0], CONV - 1 - k)
             outer = outer + tap * ahead(before_it, 8, CONV - 1 - k)
-        grad_ref[...] = inner.astype(bf16)
+        cut = FIRST // grad.shape[1]
+
+        @pl.when(j < cut)
+        def _():
+            grad_ref[...] = inner.astype(bf16)
+
+        @pl.when(j >= cut)
+        def _():
+            grad_more_ref[...] = inner.astype(bf16)
+
         last_ref[...] = inner[grad.shape[0] - 8 :]
         first_ref[...] = outer
 
@@ -1049,6 +1072,7 @@
     tokens, heads = part.shape[0], 4
     width = heads * HEADDIM
     steps = INNER // width
+    cut = FIRST // width
     inside = lambda j: jnp.minimum(j, steps - 1)
     block = lambda rows: pl.BlockSpec((rows, width), lambda j: (0, j))
     whole = lambda rows: pl.BlockSpec((rows, STATE), lambda j: (0, 0))
@@ -1071,7 +1095,8 @@
             whole(tokens),
         ],
         out_specs=[
-            block(tokens),
+            pl.BlockSpec((tokens, width), lambda j: (0, jnp.minimum(j, cut - 1))),
+            pl.BlockSpec((tokens, width), lambda j: (0, jnp.maximum(j - cut, 0))),
             block(8),
             block(8),
             block(CONV),
@@ -1080,7 +1105,8 @@
             whole(HEADS),
         ],
         out_shape=[
-            jax.ShapeDtypeStruct((tokens, CHANNELS), bf16),
+            jax.ShapeDtypeStruct((tokens, FIRST), bf16),
+            jax.ShapeDtypeStruct((tokens, CHANNELS - FIRST), bf16),
             jax.ShapeDtypeStruct((8, CHANNELS), f32),
             jax.ShapeDtypeStruct((8, CHANNELS), f32),
             jax.ShapeDtypeStruct((CONV, CHANNELS), f32),
@@ -1091,7 +1117,7 @@
         scratch_shapes=[pltpu.VMEM((tokens, STATE), f32), pltpu.VMEM((tokens, STATE), f32)],
         name="leave",
         cost_estimate=no_cost,
-        compiler_params=pltpu.CompilerParams(vmem_limit_bytes=40 * 2**20),
+        compiler_params=pltpu.CompilerParams(vmem_limit_bytes=whole_vmem),
     )(
         projected, edge, taps, shift[None], conv_low, part, grad_fresh, incoming, conv_low,
         weigh, b_part, c_part,
@@ -1133,7 +1159,7 @@
     in_rows = in_weight.T
     shared = Spread(ring, in_rows, INNER)
     shared.first(at_once=True)
-    shared.near()
+    near_rows = ring.core(in_rows)
     packed = pack(small)
     spread = jnp.zeros((ring.fsdp,) + packed.shape, bf16)
     for (d, e), place in where.items():
@@ -1155,16 +1181,20 @@
     out_spread = Spread(ring, out_weight, 0, whole_only=True)
     (spread,) = clock.tick(spread)
     shared.second()
+    near_out = ring.core(clock.now(out_weight))
     out_spread.first()
     clock.tick()
     shared.third()
     gate_pieces.send(later=1)
     clock.tick()
     shared.fourth()
-    gate_pieces.send(later=1)
+    gate_pieces.send(later=3)
     out_spread.second()
     clock.tick()
-    weight_conv = shared.whole()
+    tile = 768
+    weight_conv = {key: (array, 0) for key, array in shared.whole(near_rows).items()}
+    weight_conv[0, 0] = (in_rows, INNER // tile)
+    weight_conv[0, 1] = (near_rows, INNER // tile)
 
     position = lax.axis_index("seq") * row_count + lax.broadcasted_iota(
         jnp.int32, (row_count, 1), 0
@@ -1179,12 +1209,12 @@
         lax.dynamic_slice_in_dim(normed, place * depth, depth, axis=1) for place in where.values()
     ]
     normed_for = columns_for(ring, normed)
-    projected = project(normed_columns, list(weight_conv.values()), 896)
+    projected = project(normed_columns, list(weight_conv.values()), tile, PROJ - INNER)
     (projected,) = clock.tick(projected)
-    gate_pieces.send(later=1)
-    out_spread.third()
     edge_rows = ring.next_block(projected[row_count - 8 :, :CHANNELS], 1)
     cum, weigh, decay, cum_rows, step_rows, through = steps(projected, step_bias, rate_log)
+    cum, weigh, edge_rows = clock.tick(cum, weigh, edge_rows)
+    gate_pieces.send(later=1)
     conv_low, fresh_state = enter(
         ring,
         projected,
@@ -1198,11 +1228,9 @@
     proj_c = conv_low[:, INNER + STATE :]
     (fresh_state,) = clock.tick(fresh_state)
     blocks = lax.all_to_all(fresh_state, "seq", 0, 0, tiled=True)
+    out_spread.third()
     gate_pieces.pass_on(0)
     gate_pieces.pass_on(1)
-    out_spread.fourth()
-    gate_pieces.near()
-    out_spread.near()
     skip_row = jnp.repeat(skip_gain, HEADDIM)[None]
     base = inside(conv_low, cum, cum_rows, step_rows, skip_row)
     blocks, base = clock.tick(blocks, base)
@@ -1210,8 +1238,9 @@
     (states,) = clock.tick(carried(ring, blocks, factor, False))
     incoming = returned(ring, states).reshape(INNER, STATE)
     gate_pieces.pass_on(2)
-    weight_gate = gate_pieces.pieces()
-    weight_out = out_spread.whole()
+    out_spread.fourth()
+    weight_gate = gate_pieces.pieces(in_rows, near_rows)
+    weight_out = out_spread.whole(near_out)
     grad_pieces = Pieces(ring, grad_out)
     grad_pieces.send()
     gate_rows = gate_pieces.rows
@@ -1233,26 +1262,34 @@
     )
     blocks = lax.all_to_all(direct.reshape(ring.seq, -1, STATE), "seq", 0, 0, tiled=True)
     mixed_all = trade_columns(ring, columns_for(ring, mixed))
+    clock.defer(len(mixed_all) - 1, 2)
     grad_out_all = grad_pieces.whole()
     x_part, b_part, c_part, grad_step, grad_cum, grad_skip = inside_back(
         grad_y, grad_reach, conv_low, incoming, cum, cum_rows, step_rows, skip_row
     )
     gate_grads = Pieces(ring, grad_gate)
-    gate_grads.send()
-    gate_grads.near()
+    gate_grads.send(later=2)
+    blocks, x_part, b_part, c_part = clock.tick(blocks, x_part, b_part, c_part)
+    states = carried(ring, blocks, factor, True)
+    (states,) = clock.tick(states)
+    chain_grad = returned(ring, states)
+    mixed_all = {key: clock.now(block) for key, block in mixed_all.items()}
     total_w_out = Total(ring, weight_grad(mixed_all, grad_out_all, 384))
-    blocks, x_part, total_w_out.value = clock.tick(blocks, x_part, total_w_out.value)
-    (states,) = clock.tick(carried(ring, blocks, factor, True))
-    chain_grad = returned(ring, states)
     total_w_out.step()
     clock.defer()
+    gate_grads.near()
     total_w_gate = Total(ring, weight_grad(gate_grads.whole(), normed_all, 768))
     (total_w_gate.value,) = clock.tick(total_w_gate.value)
     total_w_gate.step()
-    clock.defer(1, 2)
-    chain_grad, b_part, c_part = clock.tick(chain_grad, b_part, c_part)
+    clock.defer()
+    mixed = clock.now(mixed)
+    mixed_columns = [
+        lax.dynamic_slice_in_dim(mixed, place * wide, wide, axis=1) for place in where.values()
+    ]
+    output = output_rows(hidden[0], mixed_columns, list(weight_out.values()))
+    chain_grad, output = clock.tick(chain_grad, output)
     total_w_out.step()
-    grad_conv, first_rows, last_rows, grad_taps, grad_shift, grad_factor, crossed = leave(
+    grad_conv, grad_more, first_rows, last_rows, grad_taps, grad_shift, grad_factor, crossed = leave(
         projected,
         edge_rows,
         conv_taps,
@@ -1265,12 +1302,19 @@
         b_part,
         c_part,
     )
-    grad_conv, last_rows, first_rows = clock.tick(grad_conv, last_rows, first_rows)
-    back_rows = ring.next_block(first_rows, -1)
+    grad_conv, grad_more, last_rows, first_rows = clock.tick(
+        grad_conv, grad_more, last_rows, first_rows
+    )
+    total_w_out.step()
+    clock.defer()
+    last_rows = (last_rows + ring.next_block(first_rows, -1)).astype(bf16)
     grad_conv = lax.dynamic_update_slice_in_dim(
-        grad_conv, (last_rows + back_rows).astype(bf16), row_count - 8, axis=0
+        grad_conv, last_rows[:, :FIRST], row_count - 8, axis=0
     )
     (grad_conv,) = clock.tick(grad_conv)
+    grad_more = lax.dynamic_update_slice_in_dim(
+        grad_more, last_rows[:, FIRST:], row_count - 8, axis=0
+    )
     grad_dt_raw, grad_step_bias, grad_rate = steps_back(
         projected,
         step_bias,
@@ -1282,45 +1326,33 @@
         clock.now(grad_factor),
         crossed,
     )
-    grad_tail = jnp.concatenate([grad_conv, grad_dt_raw[:, :HEADS]], axis=1)
-
-    cut = 1792
-    first = Pieces(ring, grad_conv[:, :cut])
-    last = Pieces(ring, jnp.concatenate([grad_conv[:, cut:], grad_dt_raw], axis=1))
+    grad_tail = jnp.concatenate([grad_conv, grad_more, grad_dt_raw[:, :HEADS]], axis=1)
+
+    first = Pieces(ring, grad_conv)
+    last = Pieces(ring, jnp.concatenate([grad_more, grad_dt_raw], axis=1))
     first.send()
     first.near()
-    total_w_out.step()
     total_w_gate.step()
     clock.tick()
     last.send(later=1)
     last.near()
-    total_w_out.step()
-    clock.defer()
     total_first = Total(ring, weight_grad(first.whole(), normed_all, 896))
     (total_first.value,) = clock.tick(total_first.value)
     total_first.step()
+    total_w_out.step()
     total_w_gate.step()
-    clock.tick()
+    grad_shards = to_model(
+        grad_gate, clock.now(grad_tail), list(weight_gate.values()), [
+            (array, block * tile) for array, block in weight_conv.values()
+        ]
+    )
+    (grad_shards,) = clock.tick(grad_shards)
+    total_last = Total(ring, weight_grad(last.whole(), normed_all, 1664))
+    (total_last.value,) = clock.tick(total_last.value)
+    total_last.step()
     total_first.step()
     total_w_out.step()
     total_w_gate.step()
-    clock.defer(3)
-    total_last = Total(ring, weight_grad(last.whole(), normed_all, 1664))
-    (total_last.value,) = clock.tick(total_last.value)
-    total_last.step()
-    (grad_gate, grad_tail, mixed) = clock.tick(grad_gate, grad_tail, mixed)
-    total_w_out.step()
-    clock.defer()
-    total_first.step()
-    total_last.step()
-    total_w_gate.step()
-    grad_shards = to_model(
-        grad_gate, grad_tail, list(weight_gate.values()), list(weight_conv.values())
-    )
-    mixed_columns = [
-        lax.dynamic_slice_in_dim(mixed, place * wide, wide, axis=1) for place in where.values()
-    ]
-    (grad_shards,) = clock.tick(grad_shards)
     grad_normed = jnp.zeros((row_count, model_width), f32)
     for k, place in enumerate(where.values()):
         grad_normed = lax.dynamic_update_slice_in_dim(
@@ -1329,19 +1361,25 @@
     grad_skip = jnp.sum(clock.now(grad_skip).reshape(HEADS, HEADDIM), axis=1)
     grad_tokens, grad_g_norm = pull_norm(grad_normed)
     hidden_grad = (grad_tokens + grad_out.astype(f32)).astype(bf16)
-
+    hidden_grad, grad_g_norm = clock.tick(hidden_grad, grad_g_norm)
+    grad_shift, grad_step_bias, grad_rate, grad_g_gate = (
+        clock.now(part) for part in (grad_shift, grad_step_bias, grad_rate, grad_g_gate)
+    )
     parts = [grad_g_norm, grad_taps, grad_shift[0], grad_step_bias[:, 0], grad_rate[:, 0]]
     parts += [grad_skip, grad_g_gate[0]]
-    output = output_rows(
-        clock.now(hidden[0]), mixed_columns, list(weight_out.values())
-    )
+    small_total = SmallSum(ring, pack(parts))
+    total_w_out.step()
+    clock.defer()
     total_first.step()
     total_last.step()
+    total_w_gate.step()
+    clock.tick()
+    small_total.step()
     total_w_gate.halves()
     clock.defer()
-    (output,) = clock.tick(output)
-    small_total = SmallSum(ring, pack(parts))
-    small_total.step()
+    total_first.step()
+    total_last.step()
+    clock.tick()
     small_total.step()
     total_first.step()
     total_last.step()
@@ -1365,8 +1403,10 @@
         )
     total_w_in = jnp.zeros((PROJ, depth), f32)
     total_w_in = place_rows(total_w_in, total_w_gate.halves(), 0, INNER)
-    total_w_in = place_rows(total_w_in, total_first.halves(), INNER, cut)
-    total_w_in = place_rows(total_w_in, total_last.halves(), INNER + cut, PROJ - INNER - cut)
+    total_w_in = place_rows(total_w_in, total_first.halves(), INNER, FIRST)
+    total_w_in = place_rows(
+        total_w_in, total_last.halves(), INNER + FIRST, PROJ - INNER - FIRST
+    )
     total_w_in = total_w_in.T
     total_w_out = total_w_out.finish()
     return (

time: 594 us -> 552 us (0.929)
  local copies, waits for them, and re-layouts: 99.1 us -> 81.3 us
  Pallas kernels: 160 us -> 144 us
  waiting for transfers between devices: 178 us -> 172 us
    unnamed x276 -> x248, local copies, waits for them, and re-layouts: 53.5 us -> 40.7 us
    ppermute x77 -> x76, waiting for transfers between devices: 178 us -> 168 us  [send(): arrived = lax.ppermute(block, ('seq', 'fsdp'), route)]
    pallas_call x4, Pallas kernels: 25.7 us -> 17.7 us  [weight_grad(): pl.pallas_call(functools.partial(sum_body, len(keys)), grid=(rows // tile...]
    slice x4 -> x0, local copies, waits for them, and re-layouts: 7.67 us -> none  [the longest x1 3.47 us: local(): gate_pieces = Pieces(ring, in_rows[:INNER], 3)]
    ppermute x77 -> x76, starting transfers between devices: 73.9 us -> 69.3 us  [send(): arrived = lax.ppermute(block, ('seq', 'fsdp'), route)]
  transfers between devices with their start and end apart: 81 -> 80, of which waited for: 22 -> 32; matrix products, arithmetic and copies ran while one was open for 14% -> 15% of each run, Pallas kernels for 27% -> 25%
where the time goes in v3:
time: 552 us; the launch traced here: 541 us
  waiting for transfers between devices  172 us (31%)
  Pallas kernels  144 us (26%)
  starting transfers between devices  91.4 us (17%)
  local copies, waits for them, and re-layouts  81.3 us (15%)
  other arithmetic  49.4 us (9%)
    ppermute x76, waiting for transfers between devices, send(): arrived = lax.ppermute(block, ('seq', 'fsdp'), route)  168 us
    ppermute x76, starting transfers between devices, send(): arrived = lax.ppermute(block, ('seq', 'fsdp'), route)  69.3 us
    unnamed x248, local copies, waits for them, and re-layouts  40.7 us
    pallas_call x1, Pallas kernels, inside_back(): pl.pallas_call(inside_back_body, grid=(pairs,), in_specs=[columns, column...  27.6 us
    pallas_call x4, Pallas kernels, weight_grad(): pl.pallas_call(functools.partial(sum_body, len(keys)), grid=(rows // tile...  17.7 us
    pallas_call x4, Pallas kernels, project(): pl.pallas_call(functools.partial(project_body, count), grid=(pl.cdiv(widt...  15.6 us
    pallas_call x1, Pallas kernels, turn(): pl.pallas_call(turn_body, grid=(2, groups), in_specs=[pl.BlockSpec((token...  15.4 us
    pallas_call x1, Pallas kernels, leave(): pl.pallas_call(functools.partial(leave_body, steps), grid=(steps + 1,), i...  15.1 us
  transfers between devices with their start and end apart: 80, of which 32 were waited for; matrix products, arithmetic and copies ran while one was open for 15% of the time, Pallas kernels for 25%

profile of v3, /device:TPU:0, one launch (start us, length us, event | category | flops | bytes accessed | tf_op | source)
XLA Modules:
  0.0 541.1 jit_solution(7818613251273316756)
XLA Ops:
  2.0 4.1 concatenate.39
  6.3 2.9 collective-permute-start.1
  13.1 14.4 %collective-permute-done.3.refs_0_ = bf16[848,384]{1,0:T(8,128)(2,1)S(1)} collective-permute-done((bf16[848,384]{1,0:T(8,128)(2,1)S(1)}, bf16[848,384]{1,0:T(8,128)(2,1)S(1)}, u32[]{:S(2)}, u32[]{:S(2)}) %collective-permute-start.3) | collective-permute-done | bytes 651296 | tf_op jit(solution)/shard_map/ppermute | solution.py:44
  28.3 2.0 constant_dynamic-slice_fusion.15
  36.2 3.1 fusion.11
  39.3 10.8 %collective-permute-done.9.refs_0_ = bf16[192,1536]{1,0:T(8,128)(2,1)} collective-permute-done((bf16[192,1536]{1,0:T(8,128)(2,1)}, bf16[192,1536]{1,0:T(8,128)(2,1)}, u32[]{:S(2)}, u32[]{:S(2)}) %collective-permute-start.9) | collective-permute-done | bytes 589856 | tf_op jit(solution)/shard_map/ppermute | solution.py:44
  59.5 5.2 collective-permute-done.11.refs_4_
  74.9 2.4 constant_dynamic-slice_fusion.9
  77.4 2.7 laid.2
  80.2 6.8 %project.4.dt_ref.proj_ref = bf16[256,3376]{1,0:T(8,128)(2,1)S(1)} custom-call(bf16[256,384]{1,0:T(8,128)(2,1)S(1)} %get-tuple-element.277.refs_0_.refs_4_, bf16[256,384]{1,0:T(8,128)(2,1)S(1)} %get-tuple-element.258.refs_1_, bf16[256,384]{1,0:T(8,128)(2,1)S(1)} %get-tuple-element.413.refs_2_, bf16[256,384]{1,0:T(8,128)(2,1)S(1)} %get-tuple-element.412.refs_3_, ...), custom_call_target="tpu_custom_call" | custom-call | tf_op jit(solution)/shard_map/project/pallas_call | solution.py:396
  87.1 2.6 collective-permute-start.19
  95.6 3.8 enter.1
  100.6 5.8 %all-to-all-start = ((f32[8,392,128]{2,1,0:T(8,128)}), f32[8,392,128]{2,1,0:T(8,128)S(1)}, u32[]{:S(2)}, u32[]{:S(2)}) async-start(f32[8,392,128]{2,1,0:T(8,128)} %copy-done.44), calls=%async_computation | async-start | bytes 3211264 | tf_op jit(solution)/shard_map/all_to_all | solution.py:1230
  109.1 2.0 collective-permute-start.22
  115.4 10.7 %inside.1.base_ref = f32[256,3072]{1,0:T(8,128)S(1)} custom-call(bf16[256,3328]{1,0:T(8,128)(2,1)S(1)} %get-tuple-element.228.x_ref.b_ref.c_ref.low_ref, bf16[256,3328]{1,0:T(8,128)(2,1)S(1)} %get-tuple-element.228.x_ref.b_ref.c_ref.low_ref, bf16[256,3328]{1,0:T(8,128)(2,1)S(1)} %get-tuple-element.228.x_ref.b_ref.c_ref.low_ref, f32[256,128]{1,0:T(8,128)S(1)} %copy-done.53, ...), custom_call_target="tpu_custom_call" | custom-call | tf_op jit(solution)/shard_map/inside/pallas_call | solution.py:829
  128.6 11.6 %collective-permute-done.23.refs_4_ = bf16[96,1536]{1,0:T(8,128)(2,1)} collective-permute-done((bf16[96,1536]{1,0:T(8,128)(2,1)}, bf16[96,1536]{1,0:T(8,128)(2,1)}, u32[]{:S(2)}, u32[]{:S(2)}) %collective-permute-start.23) | collective-permute-done | bytes 294944 | tf_op jit(solution)/shard_map/ppermute | solution.py:44
  140.3 4.1 all-to-all-done.blocks_ref
  145.4 3.7 laid.3.refs_2_.refs_6_
  149.7 4.1 all-to-all-start.1
  156.2 2.4 copy-done
  158.6 2.9 project.5.refs_0_
  162.3 2.9 project.6.refs_1_
  166.0 3.0 project.7.refs_2_
  169.1 8.8 %to_inner.1.grad_ref = f32[256,3072]{1,0:T(8,128)S(1)} custom-call(s32[4]{0:T(128)S(1)} %pad_add_fusion.1.place_ref, bf16[256,1536]{1,0:T(8,128)(2,1)S(1)} %bitcast_select_fusion.grad_ref.refs_4_, bf16[768,1536]{1,0:T(8,128)(2,1)S(1)} %copy-done.14, bf16[768,1536]{1,0:T(8,128)(2,1)S(1)} %copy-done.20, bf16[768,1536]{1,0:T(8,128)(2,1)} %laid.3.refs_2_.refs_6_, ...), custom_call_target="tpu_custom_call" | custom-call | tf_op jit(solution)/shard_map/to_inner/pallas_call | solution.py:264
  183.7 15.4 %turn.1 = (bf16[256,3072]{1,0:T(8,128)(2,1)}, bf16[256,3072]{1,0:T(8,128)(2,1)}, bf16[256,3072]{1,0:T(8,128)(2,1)}, bf16[256,3072]{1,0:T(8,128)(2,1)}, f32[3072,128]{1,0:T(8,128)}, /*index=5*/f32[1,3072]{1,0:T(1,128)}) custom-call(f32[256,3072]{1,0:T(8,128)} %copy-done.12, bf16[3072,128]{1,0:T(8,128)(2,1)} %bitcast.86, bf16[256,128]{1,0:T(8,128)(2,1)} %slice.130.c_ref, ...), custom_call_target="tpu_custom_call" | custom-call | tf_op jit(solution)/shard_map/turn/pallas_call | solution.py:947
  200.5 5.8 %all-to-all-start.2 = ((f32[8,384,128]{2,1,0:T(8,128)}), f32[8,384,128]{2,1,0:T(8,128)}, u32[]{:S(2)}, u32[]{:S(2)}) async-start(f32[8,384,128]{2,1,0:T(8,128)} %bitcast.91), calls=%async_computation.2 | async-start | bytes 3145728 | tf_op jit(solution)/shard_map/all_to_all | solution.py:1263
  207.8 2.7 constant_dynamic-slice_fusion.1
  213.8 27.6 %inside_back.1 = (f32[256,3072]{1,0:T(8,128)S(1)}, f32[256,128]{1,0:T(8,128)S(1)}, f32[256,128]{1,0:T(8,128)S(1)}, f32[48,256]{1,0:T(8,128)S(1)}, f32[48,256]{1,0:T(8,128)S(1)}, /*index=5*/f32[1,3072]{1,0:T(1,128)S(1)}) custom-call(bf16[256,3072]{1,0:T(8,128)(2,1)S(1)} %copy-done.46, bf16[256,3072]{1,0:T(8,128)(2,1)S(1)} %copy-done.47, ...), custom_call_target="tpu_custom_call" | custom-call | tf_op jit(solution)/shard_map/inside_back/pallas_call | solution.py:911
  246.4 2.6 carried.3
  249.7 6.5 %all-to-all-start.3 = ((bf16[8,384,128]{2,1,0:T(8,128)(2,1)}), bf16[8,384,128]{2,1,0:T(8,128)(2,1)}, u32[]{:S(2)}, u32[]{:S(2)}) async-start(bf16[8,384,128]{2,1,0:T(8,128)(2,1)} %carried.3), calls=%async_computation.3 | async-start | bytes 1572864 | tf_op jit(solution)/shard_map/all_to_all | solution.py:543
  256.2 3.2 collective-permute-done.39.refs_3_
  259.4 4.8 weight_grad.5
  264.2 2.2 copy-done.6
  269.0 5.9 %weight_grad.4 = f32[3072,384]{1,0:T(8,128)S(1)} custom-call(bf16[256,3072]{1,0:T(8,128)(2,1)S(1)} %copy-done.24, bf16[256,3072]{1,0:T(8,128)(2,1)} %collective-permute-done.34.refs_1_, bf16[256,3072]{1,0:T(8,128)(2,1)} %collective-permute-done.35.refs_2_, bf16[256,3072]{1,0:T(8,128)(2,1)} %collective-permute-done.36.refs_3_, ...), custom_call_target="tpu_custom_call" | custom-call | tf_op jit(solution)/shard_map/weight_grad/pallas_call | solution.py:236
  274.9 2.2 copy-done.7
  279.0 5.9 %output_rows.1 = bf16[256,1536]{1,0:T(8,128)(2,1)} custom-call(bf16[256,1536]{1,0:T(8,128)(2,1)S(1)} %bitcast.85, bf16[256,768]{1,0:T(8,128)(2,1)S(1)} %get-tuple-element.405.refs_0_, bf16[256,768]{1,0:T(8,128)(2,1)S(1)} %get-tuple-element.404.refs_1_, bf16[256,768]{1,0:T(8,128)(2,1)S(1)} %get-tuple-element.403.refs_2_, ...), custom_call_target="tpu_custom_call" | custom-call | tf_op jit(solution)/shard_map/output_rows/pallas_call | solution.py:342
  284.9 12.9 %collective-permute-done.40 = bf16[384,1536]{1,0:T(8,128)(2,1)} collective-permute-done((bf16[384,1536]{1,0:T(8,128)(2,1)}, bf16[384,1536]{1,0:T(8,128)(2,1)}, u32[]{:S(2)}, u32[]{:S(2)}) %collective-permute-start.40) | collective-permute-done | bytes 1179680 | tf_op jit(solution)/shard_map/ppermute | solution.py:44
  297.8 2.8 dynamic-slice_convert_fusion
  302.0 2.3 convert_add_fusion.1
  306.5 15.1 %leave.1 = (bf16[256,1792]{1,0:T(8,128)(2,1)}, bf16[256,1536]{1,0:T(8,128)(2,1)}, f32[8,3328]{1,0:T(8,128)}, f32[8,3328]{1,0:T(8,128)}, f32[4,3328]{1,0:T(4,128)...) custom-call(bf16[256,3376]{1,0:T(8,128)(2,1)} %copy-done.2, bf16[8,3328]{1,0:T(8,128)(2,1)} %copy-done.68, ...), custom_call_target="tpu_custom_call" | custom-call | tf_op jit(solution)/shard_map/leave/pallas_call | solution.py:1080
  321.7 7.1 %collective-permute-done.41 = bf16[1536,384]{1,0:T(8,128)(2,1)} collective-permute-done((bf16[1536,384]{1,0:T(8,128)(2,1)}, bf16[1536,384]{1,0:T(8,128)(2,1)}, u32[]{:S(2)}, u32[]{:S(2)}) %collective-permute-start.41) | collective-permute-done | bytes 1179680 | tf_op jit(solution)/shard_map/ppermute | solution.py:44
  331.8 3.9 collective-permute-done.43
  337.3 2.3 convert_add_fusion
  344.4 16.6 %collective-permute-done.44 = bf16[96,1536]{1,0:T(8,128)(2,1)S(1)} collective-permute-done((bf16[96,1536]{1,0:T(8,128)(2,1)S(1)}, bf16[96,1536]{1,0:T(8,128)(2,1)S(1)}, u32[]{:S(2)}, u32[]{:S(2)}) %collective-permute-start.44) | collective-permute-done | bytes 294944 | tf_op jit(solution)/shard_map/ppermute | solution.py:44
  366.8 3.9 weight_grad.6
  371.7 2.6 collective-permute-start.51
  379.6 13.0 %to_model.1 = f32[4,256,384]{2,1,0:T(8,128)S(1)} custom-call(bf16[256,3072]{1,0:T(8,128)(2,1)S(1)} %copy-done.25, bf16[256,3376]{1,0:T(8,128)(2,1)S(1)} %pad_maximum_fusion.tail_ref, bf16[6448,384]{1,0:T(8,128)(2,1)} %bitcast.78, bf16[6448,384]{1,0:T(8,128)(2,1)} %collective-permute-done.4.refs_5_.refs_1_, bf16[3376,384]{1,0:T(8,128)(2,1)S(1)} %copy-done.17, ...), custom_call_target="tpu_custom_call" | custom-call | tf_op jit(solution)/shard_map/to_model/pallas_call | solution.py:321
  392.6 5.5 %collective-permute-done.52 = bf16[96,1536]{1,0:T(8,128)(2,1)} collective-permute-done((bf16[96,1536]{1,0:T(8,128)(2,1)S(1)}, bf16[96,1536]{1,0:T(8,128)(2,1)}, u32[]{:S(2)}, u32[]{:S(2)}) %collective-permute-start.52) | collective-permute-done | bytes 294944 | tf_op jit(solution)/shard_map/ppermute | solution.py:44
  398.0 5.1 collective-permute-done.53
  405.5 3.2 weight_grad.7
  419.4 18.9 %collective-permute-done.58 = bf16[384,384]{1,0:T(8,128)(2,1)} collective-permute-done((bf16[384,384]{1,0:T(8,128)(2,1)}, bf16[384,384]{1,0:T(8,128)(2,1)}, u32[]{:S(2)}, u32[]{:S(2)}) %collective-permute-start.58) | collective-permute-done | bytes 294944 | tf_op jit(solution)/shard_map/ppermute | solution.py:44
  438.4 2.2 collective-permute-done.57
  453.3 6.8 %collective-permute-done.60 = bf16[416,384]{1,0:T(8,128)(2,1)} collective-permute-done((bf16[416,384]{1,0:T(8,128)(2,1)}, bf16[416,384]{1,0:T(8,128)(2,1)}, u32[]{:S(2)}, u32[]{:S(2)}) %collective-permute-start.60) | collective-permute-done | bytes 319520 | tf_op jit(solution)/shard_map/ppermute | solution.py:44
  460.1 11.2 %collective-permute-done.61 = bf16[768,384]{1,0:T(8,128)(2,1)} collective-permute-done((bf16[768,384]{1,0:T(8,128)(2,1)S(1)}, bf16[768,384]{1,0:T(8,128)(2,1)}, u32[]{:S(2)}, u32[]{:S(2)}) %collective-permute-start.61) | collective-permute-done | bytes 589856 | tf_op jit(solution)/shard_map/ppermute | solution.py:44
  476.8 3.0 collective-permute-start.65
  481.1 6.7 %collective-permute-done.65 = bf16[208,384]{1,0:T(8,128)(2,1)} collective-permute-done((bf16[208,384]{1,0:T(8,128)(2,1)S(1)}, bf16[208,384]{1,0:T(8,128)(2,1)}, u32[]{:S(2)}, u32[]{:S(2)}) %collective-permute-start.65) | collective-permute-done | bytes 159776 | tf_op jit(solution)/shard_map/ppermute | solution.py:44
  493.6 3.4 collective-permute-done.66
  497.0 2.7 collective-permute-done.69
  499.7 2.3 collective-permute-done.68
  507.3 2.2 collective-permute-start.74
  518.4 2.8 maximum_convert_fusion
  527.4 2.3 convert_dynamic-update-slice_fusion.1
  529.8 7.8 %collective-permute-done.75 = bf16[832,384]{1,0:T(8,128)(2,1)} collective-permute-done((bf16[832,384]{1,0:T(8,128)(2,1)}, bf16[832,384]{1,0:T(8,128)(2,1)}, u32[]{:S(2)}, u32[]{:S(2)}) %collective-permute-start.75) | collective-permute-done | bytes 639008 | tf_op jit(solution)/shard_map/ppermute | solution.py:44
  538.7 2.2 convert_dynamic-update-slice_fusion.4
  (507 shorter events, 159.6 us)
Async XLA Ops:
  0.7 26.8 %collective-permute-start.4 = (bf16[6448,384]{1,0:T(8,128)(2,1)}, bf16[6448,384]{1,0:T(8,128)(2,1)}, u32[]{:S(2)}, u32[]{:S(2)}) collective-permute-start(bf16[6448,384]{1,0:T(8,128)(2,1)} %bitcast.76), channel_id=1, source_target_pairs={{0,1},{1,0},{2,3},{3,2},{4,5},{5,4},{6,7},{7,6},{8,9},{9,8},{10,11... | collective-permute-start | bytes 14856200 | tf_op jit(solution)/shard_map/ppermute | solution.py:44
  10.4 17.0 %collective-permute-start.3 = (bf16[848,384]{1,0:T(8,128)(2,1)S(1)}, bf16[848,384]{1,0:T(8,128)(2,1)S(1)}, u32[]{:S(2)}, u32[]{:S(2)}) collective-permute-start(bf16[848,384]{1,0:T(8,128)(2,1)S(1)} %dynamic-slice_bitcast_fusion), channel_id=1, source_target_pairs={{0,2},{1,3},{2,0},{3,1},{4,6},{5,7},{6,4},{7,5},{8,10},{9,11},{10,... | collective-permute-start | bytes 1953800 | tf_op jit(solution)/shard_map/ppermute | solution.py:44
  28.3 21.8 %collective-permute-start.8 = (bf16[768,1536]{1,0:T(8,128)(2,1)}, bf16[768,1536]{1,0:T(8,128)(2,1)S(1)}, u32[]{:S(2)}, u32[]{:S(2)}) collective-permute-start(bf16[768,1536]{1,0:T(8,128)(2,1)} %refs_4_.1), channel_id=1, source_target_pairs={{0,1},{1,0},{2,3},{3,2},{4,5},{5,4},{6,7},{7,6},{8,9},{9,8},{10,11... | collective-permute-start | bytes 7077896 | tf_op jit(solution)/shard_map/ppermute | solution.py:44
  30.4 19.7 %collective-permute-start.5 = (bf16[848,384]{1,0:T(8,128)(2,1)}, bf16[848,384]{1,0:T(8,128)(2,1)}, u32[]{:S(2)}, u32[]{:S(2)}) collective-permute-start(bf16[848,384]{1,0:T(8,128)(2,1)} %copy-done.50), channel_id=1, source_target_pairs={{0,4},{1,5},{2,6},{3,7},{4,0},{5,1},{6,2},{7,3},{8,12},{9,13},{10,... | collective-permute-start | bytes 1953800 | tf_op jit(solution)/shard_map/ppermute | solution.py:44
  32.1 18.0 %collective-permute-start.6 = (bf16[848,384]{1,0:T(8,128)(2,1)}, bf16[848,384]{1,0:T(8,128)(2,1)}, u32[]{:S(2)}, u32[]{:S(2)}) collective-permute-start(bf16[848,384]{1,0:T(8,128)(2,1)} %copy-done.50), channel_id=1, source_target_pairs={{0,8},{1,9},{2,10},{3,11},{4,12},{5,13},{6,14},{7,15},{8,0},{9,1},... | collective-permute-start | bytes 1953800 | tf_op jit(solution)/shard_map/ppermute | solution.py:44
  33.6 16.5 %collective-permute-start.7 = (bf16[848,384]{1,0:T(8,128)(2,1)}, bf16[848,384]{1,0:T(8,128)(2,1)}, u32[]{:S(2)}, u32[]{:S(2)}) collective-permute-start(bf16[848,384]{1,0:T(8,128)(2,1)} %copy-done.50), channel_id=1, source_target_pairs={{0,1},{1,0},{2,3},{3,2},{4,5},{5,4},{6,7},{7,6},{8,9},{9,8},{10,11... | collective-permute-start | bytes 1953800 | tf_op jit(solution)/shard_map/ppermute | solution.py:44
  34.0 16.1 %collective-permute-start.9 = (bf16[192,1536]{1,0:T(8,128)(2,1)}, bf16[192,1536]{1,0:T(8,128)(2,1)}, u32[]{:S(2)}, u32[]{:S(2)}) collective-permute-start(bf16[192,1536]{1,0:T(8,128)(2,1)} %constant_dynamic-slice_fusion.15), channel_id=1, source_target_pairs={{0,2},{1,3},{2,0},{3,1},{4,6},{5,7},{6,4},{7,5},{8,10},{9,11},{10,... | collective-permute-start | bytes 1769480 | tf_op jit(solution)/shard_map/ppermute | solution.py:44
  52.6 12.2 %collective-permute-start.12 = (bf16[848,384]{1,0:T(8,128)(2,1)}, bf16[848,384]{1,0:T(8,128)(2,1)S(1)}, u32[]{:S(2)}, u32[]{:S(2)}) collective-permute-start(bf16[848,384]{1,0:T(8,128)(2,1)} %collective-permute-done.5.refs_1_), channel_id=1, source_target_pairs={{0,1},{1,0},{2,3},{3,2},{4,5},{5,4},{6,7},{7,6},{8,9},{9,8},{10,11... | collective-permute-start | bytes 1953800 | tf_op jit(solution)/shard_map/ppermute | solution.py:44
  54.4 10.4 %collective-permute-start.13 = (bf16[848,384]{1,0:T(8,128)(2,1)}, bf16[848,384]{1,0:T(8,128)(2,1)S(1)}, u32[]{:S(2)}, u32[]{:S(2)}) collective-permute-start(bf16[848,384]{1,0:T(8,128)(2,1)} %collective-permute-done.6.refs_2_), channel_id=1, source_target_pairs={{0,1},{1,0},{2,3},{3,2},{4,5},{5,4},{6,7},{7,6},{8,9},{9,8},{10,11... | collective-permute-start | bytes 1953800 | tf_op jit(solution)/shard_map/ppermute | solution.py:44
  54.9 9.9 %collective-permute-start.10 = (bf16[432,384]{1,0:T(8,128)(2,1)}, bf16[432,384]{1,0:T(8,128)(2,1)S(1)}, u32[]{:S(2)}, u32[]{:S(2)}) collective-permute-start(bf16[432,384]{1,0:T(8,128)(2,1)} %slice.114), channel_id=1, source_target_pairs={{0,4},{1,5},{2,6},{3,7},{4,0},{5,1},{6,2},{7,3},{8,12},{9,13},{10,... | collective-permute-start | bytes 995336 | tf_op jit(solution)/shard_map/ppermute | solution.py:44
  58.0 29.1 %collective-permute-start.14 = (bf16[1024,384]{1,0:T(8,128)(2,1)}, bf16[1024,384]{1,0:T(8,128)(2,1)}, u32[]{:S(2)}, u32[]{:S(2)}) collective-permute-start(bf16[1024,384]{1,0:T(8,128)(2,1)} %get-tuple-element.209), channel_id=1, source_target_pairs={{0,2},{1,3},{2,0},{3,1},{4,6},{5,7},{6,4},{7,5},{8,10},{9,11},{10,... | collective-permute-start | bytes 2359304 | tf_op jit(solution)/shard_map/ppermute | solution.py:44
  67.4 19.7 %collective-permute-start.17 = (bf16[192,1536]{1,0:T(8,128)(2,1)}, bf16[192,1536]{1,0:T(8,128)(2,1)}, u32[]{:S(2)}, u32[]{:S(2)}) collective-permute-start(bf16[192,1536]{1,0:T(8,128)(2,1)} %collective-permute-done.9.refs_0_), channel_id=1, source_target_pairs={{0,4},{1,5},{2,6},{3,7},{4,0},{5,1},{6,2},{7,3},{8,12},{9,13},{10,... | collective-permute-start | bytes 1769480 | tf_op jit(solution)/shard_map/ppermute | solution.py:44
  68.8 18.3 %collective-permute-start.18 = (bf16[192,1536]{1,0:T(8,128)(2,1)}, bf16[192,1536]{1,0:T(8,128)(2,1)}, u32[]{:S(2)}, u32[]{:S(2)}) collective-permute-start(bf16[192,1536]{1,0:T(8,128)(2,1)} %collective-permute-done.9.refs_0_), channel_id=1, source_target_pairs={{0,8},{1,9},{2,10},{3,11},{4,12},{5,13},{6,14},{7,15},{8,0},{9,1},... | collective-permute-start | bytes 1769480 | tf_op jit(solution)/shard_map/ppermute | solution.py:44
  69.4 31.2 %collective-permute-start.20 = (bf16[1024,384]{1,0:T(8,128)(2,1)}, bf16[1024,384]{1,0:T(8,128)(2,1)}, u32[]{:S(2)}, u32[]{:S(2)}) collective-permute-start(bf16[1024,384]{1,0:T(8,128)(2,1)} %get-tuple-element.225), channel_id=1, source_target_pairs={{0,2},{1,3},{2,0},{3,1},{4,6},{5,7},{6,4},{7,5},{8,10},{9,11},{10,... | collective-permute-start | bytes 2359304 | tf_op jit(solution)/shard_map/ppermute | solution.py:44
  100.6 43.8 %all-to-all-start = ((f32[8,392,128]{2,1,0:T(8,128)}), f32[8,392,128]{2,1,0:T(8,128)S(1)}, u32[]{:S(2)}, u32[]{:S(2)}) async-start(f32[8,392,128]{2,1,0:T(8,128)} %copy-done.44), calls=%async_computation | async-start | bytes 3211264 | tf_op jit(solution)/shard_map/all_to_all | solution.py:1230
  106.4 33.9 %collective-permute-start.21 = (bf16[1024,384]{1,0:T(8,128)(2,1)}, bf16[1024,384]{1,0:T(8,128)(2,1)}, u32[]{:S(2)}, u32[]{:S(2)}) collective-permute-start(bf16[1024,384]{1,0:T(8,128)(2,1)} %get-tuple-element.232), channel_id=1, source_target_pairs={{0,2},{1,3},{2,0},{3,1},{4,6},{5,7},{6,4},{7,5},{8,10},{9,11},{10,... | collective-permute-start | bytes 2359304 | tf_op jit(solution)/shard_map/ppermute | solution.py:44
  106.9 33.4 %collective-permute-start.24 = (bf16[1024,384]{1,0:T(8,128)(2,1)}, bf16[1024,384]{1,0:T(8,128)(2,1)}, u32[]{:S(2)}, u32[]{:S(2)}) collective-permute-start(bf16[1024,384]{1,0:T(8,128)(2,1)} %collective-permute-done.14.refs_6_.refs_3_), channel_id=1, source_target_pairs={{0,1},{1,0},{2,3},{3,2},{4,5},{5,4},{6,7},{7,6},{8,9},{9,8},{10,11... | collective-permute-start | bytes 2359304 | tf_op jit(solution)/shard_map/ppermute | solution.py:44
  106.9 33.4 %collective-permute-start.25 = (bf16[1024,384]{1,0:T(8,128)(2,1)}, bf16[1024,384]{1,0:T(8,128)(2,1)}, u32[]{:S(2)}, u32[]{:S(2)}) collective-permute-start(bf16[1024,384]{1,0:T(8,128)(2,1)} %collective-permute-done.20.refs_6_.refs_4_), channel_id=1, source_target_pairs={{0,1},{1,0},{2,3},{3,2},{4,5},{5,4},{6,7},{7,6},{8,9},{9,8},{10,11... | collective-permute-start | bytes 2359304 | tf_op jit(solution)/shard_map/ppermute | solution.py:44
  109.1 19.5 %collective-permute-start.22 = (bf16[96,1536]{1,0:T(8,128)(2,1)}, bf16[96,1536]{1,0:T(8,128)(2,1)}, u32[]{:S(2)}, u32[]{:S(2)}) collective-permute-start(bf16[96,1536]{1,0:T(8,128)(2,1)} %slice.127), channel_id=1, source_target_pairs={{0,4},{1,5},{2,6},{3,7},{4,0},{5,1},{6,2},{7,3},{8,12},{9,13},{10,... | collective-permute-start | bytes 884744 | tf_op jit(solution)/shard_map/ppermute | solution.py:44
  112.8 27.4 %collective-permute-start.23 = (bf16[96,1536]{1,0:T(8,128)(2,1)}, bf16[96,1536]{1,0:T(8,128)(2,1)}, u32[]{:S(2)}, u32[]{:S(2)}) collective-permute-start(bf16[96,1536]{1,0:T(8,128)(2,1)} %slice.128), channel_id=1, source_target_pairs={{0,8},{1,9},{2,10},{3,11},{4,12},{5,13},{6,14},{7,15},{8,0},{9,1},... | collective-permute-start | bytes 884744 | tf_op jit(solution)/shard_map/ppermute | solution.py:44
  149.0 20.0 %collective-permute-start.26 = (bf16[768,1536]{1,0:T(8,128)(2,1)}, bf16[768,1536]{1,0:T(8,128)(2,1)}, u32[]{:S(2)}, u32[]{:S(2)}) collective-permute-start(bf16[768,1536]{1,0:T(8,128)(2,1)} %laid.3.refs_2_.refs_6_), channel_id=1, source_target_pairs={{0,1},{1,0},{2,3},{3,2},{4,5},{5,4},{6,7},{7,6},{8,9},{9,8},{10,11... | collective-permute-start | bytes 7077896 | tf_op jit(solution)/shard_map/ppermute | solution.py:44
  149.7 29.9 %all-to-all-start.1 = ((bf16[8,384,128]{2,1,0:T(8,128)(2,1)}), bf16[8,384,128]{2,1,0:T(8,128)(2,1)S(1)}, u32[]{:S(2)}, u32[]{:S(2)}) async-start(bf16[8,384,128]{2,1,0:T(8,128)(2,1)} %copy-done.33), calls=%async_computation.1 | async-start | bytes 1572864 | tf_op jit(solution)/shard_map/all_to_all | solution.py:543
  155.2 10.8 %collective-permute-start.27 = (bf16[1024,384]{1,0:T(8,128)(2,1)}, bf16[1024,384]{1,0:T(8,128)(2,1)S(1)}, u32[]{:S(2)}, u32[]{:S(2)}) collective-permute-start(bf16[1024,384]{1,0:T(8,128)(2,1)} %collective-permute-done.21.refs_6_.refs_5_), channel_id=1, source_target_pairs={{0,1},{1,0},{2,3},{3,2},{4,5},{5,4},{6,7},{7,6},{8,9},{9,8},{10,11... | collective-permute-start | bytes 2359304 | tf_op jit(solution)/shard_map/ppermute | solution.py:44
  155.6 24.0 %collective-permute-start.28 = (bf16[256,1536]{1,0:T(8,128)(2,1)S(1)}, bf16[256,1536]{1,0:T(8,128)(2,1)}, u32[]{:S(2)}, u32[]{:S(2)}) collective-permute-start(bf16[256,1536]{1,0:T(8,128)(2,1)S(1)} %bitcast_select_fusion.grad_ref.refs_4_), channel_id=1, source_target_pairs={{0,2},{1,3},{2,0},{3,1},{4,6},{5,7},{6,4},{7,5},{8,10},{9,11},{10,... | collective-permute-start | bytes 2359304 | tf_op jit(solution)/shard_map/ppermute | solution.py:44
  179.6 20.9 %collective-permute-start.32 = (bf16[256,1536]{1,0:T(8,128)(2,1)S(1)}, bf16[256,1536]{1,0:T(8,128)(2,1)}, u32[]{:S(2)}, u32[]{:S(2)}) collective-permute-start(bf16[256,1536]{1,0:T(8,128)(2,1)S(1)} %bitcast_select_fusion.grad_ref.refs_4_), channel_id=1, source_target_pairs={{0,1},{1,0},{2,3},{3,2},{4,5},{5,4},{6,7},{7,6},{8,9},{9,8},{10,11... | collective-permute-start | bytes 2359304 | tf_op jit(solution)/shard_map/ppermute | solution.py:44
  179.7 19.4 %collective-permute-start.29 = (bf16[256,384]{1,0:T(8,128)(2,1)}, bf16[256,384]{1,0:T(8,128)(2,1)S(1)}, u32[]{:S(2)}, u32[]{:S(2)}) collective-permute-start(bf16[256,384]{1,0:T(8,128)(2,1)} %copy-done.26), channel_id=1, source_target_pairs={{0,1},{1,0},{2,3},{3,2},{4,5},{5,4},{6,7},{7,6},{8,9},{9,8},{10,11... | collective-permute-start | bytes 589832 | tf_op jit(solution)/shard_map/ppermute | solution.py:44
  180.2 19.6 %collective-permute-start.30 = (bf16[256,384]{1,0:T(8,128)(2,1)}, bf16[256,384]{1,0:T(8,128)(2,1)S(1)}, u32[]{:S(2)}, u32[]{:S(2)}) collective-permute-start(bf16[256,384]{1,0:T(8,128)(2,1)} %get-tuple-element.259), channel_id=1, source_target_pairs={{0,2},{1,3},{2,0},{3,1},{4,6},{5,7},{6,4},{7,5},{8,10},{9,11},{10,... | collective-permute-start | bytes 589832 | tf_op jit(solution)/shard_map/ppermute | solution.py:44
  181.7 18.8 %collective-permute-start.31 = (bf16[256,384]{1,0:T(8,128)(2,1)}, bf16[256,384]{1,0:T(8,128)(2,1)}, u32[]{:S(2)}, u32[]{:S(2)}) collective-permute-start(bf16[256,384]{1,0:T(8,128)(2,1)} %get-tuple-element.260), channel_id=1, source_target_pairs={{0,3},{1,2},{2,1},{3,0},{4,7},{5,6},{6,5},{7,4},{8,11},{9,10},{10,... | collective-permute-start | bytes 589832 | tf_op jit(solution)/shard_map/ppermute | solution.py:44
  200.5 45.9 %all-to-all-start.2 = ((f32[8,384,128]{2,1,0:T(8,128)}), f32[8,384,128]{2,1,0:T(8,128)}, u32[]{:S(2)}, u32[]{:S(2)}) async-start(f32[8,384,128]{2,1,0:T(8,128)} %bitcast.91), calls=%async_computation.2 | async-start | bytes 3145728 | tf_op jit(solution)/shard_map/all_to_all | solution.py:1263
  206.2 43.4 %collective-permute-start.35 = (bf16[256,3072]{1,0:T(8,128)(2,1)}, bf16[256,3072]{1,0:T(8,128)(2,1)}, u32[]{:S(2)}, u32[]{:S(2)}) collective-permute-start(bf16[256,3072]{1,0:T(8,128)(2,1)} %get-tuple-element.275.refs_0_.gate_ref), channel_id=1, source_target_pairs={{0,2},{1,3},{2,0},{3,1},{4,6},{5,7},{6,4},{7,5},{8,10},{9,11},{10,... | collective-permute-start | bytes 4718600 | tf_op jit(solution)/shard_map/ppermute | solution.py:44
  207.7 38.6 %collective-permute-start.33 = (bf16[256,1536]{1,0:T(8,128)(2,1)}, bf16[256,1536]{1,0:T(8,128)(2,1)}, u32[]{:S(2)}, u32[]{:S(2)}) collective-permute-start(bf16[256,1536]{1,0:T(8,128)(2,1)} %collective-permute-done.28.refs_6_), channel_id=1, source_target_pairs={{0,1},{1,0},{2,3},{3,2},{4,5},{5,4},{6,7},{7,6},{8,9},{9,8},{10,11... | collective-permute-start | bytes 2359304 | tf_op jit(solution)/shard_map/ppermute | solution.py:44
  210.5 45.7 %collective-permute-start.37 = (bf16[256,768]{1,0:T(8,128)(2,1)}, bf16[256,768]{1,0:T(8,128)(2,1)}, u32[]{:S(2)}, u32[]{:S(2)}) collective-permute-start(bf16[256,768]{1,0:T(8,128)(2,1)} %get-tuple-element.401), channel_id=1, source_target_pairs={{0,1},{1,0},{2,3},{3,2},{4,5},{5,4},{6,7},{7,6},{8,9},{9,8},{10,11... | collective-permute-start | bytes 1179656 | tf_op jit(solution)/shard_map/ppermute | solution.py:44
  210.9 45.3 %collective-permute-start.38 = (bf16[256,768]{1,0:T(8,128)(2,1)}, bf16[256,768]{1,0:T(8,128)(2,1)}, u32[]{:S(2)}, u32[]{:S(2)}) collective-permute-start(bf16[256,768]{1,0:T(8,128)(2,1)} %get-tuple-element.400), channel_id=1, source_target_pairs={{0,2},{1,3},{2,0},{3,1},{4,6},{5,7},{6,4},{7,5},{8,10},{9,11},{10,... | collective-permute-start | bytes 1179656 | tf_op jit(solution)/shard_map/ppermute | solution.py:44
  211.5 47.9 %collective-permute-start.39 = (bf16[256,768]{1,0:T(8,128)(2,1)}, bf16[256,768]{1,0:T(8,128)(2,1)}, u32[]{:S(2)}, u32[]{:S(2)}) collective-permute-start(bf16[256,768]{1,0:T(8,128)(2,1)} %get-tuple-element.399), channel_id=1, source_target_pairs={{0,3},{1,2},{2,1},{3,0},{4,7},{5,6},{6,5},{7,4},{8,11},{9,10},{10,... | collective-permute-start | bytes 1179656 | tf_op jit(solution)/shard_map/ppermute | solution.py:44
  249.0 20.0 %collective-permute-start.34 = (bf16[256,3072]{1,0:T(8,128)(2,1)S(1)}, bf16[256,3072]{1,0:T(8,128)(2,1)}, u32[]{:S(2)}, u32[]{:S(2)}) collective-permute-start(bf16[256,3072]{1,0:T(8,128)(2,1)S(1)} %copy-done.24), channel_id=1, source_target_pairs={{0,1},{1,0},{2,3},{3,2},{4,5},{5,4},{6,7},{7,6},{8,9},{9,8},{10,11... | collective-permute-start | bytes 4718600 | tf_op jit(solution)/shard_map/ppermute | solution.py:44
  249.7 19.3 %collective-permute-start.36 = (bf16[256,3072]{1,0:T(8,128)(2,1)}, bf16[256,3072]{1,0:T(8,128)(2,1)}, u32[]{:S(2)}, u32[]{:S(2)}) collective-permute-start(bf16[256,3072]{1,0:T(8,128)(2,1)} %collective-permute-done.35.refs_2_), channel_id=1, source_target_pairs={{0,1},{1,0},{2,3},{3,2},{4,5},{5,4},{6,7},{7,6},{8,9},{9,8},{10,11... | collective-permute-start | bytes 4718600 | tf_op jit(solution)/shard_map/ppermute | solution.py:44
  249.7 48.0 %all-to-all-start.3 = ((bf16[8,384,128]{2,1,0:T(8,128)(2,1)}), bf16[8,384,128]{2,1,0:T(8,128)(2,1)}, u32[]{:S(2)}, u32[]{:S(2)}) async-start(bf16[8,384,128]{2,1,0:T(8,128)(2,1)} %carried.3), calls=%async_computation.3 | async-start | bytes 1572864 | tf_op jit(solution)/shard_map/all_to_all | solution.py:543
  267.6 30.2 %collective-permute-start.40 = (bf16[384,1536]{1,0:T(8,128)(2,1)}, bf16[384,1536]{1,0:T(8,128)(2,1)}, u32[]{:S(2)}, u32[]{:S(2)}) collective-permute-start(bf16[384,1536]{1,0:T(8,128)(2,1)} %dynamic-slice_convert_fusion.1), channel_id=1, source_target_pairs={{0,4},{1,5},{2,6},{3,7},{4,0},{5,1},{6,2},{7,3},{8,12},{9,13},{10,... | collective-permute-start | bytes 3538952 | tf_op jit(solution)/shard_map/ppermute | solution.py:44
  300.6 28.1 %collective-permute-start.41 = (bf16[1536,384]{1,0:T(8,128)(2,1)}, bf16[1536,384]{1,0:T(8,128)(2,1)}, u32[]{:S(2)}, u32[]{:S(2)}) collective-permute-start(bf16[1536,384]{1,0:T(8,128)(2,1)} %dynamic-slice_convert_fusion), channel_id=1, source_target_pairs={{0,4},{1,5},{2,6},{3,7},{4,0},{5,1},{6,2},{7,3},{8,12},{9,13},{10,... | collective-permute-start | bytes 3538952 | tf_op jit(solution)/shard_map/ppermute | solution.py:44
  305.8 15.9 %collective-permute-start.42 = (bf16[192,1536]{1,0:T(8,128)(2,1)S(1)}, bf16[192,1536]{1,0:T(8,128)(2,1)S(1)}, u32[]{:S(2)}, u32[]{:S(2)}) collective-permute-start(bf16[192,1536]{1,0:T(8,128)(2,1)S(1)} %dynamic-slice_convert_fusion.5), channel_id=1, source_target_pairs={{0,8},{1,9},{2,10},{3,11},{4,12},{5,13},{6,14},{7,15},{8,0},{9,1},... | collective-permute-start | bytes 1769480 | tf_op jit(solution)/shard_map/ppermute | solution.py:44
  335.8 26.1 %collective-permute-start.45 = (bf16[256,1792]{1,0:T(8,128)(2,1)S(1)}, bf16[256,1792]{1,0:T(8,128)(2,1)}, u32[]{:S(2)}, u32[]{:S(2)}) collective-permute-start(bf16[256,1792]{1,0:T(8,128)(2,1)S(1)} %slice_dynamic-update-slice_fusion.refs_0_), channel_id=1, source_target_pairs={{0,2},{1,3},{2,0},{3,1},{4,6},{5,7},{6,4},{7,5},{8,10},{9,11},{10,... | collective-permute-start | bytes 2752520 | tf_op jit(solution)/shard_map/ppermute | solution.py:44
  337.3 24.5 %collective-permute-start.46 = (bf16[256,1792]{1,0:T(8,128)(2,1)S(1)}, bf16[256,1792]{1,0:T(8,128)(2,1)S(1)}, u32[]{:S(2)}, u32[]{:S(2)}) collective-permute-start(bf16[256,1792]{1,0:T(8,128)(2,1)S(1)} %slice_dynamic-update-slice_fusion.refs_0_), channel_id=1, source_target_pairs={{0,1},{1,0},{2,3},{3,2},{4,5},{5,4},{6,7},{7,6},{8,9},{9,8},{10,11... | collective-permute-start | bytes 2752520 | tf_op jit(solution)/shard_map/ppermute | solution.py:44
  339.7 22.1 %collective-permute-start.47 = (bf16[768,384]{1,0:T(8,128)(2,1)S(1)}, bf16[768,384]{1,0:T(8,128)(2,1)S(1)}, u32[]{:S(2)}, u32[]{:S(2)}) collective-permute-start(bf16[768,384]{1,0:T(8,128)(2,1)S(1)} %dynamic-slice_convert_fusion.4), channel_id=1, source_target_pairs={{0,8},{1,9},{2,10},{3,11},{4,12},{5,13},{6,14},{7,15},{8,0},{9,1},... | collective-permute-start | bytes 1769480 | tf_op jit(solution)/shard_map/ppermute | solution.py:44
  341.5 19.5 %collective-permute-start.44 = (bf16[96,1536]{1,0:T(8,128)(2,1)S(1)}, bf16[96,1536]{1,0:T(8,128)(2,1)S(1)}, u32[]{:S(2)}, u32[]{:S(2)}) collective-permute-start(bf16[96,1536]{1,0:T(8,128)(2,1)S(1)} %dynamic-slice_convert_fusion.9), channel_id=1, source_target_pairs={{0,16},{1,17},{2,18},{3,19},{4,20},{5,21},{6,22},{7,23},{8,24},{9,... | collective-permute-start | bytes 884744 | tf_op jit(solution)/shard_map/ppermute | solution.py:44
  363.5 29.1 %collective-permute-start.50 = (bf16[256,1664]{1,0:T(8,128)(2,1)S(1)}, bf16[256,1664]{1,0:T(8,128)(2,1)S(1)}, u32[]{:S(2)}, u32[]{:S(2)}) collective-permute-start(bf16[256,1664]{1,0:T(8,128)(2,1)S(1)} %pad_maximum_fusion.3.refs_0_), channel_id=1, source_target_pairs={{0,2},{1,3},{2,0},{3,1},{4,6},{5,7},{6,4},{7,5},{8,10},{9,11},{10,... | collective-permute-start | bytes 2555912 | tf_op jit(solution)/shard_map/ppermute | solution.py:44
  371.7 31.4 %collective-permute-start.51 = (bf16[896,384]{1,0:T(8,128)(2,1)}, bf16[896,384]{1,0:T(8,128)(2,1)S(1)}, u32[]{:S(2)}, u32[]{:S(2)}) collective-permute-start(bf16[896,384]{1,0:T(8,128)(2,1)} %dynamic-slice_convert_fusion.2), channel_id=1, source_target_pairs={{0,4},{1,5},{2,6},{3,7},{4,0},{5,1},{6,2},{7,3},{8,12},{9,13},{10,... | collective-permute-start | bytes 2064392 | tf_op jit(solution)/shard_map/ppermute | solution.py:44
  374.4 23.6 %collective-permute-start.52 = (bf16[96,1536]{1,0:T(8,128)(2,1)S(1)}, bf16[96,1536]{1,0:T(8,128)(2,1)}, u32[]{:S(2)}, u32[]{:S(2)}) collective-permute-start(bf16[96,1536]{1,0:T(8,128)(2,1)S(1)} %add_convert_fusion.1), channel_id=1, source_target_pairs={{0,16},{1,17},{2,18},{3,19},{4,20},{5,21},{6,22},{7,23},{8,24},{9,... | collective-permute-start | bytes 884744 | tf_op jit(solution)/shard_map/ppermute | solution.py:44
  376.1 27.1 %collective-permute-start.53 = (bf16[384,384]{1,0:T(8,128)(2,1)S(1)}, bf16[384,384]{1,0:T(8,128)(2,1)S(1)}, u32[]{:S(2)}, u32[]{:S(2)}) collective-permute-start(bf16[384,384]{1,0:T(8,128)(2,1)S(1)} %dynamic-slice_convert_fusion.8), channel_id=1, source_target_pairs={{0,16},{1,17},{2,18},{3,19},{4,20},{5,21},{6,22},{7,23},{8,24},{9,... | collective-permute-start | bytes 884744 | tf_op jit(solution)/shard_map/ppermute | solution.py:44
  409.7 30.9 %collective-permute-start.55 = (bf16[832,384]{1,0:T(8,128)(2,1)}, bf16[832,384]{1,0:T(8,128)(2,1)}, u32[]{:S(2)}, u32[]{:S(2)}) collective-permute-start(bf16[832,384]{1,0:T(8,128)(2,1)} %dynamic-slice_convert_fusion.3), channel_id=1, source_target_pairs={{0,4},{1,5},{2,6},{3,7},{4,0},{5,1},{6,2},{7,3},{8,12},{9,13},{10,... | collective-permute-start | bytes 1916936 | tf_op jit(solution)/shard_map/ppermute | solution.py:44
  411.2 27.2 %collective-permute-start.56 = (bf16[448,384]{1,0:T(8,128)(2,1)}, bf16[448,384]{1,0:T(8,128)(2,1)}, u32[]{:S(2)}, u32[]{:S(2)}) collective-permute-start(bf16[448,384]{1,0:T(8,128)(2,1)} %dynamic-slice_convert_fusion.6), channel_id=1, source_target_pairs={{0,8},{1,9},{2,10},{3,11},{4,12},{5,13},{6,14},{7,15},{8,0},{9,1},... | collective-permute-start | bytes 1032200 | tf_op jit(solution)/shard_map/ppermute | solution.py:44
  413.2 27.4 %collective-permute-start.57 = (bf16[192,1536]{1,0:T(8,128)(2,1)}, bf16[192,1536]{1,0:T(8,128)(2,1)}, u32[]{:S(2)}, u32[]{:S(2)}) collective-permute-start(bf16[192,1536]{1,0:T(8,128)(2,1)} %pad_maximum_fusion.6), channel_id=1, source_target_pairs={{0,8},{1,9},{2,10},{3,11},{4,12},{5,13},{6,14},{7,15},{8,0},{9,1},... | collective-permute-start | bytes 1769480 | tf_op jit(solution)/shard_map/ppermute | solution.py:44
  415.9 22.5 %collective-permute-start.58 = (bf16[384,384]{1,0:T(8,128)(2,1)}, bf16[384,384]{1,0:T(8,128)(2,1)}, u32[]{:S(2)}, u32[]{:S(2)}) collective-permute-start(bf16[384,384]{1,0:T(8,128)(2,1)} %add_convert_fusion), channel_id=1, source_target_pairs={{0,16},{1,17},{2,18},{3,19},{4,20},{5,21},{6,22},{7,23},{8,24},{9,... | collective-permute-start | bytes 884744 | tf_op jit(solution)/shard_map/ppermute | solution.py:44
  442.8 10.5 %collective-permute-start.59 = (bf16[224,384]{1,0:T(8,128)(2,1)}, bf16[224,384]{1,0:T(8,128)(2,1)}, u32[]{:S(2)}, u32[]{:S(2)}) collective-permute-start(bf16[224,384]{1,0:T(8,128)(2,1)} %dynamic-slice_convert_fusion.10), channel_id=1, source_target_pairs={{0,16},{1,17},{2,18},{3,19},{4,20},{5,21},{6,22},{7,23},{8,24},{9,... | collective-permute-start | bytes 516104 | tf_op jit(solution)/shard_map/ppermute | solution.py:44
  446.1 14.1 %collective-permute-start.60 = (bf16[416,384]{1,0:T(8,128)(2,1)}, bf16[416,384]{1,0:T(8,128)(2,1)}, u32[]{:S(2)}, u32[]{:S(2)}) collective-permute-start(bf16[416,384]{1,0:T(8,128)(2,1)} %dynamic-slice_convert_fusion.7), channel_id=1, source_target_pairs={{0,8},{1,9},{2,10},{3,11},{4,12},{5,13},{6,14},{7,15},{8,0},{9,1},... | collective-permute-start | bytes 958472 | tf_op jit(solution)/shard_map/ppermute | solution.py:44
  448.2 23.2 %collective-permute-start.61 = (bf16[768,384]{1,0:T(8,128)(2,1)S(1)}, bf16[768,384]{1,0:T(8,128)(2,1)}, u32[]{:S(2)}, u32[]{:S(2)}) collective-permute-start(bf16[768,384]{1,0:T(8,128)(2,1)S(1)} %pad_maximum_fusion.7), channel_id=1, source_target_pairs={{0,8},{1,9},{2,10},{3,11},{4,12},{5,13},{6,14},{7,15},{8,0},{9,1},... | collective-permute-start | bytes 1769480 | tf_op jit(solution)/shard_map/ppermute | solution.py:44
  450.8 37.1 %collective-permute-start.63 = (bf16[384,1536]{1,0:T(8,128)(2,1)S(1)}, bf16[384,1536]{1,0:T(8,128)(2,1)}, u32[]{:S(2)}, u32[]{:S(2)}) collective-permute-start(bf16[384,1536]{1,0:T(8,128)(2,1)S(1)} %pad_maximum_fusion.1), channel_id=1, source_target_pairs={{0,4},{1,5},{2,6},{3,7},{4,0},{5,1},{6,2},{7,3},{8,12},{9,13},{10,... | collective-permute-start | bytes 3538952 | tf_op jit(solution)/shard_map/ppermute | solution.py:44
  472.3 15.5 %collective-permute-start.64 = (bf16[224,384]{1,0:T(8,128)(2,1)S(1)}, bf16[224,384]{1,0:T(8,128)(2,1)}, u32[]{:S(2)}, u32[]{:S(2)}) collective-permute-start(bf16[224,384]{1,0:T(8,128)(2,1)S(1)} %add_convert_fusion.2), channel_id=1, source_target_pairs={{0,16},{1,17},{2,18},{3,19},{4,20},{5,21},{6,22},{7,23},{8,24},{9,... | collective-permute-start | bytes 516104 | tf_op jit(solution)/shard_map/ppermute | solution.py:44
  474.7 28.1 %collective-permute-start.67 = (bf16[1536,384]{1,0:T(8,128)(2,1)}, bf16[1536,384]{1,0:T(8,128)(2,1)}, u32[]{:S(2)}, u32[]{:S(2)}) collective-permute-start(bf16[1536,384]{1,0:T(8,128)(2,1)} %pad_maximum_fusion.2), channel_id=1, source_target_pairs={{0,4},{1,5},{2,6},{3,7},{4,0},{5,1},{6,2},{7,3},{8,12},{9,13},{10,... | collective-permute-start | bytes 3538952 | tf_op jit(solution)/shard_map/ppermute | solution.py:44
  476.8 11.0 %collective-permute-start.65 = (bf16[208,384]{1,0:T(8,128)(2,1)S(1)}, bf16[208,384]{1,0:T(8,128)(2,1)}, u32[]{:S(2)}, u32[]{:S(2)}) collective-permute-start(bf16[208,384]{1,0:T(8,128)(2,1)S(1)} %dynamic-slice_convert_fusion.11), channel_id=1, source_target_pairs={{0,16},{1,17},{2,18},{3,19},{4,20},{5,21},{6,22},{7,23},{8,24},{9,... | collective-permute-start | bytes 479240 | tf_op jit(solution)/shard_map/ppermute | solution.py:44
  488.8 13.2 %collective-permute-start.68 = (bf16[448,384]{1,0:T(8,128)(2,1)S(1)}, bf16[448,384]{1,0:T(8,128)(2,1)}, u32[]{:S(2)}, u32[]{:S(2)}) collective-permute-start(bf16[448,384]{1,0:T(8,128)(2,1)S(1)} %pad_maximum_fusion.8), channel_id=1, source_target_pairs={{0,8},{1,9},{2,10},{3,11},{4,12},{5,13},{6,14},{7,15},{8,0},{9,1},... | collective-permute-start | bytes 1032200 | tf_op jit(solution)/shard_map/ppermute | solution.py:44
  489.9 9.9 %collective-permute-start.69 = (bf16[208,384]{1,0:T(8,128)(2,1)S(1)}, bf16[208,384]{1,0:T(8,128)(2,1)S(1)}, u32[]{:S(2)}, u32[]{:S(2)}) collective-permute-start(bf16[208,384]{1,0:T(8,128)(2,1)S(1)} %add_convert_fusion.3), channel_id=1, source_target_pairs={{0,16},{1,17},{2,18},{3,19},{4,20},{5,21},{6,22},{7,23},{8,24},{9,... | collective-permute-start | bytes 479240 | tf_op jit(solution)/shard_map/ppermute | solution.py:44
  503.9 10.2 %collective-permute-start.72 = (bf16[416,384]{1,0:T(8,128)(2,1)S(1)}, bf16[416,384]{1,0:T(8,128)(2,1)S(1)}, u32[]{:S(2)}, u32[]{:S(2)}) collective-permute-start(bf16[416,384]{1,0:T(8,128)(2,1)S(1)} %pad_maximum_fusion.9), channel_id=1, source_target_pairs={{0,8},{1,9},{2,10},{3,11},{4,12},{5,13},{6,14},{7,15},{8,0},{9,1},... | collective-permute-start | bytes 958472 | tf_op jit(solution)/shard_map/ppermute | solution.py:44
  507.3 18.9 %collective-permute-start.74 = (bf16[896,384]{1,0:T(8,128)(2,1)}, bf16[896,384]{1,0:T(8,128)(2,1)}, u32[]{:S(2)}, u32[]{:S(2)}) collective-permute-start(bf16[896,384]{1,0:T(8,128)(2,1)} %pad_maximum_fusion.5), channel_id=1, source_target_pairs={{0,4},{1,5},{2,6},{3,7},{4,0},{5,1},{6,2},{7,3},{8,12},{9,13},{10,... | collective-permute-start | bytes 2064392 | tf_op jit(solution)/shard_map/ppermute | solution.py:44
  516.9 20.6 %collective-permute-start.75 = (bf16[832,384]{1,0:T(8,128)(2,1)}, bf16[832,384]{1,0:T(8,128)(2,1)}, u32[]{:S(2)}, u32[]{:S(2)}) collective-permute-start(bf16[832,384]{1,0:T(8,128)(2,1)} %pad_maximum_fusion.4), channel_id=1, source_target_pairs={{0,4},{1,5},{2,6},{3,7},{4,0},{5,1},{6,2},{7,3},{8,12},{9,13},{10,... | collective-permute-start | bytes 1916936 | tf_op jit(solution)/shard_map/ppermute | solution.py:44
  (139 other events, 903.9 us)

commit v4 on v3

--- a/solution.py
+++ b/solution.py
@@ -1165,6 +1165,7 @@
     for (d, e), place in where.items():
         block = ring.relative(packed, d, e)
         spread = lax.dynamic_update_slice_in_dim(spread, block[None], place, axis=0)
+    clock.defer(ring.fsdp - 1)
     spread = spread.reshape(ring.fsdp, -1)
     whole_small, at = [], 0
     for part in small:
@@ -1179,9 +1180,8 @@
 
     gate_pieces = Pieces(ring, in_rows[:INNER], 3)
     out_spread = Spread(ring, out_weight, 0, whole_only=True)
-    (spread,) = clock.tick(spread)
+    clock.tick()
     shared.second()
-    near_out = ring.core(clock.now(out_weight))
     out_spread.first()
     clock.tick()
     shared.third()
@@ -1212,6 +1212,8 @@
     projected = project(normed_columns, list(weight_conv.values()), tile, PROJ - INNER)
     (projected,) = clock.tick(projected)
     edge_rows = ring.next_block(projected[row_count - 8 :, :CHANNELS], 1)
+    near_out = ring.core(clock.now(out_weight))
+    clock.defer()
     cum, weigh, decay, cum_rows, step_rows, through = steps(projected, step_bias, rate_log)
     cum, weigh, edge_rows = clock.tick(cum, weigh, edge_rows)
     gate_pieces.send(later=1)
@@ -1341,6 +1343,7 @@
     total_first.step()
     total_w_out.step()
     total_w_gate.step()
+    clock.defer(2)
     grad_shards = to_model(
         grad_gate, clock.now(grad_tail), list(weight_gate.values()), [
             (array, block * tile) for array, block in weight_conv.values()

time: 552 us -> 535 us (0.969)
  local copies, waits for them, and re-layouts: 81.3 us -> 69.1 us
  waiting for transfers between devices: 172 us -> 165 us
    ppermute x76, waiting for transfers between devices: 168 us -> 160 us  [send(): arrived = lax.ppermute(block, ('seq', 'fsdp'), route)]
    unnamed x248 -> x232, local copies, waits for them, and re-layouts: 40.7 us -> 34 us
  transfers between devices with their start and end apart: 80 -> 80, of which waited for: 32 -> 33; matrix products, arithmetic and copies ran while one was open for 15% -> 14% of each run, Pallas kernels for 25% -> 27%
where the time goes in v4:
time: 535 us; the launch traced here: 525 us
  waiting for transfers between devices  165 us (31%)
  Pallas kernels  146 us (27%)
  starting transfers between devices  94.8 us (18%)
  local copies, waits for them, and re-layouts  69.1 us (13%)
  other arithmetic  46 us (9%)
    ppermute x76, waiting for transfers between devices, send(): arrived = lax.ppermute(block, ('seq', 'fsdp'), route)  160 us
    ppermute x76, starting transfers between devices, send(): arrived = lax.ppermute(block, ('seq', 'fsdp'), route)  74.2 us
    unnamed x232, local copies, waits for them, and re-layouts  34 us
    pallas_call x1, Pallas kernels, inside_back(): pl.pallas_call(inside_back_body, grid=(pairs,), in_specs=[columns, column...  27.6 us
    pallas_call x4, Pallas kernels, weight_grad(): pl.pallas_call(functools.partial(sum_body, len(keys)), grid=(rows // tile...  17.7 us
    pallas_call x4, Pallas kernels, project(): pl.pallas_call(functools.partial(project_body, count), grid=(pl.cdiv(widt...  15.6 us
    pallas_call x1, Pallas kernels, turn(): pl.pallas_call(turn_body, grid=(2, groups), in_specs=[pl.BlockSpec((token...  15.4 us
    pallas_call x1, Pallas kernels, leave(): pl.pallas_call(functools.partial(leave_body, steps), grid=(steps + 1,), i...  15.1 us
  transfers between devices with their start and end apart: 80, of which 33 were waited for; matrix products, arithmetic and copies ran while one was open for 14% of the time, Pallas kernels for 27%

profile of v4, /device:TPU:0, one launch (start us, length us, event | category | flops | bytes accessed | tf_op | source)
XLA Modules:
  0.0 524.6 jit_solution(1383075969888787175)
XLA Ops:
  2.4 2.7 collective-permute-start
  5.9 4.1 concatenate.39
  12.5 3.1 fusion.11
  15.6 4.7 collective-permute-done.refs_0_
  25.9 13.9 %collective-permute-done.3 = bf16[48,128]{1,0:T(8,128)(2,1)S(1)} collective-permute-done((bf16[48,128]{1,0:T(8,128)(2,1)S(1)}, bf16[48,128]{1,0:T(8,128)(2,1)S(1)}, u32[]{:S(2)}, u32[]{:S(2)}) %collective-permute-start.3) | collective-permute-done | bytes 12320 | tf_op jit(solution)/shard_map/ppermute | solution.py:44
  40.8 2.2 collective-permute-done.4
  48.6 7.4 %collective-permute-done.10.refs_4_ = bf16[416,384]{1,0:T(8,128)(2,1)} collective-permute-done((bf16[416,384]{1,0:T(8,128)(2,1)}, bf16[416,384]{1,0:T(8,128)(2,1)}, u32[]{:S(2)}, u32[]{:S(2)}) %collective-permute-start.10) | collective-permute-done | bytes 319520 | tf_op jit(solution)/shard_map/ppermute | solution.py:44
  60.4 2.5 laid.2
  63.0 6.9 %project.4.dt_ref.proj_ref = bf16[256,3376]{1,0:T(8,128)(2,1)S(1)} custom-call(bf16[256,384]{1,0:T(8,128)(2,1)S(1)} %get-tuple-element.277.refs_0_.refs_4_, bf16[256,384]{1,0:T(8,128)(2,1)S(1)} %get-tuple-element.258.refs_1_, bf16[256,384]{1,0:T(8,128)(2,1)S(1)} %get-tuple-element.413.refs_2_, bf16[256,384]{1,0:T(8,128)(2,1)S(1)} %get-tuple-element.412.refs_3_, ...), custom_call_target="tpu_custom_call" | custom-call | tf_op jit(solution)/shard_map/project/pallas_call | solution.py:396
  74.7 2.7 collective-permute-start.18
  83.3 3.8 enter.1
  88.3 3.8 collective-permute-done.19.refs_6_.refs_4_
  92.1 4.2 all-to-all-start
  106.4 10.7 %inside.1.base_ref = f32[256,3072]{1,0:T(8,128)S(1)} custom-call(bf16[256,3328]{1,0:T(8,128)(2,1)S(1)} %get-tuple-element.228.x_ref.b_ref.c_ref.low_ref, bf16[256,3328]{1,0:T(8,128)(2,1)S(1)} %get-tuple-element.228.x_ref.b_ref.c_ref.low_ref, bf16[256,3328]{1,0:T(8,128)(2,1)S(1)} %get-tuple-element.228.x_ref.b_ref.c_ref.low_ref, f32[256,128]{1,0:T(8,128)S(1)} %copy-done.48, ...), custom_call_target="tpu_custom_call" | custom-call | tf_op jit(solution)/shard_map/inside/pallas_call | solution.py:829
  118.9 10.4 %collective-permute-done.23.refs_4_ = bf16[96,1536]{1,0:T(8,128)(2,1)} collective-permute-done((bf16[96,1536]{1,0:T(8,128)(2,1)}, bf16[96,1536]{1,0:T(8,128)(2,1)}, u32[]{:S(2)}, u32[]{:S(2)}) %collective-permute-start.23) | collective-permute-done | bytes 294944 | tf_op jit(solution)/shard_map/ppermute | solution.py:44
  129.3 4.7 all-to-all-done.blocks_ref
  135.0 3.7 laid.3.refs_2_.refs_6_
  139.3 4.1 all-to-all-start.1
  146.9 2.4 copy-done
  149.3 2.9 project.5.refs_0_
  153.0 2.9 project.6.refs_1_
  156.7 2.9 project.7.refs_2_
  160.4 10.1 %to_inner.1.grad_ref = f32[256,3072]{1,0:T(8,128)S(1)} custom-call(s32[4]{0:T(128)S(1)} %pad_add_fusion.1.place_ref, bf16[256,1536]{1,0:T(8,128)(2,1)S(1)} %bitcast_select_fusion.grad_ref.refs_4_, bf16[768,1536]{1,0:T(8,128)(2,1)} %refs_4_.1, bf16[768,1536]{1,0:T(8,128)(2,1)} %collective-permute-done.20.refs_1_.refs_5_, ...), custom_call_target="tpu_custom_call" | custom-call | tf_op jit(solution)/shard_map/to_inner/pallas_call | solution.py:264
  176.3 15.4 %turn.1 = (bf16[256,3072]{1,0:T(8,128)(2,1)}, bf16[256,3072]{1,0:T(8,128)(2,1)}, bf16[256,3072]{1,0:T(8,128)(2,1)}, bf16[256,3072]{1,0:T(8,128)(2,1)}, f32[3072,128]{1,0:T(8,128)}, /*index=5*/f32[1,3072]{1,0:T(1,128)}) custom-call(f32[256,3072]{1,0:T(8,128)} %copy-done.12, bf16[3072,128]{1,0:T(8,128)(2,1)} %bitcast.86, bf16[256,128]{1,0:T(8,128)(2,1)} %slice.130.c_ref, ...), custom_call_target="tpu_custom_call" | custom-call | tf_op jit(solution)/shard_map/turn/pallas_call | solution.py:947
  193.1 5.8 %all-to-all-start.2 = ((f32[8,384,128]{2,1,0:T(8,128)}), f32[8,384,128]{2,1,0:T(8,128)}, u32[]{:S(2)}, u32[]{:S(2)}) async-start(f32[8,384,128]{2,1,0:T(8,128)} %bitcast.91), calls=%async_computation.2 | async-start | bytes 3145728 | tf_op jit(solution)/shard_map/all_to_all | solution.py:1265
  199.5 2.7 constant_dynamic-slice_fusion.1
  205.6 27.6 %inside_back.1 = (f32[256,3072]{1,0:T(8,128)S(1)}, f32[256,128]{1,0:T(8,128)S(1)}, f32[256,128]{1,0:T(8,128)S(1)}, f32[48,256]{1,0:T(8,128)S(1)}, f32[48,256]{1,0:T(8,128)S(1)}, /*index=5*/f32[1,3072]{1,0:T(1,128)S(1)}) custom-call(bf16[256,3072]{1,0:T(8,128)(2,1)S(1)} %copy-done.41, bf16[256,3072]{1,0:T(8,128)(2,1)S(1)} %copy-done.42, ...), custom_call_target="tpu_custom_call" | custom-call | tf_op jit(solution)/shard_map/inside_back/pallas_call | solution.py:911
  238.2 2.6 carried.3
  241.4 6.5 %all-to-all-start.3 = ((bf16[8,384,128]{2,1,0:T(8,128)(2,1)}), bf16[8,384,128]{2,1,0:T(8,128)(2,1)}, u32[]{:S(2)}, u32[]{:S(2)}) async-start(bf16[8,384,128]{2,1,0:T(8,128)(2,1)} %carried.3), calls=%async_computation.3 | async-start | bytes 1572864 | tf_op jit(solution)/shard_map/all_to_all | solution.py:543
  247.9 4.3 collective-permute-done.39.refs_3_
  252.2 4.8 weight_grad.5
  257.0 2.2 copy-done.6
  261.7 5.8 %weight_grad.4 = f32[3072,384]{1,0:T(8,128)S(1)} custom-call(bf16[256,3072]{1,0:T(8,128)(2,1)S(1)} %copy-done.19, bf16[256,3072]{1,0:T(8,128)(2,1)} %collective-permute-done.34.refs_1_, bf16[256,3072]{1,0:T(8,128)(2,1)} %collective-permute-done.35.refs_2_, bf16[256,3072]{1,0:T(8,128)(2,1)} %collective-permute-done.36.refs_3_, ...), custom_call_target="tpu_custom_call" | custom-call | tf_op jit(solution)/shard_map/weight_grad/pallas_call | solution.py:236
  267.6 2.2 copy-done.7
  270.9 7.2 %output_rows.1 = bf16[256,1536]{1,0:T(8,128)(2,1)} custom-call(bf16[256,1536]{1,0:T(8,128)(2,1)S(1)} %bitcast.85, bf16[256,768]{1,0:T(8,128)(2,1)S(1)} %get-tuple-element.405.refs_0_, bf16[256,768]{1,0:T(8,128)(2,1)S(1)} %get-tuple-element.404.refs_1_, bf16[256,768]{1,0:T(8,128)(2,1)S(1)} %get-tuple-element.403.refs_2_, ...), custom_call_target="tpu_custom_call" | custom-call | tf_op jit(solution)/shard_map/output_rows/pallas_call | solution.py:342
  278.2 11.6 %collective-permute-done.40 = bf16[384,1536]{1,0:T(8,128)(2,1)} collective-permute-done((bf16[384,1536]{1,0:T(8,128)(2,1)}, bf16[384,1536]{1,0:T(8,128)(2,1)}, u32[]{:S(2)}, u32[]{:S(2)}) %collective-permute-start.40) | collective-permute-done | bytes 1179680 | tf_op jit(solution)/shard_map/ppermute | solution.py:44
  289.7 2.8 dynamic-slice_convert_fusion
  292.6 2.2 collective-permute-start.41
  294.8 2.3 convert_add_fusion.1
  299.2 15.1 %leave.1 = (bf16[256,1792]{1,0:T(8,128)(2,1)}, bf16[256,1536]{1,0:T(8,128)(2,1)}, f32[8,3328]{1,0:T(8,128)}, f32[8,3328]{1,0:T(8,128)}, f32[4,3328]{1,0:T(4,128)...) custom-call(bf16[256,3376]{1,0:T(8,128)(2,1)} %copy-done.2, bf16[8,3328]{1,0:T(8,128)(2,1)} %copy-done.59, ...), custom_call_target="tpu_custom_call" | custom-call | tf_op jit(solution)/shard_map/leave/pallas_call | solution.py:1080
  314.3 7.0 %collective-permute-done.41 = bf16[1536,384]{1,0:T(8,128)(2,1)} collective-permute-done((bf16[1536,384]{1,0:T(8,128)(2,1)}, bf16[1536,384]{1,0:T(8,128)(2,1)}, u32[]{:S(2)}, u32[]{:S(2)}) %collective-permute-start.41) | collective-permute-done | bytes 1179680 | tf_op jit(solution)/shard_map/ppermute | solution.py:44
  324.4 3.9 collective-permute-done.43
  329.0 2.3 convert_add_fusion
  333.1 3.0 collective-permute-start.44
  337.1 15.5 %collective-permute-done.44 = bf16[96,1536]{1,0:T(8,128)(2,1)S(1)} collective-permute-done((bf16[96,1536]{1,0:T(8,128)(2,1)S(1)}, bf16[96,1536]{1,0:T(8,128)(2,1)S(1)}, u32[]{:S(2)}, u32[]{:S(2)}) %collective-permute-start.44) | collective-permute-done | bytes 294944 | tf_op jit(solution)/shard_map/ppermute | solution.py:44
  358.1 3.9 weight_grad.6
  362.1 2.7 collective-permute-start.51
  368.2 13.0 %to_model.1 = f32[4,256,384]{2,1,0:T(8,128)S(1)} custom-call(bf16[256,3072]{1,0:T(8,128)(2,1)S(1)} %copy-done.20, bf16[256,3376]{1,0:T(8,128)(2,1)S(1)} %pad_maximum_fusion.tail_ref, bf16[6448,384]{1,0:T(8,128)(2,1)} %bitcast.78, bf16[6448,384]{1,0:T(8,128)(2,1)} %collective-permute-done.1.refs_5_.refs_1_, bf16[3376,384]{1,0:T(8,128)(2,1)S(1)} %copy-done.15, ...), custom_call_target="tpu_custom_call" | custom-call | tf_op jit(solution)/shard_map/to_model/pallas_call | solution.py:321
  383.6 3.2 weight_grad.7
  388.4 4.9 collective-permute-done.54
  404.3 17.8 %collective-permute-done.58 = bf16[384,384]{1,0:T(8,128)(2,1)} collective-permute-done((bf16[384,384]{1,0:T(8,128)(2,1)}, bf16[384,384]{1,0:T(8,128)(2,1)}, u32[]{:S(2)}, u32[]{:S(2)}) %collective-permute-start.58) | collective-permute-done | bytes 294944 | tf_op jit(solution)/shard_map/ppermute | solution.py:44
  422.1 2.2 collective-permute-done.57
  435.7 6.0 %collective-permute-done.60 = bf16[416,384]{1,0:T(8,128)(2,1)} collective-permute-done((bf16[416,384]{1,0:T(8,128)(2,1)}, bf16[416,384]{1,0:T(8,128)(2,1)}, u32[]{:S(2)}, u32[]{:S(2)}) %collective-permute-start.60) | collective-permute-done | bytes 319520 | tf_op jit(solution)/shard_map/ppermute | solution.py:44
  441.7 10.8 %collective-permute-done.61 = bf16[768,384]{1,0:T(8,128)(2,1)} collective-permute-done((bf16[768,384]{1,0:T(8,128)(2,1)S(1)}, bf16[768,384]{1,0:T(8,128)(2,1)}, u32[]{:S(2)}, u32[]{:S(2)}) %collective-permute-start.61) | collective-permute-done | bytes 589856 | tf_op jit(solution)/shard_map/ppermute | solution.py:44
  462.2 7.5 %collective-permute-done.65 = bf16[208,384]{1,0:T(8,128)(2,1)} collective-permute-done((bf16[208,384]{1,0:T(8,128)(2,1)S(1)}, bf16[208,384]{1,0:T(8,128)(2,1)}, u32[]{:S(2)}, u32[]{:S(2)}) %collective-permute-start.65) | collective-permute-done | bytes 159776 | tf_op jit(solution)/shard_map/ppermute | solution.py:44
  471.8 2.8 collective-permute-start.69
  477.3 2.8 collective-permute-done.66
  481.2 2.3 collective-permute-done.68
  491.4 2.1 collective-permute-start.74
  495.4 2.7 collective-permute-done.71
  502.1 2.8 maximum_convert_fusion
  511.4 2.3 convert_dynamic-update-slice_fusion.1
  513.7 7.2 %collective-permute-done.75 = bf16[832,384]{1,0:T(8,128)(2,1)} collective-permute-done((bf16[832,384]{1,0:T(8,128)(2,1)}, bf16[832,384]{1,0:T(8,128)(2,1)}, u32[]{:S(2)}, u32[]{:S(2)}) %collective-permute-start.75) | collective-permute-done | bytes 639008 | tf_op jit(solution)/shard_map/ppermute | solution.py:44
  522.2 2.2 convert_dynamic-update-slice_fusion.4
  (491 shorter events, 152.1 us)
Async XLA Ops:
  0.7 19.7 %collective-permute-start.1 = (bf16[6448,384]{1,0:T(8,128)(2,1)}, bf16[6448,384]{1,0:T(8,128)(2,1)}, u32[]{:S(2)}, u32[]{:S(2)}) collective-permute-start(bf16[6448,384]{1,0:T(8,128)(2,1)} %bitcast.76), channel_id=1, source_target_pairs={{0,1},{1,0},{2,3},{3,2},{4,5},{5,4},{6,7},{7,6},{8,9},{9,8},{10,11... | collective-permute-start | bytes 14856200 | tf_op jit(solution)/shard_map/ppermute | solution.py:44
  2.4 17.9 %collective-permute-start = (bf16[848,384]{1,0:T(8,128)(2,1)S(1)}, bf16[848,384]{1,0:T(8,128)(2,1)S(1)}, u32[]{:S(2)}, u32[]{:S(2)}) collective-permute-start(bf16[848,384]{1,0:T(8,128)(2,1)S(1)} %dynamic-slice_bitcast_fusion), channel_id=1, source_target_pairs={{0,2},{1,3},{2,0},{3,1},{4,6},{5,7},{6,4},{7,5},{8,10},{9,11},{10,... | collective-permute-start | bytes 1953800 | tf_op jit(solution)/shard_map/ppermute | solution.py:44
  10.1 15.1 %collective-permute-start.2 = (bf16[48,128]{1,0:T(8,128)(2,1)S(1)}, bf16[48,128]{1,0:T(8,128)(2,1)S(1)}, u32[]{:S(2)}, u32[]{:S(2)}) collective-permute-start(bf16[48,128]{1,0:T(8,128)(2,1)S(1)} %pad_bitcast_fusion.1), channel_id=1, source_target_pairs={{0,1},{1,0},{2,3},{3,2},{4,5},{5,4},{6,7},{7,6},{8,9},{9,8},{10,11... | collective-permute-start | bytes 36872 | tf_op jit(solution)/shard_map/ppermute | solution.py:44
  20.3 22.7 %collective-permute-start.5 = (bf16[848,384]{1,0:T(8,128)(2,1)S(1)}, bf16[848,384]{1,0:T(8,128)(2,1)S(1)}, u32[]{:S(2)}, u32[]{:S(2)}) collective-permute-start(bf16[848,384]{1,0:T(8,128)(2,1)S(1)} %collective-permute-done.refs_0_), channel_id=1, source_target_pairs={{0,4},{1,5},{2,6},{3,7},{4,0},{5,1},{6,2},{7,3},{8,12},{9,13},{10,... | collective-permute-start | bytes 1953800 | tf_op jit(solution)/shard_map/ppermute | solution.py:44
  22.0 21.0 %collective-permute-start.6 = (bf16[848,384]{1,0:T(8,128)(2,1)S(1)}, bf16[848,384]{1,0:T(8,128)(2,1)S(1)}, u32[]{:S(2)}, u32[]{:S(2)}) collective-permute-start(bf16[848,384]{1,0:T(8,128)(2,1)S(1)} %collective-permute-done.refs_0_), channel_id=1, source_target_pairs={{0,8},{1,9},{2,10},{3,11},{4,12},{5,13},{6,14},{7,15},{8,0},{9,1},... | collective-permute-start | bytes 1953800 | tf_op jit(solution)/shard_map/ppermute | solution.py:44
  23.6 19.4 %collective-permute-start.7 = (bf16[848,384]{1,0:T(8,128)(2,1)S(1)}, bf16[848,384]{1,0:T(8,128)(2,1)S(1)}, u32[]{:S(2)}, u32[]{:S(2)}) collective-permute-start(bf16[848,384]{1,0:T(8,128)(2,1)S(1)} %collective-permute-done.refs_0_), channel_id=1, source_target_pairs={{0,1},{1,0},{2,3},{3,2},{4,5},{5,4},{6,7},{7,6},{8,9},{9,8},{10,11... | collective-permute-start | bytes 1953800 | tf_op jit(solution)/shard_map/ppermute | solution.py:44
  23.6 19.4 %collective-permute-start.8 = (bf16[192,1536]{1,0:T(8,128)(2,1)}, bf16[192,1536]{1,0:T(8,128)(2,1)}, u32[]{:S(2)}, u32[]{:S(2)}) collective-permute-start(bf16[192,1536]{1,0:T(8,128)(2,1)} %constant_dynamic-slice_fusion.15), channel_id=1, source_target_pairs={{0,2},{1,3},{2,0},{3,1},{4,6},{5,7},{6,4},{7,5},{8,10},{9,11},{10,... | collective-permute-start | bytes 1769480 | tf_op jit(solution)/shard_map/ppermute | solution.py:44
  25.2 14.6 %collective-permute-start.3 = (bf16[48,128]{1,0:T(8,128)(2,1)S(1)}, bf16[48,128]{1,0:T(8,128)(2,1)S(1)}, u32[]{:S(2)}, u32[]{:S(2)}) collective-permute-start(bf16[48,128]{1,0:T(8,128)(2,1)S(1)} %pad_bitcast_fusion.1), channel_id=1, source_target_pairs={{0,2},{1,3},{2,0},{3,1},{4,6},{5,7},{6,4},{7,5},{8,10},{9,11},{10,... | collective-permute-start | bytes 36872 | tf_op jit(solution)/shard_map/ppermute | solution.py:44
  43.9 12.2 %collective-permute-start.11 = (bf16[848,384]{1,0:T(8,128)(2,1)S(1)}, bf16[848,384]{1,0:T(8,128)(2,1)}, u32[]{:S(2)}, u32[]{:S(2)}) collective-permute-start(bf16[848,384]{1,0:T(8,128)(2,1)S(1)} %collective-permute-done.5.refs_1_), channel_id=1, source_target_pairs={{0,1},{1,0},{2,3},{3,2},{4,5},{5,4},{6,7},{7,6},{8,9},{9,8},{10,11... | collective-permute-start | bytes 1953800 | tf_op jit(solution)/shard_map/ppermute | solution.py:44
  44.0 12.1 %collective-permute-start.12 = (bf16[848,384]{1,0:T(8,128)(2,1)S(1)}, bf16[848,384]{1,0:T(8,128)(2,1)}, u32[]{:S(2)}, u32[]{:S(2)}) collective-permute-start(bf16[848,384]{1,0:T(8,128)(2,1)S(1)} %collective-permute-done.6.refs_2_), channel_id=1, source_target_pairs={{0,1},{1,0},{2,3},{3,2},{4,5},{5,4},{6,7},{7,6},{8,9},{9,8},{10,11... | collective-permute-start | bytes 1953800 | tf_op jit(solution)/shard_map/ppermute | solution.py:44
  45.9 10.1 %collective-permute-start.9 = (bf16[432,384]{1,0:T(8,128)(2,1)}, bf16[432,384]{1,0:T(8,128)(2,1)}, u32[]{:S(2)}, u32[]{:S(2)}) collective-permute-start(bf16[432,384]{1,0:T(8,128)(2,1)} %slice.114), channel_id=1, source_target_pairs={{0,4},{1,5},{2,6},{3,7},{4,0},{5,1},{6,2},{7,3},{8,12},{9,13},{10,... | collective-permute-start | bytes 995336 | tf_op jit(solution)/shard_map/ppermute | solution.py:44
  46.7 23.2 %collective-permute-start.13 = (bf16[1024,384]{1,0:T(8,128)(2,1)}, bf16[1024,384]{1,0:T(8,128)(2,1)}, u32[]{:S(2)}, u32[]{:S(2)}) collective-permute-start(bf16[1024,384]{1,0:T(8,128)(2,1)} %get-tuple-element.208), channel_id=1, source_target_pairs={{0,2},{1,3},{2,0},{3,1},{4,6},{5,7},{6,4},{7,5},{8,10},{9,11},{10,... | collective-permute-start | bytes 2359304 | tf_op jit(solution)/shard_map/ppermute | solution.py:44
  56.1 14.8 %collective-permute-start.16 = (bf16[192,1536]{1,0:T(8,128)(2,1)}, bf16[192,1536]{1,0:T(8,128)(2,1)}, u32[]{:S(2)}, u32[]{:S(2)}) collective-permute-start(bf16[192,1536]{1,0:T(8,128)(2,1)} %collective-permute-done.8.refs_0_), channel_id=1, source_target_pairs={{0,4},{1,5},{2,6},{3,7},{4,0},{5,1},{6,2},{7,3},{8,12},{9,13},{10,... | collective-permute-start | bytes 1769480 | tf_op jit(solution)/shard_map/ppermute | solution.py:44
  57.6 14.2 %collective-permute-start.17 = (bf16[192,1536]{1,0:T(8,128)(2,1)}, bf16[192,1536]{1,0:T(8,128)(2,1)}, u32[]{:S(2)}, u32[]{:S(2)}) collective-permute-start(bf16[192,1536]{1,0:T(8,128)(2,1)} %collective-permute-done.8.refs_0_), channel_id=1, source_target_pairs={{0,8},{1,9},{2,10},{3,11},{4,12},{5,13},{6,14},{7,15},{8,0},{9,1},... | collective-permute-start | bytes 1769480 | tf_op jit(solution)/shard_map/ppermute | solution.py:44
  71.9 20.3 %collective-permute-start.20 = (bf16[768,1536]{1,0:T(8,128)(2,1)}, bf16[768,1536]{1,0:T(8,128)(2,1)}, u32[]{:S(2)}, u32[]{:S(2)}) collective-permute-start(bf16[768,1536]{1,0:T(8,128)(2,1)} %refs_4_.1), channel_id=1, source_target_pairs={{0,1},{1,0},{2,3},{3,2},{4,5},{5,4},{6,7},{7,6},{8,9},{9,8},{10,11... | collective-permute-start | bytes 7077896 | tf_op jit(solution)/shard_map/ppermute | solution.py:44
  71.9 20.3 %collective-permute-start.19 = (bf16[1024,384]{1,0:T(8,128)(2,1)}, bf16[1024,384]{1,0:T(8,128)(2,1)}, u32[]{:S(2)}, u32[]{:S(2)}) collective-permute-start(bf16[1024,384]{1,0:T(8,128)(2,1)} %get-tuple-element.224), channel_id=1, source_target_pairs={{0,2},{1,3},{2,0},{3,1},{4,6},{5,7},{6,4},{7,5},{8,10},{9,11},{10,... | collective-permute-start | bytes 2359304 | tf_op jit(solution)/shard_map/ppermute | solution.py:44
  92.1 41.8 %all-to-all-start = ((f32[8,392,128]{2,1,0:T(8,128)}), f32[8,392,128]{2,1,0:T(8,128)S(1)}, u32[]{:S(2)}, u32[]{:S(2)}) async-start(f32[8,392,128]{2,1,0:T(8,128)} %copy-done.39), calls=%async_computation | async-start | bytes 3211264 | tf_op jit(solution)/shard_map/all_to_all | solution.py:1232
  96.4 22.5 %collective-permute-start.21 = (bf16[1024,384]{1,0:T(8,128)(2,1)}, bf16[1024,384]{1,0:T(8,128)(2,1)}, u32[]{:S(2)}, u32[]{:S(2)}) collective-permute-start(bf16[1024,384]{1,0:T(8,128)(2,1)} %get-tuple-element.232), channel_id=1, source_target_pairs={{0,2},{1,3},{2,0},{3,1},{4,6},{5,7},{6,4},{7,5},{8,10},{9,11},{10,... | collective-permute-start | bytes 2359304 | tf_op jit(solution)/shard_map/ppermute | solution.py:44
  98.0 31.4 %collective-permute-start.24 = (bf16[1024,384]{1,0:T(8,128)(2,1)}, bf16[1024,384]{1,0:T(8,128)(2,1)}, u32[]{:S(2)}, u32[]{:S(2)}) collective-permute-start(bf16[1024,384]{1,0:T(8,128)(2,1)} %collective-permute-done.13.refs_6_.refs_3_), channel_id=1, source_target_pairs={{0,1},{1,0},{2,3},{3,2},{4,5},{5,4},{6,7},{7,6},{8,9},{9,8},{10,11... | collective-permute-start | bytes 2359304 | tf_op jit(solution)/shard_map/ppermute | solution.py:44
  98.0 31.4 %collective-permute-start.25 = (bf16[1024,384]{1,0:T(8,128)(2,1)}, bf16[1024,384]{1,0:T(8,128)(2,1)}, u32[]{:S(2)}, u32[]{:S(2)}) collective-permute-start(bf16[1024,384]{1,0:T(8,128)(2,1)} %collective-permute-done.19.refs_6_.refs_4_), channel_id=1, source_target_pairs={{0,1},{1,0},{2,3},{3,2},{4,5},{5,4},{6,7},{7,6},{8,9},{9,8},{10,11... | collective-permute-start | bytes 2359304 | tf_op jit(solution)/shard_map/ppermute | solution.py:44
  100.2 18.7 %collective-permute-start.22 = (bf16[96,1536]{1,0:T(8,128)(2,1)}, bf16[96,1536]{1,0:T(8,128)(2,1)}, u32[]{:S(2)}, u32[]{:S(2)}) collective-permute-start(bf16[96,1536]{1,0:T(8,128)(2,1)} %slice.127), channel_id=1, source_target_pairs={{0,4},{1,5},{2,6},{3,7},{4,0},{5,1},{6,2},{7,3},{8,12},{9,13},{10,... | collective-permute-start | bytes 884744 | tf_op jit(solution)/shard_map/ppermute | solution.py:44
  103.9 25.4 %collective-permute-start.23 = (bf16[96,1536]{1,0:T(8,128)(2,1)}, bf16[96,1536]{1,0:T(8,128)(2,1)}, u32[]{:S(2)}, u32[]{:S(2)}) collective-permute-start(bf16[96,1536]{1,0:T(8,128)(2,1)} %slice.128), channel_id=1, source_target_pairs={{0,8},{1,9},{2,10},{3,11},{4,12},{5,13},{6,14},{7,15},{8,0},{9,1},... | collective-permute-start | bytes 884744 | tf_op jit(solution)/shard_map/ppermute | solution.py:44
  138.7 21.8 %collective-permute-start.26 = (bf16[768,1536]{1,0:T(8,128)(2,1)}, bf16[768,1536]{1,0:T(8,128)(2,1)}, u32[]{:S(2)}, u32[]{:S(2)}) collective-permute-start(bf16[768,1536]{1,0:T(8,128)(2,1)} %laid.3.refs_2_.refs_6_), channel_id=1, source_target_pairs={{0,1},{1,0},{2,3},{3,2},{4,5},{5,4},{6,7},{7,6},{8,9},{9,8},{10,11... | collective-permute-start | bytes 7077896 | tf_op jit(solution)/shard_map/ppermute | solution.py:44
  139.3 32.9 %all-to-all-start.1 = ((bf16[8,384,128]{2,1,0:T(8,128)(2,1)}), bf16[8,384,128]{2,1,0:T(8,128)(2,1)S(1)}, u32[]{:S(2)}, u32[]{:S(2)}) async-start(bf16[8,384,128]{2,1,0:T(8,128)(2,1)} %copy-done.28), calls=%async_computation.1 | async-start | bytes 1572864 | tf_op jit(solution)/shard_map/all_to_all | solution.py:543
  144.8 11.9 %collective-permute-start.27 = (bf16[1024,384]{1,0:T(8,128)(2,1)}, bf16[1024,384]{1,0:T(8,128)(2,1)S(1)}, u32[]{:S(2)}, u32[]{:S(2)}) collective-permute-start(bf16[1024,384]{1,0:T(8,128)(2,1)} %collective-permute-done.21.refs_6_.refs_5_), channel_id=1, source_target_pairs={{0,1},{1,0},{2,3},{3,2},{4,5},{5,4},{6,7},{7,6},{8,9},{9,8},{10,11... | collective-permute-start | bytes 2359304 | tf_op jit(solution)/shard_map/ppermute | solution.py:44
  145.2 27.1 %collective-permute-start.28 = (bf16[256,1536]{1,0:T(8,128)(2,1)S(1)}, bf16[256,1536]{1,0:T(8,128)(2,1)}, u32[]{:S(2)}, u32[]{:S(2)}) collective-permute-start(bf16[256,1536]{1,0:T(8,128)(2,1)S(1)} %bitcast_select_fusion.grad_ref.refs_4_), channel_id=1, source_target_pairs={{0,2},{1,3},{2,0},{3,1},{4,6},{5,7},{6,4},{7,5},{8,10},{9,11},{10,... | collective-permute-start | bytes 2359304 | tf_op jit(solution)/shard_map/ppermute | solution.py:44
  172.3 20.8 %collective-permute-start.32 = (bf16[256,1536]{1,0:T(8,128)(2,1)S(1)}, bf16[256,1536]{1,0:T(8,128)(2,1)}, u32[]{:S(2)}, u32[]{:S(2)}) collective-permute-start(bf16[256,1536]{1,0:T(8,128)(2,1)S(1)} %bitcast_select_fusion.grad_ref.refs_4_), channel_id=1, source_target_pairs={{0,1},{1,0},{2,3},{3,2},{4,5},{5,4},{6,7},{7,6},{8,9},{9,8},{10,11... | collective-permute-start | bytes 2359304 | tf_op jit(solution)/shard_map/ppermute | solution.py:44
  172.3 19.4 %collective-permute-start.29 = (bf16[256,384]{1,0:T(8,128)(2,1)}, bf16[256,384]{1,0:T(8,128)(2,1)S(1)}, u32[]{:S(2)}, u32[]{:S(2)}) collective-permute-start(bf16[256,384]{1,0:T(8,128)(2,1)} %copy-done.21), channel_id=1, source_target_pairs={{0,1},{1,0},{2,3},{3,2},{4,5},{5,4},{6,7},{7,6},{8,9},{9,8},{10,11... | collective-permute-start | bytes 589832 | tf_op jit(solution)/shard_map/ppermute | solution.py:44
  172.8 19.6 %collective-permute-start.30 = (bf16[256,384]{1,0:T(8,128)(2,1)}, bf16[256,384]{1,0:T(8,128)(2,1)S(1)}, u32[]{:S(2)}, u32[]{:S(2)}) collective-permute-start(bf16[256,384]{1,0:T(8,128)(2,1)} %get-tuple-element.259), channel_id=1, source_target_pairs={{0,2},{1,3},{2,0},{3,1},{4,6},{5,7},{6,4},{7,5},{8,10},{9,11},{10,... | collective-permute-start | bytes 589832 | tf_op jit(solution)/shard_map/ppermute | solution.py:44
  173.3 19.8 %collective-permute-start.31 = (bf16[256,384]{1,0:T(8,128)(2,1)}, bf16[256,384]{1,0:T(8,128)(2,1)}, u32[]{:S(2)}, u32[]{:S(2)}) collective-permute-start(bf16[256,384]{1,0:T(8,128)(2,1)} %get-tuple-element.260), channel_id=1, source_target_pairs={{0,3},{1,2},{2,1},{3,0},{4,7},{5,6},{6,5},{7,4},{8,11},{9,10},{10,... | collective-permute-start | bytes 589832 | tf_op jit(solution)/shard_map/ppermute | solution.py:44
  193.1 45.1 %all-to-all-start.2 = ((f32[8,384,128]{2,1,0:T(8,128)}), f32[8,384,128]{2,1,0:T(8,128)}, u32[]{:S(2)}, u32[]{:S(2)}) async-start(f32[8,384,128]{2,1,0:T(8,128)} %bitcast.91), calls=%async_computation.2 | async-start | bytes 3145728 | tf_op jit(solution)/shard_map/all_to_all | solution.py:1265
  198.9 42.4 %collective-permute-start.35 = (bf16[256,3072]{1,0:T(8,128)(2,1)}, bf16[256,3072]{1,0:T(8,128)(2,1)}, u32[]{:S(2)}, u32[]{:S(2)}) collective-permute-start(bf16[256,3072]{1,0:T(8,128)(2,1)} %get-tuple-element.275.refs_0_.gate_ref), channel_id=1, source_target_pairs={{0,2},{1,3},{2,0},{3,1},{4,6},{5,7},{6,4},{7,5},{8,10},{9,11},{10,... | collective-permute-start | bytes 4718600 | tf_op jit(solution)/shard_map/ppermute | solution.py:44
  199.4 38.7 %collective-permute-start.33 = (bf16[256,1536]{1,0:T(8,128)(2,1)}, bf16[256,1536]{1,0:T(8,128)(2,1)}, u32[]{:S(2)}, u32[]{:S(2)}) collective-permute-start(bf16[256,1536]{1,0:T(8,128)(2,1)} %collective-permute-done.28.refs_6_), channel_id=1, source_target_pairs={{0,1},{1,0},{2,3},{3,2},{4,5},{5,4},{6,7},{7,6},{8,9},{9,8},{10,11... | collective-permute-start | bytes 2359304 | tf_op jit(solution)/shard_map/ppermute | solution.py:44
  202.2 45.7 %collective-permute-start.37 = (bf16[256,768]{1,0:T(8,128)(2,1)}, bf16[256,768]{1,0:T(8,128)(2,1)}, u32[]{:S(2)}, u32[]{:S(2)}) collective-permute-start(bf16[256,768]{1,0:T(8,128)(2,1)} %get-tuple-element.401), channel_id=1, source_target_pairs={{0,1},{1,0},{2,3},{3,2},{4,5},{5,4},{6,7},{7,6},{8,9},{9,8},{10,11... | collective-permute-start | bytes 1179656 | tf_op jit(solution)/shard_map/ppermute | solution.py:44
  202.7 45.2 %collective-permute-start.38 = (bf16[256,768]{1,0:T(8,128)(2,1)}, bf16[256,768]{1,0:T(8,128)(2,1)}, u32[]{:S(2)}, u32[]{:S(2)}) collective-permute-start(bf16[256,768]{1,0:T(8,128)(2,1)} %get-tuple-element.400), channel_id=1, source_target_pairs={{0,2},{1,3},{2,0},{3,1},{4,6},{5,7},{6,4},{7,5},{8,10},{9,11},{10,... | collective-permute-start | bytes 1179656 | tf_op jit(solution)/shard_map/ppermute | solution.py:44
  204.2 48.0 %collective-permute-start.39 = (bf16[256,768]{1,0:T(8,128)(2,1)}, bf16[256,768]{1,0:T(8,128)(2,1)}, u32[]{:S(2)}, u32[]{:S(2)}) collective-permute-start(bf16[256,768]{1,0:T(8,128)(2,1)} %get-tuple-element.399), channel_id=1, source_target_pairs={{0,3},{1,2},{2,1},{3,0},{4,7},{5,6},{6,5},{7,4},{8,11},{9,10},{10,... | collective-permute-start | bytes 1179656 | tf_op jit(solution)/shard_map/ppermute | solution.py:44
  240.7 21.0 %collective-permute-start.34 = (bf16[256,3072]{1,0:T(8,128)(2,1)S(1)}, bf16[256,3072]{1,0:T(8,128)(2,1)}, u32[]{:S(2)}, u32[]{:S(2)}) collective-permute-start(bf16[256,3072]{1,0:T(8,128)(2,1)S(1)} %copy-done.19), channel_id=1, source_target_pairs={{0,1},{1,0},{2,3},{3,2},{4,5},{5,4},{6,7},{7,6},{8,9},{9,8},{10,11... | collective-permute-start | bytes 4718600 | tf_op jit(solution)/shard_map/ppermute | solution.py:44
  241.4 20.4 %collective-permute-start.36 = (bf16[256,3072]{1,0:T(8,128)(2,1)}, bf16[256,3072]{1,0:T(8,128)(2,1)}, u32[]{:S(2)}, u32[]{:S(2)}) collective-permute-start(bf16[256,3072]{1,0:T(8,128)(2,1)} %collective-permute-done.35.refs_2_), channel_id=1, source_target_pairs={{0,1},{1,0},{2,3},{3,2},{4,5},{5,4},{6,7},{7,6},{8,9},{9,8},{10,11... | collective-permute-start | bytes 4718600 | tf_op jit(solution)/shard_map/ppermute | solution.py:44
  241.4 48.3 %all-to-all-start.3 = ((bf16[8,384,128]{2,1,0:T(8,128)(2,1)}), bf16[8,384,128]{2,1,0:T(8,128)(2,1)}, u32[]{:S(2)}, u32[]{:S(2)}) async-start(bf16[8,384,128]{2,1,0:T(8,128)(2,1)} %carried.3), calls=%async_computation.3 | async-start | bytes 1572864 | tf_op jit(solution)/shard_map/all_to_all | solution.py:543
  260.3 29.5 %collective-permute-start.40 = (bf16[384,1536]{1,0:T(8,128)(2,1)}, bf16[384,1536]{1,0:T(8,128)(2,1)}, u32[]{:S(2)}, u32[]{:S(2)}) collective-permute-start(bf16[384,1536]{1,0:T(8,128)(2,1)} %dynamic-slice_convert_fusion.1), channel_id=1, source_target_pairs={{0,4},{1,5},{2,6},{3,7},{4,0},{5,1},{6,2},{7,3},{8,12},{9,13},{10,... | collective-permute-start | bytes 3538952 | tf_op jit(solution)/shard_map/ppermute | solution.py:44
  292.6 28.7 %collective-permute-start.41 = (bf16[1536,384]{1,0:T(8,128)(2,1)}, bf16[1536,384]{1,0:T(8,128)(2,1)}, u32[]{:S(2)}, u32[]{:S(2)}) collective-permute-start(bf16[1536,384]{1,0:T(8,128)(2,1)} %dynamic-slice_convert_fusion), channel_id=1, source_target_pairs={{0,4},{1,5},{2,6},{3,7},{4,0},{5,1},{6,2},{7,3},{8,12},{9,13},{10,... | collective-permute-start | bytes 3538952 | tf_op jit(solution)/shard_map/ppermute | solution.py:44
  298.6 15.7 %collective-permute-start.42 = (bf16[192,1536]{1,0:T(8,128)(2,1)S(1)}, bf16[192,1536]{1,0:T(8,128)(2,1)S(1)}, u32[]{:S(2)}, u32[]{:S(2)}) collective-permute-start(bf16[192,1536]{1,0:T(8,128)(2,1)S(1)} %dynamic-slice_convert_fusion.5), channel_id=1, source_target_pairs={{0,8},{1,9},{2,10},{3,11},{4,12},{5,13},{6,14},{7,15},{8,0},{9,1},... | collective-permute-start | bytes 1769480 | tf_op jit(solution)/shard_map/ppermute | solution.py:44
  328.3 25.2 %collective-permute-start.45 = (bf16[256,1792]{1,0:T(8,128)(2,1)S(1)}, bf16[256,1792]{1,0:T(8,128)(2,1)}, u32[]{:S(2)}, u32[]{:S(2)}) collective-permute-start(bf16[256,1792]{1,0:T(8,128)(2,1)S(1)} %slice_dynamic-update-slice_fusion.refs_0_), channel_id=1, source_target_pairs={{0,2},{1,3},{2,0},{3,1},{4,6},{5,7},{6,4},{7,5},{8,10},{9,11},{10,... | collective-permute-start | bytes 2752520 | tf_op jit(solution)/shard_map/ppermute | solution.py:44
  329.0 24.5 %collective-permute-start.46 = (bf16[256,1792]{1,0:T(8,128)(2,1)S(1)}, bf16[256,1792]{1,0:T(8,128)(2,1)S(1)}, u32[]{:S(2)}, u32[]{:S(2)}) collective-permute-start(bf16[256,1792]{1,0:T(8,128)(2,1)S(1)} %slice_dynamic-update-slice_fusion.refs_0_), channel_id=1, source_target_pairs={{0,1},{1,0},{2,3},{3,2},{4,5},{5,4},{6,7},{7,6},{8,9},{9,8},{10,11... | collective-permute-start | bytes 2752520 | tf_op jit(solution)/shard_map/ppermute | solution.py:44
  331.4 22.1 %collective-permute-start.47 = (bf16[768,384]{1,0:T(8,128)(2,1)S(1)}, bf16[768,384]{1,0:T(8,128)(2,1)S(1)}, u32[]{:S(2)}, u32[]{:S(2)}) collective-permute-start(bf16[768,384]{1,0:T(8,128)(2,1)S(1)} %dynamic-slice_convert_fusion.4), channel_id=1, source_target_pairs={{0,8},{1,9},{2,10},{3,11},{4,12},{5,13},{6,14},{7,15},{8,0},{9,1},... | collective-permute-start | bytes 1769480 | tf_op jit(solution)/shard_map/ppermute | solution.py:44
  333.1 19.5 %collective-permute-start.44 = (bf16[96,1536]{1,0:T(8,128)(2,1)S(1)}, bf16[96,1536]{1,0:T(8,128)(2,1)S(1)}, u32[]{:S(2)}, u32[]{:S(2)}) collective-permute-start(bf16[96,1536]{1,0:T(8,128)(2,1)S(1)} %dynamic-slice_convert_fusion.9), channel_id=1, source_target_pairs={{0,16},{1,17},{2,18},{3,19},{4,20},{5,21},{6,22},{7,23},{8,24},{9,... | collective-permute-start | bytes 884744 | tf_op jit(solution)/shard_map/ppermute | solution.py:44
  356.6 24.5 %collective-permute-start.50 = (bf16[256,1664]{1,0:T(8,128)(2,1)S(1)}, bf16[256,1664]{1,0:T(8,128)(2,1)S(1)}, u32[]{:S(2)}, u32[]{:S(2)}) collective-permute-start(bf16[256,1664]{1,0:T(8,128)(2,1)S(1)} %pad_maximum_fusion.3.refs_0_), channel_id=1, source_target_pairs={{0,2},{1,3},{2,0},{3,1},{4,6},{5,7},{6,4},{7,5},{8,10},{9,11},{10,... | collective-permute-start | bytes 2555912 | tf_op jit(solution)/shard_map/ppermute | solution.py:44
  362.1 19.0 %collective-permute-start.51 = (bf16[896,384]{1,0:T(8,128)(2,1)S(1)}, bf16[896,384]{1,0:T(8,128)(2,1)S(1)}, u32[]{:S(2)}, u32[]{:S(2)}) collective-permute-start(bf16[896,384]{1,0:T(8,128)(2,1)S(1)} %dynamic-slice_convert_fusion.2), channel_id=1, source_target_pairs={{0,4},{1,5},{2,6},{3,7},{4,0},{5,1},{6,2},{7,3},{8,12},{9,13},{10,... | collective-permute-start | bytes 2064392 | tf_op jit(solution)/shard_map/ppermute | solution.py:44
  364.9 23.5 %collective-permute-start.53 = (bf16[96,1536]{1,0:T(8,128)(2,1)S(1)}, bf16[96,1536]{1,0:T(8,128)(2,1)}, u32[]{:S(2)}, u32[]{:S(2)}) collective-permute-start(bf16[96,1536]{1,0:T(8,128)(2,1)S(1)} %add_convert_fusion.1), channel_id=1, source_target_pairs={{0,16},{1,17},{2,18},{3,19},{4,20},{5,21},{6,22},{7,23},{8,24},{9,... | collective-permute-start | bytes 884744 | tf_op jit(solution)/shard_map/ppermute | solution.py:44
  366.6 26.8 %collective-permute-start.54 = (bf16[384,384]{1,0:T(8,128)(2,1)S(1)}, bf16[384,384]{1,0:T(8,128)(2,1)S(1)}, u32[]{:S(2)}, u32[]{:S(2)}) collective-permute-start(bf16[384,384]{1,0:T(8,128)(2,1)S(1)} %dynamic-slice_convert_fusion.8), channel_id=1, source_target_pairs={{0,16},{1,17},{2,18},{3,19},{4,20},{5,21},{6,22},{7,23},{8,24},{9,... | collective-permute-start | bytes 884744 | tf_op jit(solution)/shard_map/ppermute | solution.py:44
  394.2 30.1 %collective-permute-start.55 = (bf16[832,384]{1,0:T(8,128)(2,1)}, bf16[832,384]{1,0:T(8,128)(2,1)}, u32[]{:S(2)}, u32[]{:S(2)}) collective-permute-start(bf16[832,384]{1,0:T(8,128)(2,1)} %dynamic-slice_convert_fusion.3), channel_id=1, source_target_pairs={{0,4},{1,5},{2,6},{3,7},{4,0},{5,1},{6,2},{7,3},{8,12},{9,13},{10,... | collective-permute-start | bytes 1916936 | tf_op jit(solution)/shard_map/ppermute | solution.py:44
  396.3 25.8 %collective-permute-start.56 = (bf16[448,384]{1,0:T(8,128)(2,1)}, bf16[448,384]{1,0:T(8,128)(2,1)}, u32[]{:S(2)}, u32[]{:S(2)}) collective-permute-start(bf16[448,384]{1,0:T(8,128)(2,1)} %dynamic-slice_convert_fusion.6), channel_id=1, source_target_pairs={{0,8},{1,9},{2,10},{3,11},{4,12},{5,13},{6,14},{7,15},{8,0},{9,1},... | collective-permute-start | bytes 1032200 | tf_op jit(solution)/shard_map/ppermute | solution.py:44
  398.3 26.0 %collective-permute-start.57 = (bf16[192,1536]{1,0:T(8,128)(2,1)}, bf16[192,1536]{1,0:T(8,128)(2,1)}, u32[]{:S(2)}, u32[]{:S(2)}) collective-permute-start(bf16[192,1536]{1,0:T(8,128)(2,1)} %pad_maximum_fusion.6), channel_id=1, source_target_pairs={{0,8},{1,9},{2,10},{3,11},{4,12},{5,13},{6,14},{7,15},{8,0},{9,1},... | collective-permute-start | bytes 1769480 | tf_op jit(solution)/shard_map/ppermute | solution.py:44
  401.0 21.1 %collective-permute-start.58 = (bf16[384,384]{1,0:T(8,128)(2,1)}, bf16[384,384]{1,0:T(8,128)(2,1)}, u32[]{:S(2)}, u32[]{:S(2)}) collective-permute-start(bf16[384,384]{1,0:T(8,128)(2,1)} %add_convert_fusion), channel_id=1, source_target_pairs={{0,16},{1,17},{2,18},{3,19},{4,20},{5,21},{6,22},{7,23},{8,24},{9,... | collective-permute-start | bytes 884744 | tf_op jit(solution)/shard_map/ppermute | solution.py:44
  430.0 11.7 %collective-permute-start.60 = (bf16[416,384]{1,0:T(8,128)(2,1)}, bf16[416,384]{1,0:T(8,128)(2,1)}, u32[]{:S(2)}, u32[]{:S(2)}) collective-permute-start(bf16[416,384]{1,0:T(8,128)(2,1)} %dynamic-slice_convert_fusion.7), channel_id=1, source_target_pairs={{0,8},{1,9},{2,10},{3,11},{4,12},{5,13},{6,14},{7,15},{8,0},{9,1},... | collective-permute-start | bytes 958472 | tf_op jit(solution)/shard_map/ppermute | solution.py:44
  432.9 19.7 %collective-permute-start.61 = (bf16[768,384]{1,0:T(8,128)(2,1)S(1)}, bf16[768,384]{1,0:T(8,128)(2,1)}, u32[]{:S(2)}, u32[]{:S(2)}) collective-permute-start(bf16[768,384]{1,0:T(8,128)(2,1)S(1)} %pad_maximum_fusion.7), channel_id=1, source_target_pairs={{0,8},{1,9},{2,10},{3,11},{4,12},{5,13},{6,14},{7,15},{8,0},{9,1},... | collective-permute-start | bytes 1769480 | tf_op jit(solution)/shard_map/ppermute | solution.py:44
  434.7 35.0 %collective-permute-start.63 = (bf16[384,1536]{1,0:T(8,128)(2,1)S(1)}, bf16[384,1536]{1,0:T(8,128)(2,1)}, u32[]{:S(2)}, u32[]{:S(2)}) collective-permute-start(bf16[384,1536]{1,0:T(8,128)(2,1)S(1)} %pad_maximum_fusion.1), channel_id=1, source_target_pairs={{0,4},{1,5},{2,6},{3,7},{4,0},{5,1},{6,2},{7,3},{8,12},{9,13},{10,... | collective-permute-start | bytes 3538952 | tf_op jit(solution)/shard_map/ppermute | solution.py:44
  453.5 16.2 %collective-permute-start.64 = (bf16[224,384]{1,0:T(8,128)(2,1)S(1)}, bf16[224,384]{1,0:T(8,128)(2,1)}, u32[]{:S(2)}, u32[]{:S(2)}) collective-permute-start(bf16[224,384]{1,0:T(8,128)(2,1)S(1)} %add_convert_fusion.2), channel_id=1, source_target_pairs={{0,16},{1,17},{2,18},{3,19},{4,20},{5,21},{6,22},{7,23},{8,24},{9,... | collective-permute-start | bytes 516104 | tf_op jit(solution)/shard_map/ppermute | solution.py:44
  457.1 28.4 %collective-permute-start.67 = (bf16[1536,384]{1,0:T(8,128)(2,1)}, bf16[1536,384]{1,0:T(8,128)(2,1)}, u32[]{:S(2)}, u32[]{:S(2)}) collective-permute-start(bf16[1536,384]{1,0:T(8,128)(2,1)} %pad_maximum_fusion.2), channel_id=1, source_target_pairs={{0,4},{1,5},{2,6},{3,7},{4,0},{5,1},{6,2},{7,3},{8,12},{9,13},{10,... | collective-permute-start | bytes 3538952 | tf_op jit(solution)/shard_map/ppermute | solution.py:44
  459.3 10.4 %collective-permute-start.65 = (bf16[208,384]{1,0:T(8,128)(2,1)S(1)}, bf16[208,384]{1,0:T(8,128)(2,1)}, u32[]{:S(2)}, u32[]{:S(2)}) collective-permute-start(bf16[208,384]{1,0:T(8,128)(2,1)S(1)} %dynamic-slice_convert_fusion.11), channel_id=1, source_target_pairs={{0,16},{1,17},{2,18},{3,19},{4,20},{5,21},{6,22},{7,23},{8,24},{9,... | collective-permute-start | bytes 479240 | tf_op jit(solution)/shard_map/ppermute | solution.py:44
  470.7 12.8 %collective-permute-start.68 = (bf16[448,384]{1,0:T(8,128)(2,1)S(1)}, bf16[448,384]{1,0:T(8,128)(2,1)}, u32[]{:S(2)}, u32[]{:S(2)}) collective-permute-start(bf16[448,384]{1,0:T(8,128)(2,1)S(1)} %pad_maximum_fusion.8), channel_id=1, source_target_pairs={{0,8},{1,9},{2,10},{3,11},{4,12},{5,13},{6,14},{7,15},{8,0},{9,1},... | collective-permute-start | bytes 1032200 | tf_op jit(solution)/shard_map/ppermute | solution.py:44
  486.7 11.4 %collective-permute-start.72 = (bf16[416,384]{1,0:T(8,128)(2,1)S(1)}, bf16[416,384]{1,0:T(8,128)(2,1)S(1)}, u32[]{:S(2)}, u32[]{:S(2)}) collective-permute-start(bf16[416,384]{1,0:T(8,128)(2,1)S(1)} %pad_maximum_fusion.9), channel_id=1, source_target_pairs={{0,8},{1,9},{2,10},{3,11},{4,12},{5,13},{6,14},{7,15},{8,0},{9,1},... | collective-permute-start | bytes 958472 | tf_op jit(solution)/shard_map/ppermute | solution.py:44
  491.4 18.8 %collective-permute-start.74 = (bf16[896,384]{1,0:T(8,128)(2,1)}, bf16[896,384]{1,0:T(8,128)(2,1)}, u32[]{:S(2)}, u32[]{:S(2)}) collective-permute-start(bf16[896,384]{1,0:T(8,128)(2,1)} %pad_maximum_fusion.5), channel_id=1, source_target_pairs={{0,4},{1,5},{2,6},{3,7},{4,0},{5,1},{6,2},{7,3},{8,12},{9,13},{10,... | collective-permute-start | bytes 2064392 | tf_op jit(solution)/shard_map/ppermute | solution.py:44
  500.7 20.3 %collective-permute-start.75 = (bf16[832,384]{1,0:T(8,128)(2,1)}, bf16[832,384]{1,0:T(8,128)(2,1)}, u32[]{:S(2)}, u32[]{:S(2)}) collective-permute-start(bf16[832,384]{1,0:T(8,128)(2,1)} %pad_maximum_fusion.4), channel_id=1, source_target_pairs={{0,4},{1,5},{2,6},{3,7},{4,0},{5,1},{6,2},{7,3},{8,12},{9,13},{10,... | collective-permute-start | bytes 1916936 | tf_op jit(solution)/shard_map/ppermute | solution.py:44
  (131 other events, 881.1 us)

commit v5 on v4

--- a/solution.py
+++ b/solution.py
@@ -483,7 +483,7 @@
 class SmallSum:
     def __init__(self, ring, vector):
         self.ring, self.value = ring, vector
-        self.steps = ["core", "row"] + cube(ring)
+        self.steps = ["core", "row"] + cube(ring)[1:] + cube(ring)[:1]
 
     def step(self):
         if not self.steps:
@@ -1378,6 +1378,7 @@
     total_w_gate.step()
     clock.tick()
     small_total.step()
+    small_total.step()
     total_w_gate.halves()
     clock.defer()
     total_first.step()
@@ -1387,7 +1388,6 @@
     total_first.step()
     total_last.step()
     clock.tick()
-    small_total.step()
     small_total.step()
     total_first.halves()
     clock.defer()

time: 535 us -> 540 us (level)
    unnamed x232 -> x230, local copies, waits for them, and re-layouts: 34 us -> 34.7 us
  transfers between devices with their start and end apart: 80 -> 80, of which waited for: 33 -> 28; matrix products, arithmetic and copies ran while one was open for 14% -> 14% of each run, Pallas kernels for 27% -> 27%
where the time goes in v5:
time: 540 us; the launch traced here: 529 us
  waiting for transfers between devices  169 us (31%)
  Pallas kernels  146 us (27%)
  starting transfers between devices  94.3 us (17%)
  local copies, waits for them, and re-layouts  70.4 us (13%)
  other arithmetic  45.9 us (8%)
    ppermute x76, waiting for transfers between devices, send(): arrived = lax.ppermute(block, ('seq', 'fsdp'), route)  164 us
    ppermute x76, starting transfers between devices, send(): arrived = lax.ppermute(block, ('seq', 'fsdp'), route)  73.7 us
    unnamed x230, local copies, waits for them, and re-layouts  34.7 us
    pallas_call x1, Pallas kernels, inside_back(): pl.pallas_call(inside_back_body, grid=(pairs,), in_specs=[columns, column...  27.6 us
    pallas_call x4, Pallas kernels, weight_grad(): pl.pallas_call(functools.partial(sum_body, len(keys)), grid=(rows // tile...  17.7 us
    pallas_call x4, Pallas kernels, project(): pl.pallas_call(functools.partial(project_body, count), grid=(pl.cdiv(widt...  15.6 us
    pallas_call x1, Pallas kernels, turn(): pl.pallas_call(turn_body, grid=(2, groups), in_specs=[pl.BlockSpec((token...  15.4 us
    pallas_call x1, Pallas kernels, leave(): pl.pallas_call(functools.partial(leave_body, steps), grid=(steps + 1,), i...  15.1 us
  transfers between devices with their start and end apart: 80, of which 28 were waited for; matrix products, arithmetic and copies ran while one was open for 14% of the time, Pallas kernels for 27%

profile of v5, /device:TPU:0, one launch (start us, length us, event | category | flops | bytes accessed | tf_op | source)
XLA Modules:
  0.0 529.1 jit_solution(8585142437404129893)
XLA Ops:
  2.4 2.7 collective-permute-start
  5.9 4.1 concatenate.39
  10.5 2.0 constant_dynamic-slice_fusion.15
  12.5 3.1 fusion.11
  15.6 4.7 collective-permute-done.refs_0_
  25.9 13.9 %collective-permute-done.3 = bf16[48,128]{1,0:T(8,128)(2,1)S(1)} collective-permute-done((bf16[48,128]{1,0:T(8,128)(2,1)S(1)}, bf16[48,128]{1,0:T(8,128)(2,1)S(1)}, u32[]{:S(2)}, u32[]{:S(2)}) %collective-permute-start.3) | collective-permute-done | bytes 12320 | tf_op jit(solution)/shard_map/ppermute | solution.py:44
  40.8 2.2 collective-permute-done.4
  48.6 7.4 %collective-permute-done.10.refs_4_ = bf16[416,384]{1,0:T(8,128)(2,1)} collective-permute-done((bf16[416,384]{1,0:T(8,128)(2,1)}, bf16[416,384]{1,0:T(8,128)(2,1)}, u32[]{:S(2)}, u32[]{:S(2)}) %collective-permute-start.10) | collective-permute-done | bytes 319520 | tf_op jit(solution)/shard_map/ppermute | solution.py:44
  60.4 2.5 laid.2
  63.0 6.9 %project.4.dt_ref.proj_ref = bf16[256,3376]{1,0:T(8,128)(2,1)S(1)} custom-call(bf16[256,384]{1,0:T(8,128)(2,1)S(1)} %get-tuple-element.277.refs_0_.refs_4_, bf16[256,384]{1,0:T(8,128)(2,1)S(1)} %get-tuple-element.258.refs_1_, bf16[256,384]{1,0:T(8,128)(2,1)S(1)} %get-tuple-element.413.refs_2_, bf16[256,384]{1,0:T(8,128)(2,1)S(1)} %get-tuple-element.412.refs_3_, ...), custom_call_target="tpu_custom_call" | custom-call | tf_op jit(solution)/shard_map/project/pallas_call | solution.py:396
  74.7 2.7 collective-permute-start.18
  83.3 3.8 enter.1
  88.4 3.8 collective-permute-done.19.refs_6_.refs_4_
  92.1 4.2 all-to-all-start
  106.4 10.7 %inside.1.base_ref = f32[256,3072]{1,0:T(8,128)S(1)} custom-call(bf16[256,3328]{1,0:T(8,128)(2,1)S(1)} %get-tuple-element.228.x_ref.b_ref.c_ref.low_ref, bf16[256,3328]{1,0:T(8,128)(2,1)S(1)} %get-tuple-element.228.x_ref.b_ref.c_ref.low_ref, bf16[256,3328]{1,0:T(8,128)(2,1)S(1)} %get-tuple-element.228.x_ref.b_ref.c_ref.low_ref, f32[256,128]{1,0:T(8,128)S(1)} %copy-done.48, ...), custom_call_target="tpu_custom_call" | custom-call | tf_op jit(solution)/shard_map/inside/pallas_call | solution.py:829
  118.9 10.4 %collective-permute-done.23.refs_4_ = bf16[96,1536]{1,0:T(8,128)(2,1)} collective-permute-done((bf16[96,1536]{1,0:T(8,128)(2,1)}, bf16[96,1536]{1,0:T(8,128)(2,1)}, u32[]{:S(2)}, u32[]{:S(2)}) %collective-permute-start.23) | collective-permute-done | bytes 294944 | tf_op jit(solution)/shard_map/ppermute | solution.py:44
  129.3 4.7 all-to-all-done.blocks_ref
  135.0 3.7 laid.3.refs_2_.refs_6_
  139.3 4.1 all-to-all-start.1
  146.9 2.4 copy-done
  149.3 2.9 project.5.refs_0_
  153.0 2.9 project.6.refs_1_
  156.7 2.9 project.7.refs_2_
  160.4 10.1 %to_inner.1.grad_ref = f32[256,3072]{1,0:T(8,128)S(1)} custom-call(s32[4]{0:T(128)S(1)} %pad_add_fusion.1.place_ref, bf16[256,1536]{1,0:T(8,128)(2,1)S(1)} %bitcast_select_fusion.grad_ref.refs_4_, bf16[768,1536]{1,0:T(8,128)(2,1)} %refs_4_.1, bf16[768,1536]{1,0:T(8,128)(2,1)} %collective-permute-done.20.refs_1_.refs_5_, ...), custom_call_target="tpu_custom_call" | custom-call | tf_op jit(solution)/shard_map/to_inner/pallas_call | solution.py:264
  176.3 15.4 %turn.1 = (bf16[256,3072]{1,0:T(8,128)(2,1)}, bf16[256,3072]{1,0:T(8,128)(2,1)}, bf16[256,3072]{1,0:T(8,128)(2,1)}, bf16[256,3072]{1,0:T(8,128)(2,1)}, f32[3072,128]{1,0:T(8,128)}, /*index=5*/f32[1,3072]{1,0:T(1,128)}) custom-call(f32[256,3072]{1,0:T(8,128)} %copy-done.12, bf16[3072,128]{1,0:T(8,128)(2,1)} %bitcast.86, bf16[256,128]{1,0:T(8,128)(2,1)} %slice.130.c_ref, ...), custom_call_target="tpu_custom_call" | custom-call | tf_op jit(solution)/shard_map/turn/pallas_call | solution.py:947
  193.1 5.8 %all-to-all-start.2 = ((f32[8,384,128]{2,1,0:T(8,128)}), f32[8,384,128]{2,1,0:T(8,128)}, u32[]{:S(2)}, u32[]{:S(2)}) async-start(f32[8,384,128]{2,1,0:T(8,128)} %bitcast.91), calls=%async_computation.2 | async-start | bytes 3145728 | tf_op jit(solution)/shard_map/all_to_all | solution.py:1265
  199.5 2.7 constant_dynamic-slice_fusion.1
  205.7 27.6 %inside_back.1 = (f32[256,3072]{1,0:T(8,128)S(1)}, f32[256,128]{1,0:T(8,128)S(1)}, f32[256,128]{1,0:T(8,128)S(1)}, f32[48,256]{1,0:T(8,128)S(1)}, f32[48,256]{1,0:T(8,128)S(1)}, /*index=5*/f32[1,3072]{1,0:T(1,128)S(1)}) custom-call(bf16[256,3072]{1,0:T(8,128)(2,1)S(1)} %copy-done.41, bf16[256,3072]{1,0:T(8,128)(2,1)S(1)} %copy-done.42, ...), custom_call_target="tpu_custom_call" | custom-call | tf_op jit(solution)/shard_map/inside_back/pallas_call | solution.py:911
  238.2 2.6 carried.3
  241.4 6.5 %all-to-all-start.3 = ((bf16[8,384,128]{2,1,0:T(8,128)(2,1)}), bf16[8,384,128]{2,1,0:T(8,128)(2,1)}, u32[]{:S(2)}, u32[]{:S(2)}) async-start(bf16[8,384,128]{2,1,0:T(8,128)(2,1)} %carried.3), calls=%async_computation.3 | async-start | bytes 1572864 | tf_op jit(solution)/shard_map/all_to_all | solution.py:543
  247.9 4.2 collective-permute-done.39.refs_3_
  252.2 4.8 weight_grad.5
  257.0 2.2 copy-done.6
  261.8 5.8 %weight_grad.4 = f32[3072,384]{1,0:T(8,128)S(1)} custom-call(bf16[256,3072]{1,0:T(8,128)(2,1)S(1)} %copy-done.19, bf16[256,3072]{1,0:T(8,128)(2,1)} %collective-permute-done.34.refs_1_, bf16[256,3072]{1,0:T(8,128)(2,1)} %collective-permute-done.35.refs_2_, bf16[256,3072]{1,0:T(8,128)(2,1)} %collective-permute-done.36.refs_3_, ...), custom_call_target="tpu_custom_call" | custom-call | tf_op jit(solution)/shard_map/weight_grad/pallas_call | solution.py:236
  267.6 2.2 copy-done.7
  270.9 7.2 %output_rows.1 = bf16[256,1536]{1,0:T(8,128)(2,1)} custom-call(bf16[256,1536]{1,0:T(8,128)(2,1)S(1)} %bitcast.85, bf16[256,768]{1,0:T(8,128)(2,1)S(1)} %get-tuple-element.405.refs_0_, bf16[256,768]{1,0:T(8,128)(2,1)S(1)} %get-tuple-element.404.refs_1_, bf16[256,768]{1,0:T(8,128)(2,1)S(1)} %get-tuple-element.403.refs_2_, ...), custom_call_target="tpu_custom_call" | custom-call | tf_op jit(solution)/shard_map/output_rows/pallas_call | solution.py:342
  278.2 11.6 %collective-permute-done.40 = bf16[384,1536]{1,0:T(8,128)(2,1)} collective-permute-done((bf16[384,1536]{1,0:T(8,128)(2,1)}, bf16[384,1536]{1,0:T(8,128)(2,1)}, u32[]{:S(2)}, u32[]{:S(2)}) %collective-permute-start.40) | collective-permute-done | bytes 1179680 | tf_op jit(solution)/shard_map/ppermute | solution.py:44
  289.8 2.9 dynamic-slice_convert_fusion
  292.6 2.2 collective-permute-start.41
  294.8 2.3 convert_add_fusion.1
  299.2 15.1 %leave.1 = (bf16[256,1792]{1,0:T(8,128)(2,1)}, bf16[256,1536]{1,0:T(8,128)(2,1)}, f32[8,3328]{1,0:T(8,128)}, f32[8,3328]{1,0:T(8,128)}, f32[4,3328]{1,0:T(4,128)...) custom-call(bf16[256,3376]{1,0:T(8,128)(2,1)} %copy-done.2, bf16[8,3328]{1,0:T(8,128)(2,1)} %copy-done.59, ...), custom_call_target="tpu_custom_call" | custom-call | tf_op jit(solution)/shard_map/leave/pallas_call | solution.py:1080
  314.3 7.0 %collective-permute-done.41 = bf16[1536,384]{1,0:T(8,128)(2,1)} collective-permute-done((bf16[1536,384]{1,0:T(8,128)(2,1)}, bf16[1536,384]{1,0:T(8,128)(2,1)}, u32[]{:S(2)}, u32[]{:S(2)}) %collective-permute-start.41) | collective-permute-done | bytes 1179680 | tf_op jit(solution)/shard_map/ppermute | solution.py:44
  324.4 3.9 collective-permute-done.43
  329.1 2.3 convert_add_fusion
  333.1 3.0 collective-permute-start.44
  337.1 15.5 %collective-permute-done.44 = bf16[96,1536]{1,0:T(8,128)(2,1)S(1)} collective-permute-done((bf16[96,1536]{1,0:T(8,128)(2,1)S(1)}, bf16[96,1536]{1,0:T(8,128)(2,1)S(1)}, u32[]{:S(2)}, u32[]{:S(2)}) %collective-permute-start.44) | collective-permute-done | bytes 294944 | tf_op jit(solution)/shard_map/ppermute | solution.py:44
  358.1 3.9 weight_grad.6
  362.2 2.7 collective-permute-start.51
  368.2 13.0 %to_model.1 = f32[4,256,384]{2,1,0:T(8,128)S(1)} custom-call(bf16[256,3072]{1,0:T(8,128)(2,1)S(1)} %copy-done.20, bf16[256,3376]{1,0:T(8,128)(2,1)S(1)} %pad_maximum_fusion.tail_ref, bf16[6448,384]{1,0:T(8,128)(2,1)} %bitcast.78, bf16[6448,384]{1,0:T(8,128)(2,1)} %collective-permute-done.1.refs_5_.refs_1_, bf16[3376,384]{1,0:T(8,128)(2,1)S(1)} %copy-done.15, ...), custom_call_target="tpu_custom_call" | custom-call | tf_op jit(solution)/shard_map/to_model/pallas_call | solution.py:321
  383.6 3.2 weight_grad.7
  388.5 4.9 collective-permute-done.54
  404.3 17.8 %collective-permute-done.58 = bf16[384,384]{1,0:T(8,128)(2,1)} collective-permute-done((bf16[384,384]{1,0:T(8,128)(2,1)}, bf16[384,384]{1,0:T(8,128)(2,1)}, u32[]{:S(2)}, u32[]{:S(2)}) %collective-permute-start.58) | collective-permute-done | bytes 294944 | tf_op jit(solution)/shard_map/ppermute | solution.py:44
  422.1 2.2 collective-permute-done.57
  436.3 5.2 collective-permute-done.60
  441.5 10.8 %collective-permute-done.61 = bf16[768,384]{1,0:T(8,128)(2,1)} collective-permute-done((bf16[768,384]{1,0:T(8,128)(2,1)S(1)}, bf16[768,384]{1,0:T(8,128)(2,1)}, u32[]{:S(2)}, u32[]{:S(2)}) %collective-permute-start.61) | collective-permute-done | bytes 589856 | tf_op jit(solution)/shard_map/ppermute | solution.py:44
  462.9 8.8 %collective-permute-done.66 = bf16[208,384]{1,0:T(8,128)(2,1)} collective-permute-done((bf16[208,384]{1,0:T(8,128)(2,1)}, bf16[208,384]{1,0:T(8,128)(2,1)}, u32[]{:S(2)}, u32[]{:S(2)}) %collective-permute-start.66) | collective-permute-done | bytes 159776 | tf_op jit(solution)/shard_map/ppermute | solution.py:44
  472.8 2.7 collective-permute-start.70
  476.5 10.3 %collective-permute-done.67 = f32[168,128]{1,0:T(8,128)S(1)} collective-permute-done((f32[168,128]{1,0:T(8,128)S(1)}, f32[168,128]{1,0:T(8,128)S(1)}, u32[]{:S(2)}, u32[]{:S(2)}) %collective-permute-start.67) | collective-permute-done | bytes 86048 | tf_op jit(solution)/shard_map/ppermute | solution.py:44
  493.0 2.3 collective-permute-start.74
  502.5 2.8 maximum_convert_fusion
  505.3 8.4 %collective-permute-done.73 = f32[168,128]{1,0:T(8,128)S(1)} collective-permute-done((f32[168,128]{1,0:T(8,128)S(1)}, f32[168,128]{1,0:T(8,128)S(1)}, u32[]{:S(2)}, u32[]{:S(2)}) %collective-permute-start.73) | collective-permute-done | bytes 86048 | tf_op jit(solution)/shard_map/ppermute | solution.py:44
  519.6 2.3 convert_dynamic-update-slice_fusion.1
  521.9 3.7 collective-permute-done.75
  526.7 2.2 convert_dynamic-update-slice_fusion.4
  (489 shorter events, 146.9 us)
Async XLA Ops:
  0.7 19.7 %collective-permute-start.1 = (bf16[6448,384]{1,0:T(8,128)(2,1)}, bf16[6448,384]{1,0:T(8,128)(2,1)}, u32[]{:S(2)}, u32[]{:S(2)}) collective-permute-start(bf16[6448,384]{1,0:T(8,128)(2,1)} %bitcast.76), channel_id=1, source_target_pairs={{0,1},{1,0},{2,3},{3,2},{4,5},{5,4},{6,7},{7,6},{8,9},{9,8},{10,11... | collective-permute-start | bytes 14856200 | tf_op jit(solution)/shard_map/ppermute | solution.py:44
  2.4 17.9 %collective-permute-start = (bf16[848,384]{1,0:T(8,128)(2,1)S(1)}, bf16[848,384]{1,0:T(8,128)(2,1)S(1)}, u32[]{:S(2)}, u32[]{:S(2)}) collective-permute-start(bf16[848,384]{1,0:T(8,128)(2,1)S(1)} %dynamic-slice_bitcast_fusion), channel_id=1, source_target_pairs={{0,2},{1,3},{2,0},{3,1},{4,6},{5,7},{6,4},{7,5},{8,10},{9,11},{10,... | collective-permute-start | bytes 1953800 | tf_op jit(solution)/shard_map/ppermute | solution.py:44
  10.1 15.1 %collective-permute-start.2 = (bf16[48,128]{1,0:T(8,128)(2,1)S(1)}, bf16[48,128]{1,0:T(8,128)(2,1)S(1)}, u32[]{:S(2)}, u32[]{:S(2)}) collective-permute-start(bf16[48,128]{1,0:T(8,128)(2,1)S(1)} %pad_bitcast_fusion.1), channel_id=1, source_target_pairs={{0,1},{1,0},{2,3},{3,2},{4,5},{5,4},{6,7},{7,6},{8,9},{9,8},{10,11... | collective-permute-start | bytes 36872 | tf_op jit(solution)/shard_map/ppermute | solution.py:44
  20.3 22.7 %collective-permute-start.5 = (bf16[848,384]{1,0:T(8,128)(2,1)S(1)}, bf16[848,384]{1,0:T(8,128)(2,1)S(1)}, u32[]{:S(2)}, u32[]{:S(2)}) collective-permute-start(bf16[848,384]{1,0:T(8,128)(2,1)S(1)} %collective-permute-done.refs_0_), channel_id=1, source_target_pairs={{0,4},{1,5},{2,6},{3,7},{4,0},{5,1},{6,2},{7,3},{8,12},{9,13},{10,... | collective-permute-start | bytes 1953800 | tf_op jit(solution)/shard_map/ppermute | solution.py:44
  22.0 21.0 %collective-permute-start.6 = (bf16[848,384]{1,0:T(8,128)(2,1)S(1)}, bf16[848,384]{1,0:T(8,128)(2,1)S(1)}, u32[]{:S(2)}, u32[]{:S(2)}) collective-permute-start(bf16[848,384]{1,0:T(8,128)(2,1)S(1)} %collective-permute-done.refs_0_), channel_id=1, source_target_pairs={{0,8},{1,9},{2,10},{3,11},{4,12},{5,13},{6,14},{7,15},{8,0},{9,1},... | collective-permute-start | bytes 1953800 | tf_op jit(solution)/shard_map/ppermute | solution.py:44
  23.6 19.4 %collective-permute-start.7 = (bf16[848,384]{1,0:T(8,128)(2,1)S(1)}, bf16[848,384]{1,0:T(8,128)(2,1)S(1)}, u32[]{:S(2)}, u32[]{:S(2)}) collective-permute-start(bf16[848,384]{1,0:T(8,128)(2,1)S(1)} %collective-permute-done.refs_0_), channel_id=1, source_target_pairs={{0,1},{1,0},{2,3},{3,2},{4,5},{5,4},{6,7},{7,6},{8,9},{9,8},{10,11... | collective-permute-start | bytes 1953800 | tf_op jit(solution)/shard_map/ppermute | solution.py:44
  23.6 19.4 %collective-permute-start.8 = (bf16[192,1536]{1,0:T(8,128)(2,1)}, bf16[192,1536]{1,0:T(8,128)(2,1)}, u32[]{:S(2)}, u32[]{:S(2)}) collective-permute-start(bf16[192,1536]{1,0:T(8,128)(2,1)} %constant_dynamic-slice_fusion.15), channel_id=1, source_target_pairs={{0,2},{1,3},{2,0},{3,1},{4,6},{5,7},{6,4},{7,5},{8,10},{9,11},{10,... | collective-permute-start | bytes 1769480 | tf_op jit(solution)/shard_map/ppermute | solution.py:44
  25.2 14.6 %collective-permute-start.3 = (bf16[48,128]{1,0:T(8,128)(2,1)S(1)}, bf16[48,128]{1,0:T(8,128)(2,1)S(1)}, u32[]{:S(2)}, u32[]{:S(2)}) collective-permute-start(bf16[48,128]{1,0:T(8,128)(2,1)S(1)} %pad_bitcast_fusion.1), channel_id=1, source_target_pairs={{0,2},{1,3},{2,0},{3,1},{4,6},{5,7},{6,4},{7,5},{8,10},{9,11},{10,... | collective-permute-start | bytes 36872 | tf_op jit(solution)/shard_map/ppermute | solution.py:44
  43.9 12.2 %collective-permute-start.11 = (bf16[848,384]{1,0:T(8,128)(2,1)S(1)}, bf16[848,384]{1,0:T(8,128)(2,1)}, u32[]{:S(2)}, u32[]{:S(2)}) collective-permute-start(bf16[848,384]{1,0:T(8,128)(2,1)S(1)} %collective-permute-done.5.refs_1_), channel_id=1, source_target_pairs={{0,1},{1,0},{2,3},{3,2},{4,5},{5,4},{6,7},{7,6},{8,9},{9,8},{10,11... | collective-permute-start | bytes 1953800 | tf_op jit(solution)/shard_map/ppermute | solution.py:44
  44.0 12.1 %collective-permute-start.12 = (bf16[848,384]{1,0:T(8,128)(2,1)S(1)}, bf16[848,384]{1,0:T(8,128)(2,1)}, u32[]{:S(2)}, u32[]{:S(2)}) collective-permute-start(bf16[848,384]{1,0:T(8,128)(2,1)S(1)} %collective-permute-done.6.refs_2_), channel_id=1, source_target_pairs={{0,1},{1,0},{2,3},{3,2},{4,5},{5,4},{6,7},{7,6},{8,9},{9,8},{10,11... | collective-permute-start | bytes 1953800 | tf_op jit(solution)/shard_map/ppermute | solution.py:44
  46.7 23.2 %collective-permute-start.13 = (bf16[1024,384]{1,0:T(8,128)(2,1)}, bf16[1024,384]{1,0:T(8,128)(2,1)}, u32[]{:S(2)}, u32[]{:S(2)}) collective-permute-start(bf16[1024,384]{1,0:T(8,128)(2,1)} %get-tuple-element.208), channel_id=1, source_target_pairs={{0,2},{1,3},{2,0},{3,1},{4,6},{5,7},{6,4},{7,5},{8,10},{9,11},{10,... | collective-permute-start | bytes 2359304 | tf_op jit(solution)/shard_map/ppermute | solution.py:44
  56.1 14.8 %collective-permute-start.16 = (bf16[192,1536]{1,0:T(8,128)(2,1)}, bf16[192,1536]{1,0:T(8,128)(2,1)}, u32[]{:S(2)}, u32[]{:S(2)}) collective-permute-start(bf16[192,1536]{1,0:T(8,128)(2,1)} %collective-permute-done.8.refs_0_), channel_id=1, source_target_pairs={{0,4},{1,5},{2,6},{3,7},{4,0},{5,1},{6,2},{7,3},{8,12},{9,13},{10,... | collective-permute-start | bytes 1769480 | tf_op jit(solution)/shard_map/ppermute | solution.py:44
  57.6 14.2 %collective-permute-start.17 = (bf16[192,1536]{1,0:T(8,128)(2,1)}, bf16[192,1536]{1,0:T(8,128)(2,1)}, u32[]{:S(2)}, u32[]{:S(2)}) collective-permute-start(bf16[192,1536]{1,0:T(8,128)(2,1)} %collective-permute-done.8.refs_0_), channel_id=1, source_target_pairs={{0,8},{1,9},{2,10},{3,11},{4,12},{5,13},{6,14},{7,15},{8,0},{9,1},... | collective-permute-start | bytes 1769480 | tf_op jit(solution)/shard_map/ppermute | solution.py:44
  71.9 20.3 %collective-permute-start.20 = (bf16[768,1536]{1,0:T(8,128)(2,1)}, bf16[768,1536]{1,0:T(8,128)(2,1)}, u32[]{:S(2)}, u32[]{:S(2)}) collective-permute-start(bf16[768,1536]{1,0:T(8,128)(2,1)} %refs_4_.1), channel_id=1, source_target_pairs={{0,1},{1,0},{2,3},{3,2},{4,5},{5,4},{6,7},{7,6},{8,9},{9,8},{10,11... | collective-permute-start | bytes 7077896 | tf_op jit(solution)/shard_map/ppermute | solution.py:44
  71.9 20.3 %collective-permute-start.19 = (bf16[1024,384]{1,0:T(8,128)(2,1)}, bf16[1024,384]{1,0:T(8,128)(2,1)}, u32[]{:S(2)}, u32[]{:S(2)}) collective-permute-start(bf16[1024,384]{1,0:T(8,128)(2,1)} %get-tuple-element.224), channel_id=1, source_target_pairs={{0,2},{1,3},{2,0},{3,1},{4,6},{5,7},{6,4},{7,5},{8,10},{9,11},{10,... | collective-permute-start | bytes 2359304 | tf_op jit(solution)/shard_map/ppermute | solution.py:44
  92.1 41.8 %all-to-all-start = ((f32[8,392,128]{2,1,0:T(8,128)}), f32[8,392,128]{2,1,0:T(8,128)S(1)}, u32[]{:S(2)}, u32[]{:S(2)}) async-start(f32[8,392,128]{2,1,0:T(8,128)} %copy-done.39), calls=%async_computation | async-start | bytes 3211264 | tf_op jit(solution)/shard_map/all_to_all | solution.py:1232
  96.4 22.5 %collective-permute-start.21 = (bf16[1024,384]{1,0:T(8,128)(2,1)}, bf16[1024,384]{1,0:T(8,128)(2,1)}, u32[]{:S(2)}, u32[]{:S(2)}) collective-permute-start(bf16[1024,384]{1,0:T(8,128)(2,1)} %get-tuple-element.232), channel_id=1, source_target_pairs={{0,2},{1,3},{2,0},{3,1},{4,6},{5,7},{6,4},{7,5},{8,10},{9,11},{10,... | collective-permute-start | bytes 2359304 | tf_op jit(solution)/shard_map/ppermute | solution.py:44
  98.0 31.4 %collective-permute-start.24 = (bf16[1024,384]{1,0:T(8,128)(2,1)}, bf16[1024,384]{1,0:T(8,128)(2,1)}, u32[]{:S(2)}, u32[]{:S(2)}) collective-permute-start(bf16[1024,384]{1,0:T(8,128)(2,1)} %collective-permute-done.13.refs_6_.refs_3_), channel_id=1, source_target_pairs={{0,1},{1,0},{2,3},{3,2},{4,5},{5,4},{6,7},{7,6},{8,9},{9,8},{10,11... | collective-permute-start | bytes 2359304 | tf_op jit(solution)/shard_map/ppermute | solution.py:44
  98.0 31.4 %collective-permute-start.25 = (bf16[1024,384]{1,0:T(8,128)(2,1)}, bf16[1024,384]{1,0:T(8,128)(2,1)}, u32[]{:S(2)}, u32[]{:S(2)}) collective-permute-start(bf16[1024,384]{1,0:T(8,128)(2,1)} %collective-permute-done.19.refs_6_.refs_4_), channel_id=1, source_target_pairs={{0,1},{1,0},{2,3},{3,2},{4,5},{5,4},{6,7},{7,6},{8,9},{9,8},{10,11... | collective-permute-start | bytes 2359304 | tf_op jit(solution)/shard_map/ppermute | solution.py:44
  100.2 18.7 %collective-permute-start.22 = (bf16[96,1536]{1,0:T(8,128)(2,1)}, bf16[96,1536]{1,0:T(8,128)(2,1)}, u32[]{:S(2)}, u32[]{:S(2)}) collective-permute-start(bf16[96,1536]{1,0:T(8,128)(2,1)} %slice.127), channel_id=1, source_target_pairs={{0,4},{1,5},{2,6},{3,7},{4,0},{5,1},{6,2},{7,3},{8,12},{9,13},{10,... | collective-permute-start | bytes 884744 | tf_op jit(solution)/shard_map/ppermute | solution.py:44
  103.9 25.4 %collective-permute-start.23 = (bf16[96,1536]{1,0:T(8,128)(2,1)}, bf16[96,1536]{1,0:T(8,128)(2,1)}, u32[]{:S(2)}, u32[]{:S(2)}) collective-permute-start(bf16[96,1536]{1,0:T(8,128)(2,1)} %slice.128), channel_id=1, source_target_pairs={{0,8},{1,9},{2,10},{3,11},{4,12},{5,13},{6,14},{7,15},{8,0},{9,1},... | collective-permute-start | bytes 884744 | tf_op jit(solution)/shard_map/ppermute | solution.py:44
  138.7 21.8 %collective-permute-start.26 = (bf16[768,1536]{1,0:T(8,128)(2,1)}, bf16[768,1536]{1,0:T(8,128)(2,1)}, u32[]{:S(2)}, u32[]{:S(2)}) collective-permute-start(bf16[768,1536]{1,0:T(8,128)(2,1)} %laid.3.refs_2_.refs_6_), channel_id=1, source_target_pairs={{0,1},{1,0},{2,3},{3,2},{4,5},{5,4},{6,7},{7,6},{8,9},{9,8},{10,11... | collective-permute-start | bytes 7077896 | tf_op jit(solution)/shard_map/ppermute | solution.py:44
  139.3 32.9 %all-to-all-start.1 = ((bf16[8,384,128]{2,1,0:T(8,128)(2,1)}), bf16[8,384,128]{2,1,0:T(8,128)(2,1)S(1)}, u32[]{:S(2)}, u32[]{:S(2)}) async-start(bf16[8,384,128]{2,1,0:T(8,128)(2,1)} %copy-done.28), calls=%async_computation.1 | async-start | bytes 1572864 | tf_op jit(solution)/shard_map/all_to_all | solution.py:543
  144.8 11.9 %collective-permute-start.27 = (bf16[1024,384]{1,0:T(8,128)(2,1)}, bf16[1024,384]{1,0:T(8,128)(2,1)S(1)}, u32[]{:S(2)}, u32[]{:S(2)}) collective-permute-start(bf16[1024,384]{1,0:T(8,128)(2,1)} %collective-permute-done.21.refs_6_.refs_5_), channel_id=1, source_target_pairs={{0,1},{1,0},{2,3},{3,2},{4,5},{5,4},{6,7},{7,6},{8,9},{9,8},{10,11... | collective-permute-start | bytes 2359304 | tf_op jit(solution)/shard_map/ppermute | solution.py:44
  145.2 27.1 %collective-permute-start.28 = (bf16[256,1536]{1,0:T(8,128)(2,1)S(1)}, bf16[256,1536]{1,0:T(8,128)(2,1)}, u32[]{:S(2)}, u32[]{:S(2)}) collective-permute-start(bf16[256,1536]{1,0:T(8,128)(2,1)S(1)} %bitcast_select_fusion.grad_ref.refs_4_), channel_id=1, source_target_pairs={{0,2},{1,3},{2,0},{3,1},{4,6},{5,7},{6,4},{7,5},{8,10},{9,11},{10,... | collective-permute-start | bytes 2359304 | tf_op jit(solution)/shard_map/ppermute | solution.py:44
  172.3 20.8 %collective-permute-start.32 = (bf16[256,1536]{1,0:T(8,128)(2,1)S(1)}, bf16[256,1536]{1,0:T(8,128)(2,1)}, u32[]{:S(2)}, u32[]{:S(2)}) collective-permute-start(bf16[256,1536]{1,0:T(8,128)(2,1)S(1)} %bitcast_select_fusion.grad_ref.refs_4_), channel_id=1, source_target_pairs={{0,1},{1,0},{2,3},{3,2},{4,5},{5,4},{6,7},{7,6},{8,9},{9,8},{10,11... | collective-permute-start | bytes 2359304 | tf_op jit(solution)/shard_map/ppermute | solution.py:44
  172.4 19.4 %collective-permute-start.29 = (bf16[256,384]{1,0:T(8,128)(2,1)}, bf16[256,384]{1,0:T(8,128)(2,1)S(1)}, u32[]{:S(2)}, u32[]{:S(2)}) collective-permute-start(bf16[256,384]{1,0:T(8,128)(2,1)} %copy-done.21), channel_id=1, source_target_pairs={{0,1},{1,0},{2,3},{3,2},{4,5},{5,4},{6,7},{7,6},{8,9},{9,8},{10,11... | collective-permute-start | bytes 589832 | tf_op jit(solution)/shard_map/ppermute | solution.py:44
  172.9 19.5 %collective-permute-start.30 = (bf16[256,384]{1,0:T(8,128)(2,1)}, bf16[256,384]{1,0:T(8,128)(2,1)S(1)}, u32[]{:S(2)}, u32[]{:S(2)}) collective-permute-start(bf16[256,384]{1,0:T(8,128)(2,1)} %get-tuple-element.259), channel_id=1, source_target_pairs={{0,2},{1,3},{2,0},{3,1},{4,6},{5,7},{6,4},{7,5},{8,10},{9,11},{10,... | collective-permute-start | bytes 589832 | tf_op jit(solution)/shard_map/ppermute | solution.py:44
  173.3 19.8 %collective-permute-start.31 = (bf16[256,384]{1,0:T(8,128)(2,1)}, bf16[256,384]{1,0:T(8,128)(2,1)}, u32[]{:S(2)}, u32[]{:S(2)}) collective-permute-start(bf16[256,384]{1,0:T(8,128)(2,1)} %get-tuple-element.260), channel_id=1, source_target_pairs={{0,3},{1,2},{2,1},{3,0},{4,7},{5,6},{6,5},{7,4},{8,11},{9,10},{10,... | collective-permute-start | bytes 589832 | tf_op jit(solution)/shard_map/ppermute | solution.py:44
  193.1 45.1 %all-to-all-start.2 = ((f32[8,384,128]{2,1,0:T(8,128)}), f32[8,384,128]{2,1,0:T(8,128)}, u32[]{:S(2)}, u32[]{:S(2)}) async-start(f32[8,384,128]{2,1,0:T(8,128)} %bitcast.91), calls=%async_computation.2 | async-start | bytes 3145728 | tf_op jit(solution)/shard_map/all_to_all | solution.py:1265
  198.9 42.4 %collective-permute-start.35 = (bf16[256,3072]{1,0:T(8,128)(2,1)}, bf16[256,3072]{1,0:T(8,128)(2,1)}, u32[]{:S(2)}, u32[]{:S(2)}) collective-permute-start(bf16[256,3072]{1,0:T(8,128)(2,1)} %get-tuple-element.275.refs_0_.gate_ref), channel_id=1, source_target_pairs={{0,2},{1,3},{2,0},{3,1},{4,6},{5,7},{6,4},{7,5},{8,10},{9,11},{10,... | collective-permute-start | bytes 4718600 | tf_op jit(solution)/shard_map/ppermute | solution.py:44
  199.4 38.7 %collective-permute-start.33 = (bf16[256,1536]{1,0:T(8,128)(2,1)}, bf16[256,1536]{1,0:T(8,128)(2,1)}, u32[]{:S(2)}, u32[]{:S(2)}) collective-permute-start(bf16[256,1536]{1,0:T(8,128)(2,1)} %collective-permute-done.28.refs_6_), channel_id=1, source_target_pairs={{0,1},{1,0},{2,3},{3,2},{4,5},{5,4},{6,7},{7,6},{8,9},{9,8},{10,11... | collective-permute-start | bytes 2359304 | tf_op jit(solution)/shard_map/ppermute | solution.py:44
  202.2 45.7 %collective-permute-start.37 = (bf16[256,768]{1,0:T(8,128)(2,1)}, bf16[256,768]{1,0:T(8,128)(2,1)}, u32[]{:S(2)}, u32[]{:S(2)}) collective-permute-start(bf16[256,768]{1,0:T(8,128)(2,1)} %get-tuple-element.401), channel_id=1, source_target_pairs={{0,1},{1,0},{2,3},{3,2},{4,5},{5,4},{6,7},{7,6},{8,9},{9,8},{10,11... | collective-permute-start | bytes 1179656 | tf_op jit(solution)/shard_map/ppermute | solution.py:44
  202.7 45.2 %collective-permute-start.38 = (bf16[256,768]{1,0:T(8,128)(2,1)}, bf16[256,768]{1,0:T(8,128)(2,1)}, u32[]{:S(2)}, u32[]{:S(2)}) collective-permute-start(bf16[256,768]{1,0:T(8,128)(2,1)} %get-tuple-element.400), channel_id=1, source_target_pairs={{0,2},{1,3},{2,0},{3,1},{4,6},{5,7},{6,4},{7,5},{8,10},{9,11},{10,... | collective-permute-start | bytes 1179656 | tf_op jit(solution)/shard_map/ppermute | solution.py:44
  204.2 48.0 %collective-permute-start.39 = (bf16[256,768]{1,0:T(8,128)(2,1)}, bf16[256,768]{1,0:T(8,128)(2,1)}, u32[]{:S(2)}, u32[]{:S(2)}) collective-permute-start(bf16[256,768]{1,0:T(8,128)(2,1)} %get-tuple-element.399), channel_id=1, source_target_pairs={{0,3},{1,2},{2,1},{3,0},{4,7},{5,6},{6,5},{7,4},{8,11},{9,10},{10,... | collective-permute-start | bytes 1179656 | tf_op jit(solution)/shard_map/ppermute | solution.py:44
  240.8 21.0 %collective-permute-start.34 = (bf16[256,3072]{1,0:T(8,128)(2,1)S(1)}, bf16[256,3072]{1,0:T(8,128)(2,1)}, u32[]{:S(2)}, u32[]{:S(2)}) collective-permute-start(bf16[256,3072]{1,0:T(8,128)(2,1)S(1)} %copy-done.19), channel_id=1, source_target_pairs={{0,1},{1,0},{2,3},{3,2},{4,5},{5,4},{6,7},{7,6},{8,9},{9,8},{10,11... | collective-permute-start | bytes 4718600 | tf_op jit(solution)/shard_map/ppermute | solution.py:44
  241.4 20.4 %collective-permute-start.36 = (bf16[256,3072]{1,0:T(8,128)(2,1)}, bf16[256,3072]{1,0:T(8,128)(2,1)}, u32[]{:S(2)}, u32[]{:S(2)}) collective-permute-start(bf16[256,3072]{1,0:T(8,128)(2,1)} %collective-permute-done.35.refs_2_), channel_id=1, source_target_pairs={{0,1},{1,0},{2,3},{3,2},{4,5},{5,4},{6,7},{7,6},{8,9},{9,8},{10,11... | collective-permute-start | bytes 4718600 | tf_op jit(solution)/shard_map/ppermute | solution.py:44
  241.4 48.3 %all-to-all-start.3 = ((bf16[8,384,128]{2,1,0:T(8,128)(2,1)}), bf16[8,384,128]{2,1,0:T(8,128)(2,1)}, u32[]{:S(2)}, u32[]{:S(2)}) async-start(bf16[8,384,128]{2,1,0:T(8,128)(2,1)} %carried.3), calls=%async_computation.3 | async-start | bytes 1572864 | tf_op jit(solution)/shard_map/all_to_all | solution.py:543
  260.3 29.5 %collective-permute-start.40 = (bf16[384,1536]{1,0:T(8,128)(2,1)}, bf16[384,1536]{1,0:T(8,128)(2,1)}, u32[]{:S(2)}, u32[]{:S(2)}) collective-permute-start(bf16[384,1536]{1,0:T(8,128)(2,1)} %dynamic-slice_convert_fusion.1), channel_id=1, source_target_pairs={{0,4},{1,5},{2,6},{3,7},{4,0},{5,1},{6,2},{7,3},{8,12},{9,13},{10,... | collective-permute-start | bytes 3538952 | tf_op jit(solution)/shard_map/ppermute | solution.py:44
  292.6 28.7 %collective-permute-start.41 = (bf16[1536,384]{1,0:T(8,128)(2,1)}, bf16[1536,384]{1,0:T(8,128)(2,1)}, u32[]{:S(2)}, u32[]{:S(2)}) collective-permute-start(bf16[1536,384]{1,0:T(8,128)(2,1)} %dynamic-slice_convert_fusion), channel_id=1, source_target_pairs={{0,4},{1,5},{2,6},{3,7},{4,0},{5,1},{6,2},{7,3},{8,12},{9,13},{10,... | collective-permute-start | bytes 3538952 | tf_op jit(solution)/shard_map/ppermute | solution.py:44
  298.6 15.7 %collective-permute-start.42 = (bf16[192,1536]{1,0:T(8,128)(2,1)S(1)}, bf16[192,1536]{1,0:T(8,128)(2,1)S(1)}, u32[]{:S(2)}, u32[]{:S(2)}) collective-permute-start(bf16[192,1536]{1,0:T(8,128)(2,1)S(1)} %dynamic-slice_convert_fusion.5), channel_id=1, source_target_pairs={{0,8},{1,9},{2,10},{3,11},{4,12},{5,13},{6,14},{7,15},{8,0},{9,1},... | collective-permute-start | bytes 1769480 | tf_op jit(solution)/shard_map/ppermute | solution.py:44
  328.3 25.3 %collective-permute-start.45 = (bf16[256,1792]{1,0:T(8,128)(2,1)S(1)}, bf16[256,1792]{1,0:T(8,128)(2,1)}, u32[]{:S(2)}, u32[]{:S(2)}) collective-permute-start(bf16[256,1792]{1,0:T(8,128)(2,1)S(1)} %slice_dynamic-update-slice_fusion.refs_0_), channel_id=1, source_target_pairs={{0,2},{1,3},{2,0},{3,1},{4,6},{5,7},{6,4},{7,5},{8,10},{9,11},{10,... | collective-permute-start | bytes 2752520 | tf_op jit(solution)/shard_map/ppermute | solution.py:44
  329.1 24.5 %collective-permute-start.46 = (bf16[256,1792]{1,0:T(8,128)(2,1)S(1)}, bf16[256,1792]{1,0:T(8,128)(2,1)S(1)}, u32[]{:S(2)}, u32[]{:S(2)}) collective-permute-start(bf16[256,1792]{1,0:T(8,128)(2,1)S(1)} %slice_dynamic-update-slice_fusion.refs_0_), channel_id=1, source_target_pairs={{0,1},{1,0},{2,3},{3,2},{4,5},{5,4},{6,7},{7,6},{8,9},{9,8},{10,11... | collective-permute-start | bytes 2752520 | tf_op jit(solution)/shard_map/ppermute | solution.py:44
  331.5 22.1 %collective-permute-start.47 = (bf16[768,384]{1,0:T(8,128)(2,1)S(1)}, bf16[768,384]{1,0:T(8,128)(2,1)S(1)}, u32[]{:S(2)}, u32[]{:S(2)}) collective-permute-start(bf16[768,384]{1,0:T(8,128)(2,1)S(1)} %dynamic-slice_convert_fusion.4), channel_id=1, source_target_pairs={{0,8},{1,9},{2,10},{3,11},{4,12},{5,13},{6,14},{7,15},{8,0},{9,1},... | collective-permute-start | bytes 1769480 | tf_op jit(solution)/shard_map/ppermute | solution.py:44
  333.1 19.5 %collective-permute-start.44 = (bf16[96,1536]{1,0:T(8,128)(2,1)S(1)}, bf16[96,1536]{1,0:T(8,128)(2,1)S(1)}, u32[]{:S(2)}, u32[]{:S(2)}) collective-permute-start(bf16[96,1536]{1,0:T(8,128)(2,1)S(1)} %dynamic-slice_convert_fusion.9), channel_id=1, source_target_pairs={{0,16},{1,17},{2,18},{3,19},{4,20},{5,21},{6,22},{7,23},{8,24},{9,... | collective-permute-start | bytes 884744 | tf_op jit(solution)/shard_map/ppermute | solution.py:44
  356.6 24.5 %collective-permute-start.50 = (bf16[256,1664]{1,0:T(8,128)(2,1)S(1)}, bf16[256,1664]{1,0:T(8,128)(2,1)S(1)}, u32[]{:S(2)}, u32[]{:S(2)}) collective-permute-start(bf16[256,1664]{1,0:T(8,128)(2,1)S(1)} %pad_maximum_fusion.3.refs_0_), channel_id=1, source_target_pairs={{0,2},{1,3},{2,0},{3,1},{4,6},{5,7},{6,4},{7,5},{8,10},{9,11},{10,... | collective-permute-start | bytes 2555912 | tf_op jit(solution)/shard_map/ppermute | solution.py:44
  362.2 19.0 %collective-permute-start.51 = (bf16[896,384]{1,0:T(8,128)(2,1)S(1)}, bf16[896,384]{1,0:T(8,128)(2,1)S(1)}, u32[]{:S(2)}, u32[]{:S(2)}) collective-permute-start(bf16[896,384]{1,0:T(8,128)(2,1)S(1)} %dynamic-slice_convert_fusion.2), channel_id=1, source_target_pairs={{0,4},{1,5},{2,6},{3,7},{4,0},{5,1},{6,2},{7,3},{8,12},{9,13},{10,... | collective-permute-start | bytes 2064392 | tf_op jit(solution)/shard_map/ppermute | solution.py:44
  365.0 23.5 %collective-permute-start.53 = (bf16[96,1536]{1,0:T(8,128)(2,1)S(1)}, bf16[96,1536]{1,0:T(8,128)(2,1)}, u32[]{:S(2)}, u32[]{:S(2)}) collective-permute-start(bf16[96,1536]{1,0:T(8,128)(2,1)S(1)} %add_convert_fusion.1), channel_id=1, source_target_pairs={{0,16},{1,17},{2,18},{3,19},{4,20},{5,21},{6,22},{7,23},{8,24},{9,... | collective-permute-start | bytes 884744 | tf_op jit(solution)/shard_map/ppermute | solution.py:44
  366.6 26.8 %collective-permute-start.54 = (bf16[384,384]{1,0:T(8,128)(2,1)S(1)}, bf16[384,384]{1,0:T(8,128)(2,1)S(1)}, u32[]{:S(2)}, u32[]{:S(2)}) collective-permute-start(bf16[384,384]{1,0:T(8,128)(2,1)S(1)} %dynamic-slice_convert_fusion.8), channel_id=1, source_target_pairs={{0,16},{1,17},{2,18},{3,19},{4,20},{5,21},{6,22},{7,23},{8,24},{9,... | collective-permute-start | bytes 884744 | tf_op jit(solution)/shard_map/ppermute | solution.py:44
  394.3 30.1 %collective-permute-start.55 = (bf16[832,384]{1,0:T(8,128)(2,1)}, bf16[832,384]{1,0:T(8,128)(2,1)}, u32[]{:S(2)}, u32[]{:S(2)}) collective-permute-start(bf16[832,384]{1,0:T(8,128)(2,1)} %dynamic-slice_convert_fusion.3), channel_id=1, source_target_pairs={{0,4},{1,5},{2,6},{3,7},{4,0},{5,1},{6,2},{7,3},{8,12},{9,13},{10,... | collective-permute-start | bytes 1916936 | tf_op jit(solution)/shard_map/ppermute | solution.py:44
  396.4 25.8 %collective-permute-start.56 = (bf16[448,384]{1,0:T(8,128)(2,1)}, bf16[448,384]{1,0:T(8,128)(2,1)}, u32[]{:S(2)}, u32[]{:S(2)}) collective-permute-start(bf16[448,384]{1,0:T(8,128)(2,1)} %dynamic-slice_convert_fusion.6), channel_id=1, source_target_pairs={{0,8},{1,9},{2,10},{3,11},{4,12},{5,13},{6,14},{7,15},{8,0},{9,1},... | collective-permute-start | bytes 1032200 | tf_op jit(solution)/shard_map/ppermute | solution.py:44
  398.3 26.0 %collective-permute-start.57 = (bf16[192,1536]{1,0:T(8,128)(2,1)}, bf16[192,1536]{1,0:T(8,128)(2,1)}, u32[]{:S(2)}, u32[]{:S(2)}) collective-permute-start(bf16[192,1536]{1,0:T(8,128)(2,1)} %pad_maximum_fusion.6), channel_id=1, source_target_pairs={{0,8},{1,9},{2,10},{3,11},{4,12},{5,13},{6,14},{7,15},{8,0},{9,1},... | collective-permute-start | bytes 1769480 | tf_op jit(solution)/shard_map/ppermute | solution.py:44
  401.1 21.1 %collective-permute-start.58 = (bf16[384,384]{1,0:T(8,128)(2,1)}, bf16[384,384]{1,0:T(8,128)(2,1)}, u32[]{:S(2)}, u32[]{:S(2)}) collective-permute-start(bf16[384,384]{1,0:T(8,128)(2,1)} %add_convert_fusion), channel_id=1, source_target_pairs={{0,16},{1,17},{2,18},{3,19},{4,20},{5,21},{6,22},{7,23},{8,24},{9,... | collective-permute-start | bytes 884744 | tf_op jit(solution)/shard_map/ppermute | solution.py:44
  429.8 11.7 %collective-permute-start.60 = (bf16[416,384]{1,0:T(8,128)(2,1)}, bf16[416,384]{1,0:T(8,128)(2,1)}, u32[]{:S(2)}, u32[]{:S(2)}) collective-permute-start(bf16[416,384]{1,0:T(8,128)(2,1)} %dynamic-slice_convert_fusion.7), channel_id=1, source_target_pairs={{0,8},{1,9},{2,10},{3,11},{4,12},{5,13},{6,14},{7,15},{8,0},{9,1},... | collective-permute-start | bytes 958472 | tf_op jit(solution)/shard_map/ppermute | solution.py:44
  432.6 19.7 %collective-permute-start.61 = (bf16[768,384]{1,0:T(8,128)(2,1)S(1)}, bf16[768,384]{1,0:T(8,128)(2,1)}, u32[]{:S(2)}, u32[]{:S(2)}) collective-permute-start(bf16[768,384]{1,0:T(8,128)(2,1)S(1)} %pad_maximum_fusion.7), channel_id=1, source_target_pairs={{0,8},{1,9},{2,10},{3,11},{4,12},{5,13},{6,14},{7,15},{8,0},{9,1},... | collective-permute-start | bytes 1769480 | tf_op jit(solution)/shard_map/ppermute | solution.py:44
  435.3 36.3 %collective-permute-start.64 = (bf16[384,1536]{1,0:T(8,128)(2,1)S(1)}, bf16[384,1536]{1,0:T(8,128)(2,1)}, u32[]{:S(2)}, u32[]{:S(2)}) collective-permute-start(bf16[384,1536]{1,0:T(8,128)(2,1)S(1)} %pad_maximum_fusion.1), channel_id=1, source_target_pairs={{0,4},{1,5},{2,6},{3,7},{4,0},{5,1},{6,2},{7,3},{8,12},{9,13},{10,... | collective-permute-start | bytes 3538952 | tf_op jit(solution)/shard_map/ppermute | solution.py:44
  453.3 18.4 %collective-permute-start.65 = (bf16[224,384]{1,0:T(8,128)(2,1)S(1)}, bf16[224,384]{1,0:T(8,128)(2,1)S(1)}, u32[]{:S(2)}, u32[]{:S(2)}) collective-permute-start(bf16[224,384]{1,0:T(8,128)(2,1)S(1)} %add_convert_fusion.2), channel_id=1, source_target_pairs={{0,16},{1,17},{2,18},{3,19},{4,20},{5,21},{6,22},{7,23},{8,24},{9,... | collective-permute-start | bytes 516104 | tf_op jit(solution)/shard_map/ppermute | solution.py:44
  456.8 30.0 %collective-permute-start.68 = (bf16[1536,384]{1,0:T(8,128)(2,1)}, bf16[1536,384]{1,0:T(8,128)(2,1)}, u32[]{:S(2)}, u32[]{:S(2)}) collective-permute-start(bf16[1536,384]{1,0:T(8,128)(2,1)} %pad_maximum_fusion.2), channel_id=1, source_target_pairs={{0,4},{1,5},{2,6},{3,7},{4,0},{5,1},{6,2},{7,3},{8,12},{9,13},{10,... | collective-permute-start | bytes 3538952 | tf_op jit(solution)/shard_map/ppermute | solution.py:44
  459.7 12.0 %collective-permute-start.66 = (bf16[208,384]{1,0:T(8,128)(2,1)}, bf16[208,384]{1,0:T(8,128)(2,1)}, u32[]{:S(2)}, u32[]{:S(2)}) collective-permute-start(bf16[208,384]{1,0:T(8,128)(2,1)} %dynamic-slice_convert_fusion.11), channel_id=1, source_target_pairs={{0,16},{1,17},{2,18},{3,19},{4,20},{5,21},{6,22},{7,23},{8,24},{9,... | collective-permute-start | bytes 479240 | tf_op jit(solution)/shard_map/ppermute | solution.py:44
  471.8 15.1 %collective-permute-start.69 = (bf16[448,384]{1,0:T(8,128)(2,1)S(1)}, bf16[448,384]{1,0:T(8,128)(2,1)}, u32[]{:S(2)}, u32[]{:S(2)}) collective-permute-start(bf16[448,384]{1,0:T(8,128)(2,1)S(1)} %pad_maximum_fusion.8), channel_id=1, source_target_pairs={{0,8},{1,9},{2,10},{3,11},{4,12},{5,13},{6,14},{7,15},{8,0},{9,1},... | collective-permute-start | bytes 1032200 | tf_op jit(solution)/shard_map/ppermute | solution.py:44
  472.8 14.0 %collective-permute-start.70 = (bf16[208,384]{1,0:T(8,128)(2,1)S(1)}, bf16[208,384]{1,0:T(8,128)(2,1)S(1)}, u32[]{:S(2)}, u32[]{:S(2)}) collective-permute-start(bf16[208,384]{1,0:T(8,128)(2,1)S(1)} %add_convert_fusion.3), channel_id=1, source_target_pairs={{0,16},{1,17},{2,18},{3,19},{4,20},{5,21},{6,22},{7,23},{8,24},{9,... | collective-permute-start | bytes 479240 | tf_op jit(solution)/shard_map/ppermute | solution.py:44
  493.0 25.4 %collective-permute-start.74 = (bf16[896,384]{1,0:T(8,128)(2,1)}, bf16[896,384]{1,0:T(8,128)(2,1)}, u32[]{:S(2)}, u32[]{:S(2)}) collective-permute-start(bf16[896,384]{1,0:T(8,128)(2,1)} %pad_maximum_fusion.5), channel_id=1, source_target_pairs={{0,4},{1,5},{2,6},{3,7},{4,0},{5,1},{6,2},{7,3},{8,12},{9,13},{10,... | collective-permute-start | bytes 2064392 | tf_op jit(solution)/shard_map/ppermute | solution.py:44
  498.1 15.7 %collective-permute-start.73 = (f32[168,128]{1,0:T(8,128)S(1)}, f32[168,128]{1,0:T(8,128)S(1)}, u32[]{:S(2)}, u32[]{:S(2)}) collective-permute-start(f32[168,128]{1,0:T(8,128)S(1)} %add.448), channel_id=1, source_target_pairs={{0,4},{1,5},{2,6},{3,7},{4,0},{5,1},{6,2},{7,3},{8,12},{9,13},{10,... | collective-permute-start | bytes 258056 | tf_op jit(solution)/shard_map/ppermute | solution.py:44
  500.8 24.8 %collective-permute-start.75 = (bf16[832,384]{1,0:T(8,128)(2,1)}, bf16[832,384]{1,0:T(8,128)(2,1)}, u32[]{:S(2)}, u32[]{:S(2)}) collective-permute-start(bf16[832,384]{1,0:T(8,128)(2,1)} %pad_maximum_fusion.4), channel_id=1, source_target_pairs={{0,4},{1,5},{2,6},{3,7},{4,0},{5,1},{6,2},{7,3},{8,12},{9,13},{10,... | collective-permute-start | bytes 1916936 | tf_op jit(solution)/shard_map/ppermute | solution.py:44
  (130 other events, 875.8 us)
